TPU v7x, 32 devices: a whole 2x2x4 slice. The times are simulated.
32 devices in a mesh: grp: 8 (over z, x), bf: 4 (over y, core).
Axes of the slice: x: 2, y: 2, z: 4, core: 2. Of those that a mesh axis runs over, the one named last changes fastest.
Arguments:
- field: float32 [16, 65536], P(None, ('grp', 'bf')), may hold values from -6 to 6
- leaf_inverse: bfloat16 [128, 512, 512], P(('grp', 'bf')), may hold values from -0.25 to 0.25
- col_factor: bfloat16 [2, 64, 65536], P(None, None, ('grp', 'bf')), may hold values from -0.125 to 0.125
- row_factor: bfloat16 [2, 64, 65536], P(None, None, ('grp', 'bf')), may hold values from -0.75 to 0.75
- mixing: bfloat16 [32, 2, 4, 2, 64, 64], P(('grp', 'bf')), may hold values from -0.5 to 0.5
- row_owner: int32 [2, 8], replicated, may hold values from 0 to 7, as said below
- rank_perm: int32 [2, 64], replicated, may hold values from 0 to 63, each once within a row
Outputs:
- applied: float32 [16, 65536], P(None, ('grp', 'bf'))
Inputs may be any that keep to these rules, and one draw needn't show every extreme that they name: row_owner[l, g] = (g + s_l) mod 8; one level has s_l = 4 and the other s_l = 7, which level takes which drawn from the seed.
All inputs are finite; a program needn't handle non-finite values.
Results may differ from a plain program's by a relative error of at most 0.004.
Values sent between devices are 32-bit elements; how exact they have to be, the bound alone decides.
No kernel may reach another device: no remote copies, remote signals or barrier semaphores. Data moves between devices by JAX's collectives and lax.ppermute only.
A program may use at most 64 MiB of HBM per device.

v0:
```python
import jax
import jax.numpy as jnp
from jax import lax
from jax.sharding import PartitionSpec as P


def partner(value, axis, distance):
    mask = 2**distance
    pairs = [(source, source ^ mask) for source in range(lax.axis_size(axis))]
    return lax.ppermute(value, axis, pairs)


def shards(field, leaf_inverse, col_factor, row_factor, mixing, row_owner, rank_perm):
    hi = lax.Precision.HIGHEST
    vectors = field.shape[0]
    rows = field.shape[1]
    order = leaf_inverse.shape[1]
    levels = col_factor.shape[0]
    sections = mixing.shape[2]
    bits = lax.axis_size("bf").bit_length() - 1
    groups = lax.axis_size("grp")
    xb = field.astype(jnp.bfloat16)
    diag = jnp.einsum(
        "rnl,nlm->rnm",
        xb.reshape(vectors, rows // order, order),
        leaf_inverse,
        preferred_element_type=jnp.float32,
    ).reshape(vectors, rows)
    projected = jnp.einsum("rn,lkn->lrk", xb, col_factor, preferred_element_type=jnp.float32)
    states = jnp.stack(
        [jnp.take(projected[level], rank_perm[level], axis=1) for level in range(levels)]
    )
    own_mats = mixing[0, :, :, 0].astype(jnp.float32)
    oth_mats = mixing[0, :, :, 1].astype(jnp.float32)
    finals = []
    for level in range(levels):
        state = states[level]
        for section in range(sections):
            other = partner(state, "bf", section % bits)
            state = jnp.dot(state, own_mats[level, section], precision=hi) + jnp.dot(
                other, oth_mats[level, section], precision=hi
            )
        finals.append(state)
    states = jnp.stack(finals)
    rank = states.astype(jnp.bfloat16)
    outputs = jnp.einsum("lrk,lkn->lrn", rank, row_factor, preferred_element_type=jnp.float32)
    segment = lax.axis_index("grp")
    owners = lax.dynamic_slice_in_dim(row_owner, segment, 1, 1)
    slots = (owners == jnp.arange(groups, dtype=jnp.int32)[None, :]).astype(jnp.float32)
    placed = jnp.einsum("lt,lrn->trn", slots, outputs, precision=hi)
    summed = lax.psum_scatter(placed, "grp", scatter_dimension=0, tiled=True)[0]
    return diag + summed


def solution(mesh):
    in_specs = (
        P(None, ("grp", "bf")),
        P(("grp", "bf"), None, None),
        P(None, None, ("grp", "bf")),
        P(None, None, ("grp", "bf")),
        P(("grp", "bf"), None, None, None, None, None),
        P(),
        P(),
    )
    out_specs = P(None, ("grp", "bf"))
    return jax.shard_map(shards, mesh=mesh, in_specs=in_specs, out_specs=out_specs, check_vma=False)
```

profile of v0, /device:TPU:0, one launch (start us, length us, event | category | flops | bytes accessed | tf_op | source)
XLA Modules:
  0.0 102.2 jit_solution(2980974666530660900)
XLA Ops:
  6.5 0.9 compare_and_fusion.1
  7.4 0.9 convert_element_type.2
  8.3 1.3 %convolution_bitcast_fusion.1 = f32[2,16,64]{2,1,0:T(8,128)S(1)} fusion(bf16[2,64,2048]{2,1,0:T(8,128)(2,1)} %param.11, bf16[16,2048]{1,0:T(8,128)(2,1)S(1)} %convert_element_type.2), kind=kOutput, calls=%fused_computation.3 | convolution fusion | flops 8388608 | bytes 598016 | tf_op jit(solution)/shard_map/rn,lkn->lrk/dot_general | solution.py:29
  9.7 0.1 copy.17
  9.8 0.6 gather_fusion
  10.4 0.1 select_bitcast_fusion.1
  10.5 0.5 collective-permute-start
  10.9 0.1 copy.18
  11.0 0.6 gather_fusion.1
  11.6 0.1 select_bitcast_fusion
  11.7 0.1 collective-permute-start.4
  11.8 1.0 slice_bitcast_fusion
  12.8 0.2 fusion.16
  13.0 0.2 fusion.12
  13.2 0.9 dynamic-slice_reduce_fusion
  14.1 0.0 collective-permute-done
  14.1 0.2 convolution_add_fusion.7
  14.3 0.1 fusion.15
  14.4 3.0 %collective-permute-start.1 = (f32[16,64]{1,0:T(8,128)S(1)}, f32[16,64]{1,0:T(8,128)S(1)}, u32[]{:S(2)}, u32[]{:S(2)}) collective-permute-start(f32[16,64]{1,0:T(8,128)S(1)} %convolution_add_fusion.7), channel_id=1, source_target_pairs={{0,2},{1,3},{2,0},{3,1},{4,6},{5,7},{6,4},{7,5},{8,10},{9,11},{10,... | collective-permute-start | bytes 12296 | tf_op jit(solution)/shard_map/ppermute | solution.py:10
  17.4 0.0 collective-permute-done.4
  17.4 0.2 convolution_add_fusion.3
  17.6 0.1 fusion.11
  17.7 1.3 %collective-permute-done.1 = f32[16,64]{1,0:T(8,128)S(1)} collective-permute-done((f32[16,64]{1,0:T(8,128)S(1)}, f32[16,64]{1,0:T(8,128)S(1)}, u32[]{:S(2)}, u32[]{:S(2)}) %collective-permute-start.1) | collective-permute-done | bytes 4128 | tf_op jit(solution)/shard_map/ppermute | solution.py:10
  19.0 0.1 convolution_add_fusion.6
  19.1 0.0 collective-permute-start.2
  19.1 0.1 fusion.14
  19.3 2.1 %collective-permute-done.5 = f32[16,64]{1,0:T(8,128)S(1)} collective-permute-done((f32[16,64]{1,0:T(8,128)S(1)}, f32[16,64]{1,0:T(8,128)S(1)}, u32[]{:S(2)}, u32[]{:S(2)}) %collective-permute-start.5) | collective-permute-done | bytes 4128 | tf_op jit(solution)/shard_map/ppermute | solution.py:10
  21.4 0.1 convolution_add_fusion.2
  21.5 0.1 fusion.10
  21.6 0.0 collective-permute-done.2
  21.6 0.1 convolution_add_fusion.5
  21.8 0.7 collective-permute-start.3
  22.5 0.1 fusion.13
  22.6 0.1 collective-permute-done.6
  22.7 0.1 convolution_add_fusion.1
  22.8 1.3 %collective-permute-start.7 = (f32[16,64]{1,0:T(8,128)S(1)}, f32[16,64]{1,0:T(8,128)S(1)}, u32[]{:S(2)}, u32[]{:S(2)}) collective-permute-start(f32[16,64]{1,0:T(8,128)S(1)} %convolution_add_fusion.1), channel_id=1, source_target_pairs={{0,2},{1,3},{2,0},{3,1},{4,6},{5,7},{6,4},{7,5},{8,10},{9,11},{10,... | collective-permute-start | bytes 12296 | tf_op jit(solution)/shard_map/ppermute | solution.py:10
  24.1 0.1 fusion.9
  24.2 1.2 %collective-permute-done.3 = f32[16,64]{1,0:T(8,128)S(1)} collective-permute-done((f32[16,64]{1,0:T(8,128)S(1)}, f32[16,64]{1,0:T(8,128)S(1)}, u32[]{:S(2)}, u32[]{:S(2)}) %collective-permute-start.3) | collective-permute-done | bytes 4128 | tf_op jit(solution)/shard_map/ppermute | solution.py:10
  25.4 0.1 fusion.3
  25.6 0.9 collective-permute-done.7
  26.5 0.1 fusion.2
  26.6 0.2 fusion.17
  26.8 0.9 fusion.4
  27.7 1.6 %copy.20 = f32[8,16,2048]{2,1,0:T(8,128)} copy(f32[8,16,2048]{2,0,1:T(8,128)S(1)} %fusion.4) | data formatting | bytes 2097152 | tf_op jit(solution)/shard_map/lt,lrn->trn/dot_general | solution.py:50
  29.3 0.0 reduce-scatter.2.cloned.1.call-update
  29.3 0.4 convolution_bitcast_fusion
  29.7 64.1 %reduce-scatter.2.cloned.1.call-done = f32[1,16,2048]{2,1,0:T(8,128)} async-done(((f32[8,16,2048]{2,1,0:T(8,128)}), f32[1,16,2048]{2,1,0:T(8,128)}) %reduce-scatter.2.cloned.1.call-update) | async-done | bytes 131088 | tf_op jit(solution)/shard_map/reduce_scatter | solution.py:51
  93.8 1.6 %bitcast_add_fusion = f32[16,2048]{1,0:T(8,128)} fusion(f32[16,2048]{1,0:T(8,128)S(1)} %bitcast.108, f32[1,16,2048]{2,1,0:T(8,128)} %reduce-scatter.2.cloned.1.call-done), kind=kLoop, calls=%fused_computation.18 | loop fusion | flops 32768 | bytes 393216 | tf_op jit(solution)/shard_map/add | solution.py:52
  (11 shorter events, 0.1 us)
Async XLA Ops:
  6.5 22.8 %copy-start = (bf16[4,512,512]{2,1,0:T(8,128)(2,1)S(1)}, bf16[4,512,512]{2,1,0:T(8,128)(2,1)}, u32[]{:S(2)}) copy-start(bf16[4,512,512]{2,1,0:T(8,128)(2,1)} %param.10) | copy-start | bytes 6291460
  6.5 20.1 %copy-start.1 = (bf16[2,64,2048]{2,1,0:T(8,128)(2,1)S(1)}, bf16[2,64,2048]{2,1,0:T(8,128)(2,1)}, u32[]{:S(2)}) copy-start(bf16[2,64,2048]{2,1,0:T(8,128)(2,1)} %param.12) | copy-start | bytes 1572868
  6.5 87.3 %reduce-scatter.2.cloned.1.call-start = ((), (), s32[]{:S(2)}) async-start(), calls=%async_computation.1 | async-start | bytes 1179648 | tf_op jit(solution)/shard_map/reduce_scatter | solution.py:51
  10.5 3.6 %collective-permute-start = (f32[16,64]{0,1:T(8,128)S(1)}, f32[16,64]{0,1:T(8,128)S(1)}, u32[]{:S(2)}, u32[]{:S(2)}) collective-permute-start(f32[16,64]{0,1:T(8,128)S(1)} %select_bitcast_fusion.1), channel_id=1, source_target_pairs={{0,1},{1,0},{2,3},{3,2},{4,5},{5,4},{6,7},{7,6},{8,9},{9,8},{10,11... | collective-permute-start | bytes 12296 | tf_op jit(solution)/shard_map/ppermute | solution.py:10
  11.7 5.7 %collective-permute-start.4 = (f32[16,64]{0,1:T(8,128)S(1)}, f32[16,64]{0,1:T(8,128)S(1)}, u32[]{:S(2)}, u32[]{:S(2)}) collective-permute-start(f32[16,64]{0,1:T(8,128)S(1)} %select_bitcast_fusion), channel_id=1, source_target_pairs={{0,1},{1,0},{2,3},{3,2},{4,5},{5,4},{6,7},{7,6},{8,9},{9,8},{10,11... | collective-permute-start | bytes 12296 | tf_op jit(solution)/shard_map/ppermute | solution.py:10
  14.4 4.6 %collective-permute-start.1 = (f32[16,64]{1,0:T(8,128)S(1)}, f32[16,64]{1,0:T(8,128)S(1)}, u32[]{:S(2)}, u32[]{:S(2)}) collective-permute-start(f32[16,64]{1,0:T(8,128)S(1)} %convolution_add_fusion.7), channel_id=1, source_target_pairs={{0,2},{1,3},{2,0},{3,1},{4,6},{5,7},{6,4},{7,5},{8,10},{9,11},{10,... | collective-permute-start | bytes 12296 | tf_op jit(solution)/shard_map/ppermute | solution.py:10
  17.7 3.7 %collective-permute-start.5 = (f32[16,64]{1,0:T(8,128)S(1)}, f32[16,64]{1,0:T(8,128)S(1)}, u32[]{:S(2)}, u32[]{:S(2)}) collective-permute-start(f32[16,64]{1,0:T(8,128)S(1)} %convolution_add_fusion.3), channel_id=1, source_target_pairs={{0,2},{1,3},{2,0},{3,1},{4,6},{5,7},{6,4},{7,5},{8,10},{9,11},{10,... | collective-permute-start | bytes 12296 | tf_op jit(solution)/shard_map/ppermute | solution.py:10
  19.1 2.5 %collective-permute-start.2 = (f32[16,64]{1,0:T(8,128)S(1)}, f32[16,64]{1,0:T(8,128)S(1)}, u32[]{:S(2)}, u32[]{:S(2)}) collective-permute-start(f32[16,64]{1,0:T(8,128)S(1)} %convolution_add_fusion.6), channel_id=1, source_target_pairs={{0,1},{1,0},{2,3},{3,2},{4,5},{5,4},{6,7},{7,6},{8,9},{9,8},{10,11... | collective-permute-start | bytes 12296 | tf_op jit(solution)/shard_map/ppermute | solution.py:10
  21.5 1.2 %collective-permute-start.6 = (f32[16,64]{1,0:T(8,128)S(1)}, f32[16,64]{1,0:T(8,128)S(1)}, u32[]{:S(2)}, u32[]{:S(2)}) collective-permute-start(f32[16,64]{1,0:T(8,128)S(1)} %convolution_add_fusion.2), channel_id=1, source_target_pairs={{0,1},{1,0},{2,3},{3,2},{4,5},{5,4},{6,7},{7,6},{8,9},{9,8},{10,11... | collective-permute-start | bytes 12296 | tf_op jit(solution)/shard_map/ppermute | solution.py:10
  21.8 3.7 %collective-permute-start.3 = (f32[16,64]{1,0:T(8,128)S(1)}, f32[16,64]{1,0:T(8,128)S(1)}, u32[]{:S(2)}, u32[]{:S(2)}) collective-permute-start(f32[16,64]{1,0:T(8,128)S(1)} %convolution_add_fusion.5), channel_id=1, source_target_pairs={{0,2},{1,3},{2,0},{3,1},{4,6},{5,7},{6,4},{7,5},{8,10},{9,11},{10,... | collective-permute-start | bytes 12296 | tf_op jit(solution)/shard_map/ppermute | solution.py:10
  22.8 3.7 %collective-permute-start.7 = (f32[16,64]{1,0:T(8,128)S(1)}, f32[16,64]{1,0:T(8,128)S(1)}, u32[]{:S(2)}, u32[]{:S(2)}) collective-permute-start(f32[16,64]{1,0:T(8,128)S(1)} %convolution_add_fusion.1), channel_id=1, source_target_pairs={{0,2},{1,3},{2,0},{3,1},{4,6},{5,7},{6,4},{7,5},{8,10},{9,11},{10,... | collective-permute-start | bytes 12296 | tf_op jit(solution)/shard_map/ppermute | solution.py:10
Sparse Core Ops, SparseCore 0:
  29.4 64.3 reduce-scatter.1
where the time goes:
time: 102 us
  waiting for transfers between devices  69.8 us (68%)
  between operations  13.4 us (13%)
  starting transfers between devices  5.58 us (5%)
  matrix products  5.06 us (5%)
  local copies, waits for them, and re-layouts  4.86 us (5%)
  other arithmetic  3.51 us (3%)
    reduce_scatter x1, waiting for transfers between devices, shards(): summed = lax.psum_scatter(placed, 'grp', scatter_dimension=0, tiled=True)[0]  64.1 us
    ppermute x8, waiting for transfers between devices, partner(): return lax.ppermute(value, axis, pairs)  5.65 us
    ppermute x8, starting transfers between devices, partner(): return lax.ppermute(value, axis, pairs)  5.58 us
  transfers between devices with their start and end apart: 9, of which 6 were waited for; matrix products, arithmetic and copies ran while one was open for 5% of the time, Pallas kernels for 0%

commit v1 on v0

v1 whole, which is shorter than its diff:
```python
import jax
import jax.numpy as jnp
from jax import lax
from jax.sharding import PartitionSpec as P

HI = lax.Precision.HIGHEST


def partner(value, axis, distance):
    mask = 2**distance
    pairs = [(source, source ^ mask) for source in range(lax.axis_size(axis))]
    return lax.ppermute(value, axis, pairs)


def shifted(value, axis, distance):
    size = lax.axis_size(axis)
    return lax.ppermute(value, axis, [(source, (source + distance) % size) for source in range(size)])


def block_diagonal(mats):
    levels, k, _ = mats.shape
    eye = jnp.eye(levels, dtype=mats.dtype)
    return (mats[:, :, None, :] * eye[:, None, :, None]).reshape(levels * k, levels * k)


def shards(field, leaf_inverse, col_factor, row_factor, mixing, row_owner, rank_perm):
    vectors, rows = field.shape
    order = leaf_inverse.shape[1]
    levels, rank_size, _ = col_factor.shape
    sections = mixing.shape[2]
    bits = lax.axis_size("bf").bit_length() - 1
    groups = lax.axis_size("grp")
    width = levels * rank_size

    xb = field.astype(jnp.bfloat16)
    state = lax.dot_general(
        xb, col_factor.reshape(width, rows), (((1,), (1,)), ((), ())), preferred_element_type=jnp.float32
    )
    picks = (jnp.arange(rank_size, dtype=jnp.int32)[None, :, None] == rank_perm[:, None, :]).astype(jnp.float32)
    mats = mixing[0].astype(jnp.float32)
    weights = []
    for section in range(sections):
        own, oth = mats[:, section, 0], mats[:, section, 1]
        if section == 0:
            own = jnp.einsum("lij,ljk->lik", picks, own)
            oth = jnp.einsum("lij,ljk->lik", picks, oth)
        weights.append((block_diagonal(own), block_diagonal(oth)))
    for section in range(sections):
        other = partner(state, "bf", section % bits)
        own, oth = weights[section]
        state = jnp.dot(state, own, precision=HI) + jnp.dot(other, oth, precision=HI)
    rank = state.astype(jnp.bfloat16)
    first_is_half = row_owner[0, 0] == groups // 2
    lane_level = lax.broadcasted_iota(jnp.int32, (vectors, width), 1) // rank_size
    half = (lane_level == 0) == first_is_half
    expand = row_factor.reshape(width, rows)
    zero = jnp.zeros_like(rank)
    out_half = jnp.dot(jnp.where(half, rank, zero), expand, preferred_element_type=jnp.float32)
    out_below = jnp.dot(jnp.where(half, zero, rank), expand, preferred_element_type=jnp.float32)
    out_half = shifted(out_half, "grp", groups // 2)
    out_below = shifted(out_below, "grp", groups - 1)
    diag = jnp.einsum(
        "rnl,nlm->rnm",
        xb.reshape(vectors, rows // order, order),
        leaf_inverse,
        preferred_element_type=jnp.float32,
    ).reshape(vectors, rows)
    return diag + out_half + out_below


def solution(mesh):
    in_specs = (
        P(None, ("grp", "bf")),
        P(("grp", "bf"), None, None),
        P(None, None, ("grp", "bf")),
        P(None, None, ("grp", "bf")),
        P(("grp", "bf"), None, None, None, None, None),
        P(),
        P(),
    )
    out_specs = P(None, ("grp", "bf"))
    return jax.shard_map(shards, mesh=mesh, in_specs=in_specs, out_specs=out_specs, check_vma=False)
```

time: 102 us -> 36.6 us (0.36)
  the two profiles are of different devices: /device:TPU:0 before, /device:TPU:24 now
where the time goes in v1:
time: 36.6 us; the launch traced here: 36.2 us
  waiting for transfers between devices  13.7 us (37%)
  matrix products  7.07 us (19%)
  other arithmetic  5.14 us (14%)
  starting transfers between devices  4.88 us (13%)
  local copies, waits for them, and re-layouts  4.72 us (13%)
  between operations  0.73 us (2%)
    ppermute x2, waiting for transfers between devices, shifted(): lax.ppermute(value, axis, [(source, (source + distance) % size) for sourc...  8.71 us
    ppermute x4, waiting for transfers between devices, partner(): return lax.ppermute(value, axis, pairs)  4.97 us
    mul x9, local copies, waits for them, and re-layouts, block_diagonal(): mats[:, :, None, :] * eye[:, None, :, None]  3.49 us
    ppermute x4, starting transfers between devices, partner(): return lax.ppermute(value, axis, pairs)  3.12 us
    ppermute x2, starting transfers between devices, shifted(): lax.ppermute(value, axis, [(source, (source + distance) % size) for sourc...  1.76 us
    dot_general x4, matrix products, shards(): jnp.dot(other, oth, precision=HI)  1.47 us
    dot_general x1, matrix products, shards(): lax.dot_general(xb, col_factor.reshape(width, rows), (((1,), (1,)), ((),...  1.28 us
    mul x1, other arithmetic, block_diagonal(): mats[:, :, None, :] * eye[:, None, :, None]  1.21 us
  transfers between devices with their start and end apart: 6, of which 4 were waited for; matrix products, arithmetic and copies ran while one was open for 30% of the time, Pallas kernels for 0%

profile of v1, /device:TPU:24, one launch (start us, length us, event | category | flops | bytes accessed | tf_op | source)
XLA Modules:
  0.0 36.2 jit_solution(14537528437097759336)
XLA Ops:
  0.0 0.0 copy-start
  0.0 1.1 %convert_element_type.38 = bf16[16,2048]{1,0:T(8,128)(2,1)S(1)} convert(f32[16,2048]{1,0:T(8,128)} %param.7) | non-fusion elementwise | flops 32768 | bytes 196608 | tf_op jit(solution)/shard_map/convert_element_type | solution.py:35
  1.1 1.3 %fusion.31 = f32[16,128]{1,0:T(8,128)S(1)} fusion(bf16[16,2048]{1,0:T(8,128)(2,1)S(1)} %convert_element_type.38, bf16[128,2048]{1,0:T(8,128)(2,1)} %bitcast.57), kind=kOutput, calls=%fused_computation.60 | convolution fusion | flops 8388608 | bytes 598016 | tf_op jit(solution)/shard_map/dot_general | solution.py:36
  2.3 0.0 collective-permute-start
  2.3 1.1 %fusion.30 = (f32[2,4,2,64,64]{4,3,0,2,1:T(8,128)S(1)}, bf16[2,4,2,64,64]{4,3,0,2,1:T(8,128)(2,1)S(1)}) fusion(bf16[1,2,4,2,64,64]{5,4,3,2,1,0:T(8,128)(2,1)} %param.11), kind=kLoop, calls=%fused_computation.59 | loop fusion | flops 65536 | bytes 524288 | tf_op jit(solution)/shard_map/convert_element_type | solution.py:40
  3.4 0.8 %fusion.3 = f32[2,64,64]{2,1,0:T(8,128)S(1)} fusion(bf16[2,4,2,64,64]{4,3,0,2,1:T(8,128)(2,1)S(1)} %get-tuple-element.12, s32[2,64]{1,0:T(2,128)} %param.13), kind=kOutput, calls=%fused_computation.25 | convolution fusion | flops 1056768 | bytes 66048 | tf_op jit(solution)/shard_map/lij,ljk->lik/dot_general | solution.py:46
  4.2 0.8 %fusion.4 = f32[2,64,64]{2,1,0:T(8,128)S(1)} fusion(bf16[2,4,2,64,64]{4,3,0,2,1:T(8,128)(2,1)S(1)} %get-tuple-element.12, s32[2,64]{1,0:T(2,128)} %param.13), kind=kOutput, calls=%fused_computation.26 | convolution fusion | flops 1056768 | bytes 66048 | tf_op jit(solution)/shard_map/lij,ljk->lik/dot_general | solution.py:45
  5.0 0.5 %iota_shift-right-logical_fusion = (s32[128]{0:T(128)}, s32[128]{0:T(128)}) fusion(), kind=kLoop, calls=%fused_computation.51 | loop fusion | flops 256 | bytes 1024 | tf_op jit(solution)/shard_map/jit(floor_divide)/div | solution.py:54
  5.6 0.0 copy-start.1
  5.6 1.2 %broadcast_multiply_fusion = (f32[2,64,2,64]{3,2,1,0:T(2,128)S(1)}, f32[2,64,2,64]{3,2,1,0:T(2,128)}, f32[2,64,2,64]{3,2,1,0:T(2,128)S(1)}, f32[2,64,2,64]{3,2,1...) fusion(f32[2,64,64]{2,1,0:T(8,128)S(1)} %get-tuple-element.5, ...), kind=kLoop, calls=%fused_computation.16 | loop fusion | flops 131072 | bytes 786448 | tf_op jit(solution)/shard_map/mul | solution.py:23
  6.8 1.0 %mul.151 = f32[128,128]{1,0:T(8,128)S(1)} reshape(f32[2,64,2,64]{3,2,1,0:T(2,128)} %get-tuple-element.20) | data formatting | bytes 131072 | tf_op jit(solution)/shard_map/mul | solution.py:23
  7.9 0.2 fusion.32
  8.0 0.6 %compare_and_fusion = pred[128]{0:T(512)(128)(4,1)} fusion(), kind=kLoop, calls=%fused_computation.50 | loop fusion | flops 640 | bytes 128 | tf_op jit(solution)/shard_map/jit(floor_divide)/and | solution.py:54
  8.6 1.6 %mul.154 = f32[128,128]{1,0:T(8,128)} reshape(f32[2,64,2,64]{3,2,1,0:T(2,128)} %get-tuple-element.14) | data formatting | bytes 131072 | tf_op jit(solution)/shard_map/mul | solution.py:23
  10.3 0.1 mul.158
  10.4 0.1 mul.162
  10.5 0.1 mul.166
  10.6 0.1 mul.170
  10.8 0.1 mul.174
  10.9 0.1 mul.178
  11.0 1.2 %slice.27 = s32[1,1]{1,0:T(1,128)} slice(s32[2,8]{1,0:T(2,128)} %param.12), slice={[0:1], [0:1]} | slice | bytes 8 | tf_op jit(solution)/shard_map/slice | solution.py:53
  12.9 0.0 collective-permute-done
  12.9 1.0 %convolution_add_fusion.3 = f32[16,128]{1,0:T(8,128)S(1)} fusion(f32[16,128]{1,0:T(8,128)S(1)} %fusion.32, f32[16,128]{1,0:T(8,128)} %collective-permute-done, f32[128,128]{1,0:T(8,128)} %mul.154), kind=kOutput, calls=%fused_computation.4 | convolution fusion | flops 3147776 | bytes 90112 | tf_op jit(solution)/shard_map/dot_general | solution.py:51
  13.9 1.6 %collective-permute-start.1 = (f32[16,128]{1,0:T(8,128)S(1)}, f32[16,128]{1,0:T(8,128)S(1)}, u32[]{:S(2)}, u32[]{:S(2)}) collective-permute-start(f32[16,128]{1,0:T(8,128)S(1)} %convolution_add_fusion.3), channel_id=1, source_target_pairs={{0,2},{1,3},{2,0},{3,1},{4,6},{5,7},{6,4},{7,5},{8,10},{9,11},{10,... | collective-permute-start | bytes 24584 | tf_op jit(solution)/shard_map/ppermute | solution.py:12
  15.5 0.2 fusion.33
  15.6 2.0 %collective-permute-done.1 = f32[16,128]{1,0:T(8,128)S(1)} collective-permute-done((f32[16,128]{1,0:T(8,128)S(1)}, f32[16,128]{1,0:T(8,128)S(1)}, u32[]{:S(2)}, u32[]{:S(2)}) %collective-permute-start.1) | collective-permute-done | bytes 8224 | tf_op jit(solution)/shard_map/ppermute | solution.py:12
  17.6 0.2 convolution_add_fusion.2
  17.7 0.0 collective-permute-start.2
  17.8 0.2 fusion.34
  17.9 1.0 %collective-permute-done.2 = f32[16,128]{1,0:T(8,128)S(1)} collective-permute-done((f32[16,128]{1,0:T(8,128)S(1)}, f32[16,128]{1,0:T(8,128)S(1)}, u32[]{:S(2)}, u32[]{:S(2)}) %collective-permute-start.2) | collective-permute-done | bytes 8224 | tf_op jit(solution)/shard_map/ppermute | solution.py:12
  18.9 0.2 convolution_add_fusion.1
  19.1 1.5 %collective-permute-start.3 = (f32[16,128]{1,0:T(8,128)S(1)}, f32[16,128]{1,0:T(8,128)S(1)}, u32[]{:S(2)}, u32[]{:S(2)}) collective-permute-start(f32[16,128]{1,0:T(8,128)S(1)} %convolution_add_fusion.1), channel_id=1, source_target_pairs={{0,2},{1,3},{2,0},{3,1},{4,6},{5,7},{6,4},{7,5},{8,10},{9,11},{10,... | collective-permute-start | bytes 24584 | tf_op jit(solution)/shard_map/ppermute | solution.py:12
  20.6 0.2 fusion.35
  20.8 2.0 %collective-permute-done.3 = f32[16,128]{1,0:T(8,128)S(1)} collective-permute-done((f32[16,128]{1,0:T(8,128)S(1)}, f32[16,128]{1,0:T(8,128)S(1)}, u32[]{:S(2)}, u32[]{:S(2)}) %collective-permute-start.3) | collective-permute-done | bytes 8224 | tf_op jit(solution)/shard_map/ppermute | solution.py:12
  22.8 0.2 fusion
  22.9 0.0 copy-done.1
  22.9 0.9 %fusion.10 = f32[16,2048]{1,0:T(8,128)S(1)} fusion(bf16[128,2048]{1,0:T(8,128)(2,1)S(1)} %bitcast.54, bf16[16,128]{1,0:T(8,128)(2,1)S(1)} %fusion, s32[128]{0:T(128)} %get-tuple-element.21, s32[128]{0:T(128)} %get-tuple-element.22, pred[]{:T(512)} %bitcast.1, pred[128]{0:T(512)(128)(4,1)} %compare_and_fusion), kind=kOutput, calls=%fused_computation.35 | convolution fusion | flops 8396800 | bytes 660609 | tf_op jit(solution)/shard_map/dot_general | solution.py:58
  23.8 0.9 %fusion.12 = f32[16,2048]{1,0:T(8,128)S(1)} fusion(bf16[128,2048]{1,0:T(8,128)(2,1)S(1)} %bitcast.55, bf16[16,128]{1,0:T(8,128)(2,1)S(1)} %fusion, s32[128]{0:T(128)} %get-tuple-element.21, s32[128]{0:T(128)} %get-tuple-element.22, pred[]{:T(512)} %bitcast.1, pred[128]{0:T(512)(128)(4,1)} %compare_and_fusion), kind=kOutput, calls=%fused_computation.36 | convolution fusion | flops 8396800 | bytes 660609 | tf_op jit(solution)/shard_map/dot_general | solution.py:59
  24.7 0.4 %collective-permute-start.4 = (f32[16,2048]{1,0:T(8,128)S(1)}, f32[16,2048]{1,0:T(8,128)S(1)}, u32[]{:S(2)}, u32[]{:S(2)}) collective-permute-start(f32[16,2048]{1,0:T(8,128)S(1)} %fusion.10), channel_id=1, source_target_pairs={{0,16},{4,20},{8,24},{12,28},{16,0},{20,4},{24,8},{28,12},{1,17},{... | collective-permute-start | bytes 393224 | tf_op jit(solution)/shard_map/ppermute | solution.py:17
  25.0 1.4 %collective-permute-start.5 = (f32[16,2048]{1,0:T(8,128)S(1)}, f32[16,2048]{1,0:T(8,128)S(1)}, u32[]{:S(2)}, u32[]{:S(2)}) collective-permute-start(f32[16,2048]{1,0:T(8,128)S(1)} %fusion.12), channel_id=1, source_target_pairs={{0,28},{4,0},{8,4},{12,8},{16,12},{20,16},{24,20},{28,24},{1,29},{... | collective-permute-start | bytes 393224 | tf_op jit(solution)/shard_map/ppermute | solution.py:17
  26.4 0.0 copy-done
  26.4 0.4 %convolution_bitcast_fusion = f32[4,2,8,512]{3,2,1,0:T(8,128)S(1)} fusion(bf16[4,512,512]{2,1,0:T(8,128)(2,1)S(1)} %copy-done, bf16[2,4,8,512]{3,2,1,0:T(8,128)(2,1)S(1)} %bitcast.56), kind=kOutput, calls=%fused_computation | convolution fusion | flops 33554432 | bytes 2293760 | tf_op jit(solution)/shard_map/rnl,nlm->rnm/dot_general | solution.py:62
  26.8 8.7 %collective-permute-done.4 = f32[16,2048]{1,0:T(8,128)S(1)} collective-permute-done((f32[16,2048]{1,0:T(8,128)S(1)}, f32[16,2048]{1,0:T(8,128)S(1)}, u32[]{:S(2)}, u32[]{:S(2)}) %collective-permute-start.4) | collective-permute-done | bytes 131104 | tf_op jit(solution)/shard_map/ppermute | solution.py:17
  35.5 0.0 collective-permute-done.5
  35.5 0.7 %add_add_fusion = f32[16,2048]{1,0:T(8,128)} fusion(f32[16,2048]{1,0:T(8,128)S(1)} %collective-permute-done.5, f32[16,2048]{1,0:T(8,128)S(1)} %bitcast.58, f32[16,2048]{1,0:T(8,128)S(1)} %collective-permute-done.4), kind=kLoop, calls=%fused_computation.7 | loop fusion | flops 65536 | bytes 524288 | tf_op jit(solution)/shard_map/add | solution.py:68
  (3 shorter events, 0.1 us)
Async XLA Ops:
  0.0 26.4 %copy-start = (bf16[4,512,512]{2,1,0:T(8,128)(2,1)S(1)}, bf16[4,512,512]{2,1,0:T(8,128)(2,1)}, u32[]{:S(2)}) copy-start(bf16[4,512,512]{2,1,0:T(8,128)(2,1)} %param.8) | copy-start | bytes 6291460
  2.3 10.5 %collective-permute-start = (f32[16,128]{1,0:T(8,128)S(1)}, f32[16,128]{1,0:T(8,128)}, u32[]{:S(2)}, u32[]{:S(2)}) collective-permute-start(f32[16,128]{1,0:T(8,128)S(1)} %fusion.31), channel_id=1, source_target_pairs={{0,1},{1,0},{2,3},{3,2},{4,5},{5,4},{6,7},{7,6},{8,9},{9,8},{10,11... | collective-permute-start | bytes 24584 | tf_op jit(solution)/shard_map/ppermute | solution.py:12
  5.6 17.3 %copy-start.1 = (bf16[2,64,2048]{2,1,0:T(8,128)(2,1)S(1)}, bf16[2,64,2048]{2,1,0:T(8,128)(2,1)}, u32[]{:S(2)}) copy-start(bf16[2,64,2048]{2,1,0:T(8,128)(2,1)} %param.10) | copy-start | bytes 1572868
  13.9 3.7 %collective-permute-start.1 = (f32[16,128]{1,0:T(8,128)S(1)}, f32[16,128]{1,0:T(8,128)S(1)}, u32[]{:S(2)}, u32[]{:S(2)}) collective-permute-start(f32[16,128]{1,0:T(8,128)S(1)} %convolution_add_fusion.3), channel_id=1, source_target_pairs={{0,2},{1,3},{2,0},{3,1},{4,6},{5,7},{6,4},{7,5},{8,10},{9,11},{10,... | collective-permute-start | bytes 24584 | tf_op jit(solution)/shard_map/ppermute | solution.py:12
  17.7 1.2 %collective-permute-start.2 = (f32[16,128]{1,0:T(8,128)S(1)}, f32[16,128]{1,0:T(8,128)S(1)}, u32[]{:S(2)}, u32[]{:S(2)}) collective-permute-start(f32[16,128]{1,0:T(8,128)S(1)} %convolution_add_fusion.2), channel_id=1, source_target_pairs={{0,1},{1,0},{2,3},{3,2},{4,5},{5,4},{6,7},{7,6},{8,9},{9,8},{10,11... | collective-permute-start | bytes 24584 | tf_op jit(solution)/shard_map/ppermute | solution.py:12
  19.1 3.7 %collective-permute-start.3 = (f32[16,128]{1,0:T(8,128)S(1)}, f32[16,128]{1,0:T(8,128)S(1)}, u32[]{:S(2)}, u32[]{:S(2)}) collective-permute-start(f32[16,128]{1,0:T(8,128)S(1)} %convolution_add_fusion.1), channel_id=1, source_target_pairs={{0,2},{1,3},{2,0},{3,1},{4,6},{5,7},{6,4},{7,5},{8,10},{9,11},{10,... | collective-permute-start | bytes 24584 | tf_op jit(solution)/shard_map/ppermute | solution.py:12
  24.7 10.9 %collective-permute-start.4 = (f32[16,2048]{1,0:T(8,128)S(1)}, f32[16,2048]{1,0:T(8,128)S(1)}, u32[]{:S(2)}, u32[]{:S(2)}) collective-permute-start(f32[16,2048]{1,0:T(8,128)S(1)} %fusion.10), channel_id=1, source_target_pairs={{0,16},{4,20},{8,24},{12,28},{16,0},{20,4},{24,8},{28,12},{1,17},{... | collective-permute-start | bytes 393224 | tf_op jit(solution)/shard_map/ppermute | solution.py:17
  25.0 10.5 %collective-permute-start.5 = (f32[16,2048]{1,0:T(8,128)S(1)}, f32[16,2048]{1,0:T(8,128)S(1)}, u32[]{:S(2)}, u32[]{:S(2)}) collective-permute-start(f32[16,2048]{1,0:T(8,128)S(1)} %fusion.12), channel_id=1, source_target_pairs={{0,28},{4,0},{8,4},{12,8},{16,12},{20,16},{24,20},{28,24},{1,29},{... | collective-permute-start | bytes 393224 | tf_op jit(solution)/shard_map/ppermute | solution.py:17

commit v2 on v1

v2 whole, which is shorter than its diff:
```python
import jax
import jax.numpy as jnp
from jax import lax
from jax.experimental import pallas as pl
from jax.experimental.pallas import tpu as pltpu
from jax.sharding import PartitionSpec as P

F32, BF16 = jnp.float32, jnp.bfloat16
VMEM = pl.BlockSpec(memory_space=pltpu.VMEM)
SMEM = pl.BlockSpec(memory_space=pltpu.SMEM)
NT = (((1,), (1,)), ((), ()))


def partner(value, axis, distance):
    mask = 2**distance
    pairs = [(source, source ^ mask) for source in range(lax.axis_size(axis))]
    return lax.ppermute(value, axis, pairs)


def shifted(value, axis, distance):
    size = lax.axis_size(axis)
    return lax.ppermute(value, axis, [(source, (source + distance) % size) for source in range(size)])


def call(body, shapes, specs, flops, moved, *operands):
    return pl.pallas_call(
        body,
        out_shape=shapes,
        in_specs=specs,
        out_specs=jax.tree.map(lambda _: VMEM, shapes),
        cost_estimate=pl.CostEstimate(flops=flops, bytes_accessed=moved, transcendentals=0),
        compiler_params=pltpu.CompilerParams(vmem_limit_bytes=16 * 2**20),
    )(*operands)


def project(field_ref, col_ref, out_ref):
    out_ref[...] = lax.dot_general(field_ref[...].astype(BF16), col_ref[...], NT, preferred_element_type=F32)


def build_weights(mixing_ref, perm_ref, out_ref):
    levels, sections, _, k, _ = mixing_ref.shape
    width = levels * k

    def placed(block, level):
        parts = [jnp.zeros((k, k), block.dtype)] * levels
        parts[level] = block
        return jnp.concatenate(parts, axis=1)

    rows = lax.broadcasted_iota(jnp.int32, (k, k), 0)
    picks = jnp.concatenate(
        [placed((rows == perm_ref[level : level + 1, :]).astype(F32), level) for level in range(levels)], axis=0
    ).astype(BF16)
    for section in range(sections):
        for side in range(2):
            mats = jnp.concatenate(
                [placed(mixing_ref[level, section, side].astype(F32), level) for level in range(levels)], axis=0
            ).astype(BF16)
            if section == 0:
                mats = jnp.dot(picks, mats, preferred_element_type=F32).astype(BF16)
            out_ref[section, side * width : (side + 1) * width, :] = mats


def exact_dot(value, factor):
    count = value.shape[0]
    high = value.astype(BF16)
    rest = value - high.astype(F32)
    middle = rest.astype(BF16)
    low = (rest - middle.astype(F32)).astype(BF16)
    terms = jnp.dot(jnp.concatenate([high, middle, low], axis=0), factor, preferred_element_type=F32)
    return terms[:count] + (terms[count : 2 * count] + terms[2 * count :])


def step(section, own_ref, other_ref, weights_ref, out_ref):
    both = jnp.concatenate([own_ref[...], other_ref[...]], axis=1)
    out_ref[...] = exact_dot(both, weights_ref[section])


def last_step(section, rank_size, half_shift, own_ref, other_ref, weights_ref, row_ref, owner_ref, half_ref, below_ref):
    both = jnp.concatenate([own_ref[...], other_ref[...]], axis=1)
    state = exact_dot(both, weights_ref[section])
    first_is_half = owner_ref[0, 0] == half_shift
    lane = lax.broadcasted_iota(jnp.int32, state.shape, 1)
    first = (lane < rank_size).astype(jnp.int32)
    half = first == first_is_half.astype(jnp.int32)
    rank_half = jnp.where(half, state, 0.0).astype(BF16)
    rank_below = jnp.where(half, 0.0, state).astype(BF16)
    count = state.shape[0]
    outs = jnp.dot(jnp.concatenate([rank_half, rank_below], axis=0), row_ref[...], preferred_element_type=F32)
    half_ref[...] = outs[:count]
    below_ref[...] = outs[count:]


def shards(field, leaf_inverse, col_factor, row_factor, mixing, row_owner, rank_perm):
    vectors, rows = field.shape
    order = leaf_inverse.shape[1]
    levels, rank_size, _ = col_factor.shape
    sections = mixing.shape[2]
    bits = lax.axis_size("bf").bit_length() - 1
    groups = lax.axis_size("grp")
    width = levels * rank_size

    state_shape = jax.ShapeDtypeStruct((vectors, width), F32)
    out_shape = jax.ShapeDtypeStruct((vectors, rows), F32)
    state = call(
        project, state_shape, [VMEM, VMEM], 2 * vectors * rows * width, 3 * rows * width,
        field, col_factor.reshape(width, rows),
    )
    weights = call(
        build_weights, jax.ShapeDtypeStruct((sections, 2 * width, width), BF16), [VMEM, VMEM],
        4 * width**3, 2 * sections * 2 * width * width, mixing[0], rank_perm,
    )
    for section in range(sections - 1):
        other = partner(state, "bf", section % bits)
        state = call(
            lambda *refs, section=section: step(section, *refs), state_shape, [VMEM] * 3,
            12 * vectors * width * width, 4 * width * width, state, other, weights,
        )
    other = partner(state, "bf", (sections - 1) % bits)
    out_half, out_below = call(
        lambda *refs: last_step(sections - 1, rank_size, groups // 2, *refs), [out_shape, out_shape],
        [VMEM] * 4 + [SMEM], 4 * vectors * width * rows, 4 * width * rows,
        state, other, weights, row_factor.reshape(width, rows), row_owner,
    )
    out_half = shifted(out_half, "grp", groups // 2)
    out_below = shifted(out_below, "grp", groups - 1)
    diag = jnp.einsum(
        "rnl,nlm->rnm",
        field.astype(BF16).reshape(vectors, rows // order, order),
        leaf_inverse,
        preferred_element_type=F32,
    ).reshape(vectors, rows)
    return diag + out_half + out_below


def solution(mesh):
    in_specs = (
        P(None, ("grp", "bf")),
        P(("grp", "bf"), None, None),
        P(None, None, ("grp", "bf")),
        P(None, None, ("grp", "bf")),
        P(("grp", "bf"), None, None, None, None, None),
        P(),
        P(),
    )
    out_specs = P(None, ("grp", "bf"))
    return jax.shard_map(shards, mesh=mesh, in_specs=in_specs, out_specs=out_specs, check_vma=False)
```

time: 36.6 us -> 25.8 us (0.70)
  matrix products: 7.07 us -> 0.37 us
  other arithmetic: 5.14 us -> 0.69 us
  Pallas kernels: 0 us -> 1.74 us
  local copies, waits for them, and re-layouts: 4.72 us -> 3.8 us
  between operations: 0.73 us -> 0.04 us
  waiting for transfers between devices: 13.7 us -> 14.1 us
    dot_general x14 -> x1, matrix products: 7.07 us -> 0.37 us  [shards(): jnp.einsum('rnl,nlm->rnm', field.astype(BF16).reshape(vectors, rows // or...]
    unnamed x4 -> x16, local copies, waits for them, and re-layouts: 0.03 us -> 3.78 us
    mul x9 -> x0, local copies, waits for them, and re-layouts: 3.49 us -> none  [block_diagonal(): mats[:, :, None, :] * eye[:, None, :, None]]
    convert_element_type x3 -> x1, other arithmetic: 2.12 us -> 0.01 us  [shards(): field.astype(BF16).reshape(vectors, rows // order, order)]
    pallas_call x0 -> x6, Pallas kernels: none -> 1.74 us  [call(): pl.pallas_call(body, out_shape=shapes, in_specs=specs, out_specs=jax.tree...]
    mul x1 -> x0, other arithmetic: 1.21 us -> none  [block_diagonal(): mats[:, :, None, :] * eye[:, None, :, None]]
    slice x1 -> x0, local copies, waits for them, and re-layouts: 1.19 us -> none  [shards(): first_is_half = row_owner[0, 0] == groups // 2]
    and x1 -> x0, other arithmetic: 0.6 us -> none  [shards(): lax.broadcasted_iota(jnp.int32, (vectors, width), 1) // rank_size]
  transfers between devices with their start and end apart: 6 -> 6, of which waited for: 4 -> 4; matrix products, arithmetic and copies ran while one was open for 30% -> 2% of each run, Pallas kernels for 0% -> 1%
where the time goes in v2:
time: 25.8 us; the launch traced here: 25.6 us
  waiting for transfers between devices  14.1 us (55%)
  starting transfers between devices  4.84 us (19%)
  local copies, waits for them, and re-layouts  3.8 us (15%)
  Pallas kernels  1.74 us (7%)
  other arithmetic  0.69 us (3%)
  matrix products  0.37 us (1%)
    ppermute x2, waiting for transfers between devices, shifted(): lax.ppermute(value, axis, [(source, (source + distance) % size) for sourc...  8.71 us
    ppermute x4, waiting for transfers between devices, partner(): return lax.ppermute(value, axis, pairs)  5.42 us
    unnamed x16, local copies, waits for them, and re-layouts  3.78 us
    ppermute x4, starting transfers between devices, partner(): return lax.ppermute(value, axis, pairs)  3.06 us
    ppermute x2, starting transfers between devices, shifted(): lax.ppermute(value, axis, [(source, (source + distance) % size) for sourc...  1.77 us
    pallas_call x6, Pallas kernels, call(): pl.pallas_call(body, out_shape=shapes, in_specs=specs, out_specs=jax.tree...  1.74 us
    add x1, other arithmetic, shards(): return diag + out_half + out_below  0.68 us
  transfers between devices with their start and end apart: 6, of which 4 were waited for; matrix products, arithmetic and copies ran while one was open for 2% of the time, Pallas kernels for 1%

profile of v2, /device:TPU:24, one launch (start us, length us, event | category | flops | bytes accessed | tf_op | source)
XLA Modules:
  0.0 25.6 jit_solution(8374456891834165027)
XLA Ops:
  0.0 0.0 copy-start
  0.0 0.0 copy-start.1
  0.0 0.0 copy-start.2
  0.0 1.2 %copy-done.2 = bf16[2,64,2048]{2,1,0:T(8,128)(2,1)S(1)} copy-done((bf16[2,64,2048]{2,1,0:T(8,128)(2,1)S(1)}, bf16[2,64,2048]{2,1,0:T(8,128)(2,1)}, u32[]{:S(2)}) %copy-start.2) | copy-done | bytes 524312
  1.2 0.0 copy-start.3
  1.2 0.9 %copy-done.3 = f32[16,2048]{1,0:T(8,128)S(1)} copy-done((f32[16,2048]{1,0:T(8,128)S(1)}, f32[16,2048]{1,0:T(8,128)}, u32[]{:S(2)}) %copy-start.3) | copy-done | bytes 131096
  2.1 0.0 copy-start.4
  2.1 0.0 copy-start.7
  2.1 0.2 shard_map.73.refs_0_
  2.3 0.0 collective-permute-start
  2.4 0.0 copy-start.5
  2.4 1.0 %copy-done.5 = bf16[1,2,4,2,64,64]{5,4,3,2,1,0:T(8,128)(2,1)S(1)} copy-done((bf16[1,2,4,2,64,64]{5,4,3,2,1,0:T(8,128)(2,1)S(1)}, bf16[1,2,4,2,64,64]{5,4,3,2,1,0:T(8,128)(2,1)}, u32[]{:S(2)}) %copy-start.5) | copy-done | bytes 131096
  3.3 0.0 copy-start.6
  3.3 0.7 %copy-done.6 = s32[2,64]{1,0:T(2,128)S(1)} copy-done((s32[2,64]{1,0:T(2,128)S(1)}, s32[2,64]{1,0:T(2,128)}, u32[]{:S(2)}) %copy-start.6) | copy-done | bytes 536
  4.0 0.2 shard_map.74.refs_2_
  4.2 0.0 collective-permute-done.refs_1_
  4.2 0.1 shard_map.75.refs_0_
  4.4 1.5 %collective-permute-start.1 = (f32[16,128]{1,0:T(8,128)S(1)}, f32[16,128]{1,0:T(8,128)S(1)}, u32[]{:S(2)}, u32[]{:S(2)}) collective-permute-start(f32[16,128]{1,0:T(8,128)S(1)} %shard_map.75.refs_0_), channel_id=1, source_target_pairs={{0,2},{1,3},{2,0},{3,1},{4,6},{5,7},{6,4},{7,5},{8,10},{9,11},{10,... | collective-permute-start | bytes 24584 | tf_op jit(solution)/shard_map/ppermute | solution.py:17
  5.9 2.1 %collective-permute-done.1.refs_1_ = f32[16,128]{1,0:T(8,128)S(1)} collective-permute-done((f32[16,128]{1,0:T(8,128)S(1)}, f32[16,128]{1,0:T(8,128)S(1)}, u32[]{:S(2)}, u32[]{:S(2)}) %collective-permute-start.1) | collective-permute-done | bytes 8224 | tf_op jit(solution)/shard_map/ppermute | solution.py:17
  8.0 0.1 shard_map.76.refs_0_
  8.2 0.0 collective-permute-start.2
  8.2 1.2 %collective-permute-done.2.refs_1_ = f32[16,128]{1,0:T(8,128)S(1)} collective-permute-done((f32[16,128]{1,0:T(8,128)S(1)}, f32[16,128]{1,0:T(8,128)S(1)}, u32[]{:S(2)}, u32[]{:S(2)}) %collective-permute-start.2) | collective-permute-done | bytes 8224 | tf_op jit(solution)/shard_map/ppermute | solution.py:17
  9.4 0.1 shard_map.77.refs_0_
  9.5 1.5 %collective-permute-start.3 = (f32[16,128]{1,0:T(8,128)S(1)}, f32[16,128]{1,0:T(8,128)S(1)}, u32[]{:S(2)}, u32[]{:S(2)}) collective-permute-start(f32[16,128]{1,0:T(8,128)S(1)} %shard_map.77.refs_0_), channel_id=1, source_target_pairs={{0,2},{1,3},{2,0},{3,1},{4,6},{5,7},{6,4},{7,5},{8,10},{9,11},{10,... | collective-permute-start | bytes 24584 | tf_op jit(solution)/shard_map/ppermute | solution.py:17
  11.0 0.0 copy-done.4
  11.0 2.1 %collective-permute-done.3.refs_1_ = f32[16,128]{1,0:T(8,128)S(1)} collective-permute-done((f32[16,128]{1,0:T(8,128)S(1)}, f32[16,128]{1,0:T(8,128)S(1)}, u32[]{:S(2)}, u32[]{:S(2)}) %collective-permute-start.3) | collective-permute-done | bytes 8224 | tf_op jit(solution)/shard_map/ppermute | solution.py:17
  13.1 0.0 copy-done.1
  13.1 0.0 copy-done.7
  13.2 0.9 %shard_map.78 = (f32[16,2048]{1,0:T(8,128)S(1)}, f32[16,2048]{1,0:T(8,128)S(1)}) custom-call(f32[16,128]{1,0:T(8,128)S(1)} %shard_map.77.refs_0_, f32[16,128]{1,0:T(8,128)S(1)} %collective-permute-done.3.refs_1_, bf16[4,256,128]{2,1,0:T(8,128)(2,1)S(1)} %shard_map.74.refs_2_, bf16[128,2048]{1,0:T(8,128)(2,1)S(1)} %bitcast.12, s32[2,8]{1,0:T(2,128)S(1)} %copy-done.7), custom_call_target="tpu_custom_call" | custom-call | flops 16777216 | bytes 1048576 | tf_op jit(solution)/shard_map/pallas_call | solution.py:26
  14.0 0.4 %collective-permute-start.4 = (f32[16,2048]{1,0:T(8,128)S(1)}, f32[16,2048]{1,0:T(8,128)S(1)}, u32[]{:S(2)}, u32[]{:S(2)}) collective-permute-start(f32[16,2048]{1,0:T(8,128)S(1)} %get-tuple-element.7), channel_id=1, source_target_pairs={{0,16},{4,20},{8,24},{12,28},{16,0},{20,4},{24,8},{28,12},{1,17},{... | collective-permute-start | bytes 393224 | tf_op jit(solution)/shard_map/ppermute | solution.py:22
  14.4 1.4 %collective-permute-start.5 = (f32[16,2048]{1,0:T(8,128)S(1)}, f32[16,2048]{1,0:T(8,128)S(1)}, u32[]{:S(2)}, u32[]{:S(2)}) collective-permute-start(f32[16,2048]{1,0:T(8,128)S(1)} %get-tuple-element.8), channel_id=1, source_target_pairs={{0,28},{4,0},{8,4},{12,8},{16,12},{20,16},{24,20},{28,24},{1,29},{... | collective-permute-start | bytes 393224 | tf_op jit(solution)/shard_map/ppermute | solution.py:22
  15.8 0.0 copy-done
  15.8 0.4 %convolution_bitcast_fusion = f32[4,2,8,512]{3,2,1,0:T(8,128)S(1)} fusion(bf16[4,512,512]{2,1,0:T(8,128)(2,1)S(1)} %copy-done, bf16[2,4,8,512]{3,2,1,0:T(8,128)(2,1)S(1)} %bitcast.16), kind=kOutput, calls=%fused_computation | convolution fusion | flops 33554432 | bytes 2293760 | tf_op jit(solution)/shard_map/rnl,nlm->rnm/dot_general | solution.py:126
  16.2 8.7 %collective-permute-done.4 = f32[16,2048]{1,0:T(8,128)S(1)} collective-permute-done((f32[16,2048]{1,0:T(8,128)S(1)}, f32[16,2048]{1,0:T(8,128)S(1)}, u32[]{:S(2)}, u32[]{:S(2)}) %collective-permute-start.4) | collective-permute-done | bytes 131104 | tf_op jit(solution)/shard_map/ppermute | solution.py:22
  24.9 0.0 collective-permute-done.5
  24.9 0.7 %add_add_fusion = f32[16,2048]{1,0:T(8,128)} fusion(f32[16,2048]{1,0:T(8,128)S(1)} %collective-permute-done.5, f32[16,2048]{1,0:T(8,128)S(1)} %bitcast.15, f32[16,2048]{1,0:T(8,128)S(1)} %collective-permute-done.4), kind=kLoop, calls=%fused_computation.1 | loop fusion | flops 65536 | bytes 524288 | tf_op jit(solution)/shard_map/add | solution.py:132
  (2 shorter events, 0.0 us)
Async XLA Ops:
  0.0 15.8 %copy-start = (bf16[4,512,512]{2,1,0:T(8,128)(2,1)S(1)}, bf16[4,512,512]{2,1,0:T(8,128)(2,1)}, u32[]{:S(2)}) copy-start(bf16[4,512,512]{2,1,0:T(8,128)(2,1)} %param.8) | copy-start | bytes 6291460
  0.0 13.1 %copy-start.1 = (bf16[2,64,2048]{2,1,0:T(8,128)(2,1)S(1)}, bf16[2,64,2048]{2,1,0:T(8,128)(2,1)}, u32[]{:S(2)}) copy-start(bf16[2,64,2048]{2,1,0:T(8,128)(2,1)} %param.10) | copy-start | bytes 1572868
  0.0 1.2 %copy-start.2 = (bf16[2,64,2048]{2,1,0:T(8,128)(2,1)S(1)}, bf16[2,64,2048]{2,1,0:T(8,128)(2,1)}, u32[]{:S(2)}) copy-start(bf16[2,64,2048]{2,1,0:T(8,128)(2,1)} %param.9) | copy-start | bytes 1572868
  1.2 0.9 %copy-start.3 = (f32[16,2048]{1,0:T(8,128)S(1)}, f32[16,2048]{1,0:T(8,128)}, u32[]{:S(2)}) copy-start(f32[16,2048]{1,0:T(8,128)} %field_ref.1) | copy-start | bytes 393220
  2.1 8.9 %copy-start.4 = (f32[16,2048]{1,0:T(8,128)S(1)}, f32[16,2048]{1,0:T(8,128)}, u32[]{:S(2)}) copy-start(f32[16,2048]{1,0:T(8,128)} %field_ref.1) | copy-start | bytes 393220
  2.1 11.0 %copy-start.7 = (s32[2,8]{1,0:T(2,128)S(1)}, s32[2,8]{1,0:T(2,128)}, u32[]{:S(2)}) copy-start(s32[2,8]{1,0:T(2,128)} %refs_4_.1) | copy-start | bytes 196
  2.3 1.9 %collective-permute-start = (f32[16,128]{1,0:T(8,128)S(1)}, f32[16,128]{1,0:T(8,128)S(1)}, u32[]{:S(2)}, u32[]{:S(2)}) collective-permute-start(f32[16,128]{1,0:T(8,128)S(1)} %shard_map.73.refs_0_), channel_id=1, source_target_pairs={{0,1},{1,0},{2,3},{3,2},{4,5},{5,4},{6,7},{7,6},{8,9},{9,8},{10,11... | collective-permute-start | bytes 24584 | tf_op jit(solution)/shard_map/ppermute | solution.py:17
  2.4 1.0 %copy-start.5 = (bf16[1,2,4,2,64,64]{5,4,3,2,1,0:T(8,128)(2,1)S(1)}, bf16[1,2,4,2,64,64]{5,4,3,2,1,0:T(8,128)(2,1)}, u32[]{:S(2)}) copy-start(bf16[1,2,4,2,64,64]{5,4,3,2,1,0:T(8,128)(2,1)} %param.11) | copy-start | bytes 393220
  3.3 0.7 %copy-start.6 = (s32[2,64]{1,0:T(2,128)S(1)}, s32[2,64]{1,0:T(2,128)}, u32[]{:S(2)}) copy-start(s32[2,64]{1,0:T(2,128)} %perm_ref.1) | copy-start | bytes 1540
  4.4 3.7 %collective-permute-start.1 = (f32[16,128]{1,0:T(8,128)S(1)}, f32[16,128]{1,0:T(8,128)S(1)}, u32[]{:S(2)}, u32[]{:S(2)}) collective-permute-start(f32[16,128]{1,0:T(8,128)S(1)} %shard_map.75.refs_0_), channel_id=1, source_target_pairs={{0,2},{1,3},{2,0},{3,1},{4,6},{5,7},{6,4},{7,5},{8,10},{9,11},{10,... | collective-permute-start | bytes 24584 | tf_op jit(solution)/shard_map/ppermute | solution.py:17
  8.2 1.2 %collective-permute-start.2 = (f32[16,128]{1,0:T(8,128)S(1)}, f32[16,128]{1,0:T(8,128)S(1)}, u32[]{:S(2)}, u32[]{:S(2)}) collective-permute-start(f32[16,128]{1,0:T(8,128)S(1)} %shard_map.76.refs_0_), channel_id=1, source_target_pairs={{0,1},{1,0},{2,3},{3,2},{4,5},{5,4},{6,7},{7,6},{8,9},{9,8},{10,11... | collective-permute-start | bytes 24584 | tf_op jit(solution)/shard_map/ppermute | solution.py:17
  9.5 3.7 %collective-permute-start.3 = (f32[16,128]{1,0:T(8,128)S(1)}, f32[16,128]{1,0:T(8,128)S(1)}, u32[]{:S(2)}, u32[]{:S(2)}) collective-permute-start(f32[16,128]{1,0:T(8,128)S(1)} %shard_map.77.refs_0_), channel_id=1, source_target_pairs={{0,2},{1,3},{2,0},{3,1},{4,6},{5,7},{6,4},{7,5},{8,10},{9,11},{10,... | collective-permute-start | bytes 24584 | tf_op jit(solution)/shard_map/ppermute | solution.py:17
  14.0 10.9 %collective-permute-start.4 = (f32[16,2048]{1,0:T(8,128)S(1)}, f32[16,2048]{1,0:T(8,128)S(1)}, u32[]{:S(2)}, u32[]{:S(2)}) collective-permute-start(f32[16,2048]{1,0:T(8,128)S(1)} %get-tuple-element.7), channel_id=1, source_target_pairs={{0,16},{4,20},{8,24},{12,28},{16,0},{20,4},{24,8},{28,12},{1,17},{... | collective-permute-start | bytes 393224 | tf_op jit(solution)/shard_map/ppermute | solution.py:22
  14.4 10.5 %collective-permute-start.5 = (f32[16,2048]{1,0:T(8,128)S(1)}, f32[16,2048]{1,0:T(8,128)S(1)}, u32[]{:S(2)}, u32[]{:S(2)}) collective-permute-start(f32[16,2048]{1,0:T(8,128)S(1)} %get-tuple-element.8), channel_id=1, source_target_pairs={{0,28},{4,0},{8,4},{12,8},{16,12},{20,16},{24,20},{28,24},{1,29},{... | collective-permute-start | bytes 393224 | tf_op jit(solution)/shard_map/ppermute | solution.py:22

commit v3 on v2

--- a/solution.py
+++ b/solution.py
@@ -7,7 +7,7 @@
 
 F32, BF16 = jnp.float32, jnp.bfloat16
 VMEM = pl.BlockSpec(memory_space=pltpu.VMEM)
-SMEM = pl.BlockSpec(memory_space=pltpu.SMEM)
+HBM = pl.BlockSpec(memory_space=pltpu.HBM)
 NT = (((1,), (1,)), ((), ()))
 
 
@@ -22,19 +22,28 @@
     return lax.ppermute(value, axis, [(source, (source + distance) % size) for source in range(size)])
 
 
-def call(body, shapes, specs, flops, moved, *operands):
+def call(body, shapes, specs, flops, moved, *operands, scratch=(), limit=16):
     return pl.pallas_call(
         body,
         out_shape=shapes,
         in_specs=specs,
         out_specs=jax.tree.map(lambda _: VMEM, shapes),
+        scratch_shapes=scratch,
         cost_estimate=pl.CostEstimate(flops=flops, bytes_accessed=moved, transcendentals=0),
-        compiler_params=pltpu.CompilerParams(vmem_limit_bytes=16 * 2**20),
+        compiler_params=pltpu.CompilerParams(vmem_limit_bytes=limit * 2**20),
     )(*operands)
 
 
-def project(field_ref, col_ref, out_ref):
+def project(field_hbm, col_hbm, mixing_hbm, perm_hbm, out_ref, mixing_ref, perm_ref, field_ref, col_ref, sems):
+    pairs = [(field_hbm, field_ref), (col_hbm, col_ref), (mixing_hbm, mixing_ref), (perm_hbm, perm_ref)]
+    copies = [pltpu.make_async_copy(source, target, sems.at[n]) for n, (source, target) in enumerate(pairs)]
+    for copy in copies:
+        copy.start()
+    copies[0].wait()
+    copies[1].wait()
     out_ref[...] = lax.dot_general(field_ref[...].astype(BF16), col_ref[...], NT, preferred_element_type=F32)
+    copies[2].wait()
+    copies[3].wait()
 
 
 def build_weights(mixing_ref, perm_ref, out_ref):
@@ -78,10 +87,9 @@
 def last_step(section, rank_size, half_shift, own_ref, other_ref, weights_ref, row_ref, owner_ref, half_ref, below_ref):
     both = jnp.concatenate([own_ref[...], other_ref[...]], axis=1)
     state = exact_dot(both, weights_ref[section])
-    first_is_half = owner_ref[0, 0] == half_shift
+    first_is_half = jnp.broadcast_to(owner_ref[0:1, 0:1], state.shape) == half_shift
     lane = lax.broadcasted_iota(jnp.int32, state.shape, 1)
-    first = (lane < rank_size).astype(jnp.int32)
-    half = first == first_is_half.astype(jnp.int32)
+    half = jnp.logical_xor(lane >= rank_size, first_is_half)
     rank_half = jnp.where(half, state, 0.0).astype(BF16)
     rank_below = jnp.where(half, 0.0, state).astype(BF16)
     count = state.shape[0]
@@ -101,13 +109,16 @@
 
     state_shape = jax.ShapeDtypeStruct((vectors, width), F32)
     out_shape = jax.ShapeDtypeStruct((vectors, rows), F32)
-    state = call(
-        project, state_shape, [VMEM, VMEM], 2 * vectors * rows * width, 3 * rows * width,
-        field, col_factor.reshape(width, rows),
+    state, mats, perm = call(
+        project,
+        [state_shape, jax.ShapeDtypeStruct(mixing.shape[1:], BF16), jax.ShapeDtypeStruct(rank_perm.shape, jnp.int32)],
+        [HBM] * 4, 2 * vectors * rows * width, 3 * rows * width,
+        *[pltpu.with_memory_space_constraint(x, pltpu.HBM) for x in (field, col_factor.reshape(width, rows), mixing[0], rank_perm)],
+        scratch=[pltpu.VMEM(field.shape, F32), pltpu.VMEM((width, rows), BF16), pltpu.SemaphoreType.DMA((4,))],
     )
     weights = call(
         build_weights, jax.ShapeDtypeStruct((sections, 2 * width, width), BF16), [VMEM, VMEM],
-        4 * width**3, 2 * sections * 2 * width * width, mixing[0], rank_perm,
+        4 * width**3, 2 * sections * 2 * width * width, mats, perm,
     )
     for section in range(sections - 1):
         other = partner(state, "bf", section % bits)
@@ -118,7 +129,7 @@
     other = partner(state, "bf", (sections - 1) % bits)
     out_half, out_below = call(
         lambda *refs: last_step(sections - 1, rank_size, groups // 2, *refs), [out_shape, out_shape],
-        [VMEM] * 4 + [SMEM], 4 * vectors * width * rows, 4 * width * rows,
+        [VMEM] * 5, 4 * vectors * width * rows, 4 * width * rows,
         state, other, weights, row_factor.reshape(width, rows), row_owner,
     )
     out_half = shifted(out_half, "grp", groups // 2)

time: 25.8 us -> 23.8 us (0.922)
  local copies, waits for them, and re-layouts: 3.8 us -> 0.04 us
  waiting for transfers between devices: 14.1 us -> 15.1 us
  Pallas kernels: 1.74 us -> 2.5 us
    unnamed x16 -> x8, local copies, waits for them, and re-layouts: 3.78 us -> 0.02 us
    ppermute x4, waiting for transfers between devices: 5.42 us -> 6.36 us  [partner(): return lax.ppermute(value, axis, pairs)]
    pallas_call x6, Pallas kernels: 1.74 us -> 2.5 us  [call(): pl.pallas_call(body, out_shape=shapes, in_specs=specs, out_specs=jax.tree...]
  transfers between devices with their start and end apart: 6 -> 6, of which waited for: 4 -> 5; matrix products, arithmetic and copies ran while one was open for 2% -> 2% of each run, Pallas kernels for 1% -> 1%
where the time goes in v3:
time: 23.8 us; the launch traced here: 23.6 us
  waiting for transfers between devices  15.1 us (63%)
  starting transfers between devices  4.9 us (21%)
  Pallas kernels  2.5 us (11%)
  other arithmetic  0.69 us (3%)
  matrix products  0.37 us (2%)
    ppermute x2, waiting for transfers between devices, shifted(): lax.ppermute(value, axis, [(source, (source + distance) % size) for sourc...  8.71 us
    ppermute x4, waiting for transfers between devices, partner(): return lax.ppermute(value, axis, pairs)  6.36 us
    ppermute x4, starting transfers between devices, partner(): return lax.ppermute(value, axis, pairs)  3.13 us
    pallas_call x6, Pallas kernels, call(): pl.pallas_call(body, out_shape=shapes, in_specs=specs, out_specs=jax.tree...  2.5 us
    ppermute x2, starting transfers between devices, shifted(): lax.ppermute(value, axis, [(source, (source + distance) % size) for sourc...  1.77 us
    add x1, other arithmetic, shards(): return diag + out_half + out_below  0.68 us
  transfers between devices with their start and end apart: 6, of which 5 were waited for; matrix products, arithmetic and copies ran while one was open for 2% of the time, Pallas kernels for 1%

profile of v3, /device:TPU:24, one launch (start us, length us, event | category | flops | bytes accessed | tf_op | source)
XLA Modules:
  0.0 23.6 jit_solution(10213001912249238377)
XLA Ops:
  0.0 0.0 copy-start
  0.0 0.0 copy-start.3
  0.0 0.0 copy-start.1
  0.0 0.0 copy-start.2
  0.0 1.5 %shard_map.73 = (f32[16,128]{1,0:T(8,128)S(1)}, bf16[2,4,2,64,64]{4,3,2,1,0:T(8,128)(2,1)S(1)}, s32[2,64]{1,0:T(2,128)S(1)}) custom-call(f32[16,2048]{1,0:T(8,128)} %field_hbm.1, bf16[128,2048]{1,0:T(8,128)(2,1)} %bitcast.13, bf16[2,4,2,64,64]{4,3,2,1,0:T(8,128)(2,1)} %bitcast.16, s32[2,64]{1,0:T(2,128)} %perm_hbm.1), custom_call_target="tpu_custom_call" | custom-call | flops 8388608 | bytes 786432 | tf_op jit(solution)/shard_map/pallas_call | solution.py:26
  1.6 0.1 collective-permute-start
  1.7 0.2 shard_map.74.refs_2_
  1.9 0.9 %collective-permute-done.refs_1_ = f32[16,128]{1,0:T(8,128)S(1)} collective-permute-done((f32[16,128]{1,0:T(8,128)S(1)}, f32[16,128]{1,0:T(8,128)S(1)}, u32[]{:S(2)}, u32[]{:S(2)}) %collective-permute-start) | collective-permute-done | bytes 8224 | tf_op jit(solution)/shard_map/ppermute | solution.py:17
  2.8 0.1 shard_map.75.refs_0_
  2.9 1.5 %collective-permute-start.1 = (f32[16,128]{1,0:T(8,128)S(1)}, f32[16,128]{1,0:T(8,128)S(1)}, u32[]{:S(2)}, u32[]{:S(2)}) collective-permute-start(f32[16,128]{1,0:T(8,128)S(1)} %shard_map.75.refs_0_), channel_id=1, source_target_pairs={{0,2},{1,3},{2,0},{3,1},{4,6},{5,7},{6,4},{7,5},{8,10},{9,11},{10,... | collective-permute-start | bytes 24584 | tf_op jit(solution)/shard_map/ppermute | solution.py:17
  4.5 2.1 %collective-permute-done.1.refs_1_ = f32[16,128]{1,0:T(8,128)S(1)} collective-permute-done((f32[16,128]{1,0:T(8,128)S(1)}, f32[16,128]{1,0:T(8,128)S(1)}, u32[]{:S(2)}, u32[]{:S(2)}) %collective-permute-start.1) | collective-permute-done | bytes 8224 | tf_op jit(solution)/shard_map/ppermute | solution.py:17
  6.6 0.1 shard_map.76.refs_0_
  6.7 0.0 collective-permute-start.2
  6.8 1.2 %collective-permute-done.2.refs_1_ = f32[16,128]{1,0:T(8,128)S(1)} collective-permute-done((f32[16,128]{1,0:T(8,128)S(1)}, f32[16,128]{1,0:T(8,128)S(1)}, u32[]{:S(2)}, u32[]{:S(2)}) %collective-permute-start.2) | collective-permute-done | bytes 8224 | tf_op jit(solution)/shard_map/ppermute | solution.py:17
  7.9 0.1 shard_map.77.refs_0_
  8.1 1.5 %collective-permute-start.3 = (f32[16,128]{1,0:T(8,128)S(1)}, f32[16,128]{1,0:T(8,128)S(1)}, u32[]{:S(2)}, u32[]{:S(2)}) collective-permute-start(f32[16,128]{1,0:T(8,128)S(1)} %shard_map.77.refs_0_), channel_id=1, source_target_pairs={{0,2},{1,3},{2,0},{3,1},{4,6},{5,7},{6,4},{7,5},{8,10},{9,11},{10,... | collective-permute-start | bytes 24584 | tf_op jit(solution)/shard_map/ppermute | solution.py:17
  9.6 0.0 copy-done.3
  9.6 2.1 %collective-permute-done.3.refs_1_ = f32[16,128]{1,0:T(8,128)S(1)} collective-permute-done((f32[16,128]{1,0:T(8,128)S(1)}, f32[16,128]{1,0:T(8,128)S(1)}, u32[]{:S(2)}, u32[]{:S(2)}) %collective-permute-start.3) | collective-permute-done | bytes 8224 | tf_op jit(solution)/shard_map/ppermute | solution.py:17
  11.7 0.0 copy-done.1
  11.7 0.0 copy-done.2
  11.7 0.3 %shard_map.78 = (f32[16,2048]{1,0:T(8,128)S(1)}, f32[16,2048]{1,0:T(8,128)S(1)}) custom-call(f32[16,128]{1,0:T(8,128)S(1)} %shard_map.77.refs_0_, f32[16,128]{1,0:T(8,128)S(1)} %collective-permute-done.3.refs_1_, bf16[4,256,128]{2,1,0:T(8,128)(2,1)S(1)} %shard_map.74.refs_2_, bf16[128,2048]{1,0:T(8,128)(2,1)S(1)} %bitcast.12, s32[2,8]{1,0:T(2,128)S(1)} %copy-done.2), custom_call_target="tpu_custom_call" | custom-call | flops 16777216 | bytes 1048576 | tf_op jit(solution)/shard_map/pallas_call | solution.py:26
  12.1 0.4 %collective-permute-start.4 = (f32[16,2048]{1,0:T(8,128)S(1)}, f32[16,2048]{1,0:T(8,128)S(1)}, u32[]{:S(2)}, u32[]{:S(2)}) collective-permute-start(f32[16,2048]{1,0:T(8,128)S(1)} %get-tuple-element.13), channel_id=1, source_target_pairs={{0,16},{4,20},{8,24},{12,28},{16,0},{20,4},{24,8},{28,12},{1,17},{... | collective-permute-start | bytes 393224 | tf_op jit(solution)/shard_map/ppermute | solution.py:22
  12.5 1.4 %collective-permute-start.5 = (f32[16,2048]{1,0:T(8,128)S(1)}, f32[16,2048]{1,0:T(8,128)S(1)}, u32[]{:S(2)}, u32[]{:S(2)}) collective-permute-start(f32[16,2048]{1,0:T(8,128)S(1)} %get-tuple-element.14), channel_id=1, source_target_pairs={{0,28},{4,0},{8,4},{12,8},{16,12},{20,16},{24,20},{28,24},{1,29},{... | collective-permute-start | bytes 393224 | tf_op jit(solution)/shard_map/ppermute | solution.py:22
  13.8 0.0 copy-done
  13.8 0.4 %convolution_bitcast_fusion = f32[4,2,8,512]{3,2,1,0:T(8,128)S(1)} fusion(bf16[4,512,512]{2,1,0:T(8,128)(2,1)S(1)} %copy-done, bf16[2,4,8,512]{3,2,1,0:T(8,128)(2,1)S(1)} %bitcast.15), kind=kOutput, calls=%fused_computation | convolution fusion | flops 33554432 | bytes 2293760 | tf_op jit(solution)/shard_map/rnl,nlm->rnm/dot_general | solution.py:137
  14.2 8.7 %collective-permute-done.4 = f32[16,2048]{1,0:T(8,128)S(1)} collective-permute-done((f32[16,2048]{1,0:T(8,128)S(1)}, f32[16,2048]{1,0:T(8,128)S(1)}, u32[]{:S(2)}, u32[]{:S(2)}) %collective-permute-start.4) | collective-permute-done | bytes 131104 | tf_op jit(solution)/shard_map/ppermute | solution.py:22
  22.9 0.0 collective-permute-done.5
  22.9 0.7 %add_add_fusion = f32[16,2048]{1,0:T(8,128)} fusion(f32[16,2048]{1,0:T(8,128)S(1)} %collective-permute-done.5, f32[16,2048]{1,0:T(8,128)S(1)} %bitcast.14, f32[16,2048]{1,0:T(8,128)S(1)} %collective-permute-done.4), kind=kLoop, calls=%fused_computation.1 | loop fusion | flops 65536 | bytes 524288 | tf_op jit(solution)/shard_map/add | solution.py:143
  (2 shorter events, 0.0 us)
Async XLA Ops:
  0.0 13.8 %copy-start = (bf16[4,512,512]{2,1,0:T(8,128)(2,1)S(1)}, bf16[4,512,512]{2,1,0:T(8,128)(2,1)}, u32[]{:S(2)}) copy-start(bf16[4,512,512]{2,1,0:T(8,128)(2,1)} %param.8) | copy-start | bytes 6291460
  0.0 9.6 %copy-start.3 = (f32[16,2048]{1,0:T(8,128)S(1)}, f32[16,2048]{1,0:T(8,128)}, u32[]{:S(2)}) copy-start(f32[16,2048]{1,0:T(8,128)} %field_hbm.1) | copy-start | bytes 393220
  0.0 11.7 %copy-start.1 = (bf16[2,64,2048]{2,1,0:T(8,128)(2,1)S(1)}, bf16[2,64,2048]{2,1,0:T(8,128)(2,1)}, u32[]{:S(2)}) copy-start(bf16[2,64,2048]{2,1,0:T(8,128)(2,1)} %param.10) | copy-start | bytes 1572868
  0.0 11.7 %copy-start.2 = (s32[2,8]{1,0:T(2,128)S(1)}, s32[2,8]{1,0:T(2,128)}, u32[]{:S(2)}) copy-start(s32[2,8]{1,0:T(2,128)} %refs_4_.1) | copy-start | bytes 196
  1.6 1.2 %collective-permute-start = (f32[16,128]{1,0:T(8,128)S(1)}, f32[16,128]{1,0:T(8,128)S(1)}, u32[]{:S(2)}, u32[]{:S(2)}) collective-permute-start(f32[16,128]{1,0:T(8,128)S(1)} %get-tuple-element.10.refs_0_), channel_id=1, source_target_pairs={{0,1},{1,0},{2,3},{3,2},{4,5},{5,4},{6,7},{7,6},{8,9},{9,8},{10,11... | collective-permute-start | bytes 24584 | tf_op jit(solution)/shard_map/ppermute | solution.py:17
  2.9 3.7 %collective-permute-start.1 = (f32[16,128]{1,0:T(8,128)S(1)}, f32[16,128]{1,0:T(8,128)S(1)}, u32[]{:S(2)}, u32[]{:S(2)}) collective-permute-start(f32[16,128]{1,0:T(8,128)S(1)} %shard_map.75.refs_0_), channel_id=1, source_target_pairs={{0,2},{1,3},{2,0},{3,1},{4,6},{5,7},{6,4},{7,5},{8,10},{9,11},{10,... | collective-permute-start | bytes 24584 | tf_op jit(solution)/shard_map/ppermute | solution.py:17
  6.7 1.2 %collective-permute-start.2 = (f32[16,128]{1,0:T(8,128)S(1)}, f32[16,128]{1,0:T(8,128)S(1)}, u32[]{:S(2)}, u32[]{:S(2)}) collective-permute-start(f32[16,128]{1,0:T(8,128)S(1)} %shard_map.76.refs_0_), channel_id=1, source_target_pairs={{0,1},{1,0},{2,3},{3,2},{4,5},{5,4},{6,7},{7,6},{8,9},{9,8},{10,11... | collective-permute-start | bytes 24584 | tf_op jit(solution)/shard_map/ppermute | solution.py:17
  8.1 3.7 %collective-permute-start.3 = (f32[16,128]{1,0:T(8,128)S(1)}, f32[16,128]{1,0:T(8,128)S(1)}, u32[]{:S(2)}, u32[]{:S(2)}) collective-permute-start(f32[16,128]{1,0:T(8,128)S(1)} %shard_map.77.refs_0_), channel_id=1, source_target_pairs={{0,2},{1,3},{2,0},{3,1},{4,6},{5,7},{6,4},{7,5},{8,10},{9,11},{10,... | collective-permute-start | bytes 24584 | tf_op jit(solution)/shard_map/ppermute | solution.py:17
  12.1 10.9 %collective-permute-start.4 = (f32[16,2048]{1,0:T(8,128)S(1)}, f32[16,2048]{1,0:T(8,128)S(1)}, u32[]{:S(2)}, u32[]{:S(2)}) collective-permute-start(f32[16,2048]{1,0:T(8,128)S(1)} %get-tuple-element.13), channel_id=1, source_target_pairs={{0,16},{4,20},{8,24},{12,28},{16,0},{20,4},{24,8},{28,12},{1,17},{... | collective-permute-start | bytes 393224 | tf_op jit(solution)/shard_map/ppermute | solution.py:22
  12.5 10.5 %collective-permute-start.5 = (f32[16,2048]{1,0:T(8,128)S(1)}, f32[16,2048]{1,0:T(8,128)S(1)}, u32[]{:S(2)}, u32[]{:S(2)}) collective-permute-start(f32[16,2048]{1,0:T(8,128)S(1)} %get-tuple-element.14), channel_id=1, source_target_pairs={{0,28},{4,0},{8,4},{12,8},{16,12},{20,16},{24,20},{28,24},{1,29},{... | collective-permute-start | bytes 393224 | tf_op jit(solution)/shard_map/ppermute | solution.py:22

commit v4 on v2

v4 whole, which is shorter than its diff:
```python
import jax
import jax.numpy as jnp
from jax import lax
from jax.experimental import pallas as pl
from jax.experimental.pallas import tpu as pltpu
from jax.sharding import PartitionSpec as P

F32, BF16 = jnp.float32, jnp.bfloat16
VMEM = pl.BlockSpec(memory_space=pltpu.VMEM)
HBM = pl.BlockSpec(memory_space=pltpu.HBM)
NT = (((1,), (1,)), ((), ()))


def partner(value, axis, distance):
    mask = 2**distance
    pairs = [(source, source ^ mask) for source in range(lax.axis_size(axis))]
    return lax.ppermute(value, axis, pairs)


def shifted(value, axis, distance):
    size = lax.axis_size(axis)
    return lax.ppermute(value, axis, [(source, (source + distance) % size) for source in range(size)])


def gathered(copies, axis, low, high):
    size = lax.axis_size(axis)
    bases = [base for base in range(size) if not base & (1 << low) and not base & (1 << high)]
    groups = [[base, base | 1 << low, base | 1 << high, base | 1 << low | 1 << high] for base in bases]
    return lax.all_to_all(copies, axis, 0, 0, axis_index_groups=groups if len(groups) > 1 else None)


def call(body, shapes, specs, flops, moved, *operands, scratch=()):
    return pl.pallas_call(
        body,
        out_shape=shapes,
        in_specs=specs,
        out_specs=jax.tree.map(lambda _: VMEM, shapes),
        scratch_shapes=scratch,
        cost_estimate=pl.CostEstimate(flops=flops, bytes_accessed=moved, transcendentals=0),
        compiler_params=pltpu.CompilerParams(vmem_limit_bytes=16 * 2**20),
    )(*operands)


def block_diagonal(compact, levels):
    k = compact.shape[0]
    lane = lax.broadcasted_iota(jnp.int32, compact.shape, 1)
    parts = []
    for level in range(levels):
        mine = jnp.logical_and(lane >= level * k, lane < (level + 1) * k)
        parts.append(jnp.where(mine, compact, 0.0))
    return jnp.concatenate(parts, axis=0)


def load(field_hbm, col_hbm, mixing_hbm, perm_hbm, field_ref, col_ref, compact_ref, mixing_ref, perm_ref, sems):
    pairs = [(mixing_hbm, mixing_ref), (perm_hbm, perm_ref), (field_hbm, field_ref), (col_hbm, col_ref)]
    copies = [pltpu.make_async_copy(source, target, sems.at[n]) for n, (source, target) in enumerate(pairs)]
    for copy in copies:
        copy.start()
    copies[0].wait()
    copies[1].wait()
    levels, sections, _, k, _ = mixing_ref.shape
    row = lax.broadcasted_iota(jnp.int32, (k, k), 0)
    picks = jnp.concatenate(
        [(row == perm_ref[level : level + 1, :]).astype(F32) for level in range(levels)], axis=1
    )
    picks = block_diagonal(picks, levels).astype(BF16)
    for section in range(sections):
        for side in range(2):
            mats = jnp.concatenate(
                [mixing_ref[level, section, side].astype(F32) for level in range(levels)], axis=1
            )
            if section == 0:
                mats = jnp.dot(picks, block_diagonal(mats, levels).astype(BF16), preferred_element_type=F32)
                mats = sum(mats[level * k : (level + 1) * k] for level in range(levels))
            compact_ref[section, side * k : (side + 1) * k, :] = mats
    copies[2].wait()
    copies[3].wait()


def project(field_ref, col_ref, out_ref):
    state = lax.dot_general(field_ref[...].astype(BF16), col_ref[...], NT, preferred_element_type=F32)
    for n in range(out_ref.shape[0]):
        out_ref[n] = state


def exact_dot(value, factor):
    count = value.shape[0]
    high = value.astype(BF16)
    rest = value - high.astype(F32)
    middle = rest.astype(BF16)
    low = (rest - middle.astype(F32)).astype(BF16)
    terms = jnp.dot(jnp.concatenate([high, middle, low], axis=0), factor, preferred_element_type=F32)
    return terms[:count] + (terms[count : 2 * count] + terms[2 * count :])


def section_product(own, other, compact, levels):
    k = compact.shape[0] // 2
    weights = jnp.concatenate([block_diagonal(compact[:k], levels), block_diagonal(compact[k:], levels)], axis=0)
    return exact_dot(jnp.concatenate([own, other], axis=1), weights.astype(BF16))


def two_sections(levels, section, first_bit, second_bit, states_ref, compact_ref, partner_ref):
    place = lax.axis_index("bf")
    low, high = sorted((first_bit, second_bit))
    mine = lax.rem(place >> low, 2) + 2 * lax.rem(place >> high, 2)
    first, second = (1, 2) if first_bit < second_bit else (2, 1)
    own = section_product(states_ref[mine], states_ref[mine ^ first], compact_ref[section], levels)
    other = section_product(states_ref[mine ^ second], states_ref[mine ^ 3], partner_ref[...], levels)
    return section_product(own, other, compact_ref[section + 1], levels)


def middle_step(static, states_ref, compact_ref, partner_ref, out_ref):
    state = two_sections(*static, states_ref, compact_ref, partner_ref)
    for n in range(out_ref.shape[0]):
        out_ref[n] = state


def last_step(static, rank_size, half_shift, states_ref, compact_ref, partner_ref, row_ref, owner_ref, half_ref, below_ref):
    state = two_sections(*static, states_ref, compact_ref, partner_ref)
    first_is_half = jnp.broadcast_to(owner_ref[0:1, 0:1], state.shape) == half_shift
    lane = lax.broadcasted_iota(jnp.int32, state.shape, 1)
    half = jnp.logical_xor(lane >= rank_size, first_is_half)
    rank_half = jnp.where(half, state, 0.0).astype(BF16)
    rank_below = jnp.where(half, 0.0, state).astype(BF16)
    count = state.shape[0]
    outs = jnp.dot(jnp.concatenate([rank_half, rank_below], axis=0), row_ref[...], preferred_element_type=F32)
    half_ref[...] = outs[:count]
    below_ref[...] = outs[count:]


def shards(field, leaf_inverse, col_factor, row_factor, mixing, row_owner, rank_perm):
    vectors, rows = field.shape
    order = leaf_inverse.shape[1]
    levels, rank_size, _ = col_factor.shape
    sections = mixing.shape[2]
    bits = lax.axis_size("bf").bit_length() - 1
    groups = lax.axis_size("grp")
    width = levels * rank_size

    states_shape = jax.ShapeDtypeStruct((4, vectors, width), F32)
    out_shape = jax.ShapeDtypeStruct((vectors, rows), F32)
    in_hbm = [
        pltpu.with_memory_space_constraint(x, pltpu.HBM)
        for x in (field, col_factor.reshape(width, rows), mixing[0], rank_perm)
    ]
    field_here, col_here, compact = call(
        load,
        [
            jax.ShapeDtypeStruct((vectors, rows), F32),
            jax.ShapeDtypeStruct((width, rows), BF16),
            jax.ShapeDtypeStruct((sections, 2 * rank_size, width), F32),
        ],
        [HBM] * 4, 8 * width**3, 3 * rows * width, *in_hbm,
        scratch=[
            pltpu.VMEM(mixing.shape[1:], BF16),
            pltpu.VMEM(rank_perm.shape, jnp.int32),
            pltpu.SemaphoreType.DMA((4,)),
        ],
    )
    pair_bits = [(section % bits, (section + 1) % bits) for section in range(0, sections, 2)]
    partners = [partner(compact[2 * n], "bf", second) for n, (_, second) in enumerate(pair_bits)]
    states = call(
        project, states_shape, [VMEM, VMEM], 2 * vectors * rows * width, 3 * rows * width, field_here, col_here
    )
    step_flops = 36 * vectors * width * width
    for n, pair in enumerate(pair_bits):
        states = gathered(states, "bf", min(pair), max(pair))
        static = (levels, 2 * n, *pair)
        if n < len(pair_bits) - 1:
            states = call(
                lambda *refs, static=static: middle_step(static, *refs), states_shape, [VMEM] * 3,
                step_flops, 12 * width * width, states, compact, partners[n],
            )
    out_half, out_below = call(
        lambda *refs: last_step(static, rank_size, groups // 2, *refs), [out_shape, out_shape],
        [VMEM] * 5, step_flops + 4 * vectors * width * rows, 4 * width * rows,
        states, compact, partners[-1], row_factor.reshape(width, rows), row_owner,
    )
    out_half = shifted(out_half, "grp", groups // 2)
    out_below = shifted(out_below, "grp", groups - 1)
    diag = jnp.einsum(
        "rnl,nlm->rnm",
        field_here.astype(BF16).reshape(vectors, rows // order, order),
        leaf_inverse,
        preferred_element_type=F32,
    ).reshape(vectors, rows)
    return diag + out_half + out_below


def solution(mesh):
    in_specs = (
        P(None, ("grp", "bf")),
        P(("grp", "bf"), None, None),
        P(None, None, ("grp", "bf")),
        P(None, None, ("grp", "bf")),
        P(("grp", "bf"), None, None, None, None, None),
        P(),
        P(),
    )
    out_specs = P(None, ("grp", "bf"))
    return jax.shard_map(shards, mesh=mesh, in_specs=in_specs, out_specs=out_specs, check_vma=False)
```

time: 25.8 us -> 31.6 us (1.22)
  blocking collectives: 0 us -> 6.54 us
  local copies, waits for them, and re-layouts: 3.8 us -> 0.04 us
  starting transfers between devices: 4.84 us -> 7.13 us
  Pallas kernels: 1.74 us -> 2.98 us
  waiting for transfers between devices: 14.1 us -> 13.3 us
    all_to_all x0 -> x1, blocking collectives: none -> 6.54 us  [gathered(): lax.all_to_all(copies, axis, 0, 0, axis_index_groups=groups if len(groups...]
    ppermute x4 -> x2, waiting for transfers between devices: 5.42 us -> 0.01 us  [partner(): return lax.ppermute(value, axis, pairs)]
    all_to_all x0 -> x1, waiting for transfers between devices: none -> 3.88 us  [gathered(): lax.all_to_all(copies, axis, 0, 0, axis_index_groups=groups if len(groups...]
    unnamed x16 -> x6, local copies, waits for them, and re-layouts: 3.78 us -> 0.01 us
    all_to_all x0 -> x1, starting transfers between devices: none -> 3.26 us  [gathered(): lax.all_to_all(copies, axis, 0, 0, axis_index_groups=groups if len(groups...]
    pallas_call x6 -> x4, Pallas kernels: 1.74 us -> 2.98 us  [call(): pl.pallas_call(body, out_shape=shapes, in_specs=specs, out_specs=jax.tree...]
    ppermute x4 -> x2, starting transfers between devices: 3.06 us -> 2.09 us  [partner(): return lax.ppermute(value, axis, pairs)]
    ppermute x2, waiting for transfers between devices: 8.71 us -> 9.42 us  [shifted(): lax.ppermute(value, axis, [(source, (source + distance) % size) for sourc...]
  transfers between devices with their start and end apart: 6 -> 5, of which waited for: 4 -> 2; matrix products, arithmetic and copies ran while one was open for 2% -> 1% of each run, Pallas kernels for 1% -> 4%
where the time goes in v4:
time: 31.6 us; the launch traced here: 31.1 us
  waiting for transfers between devices  13.3 us (42%)
  starting transfers between devices  7.13 us (23%)
  blocking collectives  6.54 us (21%)
  Pallas kernels  2.98 us (9%)
  other arithmetic  0.69 us (2%)
  matrix products  0.37 us (1%)
    ppermute x2, waiting for transfers between devices, shifted(): lax.ppermute(value, axis, [(source, (source + distance) % size) for sourc...  9.42 us
    all_to_all x1, blocking collectives, gathered(): lax.all_to_all(copies, axis, 0, 0, axis_index_groups=groups if len(groups...  6.54 us
    all_to_all x1, waiting for transfers between devices, gathered(): lax.all_to_all(copies, axis, 0, 0, axis_index_groups=groups if len(groups...  3.88 us
    all_to_all x1, starting transfers between devices, gathered(): lax.all_to_all(copies, axis, 0, 0, axis_index_groups=groups if len(groups...  3.26 us
    pallas_call x4, Pallas kernels, call(): pl.pallas_call(body, out_shape=shapes, in_specs=specs, out_specs=jax.tree...  2.98 us
    ppermute x2, starting transfers between devices, partner(): return lax.ppermute(value, axis, pairs)  2.09 us
    ppermute x2, starting transfers between devices, shifted(): lax.ppermute(value, axis, [(source, (source + distance) % size) for sourc...  1.77 us
    add x1, other arithmetic, shards(): return diag + out_half + out_below  0.68 us
  transfers between devices with their start and end apart: 5, of which 2 were waited for; matrix products, arithmetic and copies ran while one was open for 1% of the time, Pallas kernels for 4%

profile of v4, /device:TPU:24, one launch (start us, length us, event | category | flops | bytes accessed | tf_op | source)
XLA Modules:
  0.0 31.1 jit_solution(3520671721871087945)
XLA Ops:
  0.0 0.0 copy-start
  0.0 0.0 copy-start.2
  0.0 0.0 copy-start.1
  0.0 1.4 %shard_map.73 = (f32[16,2048]{1,0:T(8,128)S(1)}, bf16[128,2048]{1,0:T(8,128)(2,1)S(1)}, f32[4,128,128]{2,1,0:T(8,128)S(1)}) custom-call(f32[16,2048]{1,0:T(8,128)} %field_hbm.1, bf16[128,2048]{1,0:T(8,128)(2,1)} %bitcast.17, bf16[2,4,2,64,64]{4,3,2,1,0:T(8,128)(2,1)} %bitcast.20, s32[2,64]{1,0:T(2,128)} %perm_hbm.1), custom_call_target="tpu_custom_call" | custom-call | flops 16777216 | bytes 786432 | tf_op jit(solution)/shard_map/pallas_call | solution.py:33
  1.4 1.6 %collective-permute-start = (f32[128,128]{1,0:T(8,128)S(1)}, f32[128,128]{1,0:T(8,128)S(1)}, u32[]{:S(2)}, u32[]{:S(2)}) collective-permute-start(f32[128,128]{1,0:T(8,128)S(1)} %get-tuple-element.16), channel_id=1, source_target_pairs={{0,2},{1,3},{2,0},{3,1},{4,6},{5,7},{6,4},{7,5},{8,10},{9,11},{10,... | collective-permute-start | bytes 196616 | tf_op jit(solution)/shard_map/ppermute | solution.py:17
  3.0 0.5 %collective-permute-start.1 = (f32[128,128]{1,0:T(8,128)S(1)}, f32[128,128]{1,0:T(8,128)S(1)}, u32[]{:S(2)}, u32[]{:S(2)}) collective-permute-start(f32[128,128]{1,0:T(8,128)S(1)} %get-tuple-element.15), channel_id=1, source_target_pairs={{0,2},{1,3},{2,0},{3,1},{4,6},{5,7},{6,4},{7,5},{8,10},{9,11},{10,... | collective-permute-start | bytes 196616 | tf_op jit(solution)/shard_map/ppermute | solution.py:17
  3.5 0.2 shard_map.74
  3.8 6.5 %all_to_all.10.refs_0_ = f32[4,16,128]{2,1,0:T(8,128)S(1)} all-to-all(f32[4,16,128]{2,1,0:T(8,128)S(1)} %shard_map.74), channel_id=1, replica_groups=mesh['grp'=8,'bf'=4] {'bf'}, dimensions={0} | all-to-all | bytes 65536 | tf_op jit(solution)/shard_map/all_to_all | solution.py:29
  10.3 0.0 collective-permute-done.refs_2_
  10.3 0.9 %shard_map.75 = f32[4,16,128]{2,1,0:T(8,128)} custom-call(f32[4,16,128]{2,1,0:T(8,128)S(1)} %all_to_all.10.refs_0_, f32[4,128,128]{2,1,0:T(8,128)S(1)} %get-tuple-element.12.refs_1_, f32[128,128]{1,0:T(8,128)S(1)} %collective-permute-done.refs_2_), custom_call_target="tpu_custom_call" | custom-call | flops 9437184 | bytes 196608 | tf_op jit(solution)/shard_map/pallas_call | solution.py:33
  11.2 3.3 %all-to-all-start.1 = ((f32[4,16,128]{2,1,0:T(8,128)}), f32[4,16,128]{2,1,0:T(8,128)S(1)}, u32[]{:S(2)}, u32[]{:S(2)}) async-start(f32[4,16,128]{2,1,0:T(8,128)} %shard_map.75), calls=%async_computation.1 | async-start | bytes 65536 | tf_op jit(solution)/shard_map/all_to_all | solution.py:29
  14.5 0.0 collective-permute-done.1.refs_2_
  14.5 3.9 %all-to-all-done.1.refs_0_ = f32[4,16,128]{2,1,0:T(8,128)S(1)} async-done(((f32[4,16,128]{2,1,0:T(8,128)}), f32[4,16,128]{2,1,0:T(8,128)S(1)}, u32[]{:S(2)}, u32[]{:S(2)}) %all-to-all-start.1) | async-done | bytes 32800 | tf_op jit(solution)/shard_map/all_to_all | solution.py:29
  18.4 0.0 copy-done.2
  18.4 0.0 copy-done.1
  18.4 0.5 %shard_map.76 = (f32[16,2048]{1,0:T(8,128)S(1)}, f32[16,2048]{1,0:T(8,128)S(1)}) custom-call(f32[4,16,128]{2,1,0:T(8,128)S(1)} %all-to-all-done.1.refs_0_, f32[4,128,128]{2,1,0:T(8,128)S(1)} %get-tuple-element.12.refs_1_, f32[128,128]{1,0:T(8,128)S(1)} %collective-permute-done.1.refs_2_, bf16[128,2048]{1,0:T(8,128)(2,1)S(1)} %bitcast.16, s32[2,8]{1,0:T(2,128)S(1)} %copy-done.2), custom_call_target="tpu_custom_call" | custom-call | flops 26214400 | bytes 1048576 | tf_op jit(solution)/shard_map/pallas_call | solution.py:33
  18.8 0.4 %collective-permute-start.2 = (f32[16,2048]{1,0:T(8,128)S(1)}, f32[16,2048]{1,0:T(8,128)S(1)}, u32[]{:S(2)}, u32[]{:S(2)}) collective-permute-start(f32[16,2048]{1,0:T(8,128)S(1)} %get-tuple-element.13), channel_id=1, source_target_pairs={{0,16},{4,20},{8,24},{12,28},{16,0},{20,4},{24,8},{28,12},{1,17},{... | collective-permute-start | bytes 393224 | tf_op jit(solution)/shard_map/ppermute | solution.py:22
  19.2 1.4 %collective-permute-start.3 = (f32[16,2048]{1,0:T(8,128)S(1)}, f32[16,2048]{1,0:T(8,128)S(1)}, u32[]{:S(2)}, u32[]{:S(2)}) collective-permute-start(f32[16,2048]{1,0:T(8,128)S(1)} %get-tuple-element.14), channel_id=1, source_target_pairs={{0,28},{4,0},{8,4},{12,8},{16,12},{20,16},{24,20},{28,24},{1,29},{... | collective-permute-start | bytes 393224 | tf_op jit(solution)/shard_map/ppermute | solution.py:22
  20.6 0.0 copy-done
  20.6 0.4 %convolution_bitcast_fusion = f32[4,2,8,512]{3,2,1,0:T(8,128)S(1)} fusion(bf16[4,512,512]{2,1,0:T(8,128)(2,1)S(1)} %copy-done, bf16[2,4,8,512]{3,2,1,0:T(8,128)(2,1)S(1)} %bitcast.19), kind=kOutput, calls=%fused_computation | convolution fusion | flops 33554432 | bytes 2293760 | tf_op jit(solution)/shard_map/rnl,nlm->rnm/dot_general | solution.py:181
  21.0 9.4 %collective-permute-done.2 = f32[16,2048]{1,0:T(8,128)S(1)} collective-permute-done((f32[16,2048]{1,0:T(8,128)S(1)}, f32[16,2048]{1,0:T(8,128)S(1)}, u32[]{:S(2)}, u32[]{:S(2)}) %collective-permute-start.2) | collective-permute-done | bytes 131104 | tf_op jit(solution)/shard_map/ppermute | solution.py:22
  30.4 0.0 collective-permute-done.3
  30.4 0.7 %add_add_fusion = f32[16,2048]{1,0:T(8,128)} fusion(f32[16,2048]{1,0:T(8,128)S(1)} %collective-permute-done.3, f32[16,2048]{1,0:T(8,128)S(1)} %bitcast.18, f32[16,2048]{1,0:T(8,128)S(1)} %collective-permute-done.2), kind=kLoop, calls=%fused_computation.1 | loop fusion | flops 65536 | bytes 524288 | tf_op jit(solution)/shard_map/add | solution.py:187
  (3 shorter events, 0.0 us)
Async XLA Ops:
  0.0 20.6 %copy-start = (bf16[4,512,512]{2,1,0:T(8,128)(2,1)S(1)}, bf16[4,512,512]{2,1,0:T(8,128)(2,1)}, u32[]{:S(2)}) copy-start(bf16[4,512,512]{2,1,0:T(8,128)(2,1)} %param.8) | copy-start | bytes 6291460
  0.0 18.4 %copy-start.2 = (s32[2,8]{1,0:T(2,128)S(1)}, s32[2,8]{1,0:T(2,128)}, u32[]{:S(2)}) copy-start(s32[2,8]{1,0:T(2,128)} %refs_4_.1) | copy-start | bytes 196
  0.0 18.4 %copy-start.1 = (bf16[2,64,2048]{2,1,0:T(8,128)(2,1)S(1)}, bf16[2,64,2048]{2,1,0:T(8,128)(2,1)}, u32[]{:S(2)}) copy-start(bf16[2,64,2048]{2,1,0:T(8,128)(2,1)} %param.10) | copy-start | bytes 1572868
  1.4 8.9 %collective-permute-start = (f32[128,128]{1,0:T(8,128)S(1)}, f32[128,128]{1,0:T(8,128)S(1)}, u32[]{:S(2)}, u32[]{:S(2)}) collective-permute-start(f32[128,128]{1,0:T(8,128)S(1)} %get-tuple-element.16), channel_id=1, source_target_pairs={{0,2},{1,3},{2,0},{3,1},{4,6},{5,7},{6,4},{7,5},{8,10},{9,11},{10,... | collective-permute-start | bytes 196616 | tf_op jit(solution)/shard_map/ppermute | solution.py:17
  3.0 11.5 %collective-permute-start.1 = (f32[128,128]{1,0:T(8,128)S(1)}, f32[128,128]{1,0:T(8,128)S(1)}, u32[]{:S(2)}, u32[]{:S(2)}) collective-permute-start(f32[128,128]{1,0:T(8,128)S(1)} %get-tuple-element.15), channel_id=1, source_target_pairs={{0,2},{1,3},{2,0},{3,1},{4,6},{5,7},{6,4},{7,5},{8,10},{9,11},{10,... | collective-permute-start | bytes 196616 | tf_op jit(solution)/shard_map/ppermute | solution.py:17
  11.2 7.2 %all-to-all-start.1 = ((f32[4,16,128]{2,1,0:T(8,128)}), f32[4,16,128]{2,1,0:T(8,128)S(1)}, u32[]{:S(2)}, u32[]{:S(2)}) async-start(f32[4,16,128]{2,1,0:T(8,128)} %shard_map.75), calls=%async_computation.1 | async-start | bytes 65536 | tf_op jit(solution)/shard_map/all_to_all | solution.py:29
  18.8 11.6 %collective-permute-start.2 = (f32[16,2048]{1,0:T(8,128)S(1)}, f32[16,2048]{1,0:T(8,128)S(1)}, u32[]{:S(2)}, u32[]{:S(2)}) collective-permute-start(f32[16,2048]{1,0:T(8,128)S(1)} %get-tuple-element.13), channel_id=1, source_target_pairs={{0,16},{4,20},{8,24},{12,28},{16,0},{20,4},{24,8},{28,12},{1,17},{... | collective-permute-start | bytes 393224 | tf_op jit(solution)/shard_map/ppermute | solution.py:22
  19.2 11.2 %collective-permute-start.3 = (f32[16,2048]{1,0:T(8,128)S(1)}, f32[16,2048]{1,0:T(8,128)S(1)}, u32[]{:S(2)}, u32[]{:S(2)}) collective-permute-start(f32[16,2048]{1,0:T(8,128)S(1)} %get-tuple-element.14), channel_id=1, source_target_pairs={{0,28},{4,0},{8,4},{12,8},{16,12},{20,16},{24,20},{28,24},{1,29},{... | collective-permute-start | bytes 393224 | tf_op jit(solution)/shard_map/ppermute | solution.py:22

commit v5 on v4

v5 whole, which is shorter than its diff:
```python
import jax
import jax.numpy as jnp
from jax import lax
from jax.experimental import pallas as pl
from jax.experimental.pallas import tpu as pltpu
from jax.sharding import PartitionSpec as P

F32, BF16 = jnp.float32, jnp.bfloat16
VMEM = pl.BlockSpec(memory_space=pltpu.VMEM)
HBM = pl.BlockSpec(memory_space=pltpu.HBM)
NT = (((1,), (1,)), ((), ()))


def shifted(value, axis, distance):
    size = lax.axis_size(axis)
    return lax.ppermute(value, axis, [(source, (source + distance) % size) for source in range(size)])


def to_odd(value):
    return lax.ppermute(value, "bf", [(n, n + 1) for n in range(0, lax.axis_size("bf"), 2)])


def to_even(value):
    return lax.ppermute(value, "bf", [(n + 1, n) for n in range(0, lax.axis_size("bf"), 2)])


def among_odd(value, bit):
    return lax.ppermute(value, "bf", [(n, n ^ 1 << bit) for n in range(1, lax.axis_size("bf"), 2)])


def call(body, shapes, specs, flops, moved, *operands, scratch=()):
    return pl.pallas_call(
        body,
        out_shape=shapes,
        in_specs=specs,
        out_specs=jax.tree.map(lambda _: VMEM, shapes),
        scratch_shapes=scratch,
        cost_estimate=pl.CostEstimate(flops=flops, bytes_accessed=moved, transcendentals=0),
        compiler_params=pltpu.CompilerParams(vmem_limit_bytes=16 * 2**20),
    )(*operands)


def block_diagonal(compact, levels):
    k = compact.shape[0]
    lane = lax.broadcasted_iota(jnp.int32, compact.shape, 1)
    parts = []
    for level in range(levels):
        mine = jnp.logical_and(lane >= level * k, lane < (level + 1) * k)
        parts.append(jnp.where(mine, compact, 0.0))
    return jnp.concatenate(parts, axis=0)


def section_weights(compact, levels):
    k = compact.shape[0] // 2
    parts = [block_diagonal(compact[:k], levels), block_diagonal(compact[k:], levels)]
    return jnp.concatenate(parts, axis=0).astype(BF16)


def compact_section(mixing_ref, section, side):
    levels = mixing_ref.shape[0]
    return jnp.concatenate([mixing_ref[level, section, side].astype(F32) for level in range(levels)], axis=1)


def load(field_hbm, col_hbm, mixing_hbm, perm_hbm, xb_ref, first_ref, mixing_ref, field_ref, col_ref, perm_ref, sems):
    pairs = [(mixing_hbm, mixing_ref), (perm_hbm, perm_ref), (field_hbm, field_ref), (col_hbm, col_ref)]
    copies = [pltpu.make_async_copy(source, target, sems.at[n]) for n, (source, target) in enumerate(pairs)]
    for copy in copies:
        copy.start()
    copies[0].wait()
    copies[1].wait()
    levels, sections, _, k, _ = mixing_ref.shape
    vectors = field_ref.shape[0]
    row = lax.broadcasted_iota(jnp.int32, (k, k), 0)
    picks = jnp.concatenate([(row == perm_ref[level : level + 1, :]).astype(F32) for level in range(levels)], axis=1)
    picks = block_diagonal(picks, levels).astype(BF16)
    for side in range(2):
        mats = block_diagonal(compact_section(mixing_ref, 0, side), levels).astype(BF16)
        mats = jnp.dot(picks, mats, preferred_element_type=F32)
        mats = sum(mats[level * k : (level + 1) * k] for level in range(levels))
        first_ref[vectors + side * k : vectors + (side + 1) * k, :] = mats
    copies[2].wait()
    copies[3].wait()
    xb = field_ref[...].astype(BF16)
    xb_ref[...] = xb
    first_ref[:vectors, :] = lax.dot_general(xb, col_ref[...], NT, preferred_element_type=F32)


def build_own(levels, mixing_ref, compact_ref, weights_ref):
    k = mixing_ref.shape[3]
    for n in range(compact_ref.shape[0]):
        for side in range(2):
            compact_ref[n, side * k : (side + 1) * k, :] = compact_section(mixing_ref, n + 1, side)
        weights_ref[n] = section_weights(compact_ref[n], levels)


def build_weights(levels, compact_ref, weights_ref):
    for n in range(compact_ref.shape[0]):
        weights_ref[n] = section_weights(compact_ref[n], levels)


def exact_dot(value, factor):
    count = value.shape[0]
    high = value.astype(BF16)
    rest = value - high.astype(F32)
    middle = rest.astype(BF16)
    low = (rest - middle.astype(F32)).astype(BF16)
    terms = jnp.dot(jnp.concatenate([high, middle, low], axis=0), factor, preferred_element_type=F32)
    return terms[:count] + (terms[count : 2 * count] + terms[2 * count :])


def section_product(own, other, weights):
    return exact_dot(jnp.concatenate([own, other], axis=1), weights)


def first_section(levels, mine_ref, theirs_ref, out_ref):
    vectors = out_ref.shape[1]
    odd, even = mine_ref[:vectors, :], theirs_ref[:vectors, :]
    out_ref[0] = section_product(even, odd, section_weights(theirs_ref[vectors:, :], levels))
    out_ref[1] = section_product(odd, even, section_weights(mine_ref[vectors:, :], levels))


def next_sections(sections, states_ref, other_ref, mine_ref, theirs_ref, *out_refs):
    weights = (theirs_ref, mine_ref)
    states = [section_product(states_ref[n], other_ref[n], weights[n][sections[0] - 1]) for n in range(2)]
    for section in sections[1:]:
        states = [section_product(states[n], states[1 - n], weights[n][section - 1]) for n in range(2)]
    for n in range(2):
        if len(out_refs) == 1:
            out_refs[0][n] = states[n]
        else:
            out_refs[n][...] = states[n]


def expand(rank_size, half_shift, state_ref, back_ref, row_ref, owner_ref, half_ref, below_ref):
    odd = jnp.broadcast_to(lax.rem(lax.axis_index("bf"), 2), back_ref.shape) == 1
    state = jnp.where(odd, state_ref[...], back_ref[...])
    first_is_half = jnp.broadcast_to(owner_ref[0:1, 0:1], state.shape) == half_shift
    lane = lax.broadcasted_iota(jnp.int32, state.shape, 1)
    half = jnp.logical_xor(lane >= rank_size, first_is_half)
    rank_half = jnp.where(half, state, 0.0).astype(BF16)
    rank_below = jnp.where(half, 0.0, state).astype(BF16)
    count = state.shape[0]
    outs = jnp.dot(jnp.concatenate([rank_half, rank_below], axis=0), row_ref[...], preferred_element_type=F32)
    half_ref[...] = outs[:count]
    below_ref[...] = outs[count:]


def shards(field, leaf_inverse, col_factor, row_factor, mixing, row_owner, rank_perm):
    vectors, rows = field.shape
    order = leaf_inverse.shape[1]
    levels, rank_size, _ = col_factor.shape
    sections = mixing.shape[2]
    bits = lax.axis_size("bf").bit_length() - 1
    groups = lax.axis_size("grp")
    width = levels * rank_size

    def array(*shape, kind=F32):
        return jax.ShapeDtypeStruct(shape, kind)

    in_hbm = [
        pltpu.with_memory_space_constraint(x, pltpu.HBM)
        for x in (field, col_factor.reshape(width, rows), mixing[0], rank_perm)
    ]
    xb, first, mixing_here = call(
        load,
        [
            array(vectors, rows, kind=BF16),
            array(vectors + 2 * rank_size, width),
            array(*mixing.shape[1:], kind=BF16),
        ],
        [HBM] * 4, 2 * vectors * rows * width, 3 * rows * width, *in_hbm,
        scratch=[
            pltpu.VMEM(field.shape, F32),
            pltpu.VMEM((width, rows), BF16),
            pltpu.VMEM(rank_perm.shape, jnp.int32),
            pltpu.SemaphoreType.DMA((4,)),
        ],
    )
    first_theirs = to_odd(first)
    weight_cost = (4 * width * width * sections, 8 * width * width * sections)
    weights_shape = array(sections - 1, 2 * width, width, kind=BF16)
    later, mine = call(
        lambda *refs: build_own(levels, *refs), [array(sections - 1, 2 * rank_size, width), weights_shape],
        [VMEM], *weight_cost, mixing_here,
    )
    theirs = call(
        lambda *refs: build_weights(levels, *refs), weights_shape, [VMEM], *weight_cost, to_odd(later)
    )
    step_cost = (24 * vectors * width * width, 8 * width * width)
    states = call(
        lambda *refs: first_section(levels, *refs), array(2, vectors, width), [VMEM] * 2, *step_cost, first, first_theirs
    )
    runs = []
    for section in range(1, sections):
        if section % bits:
            runs.append([section])
        else:
            runs[-1].append(section)
    for n, run in enumerate(runs):
        other = among_odd(states, run[0] % bits)
        last = n == len(runs) - 1
        states = call(
            lambda *refs, run=run: next_sections(run, *refs),
            [array(vectors, width)] * 2 if last else array(2, vectors, width),
            [VMEM] * 4, *step_cost, states, other, mine, theirs,
        )
    out_half, out_below = call(
        lambda *refs: expand(rank_size, groups // 2, *refs), [array(vectors, rows)] * 2,
        [VMEM] * 4, 4 * vectors * width * rows, 4 * width * rows,
        states[1], to_even(states[0]), row_factor.reshape(width, rows), row_owner,
    )
    out_half = shifted(out_half, "grp", groups // 2)
    out_below = shifted(out_below, "grp", groups - 1)
    diag = jnp.einsum(
        "rnl,nlm->rnm",
        xb.reshape(vectors, rows // order, order),
        leaf_inverse,
        preferred_element_type=F32,
    ).reshape(vectors, rows)
    return diag + out_half + out_below


def solution(mesh):
    in_specs = (
        P(None, ("grp", "bf")),
        P(("grp", "bf"), None, None),
        P(None, None, ("grp", "bf")),
        P(None, None, ("grp", "bf")),
        P(("grp", "bf"), None, None, None, None, None),
        P(),
        P(),
    )
    out_specs = P(None, ("grp", "bf"))
    return jax.shard_map(shards, mesh=mesh, in_specs=in_specs, out_specs=out_specs, check_vma=False)
```

time: 31.6 us -> 30.9 us (0.978)
  blocking collectives: 6.54 us -> 0 us
  waiting for transfers between devices: 13.3 us -> 19.3 us
  Pallas kernels: 2.98 us -> 2.53 us
    ppermute x2 -> x5, waiting for transfers between devices: 0.01 us -> 9.45 us  [the longest x1 8.56 us: to_even(): lax.ppermute(value, 'bf', [(n + 1, n) for n in range(0, lax.axis_size('bf...]
    all_to_all x1 -> x0, blocking collectives: 6.54 us -> none  [gathered(): lax.all_to_all(copies, axis, 0, 0, axis_index_groups=groups if len(groups...]
    all_to_all x1 -> x0, waiting for transfers between devices: 3.88 us -> none  [gathered(): lax.all_to_all(copies, axis, 0, 0, axis_index_groups=groups if len(groups...]
    ppermute x2 -> x5, starting transfers between devices: 2.09 us -> 5.66 us  [the longest x2 3.04 us: to_odd(): lax.ppermute(value, 'bf', [(n, n + 1) for n in range(0, lax.axis_size('bf...]
    all_to_all x1 -> x0, starting transfers between devices: 3.26 us -> none  [gathered(): lax.all_to_all(copies, axis, 0, 0, axis_index_groups=groups if len(groups...]
    pallas_call x4 -> x7, Pallas kernels: 2.98 us -> 2.53 us  [call(): pl.pallas_call(body, out_shape=shapes, in_specs=specs, out_specs=jax.tree...]
    ppermute x2, waiting for transfers between devices: 9.42 us -> 9.86 us  [shifted(): lax.ppermute(value, axis, [(source, (source + distance) % size) for sourc...]
  transfers between devices with their start and end apart: 5 -> 7, of which waited for: 2 -> 3; matrix products, arithmetic and copies ran while one was open for 1% -> 1% of each run, Pallas kernels for 4% -> 1%
where the time goes in v5:
time: 30.9 us; the launch traced here: 30.5 us
  waiting for transfers between devices  19.3 us (62%)
  starting transfers between devices  7.43 us (24%)
  Pallas kernels  2.53 us (8%)
  other arithmetic  0.68 us (2%)
  matrix products  0.37 us (1%)
    ppermute x2, waiting for transfers between devices, shifted(): lax.ppermute(value, axis, [(source, (source + distance) % size) for sourc...  9.86 us
    ppermute x1, waiting for transfers between devices, to_even(): lax.ppermute(value, 'bf', [(n + 1, n) for n in range(0, lax.axis_size('bf...  8.56 us
    ppermute x2, starting transfers between devices, to_odd(): lax.ppermute(value, 'bf', [(n, n + 1) for n in range(0, lax.axis_size('bf...  3.04 us
    pallas_call x7, Pallas kernels, call(): pl.pallas_call(body, out_shape=shapes, in_specs=specs, out_specs=jax.tree...  2.53 us
    ppermute x2, starting transfers between devices, shifted(): lax.ppermute(value, axis, [(source, (source + distance) % size) for sourc...  1.77 us
    ppermute x2, starting transfers between devices, among_odd(): lax.ppermute(value, 'bf', [(n, n ^ 1 << bit) for n in range(1, lax.axis_s...  1.32 us
    ppermute x1, starting transfers between devices, to_even(): lax.ppermute(value, 'bf', [(n + 1, n) for n in range(0, lax.axis_size('bf...  1.29 us
    ppermute x2, waiting for transfers between devices, to_odd(): lax.ppermute(value, 'bf', [(n, n + 1) for n in range(0, lax.axis_size('bf...  0.89 us
  transfers between devices with their start and end apart: 7, of which 3 were waited for; matrix products, arithmetic and copies ran while one was open for 1% of the time, Pallas kernels for 1%

profile of v5, /device:TPU:24, one launch (start us, length us, event | category | flops | bytes accessed | tf_op | source)
XLA Modules:
  0.0 30.5 jit_solution(3560208456575806891)
XLA Ops:
  0.0 0.0 copy-start
  0.0 0.0 copy-start.1
  0.0 0.0 copy-start.2
  0.0 1.6 %shard_map.73 = (bf16[16,2048]{1,0:T(8,128)(2,1)S(1)}, f32[144,128]{1,0:T(8,128)S(1)}, bf16[2,4,2,64,64]{4,3,2,1,0:T(8,128)(2,1)S(1)}) custom-call(f32[16,2048]{1,0:T(8,128)} %field_hbm.1, bf16[128,2048]{1,0:T(8,128)(2,1)} %bitcast.14, bf16[2,4,2,64,64]{4,3,2,1,0:T(8,128)(2,1)} %bitcast.16, s32[2,64]{1,0:T(2,128)} %perm_hbm.1), custom_call_target="tpu_custom_call" | custom-call | flops 8388608 | bytes 786432 | tf_op jit(solution)/shard_map/pallas_call | solution.py:32
  1.7 0.1 shard_map.75
  1.8 1.8 %collective-permute-start.2 = (f32[3,128,128]{2,1,0:T(8,128)S(1)}, f32[3,128,128]{2,1,0:T(8,128)S(1)}, u32[]{:S(2)}, u32[]{:S(2)}) collective-permute-start(f32[3,128,128]{2,1,0:T(8,128)S(1)} %get-tuple-element.18), channel_id=1, source_target_pairs={{0,1},{2,3},{4,5},{6,7},{8,9},{10,11},{12,13},{14,15},{16,17},{18,... | collective-permute-start | bytes 589832 | tf_op jit(solution)/shard_map/ppermute | solution.py:20
  3.5 1.3 %collective-permute-start = (f32[144,128]{1,0:T(8,128)S(1)}, f32[144,128]{1,0:T(8,128)S(1)}, u32[]{:S(2)}, u32[]{:S(2)}) collective-permute-start(f32[144,128]{1,0:T(8,128)S(1)} %get-tuple-element.15.refs_0_), channel_id=1, source_target_pairs={{0,1},{2,3},{4,5},{6,7},{8,9},{10,11},{12,13},{14,15},{16,17},{18,... | collective-permute-start | bytes 221192 | tf_op jit(solution)/shard_map/ppermute | solution.py:20
  4.8 0.9 %collective-permute-done.refs_1_ = f32[144,128]{1,0:T(8,128)S(1)} collective-permute-done((f32[144,128]{1,0:T(8,128)S(1)}, f32[144,128]{1,0:T(8,128)S(1)}, u32[]{:S(2)}, u32[]{:S(2)}) %collective-permute-start) | collective-permute-done | bytes 73760 | tf_op jit(solution)/shard_map/ppermute | solution.py:20
  5.7 0.1 shard_map.74.refs_0_
  5.9 0.7 %collective-permute-start.1 = (f32[2,16,128]{2,1,0:T(8,128)S(1)}, f32[2,16,128]{2,1,0:T(8,128)S(1)}, u32[]{:S(2)}, u32[]{:S(2)}) collective-permute-start(f32[2,16,128]{2,1,0:T(8,128)S(1)} %shard_map.74.refs_0_), channel_id=1, source_target_pairs={{1,3},{3,1},{5,7},{7,5},{9,11},{11,9},{13,15},{15,13},{17,19},{19,... | collective-permute-start | bytes 49160 | tf_op jit(solution)/shard_map/ppermute | solution.py:28
  6.5 0.0 collective-permute-done.2.refs_0_
  6.6 0.0 collective-permute-done.1.refs_1_
  6.6 0.3 shard_map.77.refs_0_
  6.9 0.7 %collective-permute-start.3 = (f32[2,16,128]{2,1,0:T(8,128)S(1)}, f32[2,16,128]{2,1,0:T(8,128)S(1)}, u32[]{:S(2)}, u32[]{:S(2)}) collective-permute-start(f32[2,16,128]{2,1,0:T(8,128)S(1)} %shard_map.77.refs_0_), channel_id=1, source_target_pairs={{1,3},{3,1},{5,7},{7,5},{9,11},{11,9},{13,15},{15,13},{17,19},{19,... | collective-permute-start | bytes 49160 | tf_op jit(solution)/shard_map/ppermute | solution.py:28
  7.5 0.0 collective-permute-done.3.refs_1_
  7.5 0.1 shard_map.78
  7.7 1.3 %collective-permute-start.4 = (f32[16,128]{1,0:T(8,128)S(1)}, f32[16,128]{1,0:T(8,128)S(1)}, u32[]{:S(2)}, u32[]{:S(2)}) collective-permute-start(f32[16,128]{1,0:T(8,128)S(1)} %get-tuple-element.20), channel_id=1, source_target_pairs={{1,0},{3,2},{5,4},{7,6},{9,8},{11,10},{13,12},{15,14},{17,16},{19,... | collective-permute-start | bytes 24584 | tf_op jit(solution)/shard_map/ppermute | solution.py:24
  9.0 8.6 %collective-permute-done.4.refs_1_ = f32[16,128]{1,0:T(8,128)S(1)} collective-permute-done((f32[16,128]{1,0:T(8,128)S(1)}, f32[16,128]{1,0:T(8,128)S(1)}, u32[]{:S(2)}, u32[]{:S(2)}) %collective-permute-start.4) | collective-permute-done | bytes 8224 | tf_op jit(solution)/shard_map/ppermute | solution.py:24
  17.5 0.0 copy-done.1
  17.5 0.0 copy-done.2
  17.5 0.2 shard_map.79
  17.8 0.4 %collective-permute-start.5 = (f32[16,2048]{1,0:T(8,128)S(1)}, f32[16,2048]{1,0:T(8,128)S(1)}, u32[]{:S(2)}, u32[]{:S(2)}) collective-permute-start(f32[16,2048]{1,0:T(8,128)S(1)} %get-tuple-element.21), channel_id=1, source_target_pairs={{0,16},{4,20},{8,24},{12,28},{16,0},{20,4},{24,8},{28,12},{1,17},{... | collective-permute-start | bytes 393224 | tf_op jit(solution)/shard_map/ppermute | solution.py:16
  18.2 1.4 %collective-permute-start.6 = (f32[16,2048]{1,0:T(8,128)S(1)}, f32[16,2048]{1,0:T(8,128)S(1)}, u32[]{:S(2)}, u32[]{:S(2)}) collective-permute-start(f32[16,2048]{1,0:T(8,128)S(1)} %get-tuple-element.22), channel_id=1, source_target_pairs={{0,28},{4,0},{8,4},{12,8},{16,12},{20,16},{24,20},{28,24},{1,29},{... | collective-permute-start | bytes 393224 | tf_op jit(solution)/shard_map/ppermute | solution.py:16
  19.5 0.0 copy-done
  19.5 0.4 %convolution_bitcast_fusion = f32[4,2,8,512]{3,2,1,0:T(8,128)S(1)} fusion(bf16[4,512,512]{2,1,0:T(8,128)(2,1)S(1)} %copy-done, bf16[2,4,8,512]{3,2,1,0:T(8,128)(2,1)S(1)} %bitcast.13), kind=kOutput, calls=%fused_computation | convolution fusion | flops 33554432 | bytes 2293760 | tf_op jit(solution)/shard_map/rnl,nlm->rnm/dot_general | solution.py:214
  19.9 9.9 %collective-permute-done.5 = f32[16,2048]{1,0:T(8,128)S(1)} collective-permute-done((f32[16,2048]{1,0:T(8,128)S(1)}, f32[16,2048]{1,0:T(8,128)S(1)}, u32[]{:S(2)}, u32[]{:S(2)}) %collective-permute-start.5) | collective-permute-done | bytes 131104 | tf_op jit(solution)/shard_map/ppermute | solution.py:16
  29.8 0.0 collective-permute-done.6
  29.8 0.7 %add_add_fusion = f32[16,2048]{1,0:T(8,128)} fusion(f32[16,2048]{1,0:T(8,128)S(1)} %collective-permute-done.6, f32[16,2048]{1,0:T(8,128)S(1)} %bitcast.15, f32[16,2048]{1,0:T(8,128)S(1)} %collective-permute-done.5), kind=kLoop, calls=%fused_computation.1 | loop fusion | flops 65536 | bytes 524288 | tf_op jit(solution)/shard_map/add | solution.py:220
  (2 shorter events, 0.0 us)
Async XLA Ops:
  0.0 19.5 %copy-start = (bf16[4,512,512]{2,1,0:T(8,128)(2,1)S(1)}, bf16[4,512,512]{2,1,0:T(8,128)(2,1)}, u32[]{:S(2)}) copy-start(bf16[4,512,512]{2,1,0:T(8,128)(2,1)} %param.8) | copy-start | bytes 6291460
  0.0 17.5 %copy-start.1 = (bf16[2,64,2048]{2,1,0:T(8,128)(2,1)S(1)}, bf16[2,64,2048]{2,1,0:T(8,128)(2,1)}, u32[]{:S(2)}) copy-start(bf16[2,64,2048]{2,1,0:T(8,128)(2,1)} %param.10) | copy-start | bytes 1572868
  0.0 17.5 %copy-start.2 = (s32[2,8]{1,0:T(2,128)S(1)}, s32[2,8]{1,0:T(2,128)}, u32[]{:S(2)}) copy-start(s32[2,8]{1,0:T(2,128)} %refs_3_.1) | copy-start | bytes 196
  1.8 4.8 %collective-permute-start.2 = (f32[3,128,128]{2,1,0:T(8,128)S(1)}, f32[3,128,128]{2,1,0:T(8,128)S(1)}, u32[]{:S(2)}, u32[]{:S(2)}) collective-permute-start(f32[3,128,128]{2,1,0:T(8,128)S(1)} %get-tuple-element.18), channel_id=1, source_target_pairs={{0,1},{2,3},{4,5},{6,7},{8,9},{10,11},{12,13},{14,15},{16,17},{18,... | collective-permute-start | bytes 589832 | tf_op jit(solution)/shard_map/ppermute | solution.py:20
  3.5 2.2 %collective-permute-start = (f32[144,128]{1,0:T(8,128)S(1)}, f32[144,128]{1,0:T(8,128)S(1)}, u32[]{:S(2)}, u32[]{:S(2)}) collective-permute-start(f32[144,128]{1,0:T(8,128)S(1)} %get-tuple-element.15.refs_0_), channel_id=1, source_target_pairs={{0,1},{2,3},{4,5},{6,7},{8,9},{10,11},{12,13},{14,15},{16,17},{18,... | collective-permute-start | bytes 221192 | tf_op jit(solution)/shard_map/ppermute | solution.py:20
  5.9 0.7 %collective-permute-start.1 = (f32[2,16,128]{2,1,0:T(8,128)S(1)}, f32[2,16,128]{2,1,0:T(8,128)S(1)}, u32[]{:S(2)}, u32[]{:S(2)}) collective-permute-start(f32[2,16,128]{2,1,0:T(8,128)S(1)} %shard_map.74.refs_0_), channel_id=1, source_target_pairs={{1,3},{3,1},{5,7},{7,5},{9,11},{11,9},{13,15},{15,13},{17,19},{19,... | collective-permute-start | bytes 49160 | tf_op jit(solution)/shard_map/ppermute | solution.py:28
  6.9 0.7 %collective-permute-start.3 = (f32[2,16,128]{2,1,0:T(8,128)S(1)}, f32[2,16,128]{2,1,0:T(8,128)S(1)}, u32[]{:S(2)}, u32[]{:S(2)}) collective-permute-start(f32[2,16,128]{2,1,0:T(8,128)S(1)} %shard_map.77.refs_0_), channel_id=1, source_target_pairs={{1,3},{3,1},{5,7},{7,5},{9,11},{11,9},{13,15},{15,13},{17,19},{19,... | collective-permute-start | bytes 49160 | tf_op jit(solution)/shard_map/ppermute | solution.py:28
  7.7 9.9 %collective-permute-start.4 = (f32[16,128]{1,0:T(8,128)S(1)}, f32[16,128]{1,0:T(8,128)S(1)}, u32[]{:S(2)}, u32[]{:S(2)}) collective-permute-start(f32[16,128]{1,0:T(8,128)S(1)} %get-tuple-element.20), channel_id=1, source_target_pairs={{1,0},{3,2},{5,4},{7,6},{9,8},{11,10},{13,12},{15,14},{17,16},{19,... | collective-permute-start | bytes 24584 | tf_op jit(solution)/shard_map/ppermute | solution.py:24
  17.8 12.0 %collective-permute-start.5 = (f32[16,2048]{1,0:T(8,128)S(1)}, f32[16,2048]{1,0:T(8,128)S(1)}, u32[]{:S(2)}, u32[]{:S(2)}) collective-permute-start(f32[16,2048]{1,0:T(8,128)S(1)} %get-tuple-element.21), channel_id=1, source_target_pairs={{0,16},{4,20},{8,24},{12,28},{16,0},{20,4},{24,8},{28,12},{1,17},{... | collective-permute-start | bytes 393224 | tf_op jit(solution)/shard_map/ppermute | solution.py:16
  18.2 11.6 %collective-permute-start.6 = (f32[16,2048]{1,0:T(8,128)S(1)}, f32[16,2048]{1,0:T(8,128)S(1)}, u32[]{:S(2)}, u32[]{:S(2)}) collective-permute-start(f32[16,2048]{1,0:T(8,128)S(1)} %get-tuple-element.22), channel_id=1, source_target_pairs={{0,28},{4,0},{8,4},{12,8},{16,12},{20,16},{24,20},{28,24},{1,29},{... | collective-permute-start | bytes 393224 | tf_op jit(solution)/shard_map/ppermute | solution.py:16

commit v6 on v5

--- a/solution.py
+++ b/solution.py
@@ -16,16 +16,12 @@
     return lax.ppermute(value, axis, [(source, (source + distance) % size) for source in range(size)])
 
 
-def to_odd(value):
-    return lax.ppermute(value, "bf", [(n, n + 1) for n in range(0, lax.axis_size("bf"), 2)])
-
-
-def to_even(value):
-    return lax.ppermute(value, "bf", [(n + 1, n) for n in range(0, lax.axis_size("bf"), 2)])
+def swapped(value):
+    return lax.ppermute(value, "bf", [(n, n ^ 1) for n in range(lax.axis_size("bf"))])
 
 
 def among_odd(value, bit):
-    return lax.ppermute(value, "bf", [(n, n ^ 1 << bit) for n in range(1, lax.axis_size("bf"), 2)])
+    return lax.ppermute(value, "bf", [(n, n ^ 1 << bit if n % 2 else n) for n in range(lax.axis_size("bf"))])
 
 
 def call(body, shapes, specs, flops, moved, *operands, scratch=()):
@@ -61,7 +57,7 @@
     return jnp.concatenate([mixing_ref[level, section, side].astype(F32) for level in range(levels)], axis=1)
 
 
-def load(field_hbm, col_hbm, mixing_hbm, perm_hbm, xb_ref, first_ref, mixing_ref, field_ref, col_ref, perm_ref, sems):
+def load(field_hbm, col_hbm, mixing_hbm, perm_hbm, xb_ref, sent_ref, field_ref, col_ref, mixing_ref, perm_ref, sems):
     pairs = [(mixing_hbm, mixing_ref), (perm_hbm, perm_ref), (field_hbm, field_ref), (col_hbm, col_ref)]
     copies = [pltpu.make_async_copy(source, target, sems.at[n]) for n, (source, target) in enumerate(pairs)]
     for copy in copies:
@@ -73,29 +69,26 @@
     row = lax.broadcasted_iota(jnp.int32, (k, k), 0)
     picks = jnp.concatenate([(row == perm_ref[level : level + 1, :]).astype(F32) for level in range(levels)], axis=1)
     picks = block_diagonal(picks, levels).astype(BF16)
-    for side in range(2):
-        mats = block_diagonal(compact_section(mixing_ref, 0, side), levels).astype(BF16)
-        mats = jnp.dot(picks, mats, preferred_element_type=F32)
-        mats = sum(mats[level * k : (level + 1) * k] for level in range(levels))
-        first_ref[vectors + side * k : vectors + (side + 1) * k, :] = mats
+    for section in range(sections):
+        for side in range(2):
+            mats = jnp.concatenate([mixing_ref[level, section, side].astype(F32) for level in range(levels)], axis=1)
+            if section == 0:
+                mats = jnp.dot(picks, block_diagonal(mats, levels).astype(BF16), preferred_element_type=F32)
+                mats = sum(mats[level * k : (level + 1) * k] for level in range(levels))
+            start = vectors + (2 * section + side) * k
+            sent_ref[start : start + k, :] = mats
     copies[2].wait()
     copies[3].wait()
     xb = field_ref[...].astype(BF16)
     xb_ref[...] = xb
-    first_ref[:vectors, :] = lax.dot_general(xb, col_ref[...], NT, preferred_element_type=F32)
-
-
-def build_own(levels, mixing_ref, compact_ref, weights_ref):
-    k = mixing_ref.shape[3]
-    for n in range(compact_ref.shape[0]):
-        for side in range(2):
-            compact_ref[n, side * k : (side + 1) * k, :] = compact_section(mixing_ref, n + 1, side)
-        weights_ref[n] = section_weights(compact_ref[n], levels)
-
-
-def build_weights(levels, compact_ref, weights_ref):
-    for n in range(compact_ref.shape[0]):
-        weights_ref[n] = section_weights(compact_ref[n], levels)
+    sent_ref[:vectors, :] = lax.dot_general(xb, col_ref[...], NT, preferred_element_type=F32)
+
+
+def build_weights(levels, vectors, first, compact_ref, weights_ref):
+    size = weights_ref.shape[2] // levels * 2
+    for n in range(weights_ref.shape[0]):
+        start = vectors + (first + n) * size
+        weights_ref[n] = section_weights(compact_ref[start : start + size, :], levels)
 
 
 def exact_dot(value, factor):
@@ -112,18 +105,19 @@
     return exact_dot(jnp.concatenate([own, other], axis=1), weights)
 
 
-def first_section(levels, mine_ref, theirs_ref, out_ref):
-    vectors = out_ref.shape[1]
+def first_section(levels, mine_ref, theirs_ref, weights_ref, out_ref):
+    vectors, width = out_ref.shape[1:]
     odd, even = mine_ref[:vectors, :], theirs_ref[:vectors, :]
-    out_ref[0] = section_product(even, odd, section_weights(theirs_ref[vectors:, :], levels))
-    out_ref[1] = section_product(odd, even, section_weights(mine_ref[vectors:, :], levels))
+    theirs = section_weights(theirs_ref[vectors : vectors + 2 * width // levels, :], levels)
+    out_ref[0] = section_product(even, odd, theirs)
+    out_ref[1] = section_product(odd, even, weights_ref[0])
 
 
 def next_sections(sections, states_ref, other_ref, mine_ref, theirs_ref, *out_refs):
-    weights = (theirs_ref, mine_ref)
-    states = [section_product(states_ref[n], other_ref[n], weights[n][sections[0] - 1]) for n in range(2)]
+    weights = [lambda section: theirs_ref[section - 1], lambda section: mine_ref[section]]
+    states = [section_product(states_ref[n], other_ref[n], weights[n](sections[0])) for n in range(2)]
     for section in sections[1:]:
-        states = [section_product(states[n], states[1 - n], weights[n][section - 1]) for n in range(2)]
+        states = [section_product(states[n], states[1 - n], weights[n](section)) for n in range(2)]
     for n in range(2):
         if len(out_refs) == 1:
             out_refs[0][n] = states[n]
@@ -161,34 +155,30 @@
         pltpu.with_memory_space_constraint(x, pltpu.HBM)
         for x in (field, col_factor.reshape(width, rows), mixing[0], rank_perm)
     ]
-    xb, first, mixing_here = call(
+    xb, sent = call(
         load,
-        [
-            array(vectors, rows, kind=BF16),
-            array(vectors + 2 * rank_size, width),
-            array(*mixing.shape[1:], kind=BF16),
-        ],
+        [array(vectors, rows, kind=BF16), array(vectors + 2 * sections * rank_size, width)],
         [HBM] * 4, 2 * vectors * rows * width, 3 * rows * width, *in_hbm,
         scratch=[
             pltpu.VMEM(field.shape, F32),
             pltpu.VMEM((width, rows), BF16),
+            pltpu.VMEM(mixing.shape[1:], BF16),
             pltpu.VMEM(rank_perm.shape, jnp.int32),
             pltpu.SemaphoreType.DMA((4,)),
         ],
     )
-    first_theirs = to_odd(first)
-    weight_cost = (4 * width * width * sections, 8 * width * width * sections)
-    weights_shape = array(sections - 1, 2 * width, width, kind=BF16)
-    later, mine = call(
-        lambda *refs: build_own(levels, *refs), [array(sections - 1, 2 * rank_size, width), weights_shape],
-        [VMEM], *weight_cost, mixing_here,
-    )
-    theirs = call(
-        lambda *refs: build_weights(levels, *refs), weights_shape, [VMEM], *weight_cost, to_odd(later)
-    )
+    received = swapped(sent)
+    mine, theirs = [
+        call(
+            lambda *refs, first=first: build_weights(levels, vectors, first, *refs),
+            array(sections - first, 2 * width, width, kind=BF16),
+            [VMEM], 4 * width * width * sections, 8 * width * width * sections, compact,
+        )
+        for first, compact in enumerate((sent, received))
+    ]
     step_cost = (24 * vectors * width * width, 8 * width * width)
     states = call(
-        lambda *refs: first_section(levels, *refs), array(2, vectors, width), [VMEM] * 2, *step_cost, first, first_theirs
+        lambda *refs: first_section(levels, *refs), array(2, vectors, width), [VMEM] * 3, *step_cost, sent, received, mine
     )
     runs = []
     for section in range(1, sections):
@@ -207,7 +197,7 @@
     out_half, out_below = call(
         lambda *refs: expand(rank_size, groups // 2, *refs), [array(vectors, rows)] * 2,
         [VMEM] * 4, 4 * vectors * width * rows, 4 * width * rows,
-        states[1], to_even(states[0]), row_factor.reshape(width, rows), row_owner,
+        states[1], swapped(states[0]), row_factor.reshape(width, rows), row_owner,
     )
     out_half = shifted(out_half, "grp", groups // 2)
     out_below = shifted(out_below, "grp", groups - 1)

time: 30.9 us -> 27.3 us (0.88)
  waiting for transfers between devices: 19.3 us -> 12.4 us
  starting transfers between devices: 7.43 us -> 10.9 us
    ppermute x5 -> x4, waiting for transfers between devices: 9.45 us -> 2.33 us  [the longest x2 2.32 us: swapped(): lax.ppermute(value, 'bf', [(n, n ^ 1) for n in range(lax.axis_size('bf'))])]
    ppermute x5 -> x4, starting transfers between devices: 5.66 us -> 9.17 us  [the longest x2 7.84 us: swapped(): lax.ppermute(value, 'bf', [(n, n ^ 1) for n in range(lax.axis_size('bf'))])]
  transfers between devices with their start and end apart: 7 -> 6, of which waited for: 3 -> 3; matrix products, arithmetic and copies ran while one was open for 1% -> 1% of each run, Pallas kernels for 1% -> 0%
where the time goes in v6:
time: 27.3 us; the launch traced here: 27 us
  waiting for transfers between devices  12.4 us (45%)
  starting transfers between devices  10.9 us (40%)
  Pallas kernels  2.46 us (9%)
  other arithmetic  0.68 us (2%)
  matrix products  0.37 us (1%)
    ppermute x2, waiting for transfers between devices, shifted(): lax.ppermute(value, axis, [(source, (source + distance) % size) for sourc...  10 us
    ppermute x2, starting transfers between devices, swapped(): lax.ppermute(value, 'bf', [(n, n ^ 1) for n in range(lax.axis_size('bf'))])  7.84 us
    pallas_call x7, Pallas kernels, call(): pl.pallas_call(body, out_shape=shapes, in_specs=specs, out_specs=jax.tree...  2.46 us
    ppermute x2, waiting for transfers between devices, swapped(): lax.ppermute(value, 'bf', [(n, n ^ 1) for n in range(lax.axis_size('bf'))])  2.32 us
    ppermute x2, starting transfers between devices, shifted(): lax.ppermute(value, axis, [(source, (source + distance) % size) for sourc...  1.77 us
    ppermute x2, starting transfers between devices, among_odd(): lax.ppermute(value, 'bf', [(n, n ^ 1 << bit if n % 2 else n) for n in ran...  1.32 us
    add x1, other arithmetic, shards(): return diag + out_half + out_below  0.68 us
  transfers between devices with their start and end apart: 6, of which 3 were waited for; matrix products, arithmetic and copies ran while one was open for 1% of the time, Pallas kernels for 0%

profile of v6, /device:TPU:24, one launch (start us, length us, event | category | flops | bytes accessed | tf_op | source)
XLA Modules:
  0.0 27.0 jit_solution(4809375221727454574)
XLA Ops:
  0.0 0.0 copy-start
  0.0 0.0 copy-start.1
  0.0 0.0 copy-start.2
  0.0 1.6 %shard_map.73 = (bf16[16,2048]{1,0:T(8,128)(2,1)S(1)}, f32[528,128]{1,0:T(8,128)S(1)}) custom-call(f32[16,2048]{1,0:T(8,128)} %field_hbm.1, bf16[128,2048]{1,0:T(8,128)(2,1)} %bitcast.14, bf16[2,4,2,64,64]{4,3,2,1,0:T(8,128)(2,1)} %bitcast.16, s32[2,64]{1,0:T(2,128)} %perm_hbm.1), custom_call_target="tpu_custom_call" | custom-call | flops 8388608 | bytes 786432 | tf_op jit(solution)/shard_map/pallas_call | solution.py:28
  1.7 0.1 collective-permute-start
  1.8 1.5 %collective-permute-done.refs_1_.refs_0_ = f32[528,128]{1,0:T(8,128)S(1)} collective-permute-done((f32[528,128]{1,0:T(8,128)S(1)}, f32[528,128]{1,0:T(8,128)S(1)}, u32[]{:S(2)}, u32[]{:S(2)}) %collective-permute-start) | collective-permute-done | bytes 270368 | tf_op jit(solution)/shard_map/ppermute | solution.py:20
  3.3 0.1 shard_map.75.refs_0_
  3.4 0.7 %collective-permute-start.1 = (f32[2,16,128]{2,1,0:T(8,128)S(1)}, f32[2,16,128]{2,1,0:T(8,128)S(1)}, u32[]{:S(2)}, u32[]{:S(2)}) collective-permute-start(f32[2,16,128]{2,1,0:T(8,128)S(1)} %shard_map.75.refs_0_), channel_id=1, source_target_pairs={{0,0},{1,3},{2,2},{3,1},{4,4},{5,7},{6,6},{7,5},{8,8},{9,11},{10,1... | collective-permute-start | bytes 49160 | tf_op jit(solution)/shard_map/ppermute | solution.py:24
  4.1 0.0 collective-permute-done.1.refs_1_
  4.1 0.3 shard_map.77.refs_0_
  4.4 0.7 %collective-permute-start.2 = (f32[2,16,128]{2,1,0:T(8,128)S(1)}, f32[2,16,128]{2,1,0:T(8,128)S(1)}, u32[]{:S(2)}, u32[]{:S(2)}) collective-permute-start(f32[2,16,128]{2,1,0:T(8,128)S(1)} %shard_map.77.refs_0_), channel_id=1, source_target_pairs={{0,0},{1,3},{2,2},{3,1},{4,4},{5,7},{6,6},{7,5},{8,8},{9,11},{10,1... | collective-permute-start | bytes 49160 | tf_op jit(solution)/shard_map/ppermute | solution.py:24
  5.1 0.0 collective-permute-done.2.refs_1_
  5.1 0.1 shard_map.78
  5.2 7.8 %collective-permute-start.3 = (f32[16,128]{1,0:T(8,128)S(1)}, f32[16,128]{1,0:T(8,128)S(1)}, u32[]{:S(2)}, u32[]{:S(2)}) collective-permute-start(f32[16,128]{1,0:T(8,128)S(1)} %get-tuple-element.14), channel_id=1, source_target_pairs={{0,1},{1,0},{2,3},{3,2},{4,5},{5,4},{6,7},{7,6},{8,9},{9,8},{10,11... | collective-permute-start | bytes 24584 | tf_op jit(solution)/shard_map/ppermute | solution.py:20
  13.0 0.8 %collective-permute-done.3.refs_1_ = f32[16,128]{1,0:T(8,128)S(1)} collective-permute-done((f32[16,128]{1,0:T(8,128)S(1)}, f32[16,128]{1,0:T(8,128)S(1)}, u32[]{:S(2)}, u32[]{:S(2)}) %collective-permute-start.3) | collective-permute-done | bytes 8224 | tf_op jit(solution)/shard_map/ppermute | solution.py:20
  13.8 0.0 copy-done.1
  13.8 0.0 copy-done.2
  13.8 0.2 shard_map.79
  14.1 0.4 %collective-permute-start.4 = (f32[16,2048]{1,0:T(8,128)S(1)}, f32[16,2048]{1,0:T(8,128)S(1)}, u32[]{:S(2)}, u32[]{:S(2)}) collective-permute-start(f32[16,2048]{1,0:T(8,128)S(1)} %get-tuple-element.15), channel_id=1, source_target_pairs={{0,16},{4,20},{8,24},{12,28},{16,0},{20,4},{24,8},{28,12},{1,17},{... | collective-permute-start | bytes 393224 | tf_op jit(solution)/shard_map/ppermute | solution.py:16
  14.5 1.4 %collective-permute-start.5 = (f32[16,2048]{1,0:T(8,128)S(1)}, f32[16,2048]{1,0:T(8,128)S(1)}, u32[]{:S(2)}, u32[]{:S(2)}) collective-permute-start(f32[16,2048]{1,0:T(8,128)S(1)} %get-tuple-element.16), channel_id=1, source_target_pairs={{0,28},{4,0},{8,4},{12,8},{16,12},{20,16},{24,20},{28,24},{1,29},{... | collective-permute-start | bytes 393224 | tf_op jit(solution)/shard_map/ppermute | solution.py:16
  15.8 0.0 copy-done
  15.8 0.4 %convolution_bitcast_fusion = f32[4,2,8,512]{3,2,1,0:T(8,128)S(1)} fusion(bf16[4,512,512]{2,1,0:T(8,128)(2,1)S(1)} %copy-done, bf16[2,4,8,512]{3,2,1,0:T(8,128)(2,1)S(1)} %bitcast.13), kind=kOutput, calls=%fused_computation | convolution fusion | flops 33554432 | bytes 2293760 | tf_op jit(solution)/shard_map/rnl,nlm->rnm/dot_general | solution.py:204
  16.2 10.0 %collective-permute-done.4 = f32[16,2048]{1,0:T(8,128)S(1)} collective-permute-done((f32[16,2048]{1,0:T(8,128)S(1)}, f32[16,2048]{1,0:T(8,128)S(1)}, u32[]{:S(2)}, u32[]{:S(2)}) %collective-permute-start.4) | collective-permute-done | bytes 131104 | tf_op jit(solution)/shard_map/ppermute | solution.py:16
  26.3 0.0 collective-permute-done.5
  26.3 0.7 %add_add_fusion = f32[16,2048]{1,0:T(8,128)} fusion(f32[16,2048]{1,0:T(8,128)S(1)} %collective-permute-done.5, f32[16,2048]{1,0:T(8,128)S(1)} %bitcast.15, f32[16,2048]{1,0:T(8,128)S(1)} %collective-permute-done.4), kind=kLoop, calls=%fused_computation.1 | loop fusion | flops 65536 | bytes 524288 | tf_op jit(solution)/shard_map/add | solution.py:210
  (3 shorter events, 0.1 us)
Async XLA Ops:
  0.0 15.8 %copy-start = (bf16[4,512,512]{2,1,0:T(8,128)(2,1)S(1)}, bf16[4,512,512]{2,1,0:T(8,128)(2,1)}, u32[]{:S(2)}) copy-start(bf16[4,512,512]{2,1,0:T(8,128)(2,1)} %param.8) | copy-start | bytes 6291460
  0.0 13.8 %copy-start.1 = (bf16[2,64,2048]{2,1,0:T(8,128)(2,1)S(1)}, bf16[2,64,2048]{2,1,0:T(8,128)(2,1)}, u32[]{:S(2)}) copy-start(bf16[2,64,2048]{2,1,0:T(8,128)(2,1)} %param.10) | copy-start | bytes 1572868
  0.0 13.8 %copy-start.2 = (s32[2,8]{1,0:T(2,128)S(1)}, s32[2,8]{1,0:T(2,128)}, u32[]{:S(2)}) copy-start(s32[2,8]{1,0:T(2,128)} %refs_3_.1) | copy-start | bytes 196
  1.7 1.6 %collective-permute-start = (f32[528,128]{1,0:T(8,128)S(1)}, f32[528,128]{1,0:T(8,128)S(1)}, u32[]{:S(2)}, u32[]{:S(2)}) collective-permute-start(f32[528,128]{1,0:T(8,128)S(1)} %get-tuple-element.12.refs_0_), channel_id=1, source_target_pairs={{0,1},{1,0},{2,3},{3,2},{4,5},{5,4},{6,7},{7,6},{8,9},{9,8},{10,11... | collective-permute-start | bytes 811016 | tf_op jit(solution)/shard_map/ppermute | solution.py:20
  3.4 0.7 %collective-permute-start.1 = (f32[2,16,128]{2,1,0:T(8,128)S(1)}, f32[2,16,128]{2,1,0:T(8,128)S(1)}, u32[]{:S(2)}, u32[]{:S(2)}) collective-permute-start(f32[2,16,128]{2,1,0:T(8,128)S(1)} %shard_map.75.refs_0_), channel_id=1, source_target_pairs={{0,0},{1,3},{2,2},{3,1},{4,4},{5,7},{6,6},{7,5},{8,8},{9,11},{10,1... | collective-permute-start | bytes 49160 | tf_op jit(solution)/shard_map/ppermute | solution.py:24
  4.4 0.7 %collective-permute-start.2 = (f32[2,16,128]{2,1,0:T(8,128)S(1)}, f32[2,16,128]{2,1,0:T(8,128)S(1)}, u32[]{:S(2)}, u32[]{:S(2)}) collective-permute-start(f32[2,16,128]{2,1,0:T(8,128)S(1)} %shard_map.77.refs_0_), channel_id=1, source_target_pairs={{0,0},{1,3},{2,2},{3,1},{4,4},{5,7},{6,6},{7,5},{8,8},{9,11},{10,1... | collective-permute-start | bytes 49160 | tf_op jit(solution)/shard_map/ppermute | solution.py:24
  5.2 8.6 %collective-permute-start.3 = (f32[16,128]{1,0:T(8,128)S(1)}, f32[16,128]{1,0:T(8,128)S(1)}, u32[]{:S(2)}, u32[]{:S(2)}) collective-permute-start(f32[16,128]{1,0:T(8,128)S(1)} %get-tuple-element.14), channel_id=1, source_target_pairs={{0,1},{1,0},{2,3},{3,2},{4,5},{5,4},{6,7},{7,6},{8,9},{9,8},{10,11... | collective-permute-start | bytes 24584 | tf_op jit(solution)/shard_map/ppermute | solution.py:20
  14.1 12.2 %collective-permute-start.4 = (f32[16,2048]{1,0:T(8,128)S(1)}, f32[16,2048]{1,0:T(8,128)S(1)}, u32[]{:S(2)}, u32[]{:S(2)}) collective-permute-start(f32[16,2048]{1,0:T(8,128)S(1)} %get-tuple-element.15), channel_id=1, source_target_pairs={{0,16},{4,20},{8,24},{12,28},{16,0},{20,4},{24,8},{28,12},{1,17},{... | collective-permute-start | bytes 393224 | tf_op jit(solution)/shard_map/ppermute | solution.py:16
  14.5 11.8 %collective-permute-start.5 = (f32[16,2048]{1,0:T(8,128)S(1)}, f32[16,2048]{1,0:T(8,128)S(1)}, u32[]{:S(2)}, u32[]{:S(2)}) collective-permute-start(f32[16,2048]{1,0:T(8,128)S(1)} %get-tuple-element.16), channel_id=1, source_target_pairs={{0,28},{4,0},{8,4},{12,8},{16,12},{20,16},{24,20},{28,24},{1,29},{... | collective-permute-start | bytes 393224 | tf_op jit(solution)/shard_map/ppermute | solution.py:16

commit v7 on v6

v7 whole, which is shorter than its diff:
```python
import jax
import jax.numpy as jnp
from jax import lax
from jax.experimental import pallas as pl
from jax.experimental.pallas import tpu as pltpu
from jax.sharding import PartitionSpec as P

F32, BF16 = jnp.float32, jnp.bfloat16
VMEM = pl.BlockSpec(memory_space=pltpu.VMEM)
HBM = pl.BlockSpec(memory_space=pltpu.HBM)
NT = (((1,), (1,)), ((), ()))


def shifted(value, axis, distance):
    size = lax.axis_size(axis)
    return lax.ppermute(value, axis, [(source, (source + distance) % size) for source in range(size)])


def swapped(value):
    return lax.ppermute(value, "bf", [(n, n ^ 1) for n in range(lax.axis_size("bf"))])


def across(value, bit):
    return lax.ppermute(value, "bf", [(n, n ^ (1 << bit | 1)) for n in range(lax.axis_size("bf"))])


def call(body, shapes, specs, flops, moved, *operands, scratch=()):
    return pl.pallas_call(
        body,
        out_shape=shapes,
        in_specs=specs,
        out_specs=jax.tree.map(lambda _: VMEM, shapes),
        scratch_shapes=scratch,
        cost_estimate=pl.CostEstimate(flops=flops, bytes_accessed=moved, transcendentals=0),
        compiler_params=pltpu.CompilerParams(vmem_limit_bytes=16 * 2**20),
    )(*operands)


def block_diagonal(compact, levels):
    k = compact.shape[0]
    lane = lax.broadcasted_iota(jnp.int32, compact.shape, 1)
    parts = []
    for level in range(levels):
        mine = jnp.logical_and(lane >= level * k, lane < (level + 1) * k)
        parts.append(jnp.where(mine, compact, 0.0))
    return jnp.concatenate(parts, axis=0)


def section_weights(compact, levels):
    k = compact.shape[0] // 2
    parts = [block_diagonal(compact[:k], levels), block_diagonal(compact[k:], levels)]
    return jnp.concatenate(parts, axis=0).astype(BF16)


def compact_section(mixing_ref, section, side):
    levels = mixing_ref.shape[0]
    return jnp.concatenate([mixing_ref[level, section, side].astype(F32) for level in range(levels)], axis=1)


def load(field_hbm, col_hbm, mixing_hbm, perm_hbm, xb_ref, col_ref, sent_ref, kept_ref, field_ref, mixing_ref, perm_ref, sems):
    pairs = [(mixing_hbm, mixing_ref), (perm_hbm, perm_ref), (field_hbm, field_ref), (col_hbm, col_ref)]
    copies = [pltpu.make_async_copy(source, target, sems.at[n]) for n, (source, target) in enumerate(pairs)]
    for copy in copies:
        copy.start()
    copies[0].wait()
    copies[1].wait()
    levels, sections, _, k, _ = mixing_ref.shape
    row = lax.broadcasted_iota(jnp.int32, (k, k), 0)
    picks = jnp.concatenate([(row == perm_ref[level : level + 1, :]).astype(F32) for level in range(levels)], axis=1)
    picks = block_diagonal(picks, levels).astype(BF16)
    for section in range(sections):
        for side in range(2):
            mats = jnp.concatenate([mixing_ref[level, section, side].astype(F32) for level in range(levels)], axis=1)
            if section == 0:
                mats = jnp.dot(picks, block_diagonal(mats, levels).astype(BF16), preferred_element_type=F32)
                mats = sum(mats[level * k : (level + 1) * k] for level in range(levels))
            if section < sections - 1:
                sent_ref[section, side * k : (side + 1) * k, :] = mats
            else:
                kept_ref[0, side * k : (side + 1) * k, :] = mats
    copies[2].wait()
    xb_ref[...] = field_ref[...].astype(BF16)
    copies[3].wait()


def project(xb_ref, col_ref, out_ref):
    out_ref[...] = lax.dot_general(xb_ref[...], col_ref[...], NT, preferred_element_type=F32)


def build_weights(levels, *refs):
    *compact_refs, weights_ref = refs
    n = 0
    for compact_ref in compact_refs:
        for section in range(compact_ref.shape[0]):
            weights_ref[n] = section_weights(compact_ref[section], levels)
            n += 1


def exact_dot(value, factor):
    count = value.shape[0]
    high = value.astype(BF16)
    rest = value - high.astype(F32)
    middle = rest.astype(BF16)
    low = (rest - middle.astype(F32)).astype(BF16)
    terms = jnp.dot(jnp.concatenate([high, middle, low], axis=0), factor, preferred_element_type=F32)
    return terms[:count] + (terms[count : 2 * count] + terms[2 * count :])


def section_product(own, other, weights):
    return exact_dot(jnp.concatenate([own, other], axis=1), weights)


def run_sections(sections, final, first_refs, mine_ref, theirs_ref, out_ref):
    weights = (mine_ref, theirs_ref)
    if sections[0]:
        states_ref, other_ref = first_refs
        states, others = [states_ref[0], states_ref[1]], [other_ref[1], other_ref[0]]
    else:
        states = [ref[...] for ref in first_refs]
        others = states[::-1]
    for section in sections:
        count = 1 if section == final else 2
        states = [section_product(states[n], others[n], weights[n][section]) for n in range(count)]
        others = states[::-1]
    if count == 1:
        return states[0]
    out_ref[0], out_ref[1] = states


def step(sections, final, first_ref, second_ref, mine_ref, theirs_ref, out_ref):
    run_sections(sections, final, (first_ref, second_ref), mine_ref, theirs_ref, out_ref)


def last_step(sections, final, rank_size, half_shift, first_ref, second_ref, mine_ref, theirs_ref, row_ref, owner_ref, half_ref, below_ref):
    state = run_sections(sections, final, (first_ref, second_ref), mine_ref, theirs_ref, None)
    first_is_half = jnp.broadcast_to(owner_ref[0:1, 0:1], state.shape) == half_shift
    lane = lax.broadcasted_iota(jnp.int32, state.shape, 1)
    half = jnp.logical_xor(lane >= rank_size, first_is_half)
    rank_half = jnp.where(half, state, 0.0).astype(BF16)
    rank_below = jnp.where(half, 0.0, state).astype(BF16)
    count = state.shape[0]
    outs = jnp.dot(jnp.concatenate([rank_half, rank_below], axis=0), row_ref[...], preferred_element_type=F32)
    half_ref[...] = outs[:count]
    below_ref[...] = outs[count:]


def shards(field, leaf_inverse, col_factor, row_factor, mixing, row_owner, rank_perm):
    vectors, rows = field.shape
    order = leaf_inverse.shape[1]
    levels, rank_size, _ = col_factor.shape
    sections = mixing.shape[2]
    bits = lax.axis_size("bf").bit_length() - 1
    groups = lax.axis_size("grp")
    width = levels * rank_size

    def array(*shape, kind=F32):
        return jax.ShapeDtypeStruct(shape, kind)

    in_hbm = [
        pltpu.with_memory_space_constraint(x, pltpu.HBM)
        for x in (field, col_factor.reshape(width, rows), mixing[0], rank_perm)
    ]
    xb, col_here, sent, kept = call(
        load,
        [
            array(vectors, rows, kind=BF16),
            array(width, rows, kind=BF16),
            array(sections - 1, 2 * rank_size, width),
            array(1, 2 * rank_size, width),
        ],
        [HBM] * 4, 8 * width**3, 3 * rows * width, *in_hbm,
        scratch=[
            pltpu.VMEM(field.shape, F32),
            pltpu.VMEM(mixing.shape[1:], BF16),
            pltpu.VMEM(rank_perm.shape, jnp.int32),
            pltpu.SemaphoreType.DMA((4,)),
        ],
    )
    received = swapped(sent)
    state = call(
        project, array(vectors, width), [VMEM, VMEM], 2 * vectors * rows * width, 3 * rows * width, xb, col_here
    )
    first_states = (state, swapped(state))
    weight_cost = (4 * width * width * sections, 8 * width * width * sections)
    mine, theirs = [
        call(
            lambda *refs: build_weights(levels, *refs),
            array(sum(x.shape[0] for x in compacts), 2 * width, width, kind=BF16),
            [VMEM] * len(compacts), *weight_cost, *compacts,
        )
        for compacts in ((sent, kept), (received,))
    ]
    runs = []
    for section in range(sections):
        if section % bits or not section:
            runs.append([section])
        else:
            runs[-1].append(section)
    step_cost = (24 * vectors * width * width, 8 * width * width)
    final = sections - 1
    for run in runs[:-1]:
        states = call(
            lambda *refs, run=run: step(run, final, *refs), array(2, vectors, width), [VMEM] * 4, *step_cost,
            *first_states, mine, theirs,
        )
        first_states = (states, across(states, (run[-1] + 1) % bits))
    out_half, out_below = call(
        lambda *refs: last_step(runs[-1], final, rank_size, groups // 2, *refs), [array(vectors, rows)] * 2,
        [VMEM] * 6, 4 * vectors * width * rows, 4 * width * rows,
        *first_states, mine, theirs, row_factor.reshape(width, rows), row_owner,
    )
    out_half = shifted(out_half, "grp", groups // 2)
    out_below = shifted(out_below, "grp", groups - 1)
    diag = jnp.einsum(
        "rnl,nlm->rnm",
        xb.reshape(vectors, rows // order, order),
        leaf_inverse,
        preferred_element_type=F32,
    ).reshape(vectors, rows)
    return diag + out_half + out_below


def solution(mesh):
    in_specs = (
        P(None, ("grp", "bf")),
        P(("grp", "bf"), None, None),
        P(None, None, ("grp", "bf")),
        P(None, None, ("grp", "bf")),
        P(("grp", "bf"), None, None, None, None, None),
        P(),
        P(),
    )
    out_specs = P(None, ("grp", "bf"))
    return jax.shard_map(shards, mesh=mesh, in_specs=in_specs, out_specs=out_specs, check_vma=False)
```

time: 27.3 us -> 26.3 us (0.963)
  the two profiles are of different devices: /device:TPU:24 before, /device:TPU:0 now
where the time goes in v7:
time: 26.3 us; the launch traced here: 26.2 us
  waiting for transfers between devices  12.7 us (48%)
  starting transfers between devices  9.9 us (38%)
  Pallas kernels  2.42 us (9%)
  other arithmetic  0.68 us (3%)
  matrix products  0.37 us (1%)
    ppermute x2, waiting for transfers between devices, shifted(): lax.ppermute(value, axis, [(source, (source + distance) % size) for sourc...  8.77 us
    ppermute x2, starting transfers between devices, shifted(): lax.ppermute(value, axis, [(source, (source + distance) % size) for sourc...  4.83 us
    ppermute x2, starting transfers between devices, across(): lax.ppermute(value, 'bf', [(n, n ^ (1 << bit | 1)) for n in range(lax.axi...  4.48 us
    ppermute x2, waiting for transfers between devices, across(): lax.ppermute(value, 'bf', [(n, n ^ (1 << bit | 1)) for n in range(lax.axi...  2.89 us
    pallas_call x7, Pallas kernels, call(): pl.pallas_call(body, out_shape=shapes, in_specs=specs, out_specs=jax.tree...  2.42 us
    ppermute x2, waiting for transfers between devices, swapped(): lax.ppermute(value, 'bf', [(n, n ^ 1) for n in range(lax.axis_size('bf'))])  1.06 us
    add x1, other arithmetic, shards(): return diag + out_half + out_below  0.68 us
    ppermute x2, starting transfers between devices, swapped(): lax.ppermute(value, 'bf', [(n, n ^ 1) for n in range(lax.axis_size('bf'))])  0.59 us
  transfers between devices with their start and end apart: 6, of which 6 were waited for; matrix products, arithmetic and copies ran while one was open for 2% of the time, Pallas kernels for 1%

profile of v7, /device:TPU:0, one launch (start us, length us, event | category | flops | bytes accessed | tf_op | source)
XLA Modules:
  0.0 26.2 jit_solution(13817957981819517642)
XLA Ops:
  0.0 0.0 copy-start
  0.0 0.0 copy-start.1
  0.0 0.0 copy-start.2
  0.0 1.4 %shard_map.73 = (bf16[16,2048]{1,0:T(8,128)(2,1)S(1)}, bf16[128,2048]{1,0:T(8,128)(2,1)S(1)}, f32[3,128,128]{2,1,0:T(8,128)S(1)}, f32[1,128,128]{2,1,0:T(8,128)S(1)}) custom-call(f32[16,2048]{1,0:T(8,128)} %field_hbm.1, bf16[128,2048]{1,0:T(8,128)(2,1)} %bitcast.14, bf16[2,4,2,64,64]{4,3,2,1,0:T(8,128)(2,1)} %bitcast.16, s32[2,64]{1,0:T(2,128)} %perm_hbm.1), custom_call_target="tpu_custom_call" | custom-call | flops 16777216 | bytes 786432 | tf_op jit(solution)/shard_map/pallas_call | solution.py:28
  1.4 0.5 %collective-permute-start.1 = (f32[3,128,128]{2,1,0:T(8,128)S(1)}, f32[3,128,128]{2,1,0:T(8,128)S(1)}, u32[]{:S(2)}, u32[]{:S(2)}) collective-permute-start(f32[3,128,128]{2,1,0:T(8,128)S(1)} %get-tuple-element.13.refs_0_), channel_id=1, source_target_pairs={{0,1},{1,0},{2,3},{3,2},{4,5},{5,4},{6,7},{7,6},{8,9},{9,8},{10,11... | collective-permute-start | bytes 589832 | tf_op jit(solution)/shard_map/ppermute | solution.py:20
  1.9 0.2 shard_map.74.refs_0_
  2.2 0.1 collective-permute-start
  2.3 0.7 %collective-permute-done.1.refs_0_ = f32[3,128,128]{2,1,0:T(8,128)S(1)} collective-permute-done((f32[3,128,128]{2,1,0:T(8,128)S(1)}, f32[3,128,128]{2,1,0:T(8,128)S(1)}, u32[]{:S(2)}, u32[]{:S(2)}) %collective-permute-start.1) | collective-permute-done | bytes 196640 | tf_op jit(solution)/shard_map/ppermute | solution.py:20
  3.0 0.3 %collective-permute-done.refs_1_ = f32[16,128]{1,0:T(8,128)S(1)} collective-permute-done((f32[16,128]{1,0:T(8,128)S(1)}, f32[16,128]{1,0:T(8,128)S(1)}, u32[]{:S(2)}, u32[]{:S(2)}) %collective-permute-start) | collective-permute-done | bytes 8224 | tf_op jit(solution)/shard_map/ppermute | solution.py:20
  3.3 0.1 shard_map.77.refs_0_
  3.5 2.7 %collective-permute-start.2 = (f32[2,16,128]{2,1,0:T(8,128)S(1)}, f32[2,16,128]{2,1,0:T(8,128)S(1)}, u32[]{:S(2)}, u32[]{:S(2)}) collective-permute-start(f32[2,16,128]{2,1,0:T(8,128)S(1)} %shard_map.77.refs_0_), channel_id=1, source_target_pairs={{0,3},{1,2},{2,1},{3,0},{4,7},{5,6},{6,5},{7,4},{8,11},{9,10},{10,... | collective-permute-start | bytes 49160 | tf_op jit(solution)/shard_map/ppermute | solution.py:24
  6.2 1.4 %collective-permute-done.2.refs_1_ = f32[2,16,128]{2,1,0:T(8,128)S(1)} collective-permute-done((f32[2,16,128]{2,1,0:T(8,128)S(1)}, f32[2,16,128]{2,1,0:T(8,128)S(1)}, u32[]{:S(2)}, u32[]{:S(2)}) %collective-permute-start.2) | collective-permute-done | bytes 16416 | tf_op jit(solution)/shard_map/ppermute | solution.py:24
  7.6 0.3 %shard_map.78.refs_0_ = f32[2,16,128]{2,1,0:T(8,128)S(1)} custom-call(f32[2,16,128]{2,1,0:T(8,128)S(1)} %shard_map.77.refs_0_, f32[2,16,128]{2,1,0:T(8,128)S(1)} %collective-permute-done.2.refs_1_, bf16[4,256,128]{2,1,0:T(8,128)(2,1)S(1)} %shard_map.75.refs_2_, bf16[3,256,128]{2,1,0:T(8,128)(2,1)S(1)} %shard_map.76.refs_3_), custom_call_target="tpu_custom_call" | custom-call | flops 6291456 | bytes 131072 | tf_op jit(solution)/shard_map/pallas_call | solution.py:28
  7.9 1.8 %collective-permute-start.3 = (f32[2,16,128]{2,1,0:T(8,128)S(1)}, f32[2,16,128]{2,1,0:T(8,128)S(1)}, u32[]{:S(2)}, u32[]{:S(2)}) collective-permute-start(f32[2,16,128]{2,1,0:T(8,128)S(1)} %shard_map.78.refs_0_), channel_id=1, source_target_pairs={{0,3},{1,2},{2,1},{3,0},{4,7},{5,6},{6,5},{7,4},{8,11},{9,10},{10,... | collective-permute-start | bytes 49160 | tf_op jit(solution)/shard_map/ppermute | solution.py:24
  9.7 1.4 %collective-permute-done.3.refs_1_ = f32[2,16,128]{2,1,0:T(8,128)S(1)} collective-permute-done((f32[2,16,128]{2,1,0:T(8,128)S(1)}, f32[2,16,128]{2,1,0:T(8,128)S(1)}, u32[]{:S(2)}, u32[]{:S(2)}) %collective-permute-start.3) | collective-permute-done | bytes 16416 | tf_op jit(solution)/shard_map/ppermute | solution.py:24
  11.1 0.0 copy-done.1
  11.1 0.0 copy-done.2
  11.1 0.3 %shard_map.79 = (f32[16,2048]{1,0:T(8,128)S(1)}, f32[16,2048]{1,0:T(8,128)S(1)}) custom-call(f32[2,16,128]{2,1,0:T(8,128)S(1)} %shard_map.78.refs_0_, f32[2,16,128]{2,1,0:T(8,128)S(1)} %collective-permute-done.3.refs_1_, bf16[4,256,128]{2,1,0:T(8,128)(2,1)S(1)} %shard_map.75.refs_2_, bf16[3,256,128]{2,1,0:T(8,128)(2,1)S(1)} %shard_map.76.refs_3_, ...), custom_call_target="tpu_custom_call" | custom-call | flops 16777216 | bytes 1048576 | tf_op jit(solution)/shard_map/pallas_call | solution.py:28
  11.5 4.8 %collective-permute-start.5 = (f32[16,2048]{1,0:T(8,128)S(1)}, f32[16,2048]{1,0:T(8,128)S(1)}, u32[]{:S(2)}, u32[]{:S(2)}) collective-permute-start(f32[16,2048]{1,0:T(8,128)S(1)} %get-tuple-element.16), channel_id=1, source_target_pairs={{0,28},{4,0},{8,4},{12,8},{16,12},{20,16},{24,20},{28,24},{1,29},{... | collective-permute-start | bytes 393224 | tf_op jit(solution)/shard_map/ppermute | solution.py:16
  16.3 0.0 collective-permute-start.4
  16.3 0.0 copy-done
  16.3 0.4 %convolution_bitcast_fusion = f32[4,2,8,512]{3,2,1,0:T(8,128)S(1)} fusion(bf16[4,512,512]{2,1,0:T(8,128)(2,1)S(1)} %copy-done, bf16[2,4,8,512]{3,2,1,0:T(8,128)(2,1)S(1)} %bitcast.13), kind=kOutput, calls=%fused_computation | convolution fusion | flops 33554432 | bytes 2293760 | tf_op jit(solution)/shard_map/rnl,nlm->rnm/dot_general | solution.py:214
  16.7 3.5 %collective-permute-done.5 = f32[16,2048]{1,0:T(8,128)S(1)} collective-permute-done((f32[16,2048]{1,0:T(8,128)S(1)}, f32[16,2048]{1,0:T(8,128)S(1)}, u32[]{:S(2)}, u32[]{:S(2)}) %collective-permute-start.5) | collective-permute-done | bytes 131104 | tf_op jit(solution)/shard_map/ppermute | solution.py:16
  20.2 5.3 %collective-permute-done.4 = f32[16,2048]{1,0:T(8,128)S(1)} collective-permute-done((f32[16,2048]{1,0:T(8,128)S(1)}, f32[16,2048]{1,0:T(8,128)S(1)}, u32[]{:S(2)}, u32[]{:S(2)}) %collective-permute-start.4) | collective-permute-done | bytes 131104 | tf_op jit(solution)/shard_map/ppermute | solution.py:16
  25.5 0.7 %add_add_fusion = f32[16,2048]{1,0:T(8,128)} fusion(f32[16,2048]{1,0:T(8,128)S(1)} %collective-permute-done.5, f32[16,2048]{1,0:T(8,128)S(1)} %bitcast.15, f32[16,2048]{1,0:T(8,128)S(1)} %collective-permute-done.4), kind=kLoop, calls=%fused_computation.1 | loop fusion | flops 65536 | bytes 524288 | tf_op jit(solution)/shard_map/add | solution.py:220
  (3 shorter events, 0.1 us)
Async XLA Ops:
  0.0 16.3 %copy-start = (bf16[4,512,512]{2,1,0:T(8,128)(2,1)S(1)}, bf16[4,512,512]{2,1,0:T(8,128)(2,1)}, u32[]{:S(2)}) copy-start(bf16[4,512,512]{2,1,0:T(8,128)(2,1)} %param.8) | copy-start | bytes 6291460
  0.0 11.1 %copy-start.1 = (bf16[2,64,2048]{2,1,0:T(8,128)(2,1)S(1)}, bf16[2,64,2048]{2,1,0:T(8,128)(2,1)}, u32[]{:S(2)}) copy-start(bf16[2,64,2048]{2,1,0:T(8,128)(2,1)} %param.10) | copy-start | bytes 1572868
  0.0 11.1 %copy-start.2 = (s32[2,8]{1,0:T(2,128)S(1)}, s32[2,8]{1,0:T(2,128)}, u32[]{:S(2)}) copy-start(s32[2,8]{1,0:T(2,128)} %refs_5_.1) | copy-start | bytes 196
  1.4 1.6 %collective-permute-start.1 = (f32[3,128,128]{2,1,0:T(8,128)S(1)}, f32[3,128,128]{2,1,0:T(8,128)S(1)}, u32[]{:S(2)}, u32[]{:S(2)}) collective-permute-start(f32[3,128,128]{2,1,0:T(8,128)S(1)} %get-tuple-element.13.refs_0_), channel_id=1, source_target_pairs={{0,1},{1,0},{2,3},{3,2},{4,5},{5,4},{6,7},{7,6},{8,9},{9,8},{10,11... | collective-permute-start | bytes 589832 | tf_op jit(solution)/shard_map/ppermute | solution.py:20
  2.2 1.2 %collective-permute-start = (f32[16,128]{1,0:T(8,128)S(1)}, f32[16,128]{1,0:T(8,128)S(1)}, u32[]{:S(2)}, u32[]{:S(2)}) collective-permute-start(f32[16,128]{1,0:T(8,128)S(1)} %shard_map.74.refs_0_), channel_id=1, source_target_pairs={{0,1},{1,0},{2,3},{3,2},{4,5},{5,4},{6,7},{7,6},{8,9},{9,8},{10,11... | collective-permute-start | bytes 24584 | tf_op jit(solution)/shard_map/ppermute | solution.py:20
  3.5 4.1 %collective-permute-start.2 = (f32[2,16,128]{2,1,0:T(8,128)S(1)}, f32[2,16,128]{2,1,0:T(8,128)S(1)}, u32[]{:S(2)}, u32[]{:S(2)}) collective-permute-start(f32[2,16,128]{2,1,0:T(8,128)S(1)} %shard_map.77.refs_0_), channel_id=1, source_target_pairs={{0,3},{1,2},{2,1},{3,0},{4,7},{5,6},{6,5},{7,4},{8,11},{9,10},{10,... | collective-permute-start | bytes 49160 | tf_op jit(solution)/shard_map/ppermute | solution.py:24
  7.9 3.2 %collective-permute-start.3 = (f32[2,16,128]{2,1,0:T(8,128)S(1)}, f32[2,16,128]{2,1,0:T(8,128)S(1)}, u32[]{:S(2)}, u32[]{:S(2)}) collective-permute-start(f32[2,16,128]{2,1,0:T(8,128)S(1)} %shard_map.78.refs_0_), channel_id=1, source_target_pairs={{0,3},{1,2},{2,1},{3,0},{4,7},{5,6},{6,5},{7,4},{8,11},{9,10},{10,... | collective-permute-start | bytes 49160 | tf_op jit(solution)/shard_map/ppermute | solution.py:24
  11.5 8.7 %collective-permute-start.5 = (f32[16,2048]{1,0:T(8,128)S(1)}, f32[16,2048]{1,0:T(8,128)S(1)}, u32[]{:S(2)}, u32[]{:S(2)}) collective-permute-start(f32[16,2048]{1,0:T(8,128)S(1)} %get-tuple-element.16), channel_id=1, source_target_pairs={{0,28},{4,0},{8,4},{12,8},{16,12},{20,16},{24,20},{28,24},{1,29},{... | collective-permute-start | bytes 393224 | tf_op jit(solution)/shard_map/ppermute | solution.py:16
  16.3 9.2 %collective-permute-start.4 = (f32[16,2048]{1,0:T(8,128)S(1)}, f32[16,2048]{1,0:T(8,128)S(1)}, u32[]{:S(2)}, u32[]{:S(2)}) collective-permute-start(f32[16,2048]{1,0:T(8,128)S(1)} %get-tuple-element.15), channel_id=1, source_target_pairs={{0,16},{4,20},{8,24},{12,28},{16,0},{20,4},{24,8},{28,12},{1,17},{... | collective-permute-start | bytes 393224 | tf_op jit(solution)/shard_map/ppermute | solution.py:16

commit v8 on v7

--- a/solution.py
+++ b/solution.py
@@ -21,7 +21,7 @@
 
 
 def across(value, bit):
-    return lax.ppermute(value, "bf", [(n, n ^ (1 << bit | 1)) for n in range(lax.axis_size("bf"))])
+    return lax.ppermute(value, "bf", [(n, n ^ 1 << bit) for n in range(lax.axis_size("bf"))])
 
 
 def call(body, shapes, specs, flops, moved, *operands, scratch=()):
@@ -114,7 +114,7 @@
     weights = (mine_ref, theirs_ref)
     if sections[0]:
         states_ref, other_ref = first_refs
-        states, others = [states_ref[0], states_ref[1]], [other_ref[1], other_ref[0]]
+        states, others = [states_ref[0], states_ref[1]], [other_ref[0], other_ref[1]]
     else:
         states = [ref[...] for ref in first_refs]
         others = states[::-1]
@@ -131,17 +131,23 @@
     run_sections(sections, final, (first_ref, second_ref), mine_ref, theirs_ref, out_ref)
 
 
-def last_step(sections, final, rank_size, half_shift, first_ref, second_ref, mine_ref, theirs_ref, row_ref, owner_ref, half_ref, below_ref):
-    state = run_sections(sections, final, (first_ref, second_ref), mine_ref, theirs_ref, None)
+def level_rank(state, rank_size, half_shift, owner_ref, half):
     first_is_half = jnp.broadcast_to(owner_ref[0:1, 0:1], state.shape) == half_shift
     lane = lax.broadcasted_iota(jnp.int32, state.shape, 1)
-    half = jnp.logical_xor(lane >= rank_size, first_is_half)
-    rank_half = jnp.where(half, state, 0.0).astype(BF16)
-    rank_below = jnp.where(half, 0.0, state).astype(BF16)
-    count = state.shape[0]
-    outs = jnp.dot(jnp.concatenate([rank_half, rank_below], axis=0), row_ref[...], preferred_element_type=F32)
-    half_ref[...] = outs[:count]
-    below_ref[...] = outs[count:]
+    chosen = jnp.logical_xor(lane >= rank_size, first_is_half)
+    return (jnp.where(chosen, state, 0.0) if half else jnp.where(chosen, 0.0, state)).astype(BF16)
+
+
+def last_step(sections, final, rank_size, half_shift, first_ref, second_ref, mine_ref, theirs_ref, row_ref, owner_ref, state_ref, half_ref):
+    state = run_sections(sections, final, (first_ref, second_ref), mine_ref, theirs_ref, None)
+    state_ref[...] = state
+    rank = level_rank(state, rank_size, half_shift, owner_ref, True)
+    half_ref[...] = jnp.dot(rank, row_ref[...], preferred_element_type=F32)
+
+
+def expand_below(rank_size, half_shift, state_ref, row_ref, owner_ref, below_ref):
+    rank = level_rank(state_ref[...], rank_size, half_shift, owner_ref, False)
+    below_ref[...] = jnp.dot(rank, row_ref[...], preferred_element_type=F32)
 
 
 def shards(field, leaf_inverse, col_factor, row_factor, mixing, row_owner, rank_perm):
@@ -204,10 +210,16 @@
             *first_states, mine, theirs,
         )
         first_states = (states, across(states, (run[-1] + 1) % bits))
-    out_half, out_below = call(
-        lambda *refs: last_step(runs[-1], final, rank_size, groups // 2, *refs), [array(vectors, rows)] * 2,
-        [VMEM] * 6, 4 * vectors * width * rows, 4 * width * rows,
-        *first_states, mine, theirs, row_factor.reshape(width, rows), row_owner,
+    expand_cost = (2 * vectors * width * rows, 4 * width * rows)
+    expand = row_factor.reshape(width, rows)
+    state, out_half = call(
+        lambda *refs: last_step(runs[-1], final, rank_size, groups // 2, *refs),
+        [array(vectors, width), array(vectors, rows)],
+        [VMEM] * 6, *expand_cost, *first_states, mine, theirs, expand, row_owner,
+    )
+    out_below = call(
+        lambda *refs: expand_below(rank_size, groups // 2, *refs), array(vectors, rows),
+        [VMEM] * 3, *expand_cost, state, expand, row_owner,
     )
     out_half = shifted(out_half, "grp", groups // 2)
     out_below = shifted(out_below, "grp", groups - 1)

time: 26.3 us -> 25.9 us (0.985)
  waiting for transfers between devices: 12.7 us -> 11.6 us
  starting transfers between devices: 9.9 us -> 10.5 us
    ppermute x2, waiting for transfers between devices: 8.77 us -> 7.08 us  [shifted(): lax.ppermute(value, axis, [(source, (source + distance) % size) for sourc...]
    ppermute x2, waiting for transfers between devices: 2.89 us -> 3.44 us  [across(): lax.ppermute(value, 'bf', [(n, n ^ 1 << bit) for n in range(lax.axis_size...]
    ppermute x2, starting transfers between devices: 4.48 us -> 4.83 us  [across(): lax.ppermute(value, 'bf', [(n, n ^ 1 << bit) for n in range(lax.axis_size...]
    pallas_call x7 -> x8, Pallas kernels: 2.42 us -> 2.59 us  [call(): pl.pallas_call(body, out_shape=shapes, in_specs=specs, out_specs=jax.tree...]
where the time goes in v8:
time: 25.9 us; the launch traced here: 25.8 us
  waiting for transfers between devices  11.6 us (45%)
  starting transfers between devices  10.5 us (41%)
  Pallas kernels  2.59 us (10%)
  other arithmetic  0.68 us (3%)
  matrix products  0.37 us (1%)
    ppermute x2, waiting for transfers between devices, shifted(): lax.ppermute(value, axis, [(source, (source + distance) % size) for sourc...  7.08 us
    ppermute x2, starting transfers between devices, shifted(): lax.ppermute(value, axis, [(source, (source + distance) % size) for sourc...  5.05 us
    ppermute x2, starting transfers between devices, across(): lax.ppermute(value, 'bf', [(n, n ^ 1 << bit) for n in range(lax.axis_size...  4.83 us
    ppermute x2, waiting for transfers between devices, across(): lax.ppermute(value, 'bf', [(n, n ^ 1 << bit) for n in range(lax.axis_size...  3.44 us
    pallas_call x8, Pallas kernels, call(): pl.pallas_call(body, out_shape=shapes, in_specs=specs, out_specs=jax.tree...  2.59 us
    ppermute x2, waiting for transfers between devices, swapped(): lax.ppermute(value, 'bf', [(n, n ^ 1) for n in range(lax.axis_size('bf'))])  1.06 us
    add x1, other arithmetic, shards(): return diag + out_half + out_below  0.68 us
    ppermute x2, starting transfers between devices, swapped(): lax.ppermute(value, 'bf', [(n, n ^ 1) for n in range(lax.axis_size('bf'))])  0.59 us
  transfers between devices with their start and end apart: 6, of which 6 were waited for; matrix products, arithmetic and copies ran while one was open for 2% of the time, Pallas kernels for 1%

profile of v8, /device:TPU:0, one launch (start us, length us, event | category | flops | bytes accessed | tf_op | source)
XLA Modules:
  0.0 25.8 jit_solution(12820961313673705429)
XLA Ops:
  0.0 0.0 copy-start
  0.0 0.0 copy-start.1
  0.0 0.0 copy-start.2
  0.0 1.4 %shard_map.73 = (bf16[16,2048]{1,0:T(8,128)(2,1)S(1)}, bf16[128,2048]{1,0:T(8,128)(2,1)S(1)}, f32[3,128,128]{2,1,0:T(8,128)S(1)}, f32[1,128,128]{2,1,0:T(8,128)S(1)}) custom-call(f32[16,2048]{1,0:T(8,128)} %field_hbm.1, bf16[128,2048]{1,0:T(8,128)(2,1)} %bitcast.15, bf16[2,4,2,64,64]{4,3,2,1,0:T(8,128)(2,1)} %bitcast.17, s32[2,64]{1,0:T(2,128)} %perm_hbm.1), custom_call_target="tpu_custom_call" | custom-call | flops 16777216 | bytes 786432 | tf_op jit(solution)/shard_map/pallas_call | solution.py:28
  1.4 0.5 %collective-permute-start.1 = (f32[3,128,128]{2,1,0:T(8,128)S(1)}, f32[3,128,128]{2,1,0:T(8,128)S(1)}, u32[]{:S(2)}, u32[]{:S(2)}) collective-permute-start(f32[3,128,128]{2,1,0:T(8,128)S(1)} %get-tuple-element.13.refs_0_), channel_id=1, source_target_pairs={{0,1},{1,0},{2,3},{3,2},{4,5},{5,4},{6,7},{7,6},{8,9},{9,8},{10,11... | collective-permute-start | bytes 589832 | tf_op jit(solution)/shard_map/ppermute | solution.py:20
  1.9 0.2 shard_map.74.refs_0_
  2.2 0.1 collective-permute-start
  2.3 0.7 %collective-permute-done.1.refs_0_ = f32[3,128,128]{2,1,0:T(8,128)S(1)} collective-permute-done((f32[3,128,128]{2,1,0:T(8,128)S(1)}, f32[3,128,128]{2,1,0:T(8,128)S(1)}, u32[]{:S(2)}, u32[]{:S(2)}) %collective-permute-start.1) | collective-permute-done | bytes 196640 | tf_op jit(solution)/shard_map/ppermute | solution.py:20
  3.0 0.3 %collective-permute-done.refs_1_ = f32[16,128]{1,0:T(8,128)S(1)} collective-permute-done((f32[16,128]{1,0:T(8,128)S(1)}, f32[16,128]{1,0:T(8,128)S(1)}, u32[]{:S(2)}, u32[]{:S(2)}) %collective-permute-start) | collective-permute-done | bytes 8224 | tf_op jit(solution)/shard_map/ppermute | solution.py:20
  3.3 0.1 shard_map.77.refs_0_
  3.5 2.7 %collective-permute-start.2 = (f32[2,16,128]{2,1,0:T(8,128)S(1)}, f32[2,16,128]{2,1,0:T(8,128)S(1)}, u32[]{:S(2)}, u32[]{:S(2)}) collective-permute-start(f32[2,16,128]{2,1,0:T(8,128)S(1)} %shard_map.77.refs_0_), channel_id=1, source_target_pairs={{0,2},{1,3},{2,0},{3,1},{4,6},{5,7},{6,4},{7,5},{8,10},{9,11},{10,... | collective-permute-start | bytes 49160 | tf_op jit(solution)/shard_map/ppermute | solution.py:24
  6.2 1.7 %collective-permute-done.2.refs_1_ = f32[2,16,128]{2,1,0:T(8,128)S(1)} collective-permute-done((f32[2,16,128]{2,1,0:T(8,128)S(1)}, f32[2,16,128]{2,1,0:T(8,128)S(1)}, u32[]{:S(2)}, u32[]{:S(2)}) %collective-permute-start.2) | collective-permute-done | bytes 16416 | tf_op jit(solution)/shard_map/ppermute | solution.py:24
  8.0 0.3 %shard_map.78.refs_0_ = f32[2,16,128]{2,1,0:T(8,128)S(1)} custom-call(f32[2,16,128]{2,1,0:T(8,128)S(1)} %shard_map.77.refs_0_, f32[2,16,128]{2,1,0:T(8,128)S(1)} %collective-permute-done.2.refs_1_, bf16[4,256,128]{2,1,0:T(8,128)(2,1)S(1)} %shard_map.75.refs_2_, bf16[3,256,128]{2,1,0:T(8,128)(2,1)S(1)} %shard_map.76.refs_3_), custom_call_target="tpu_custom_call" | custom-call | flops 6291456 | bytes 131072 | tf_op jit(solution)/shard_map/pallas_call | solution.py:28
  8.2 2.1 %collective-permute-start.3 = (f32[2,16,128]{2,1,0:T(8,128)S(1)}, f32[2,16,128]{2,1,0:T(8,128)S(1)}, u32[]{:S(2)}, u32[]{:S(2)}) collective-permute-start(f32[2,16,128]{2,1,0:T(8,128)S(1)} %shard_map.78.refs_0_), channel_id=1, source_target_pairs={{0,2},{1,3},{2,0},{3,1},{4,6},{5,7},{6,4},{7,5},{8,10},{9,11},{10,... | collective-permute-start | bytes 49160 | tf_op jit(solution)/shard_map/ppermute | solution.py:24
  10.3 1.7 %collective-permute-done.3.refs_1_ = f32[2,16,128]{2,1,0:T(8,128)S(1)} collective-permute-done((f32[2,16,128]{2,1,0:T(8,128)S(1)}, f32[2,16,128]{2,1,0:T(8,128)S(1)}, u32[]{:S(2)}, u32[]{:S(2)}) %collective-permute-start.3) | collective-permute-done | bytes 16416 | tf_op jit(solution)/shard_map/ppermute | solution.py:24
  12.0 0.0 copy-done.1
  12.0 0.0 copy-done.2
  12.1 0.3 %shard_map.79 = (f32[16,128]{1,0:T(8,128)S(1)}, f32[16,2048]{1,0:T(8,128)S(1)}) custom-call(f32[2,16,128]{2,1,0:T(8,128)S(1)} %shard_map.78.refs_0_, f32[2,16,128]{2,1,0:T(8,128)S(1)} %collective-permute-done.3.refs_1_, bf16[4,256,128]{2,1,0:T(8,128)(2,1)S(1)} %shard_map.75.refs_2_, bf16[3,256,128]{2,1,0:T(8,128)(2,1)S(1)} %shard_map.76.refs_3_, ...), custom_call_target="tpu_custom_call" | custom-call | flops 8388608 | bytes 1048576 | tf_op jit(solution)/shard_map/pallas_call | solution.py:28
  12.4 0.2 shard_map.80
  12.6 5.1 %collective-permute-start.5 = (f32[16,2048]{1,0:T(8,128)S(1)}, f32[16,2048]{1,0:T(8,128)S(1)}, u32[]{:S(2)}, u32[]{:S(2)}) collective-permute-start(f32[16,2048]{1,0:T(8,128)S(1)} %shard_map.80), channel_id=1, source_target_pairs={{0,28},{4,0},{8,4},{12,8},{16,12},{20,16},{24,20},{28,24},{1,29},{... | collective-permute-start | bytes 393224 | tf_op jit(solution)/shard_map/ppermute | solution.py:16
  17.6 0.0 collective-permute-start.4
  17.6 0.0 copy-done
  17.6 0.4 %convolution_bitcast_fusion = f32[4,2,8,512]{3,2,1,0:T(8,128)S(1)} fusion(bf16[4,512,512]{2,1,0:T(8,128)(2,1)S(1)} %copy-done, bf16[2,4,8,512]{3,2,1,0:T(8,128)(2,1)S(1)} %bitcast.14), kind=kOutput, calls=%fused_computation | convolution fusion | flops 33554432 | bytes 2293760 | tf_op jit(solution)/shard_map/rnl,nlm->rnm/dot_general | solution.py:226
  18.0 2.1 %collective-permute-done.5 = f32[16,2048]{1,0:T(8,128)S(1)} collective-permute-done((f32[16,2048]{1,0:T(8,128)S(1)}, f32[16,2048]{1,0:T(8,128)S(1)}, u32[]{:S(2)}, u32[]{:S(2)}) %collective-permute-start.5) | collective-permute-done | bytes 131104 | tf_op jit(solution)/shard_map/ppermute | solution.py:16
  20.1 5.0 %collective-permute-done.4 = f32[16,2048]{1,0:T(8,128)S(1)} collective-permute-done((f32[16,2048]{1,0:T(8,128)S(1)}, f32[16,2048]{1,0:T(8,128)S(1)}, u32[]{:S(2)}, u32[]{:S(2)}) %collective-permute-start.4) | collective-permute-done | bytes 131104 | tf_op jit(solution)/shard_map/ppermute | solution.py:16
  25.1 0.7 %add_add_fusion = f32[16,2048]{1,0:T(8,128)} fusion(f32[16,2048]{1,0:T(8,128)S(1)} %collective-permute-done.5, f32[16,2048]{1,0:T(8,128)S(1)} %bitcast.16, f32[16,2048]{1,0:T(8,128)S(1)} %collective-permute-done.4), kind=kLoop, calls=%fused_computation.1 | loop fusion | flops 65536 | bytes 524288 | tf_op jit(solution)/shard_map/add | solution.py:232
  (3 shorter events, 0.1 us)
Async XLA Ops:
  0.0 17.6 %copy-start = (bf16[4,512,512]{2,1,0:T(8,128)(2,1)S(1)}, bf16[4,512,512]{2,1,0:T(8,128)(2,1)}, u32[]{:S(2)}) copy-start(bf16[4,512,512]{2,1,0:T(8,128)(2,1)} %param.8) | copy-start | bytes 6291460
  0.0 12.0 %copy-start.1 = (bf16[2,64,2048]{2,1,0:T(8,128)(2,1)S(1)}, bf16[2,64,2048]{2,1,0:T(8,128)(2,1)}, u32[]{:S(2)}) copy-start(bf16[2,64,2048]{2,1,0:T(8,128)(2,1)} %param.10) | copy-start | bytes 1572868
  0.0 12.0 %copy-start.2 = (s32[2,8]{1,0:T(2,128)S(1)}, s32[2,8]{1,0:T(2,128)}, u32[]{:S(2)}) copy-start(s32[2,8]{1,0:T(2,128)} %refs_2_.1) | copy-start | bytes 196
  1.4 1.6 %collective-permute-start.1 = (f32[3,128,128]{2,1,0:T(8,128)S(1)}, f32[3,128,128]{2,1,0:T(8,128)S(1)}, u32[]{:S(2)}, u32[]{:S(2)}) collective-permute-start(f32[3,128,128]{2,1,0:T(8,128)S(1)} %get-tuple-element.13.refs_0_), channel_id=1, source_target_pairs={{0,1},{1,0},{2,3},{3,2},{4,5},{5,4},{6,7},{7,6},{8,9},{9,8},{10,11... | collective-permute-start | bytes 589832 | tf_op jit(solution)/shard_map/ppermute | solution.py:20
  2.2 1.2 %collective-permute-start = (f32[16,128]{1,0:T(8,128)S(1)}, f32[16,128]{1,0:T(8,128)S(1)}, u32[]{:S(2)}, u32[]{:S(2)}) collective-permute-start(f32[16,128]{1,0:T(8,128)S(1)} %shard_map.74.refs_0_), channel_id=1, source_target_pairs={{0,1},{1,0},{2,3},{3,2},{4,5},{5,4},{6,7},{7,6},{8,9},{9,8},{10,11... | collective-permute-start | bytes 24584 | tf_op jit(solution)/shard_map/ppermute | solution.py:20
  3.5 4.5 %collective-permute-start.2 = (f32[2,16,128]{2,1,0:T(8,128)S(1)}, f32[2,16,128]{2,1,0:T(8,128)S(1)}, u32[]{:S(2)}, u32[]{:S(2)}) collective-permute-start(f32[2,16,128]{2,1,0:T(8,128)S(1)} %shard_map.77.refs_0_), channel_id=1, source_target_pairs={{0,2},{1,3},{2,0},{3,1},{4,6},{5,7},{6,4},{7,5},{8,10},{9,11},{10,... | collective-permute-start | bytes 49160 | tf_op jit(solution)/shard_map/ppermute | solution.py:24
  8.2 3.8 %collective-permute-start.3 = (f32[2,16,128]{2,1,0:T(8,128)S(1)}, f32[2,16,128]{2,1,0:T(8,128)S(1)}, u32[]{:S(2)}, u32[]{:S(2)}) collective-permute-start(f32[2,16,128]{2,1,0:T(8,128)S(1)} %shard_map.78.refs_0_), channel_id=1, source_target_pairs={{0,2},{1,3},{2,0},{3,1},{4,6},{5,7},{6,4},{7,5},{8,10},{9,11},{10,... | collective-permute-start | bytes 49160 | tf_op jit(solution)/shard_map/ppermute | solution.py:24
  12.6 7.6 %collective-permute-start.5 = (f32[16,2048]{1,0:T(8,128)S(1)}, f32[16,2048]{1,0:T(8,128)S(1)}, u32[]{:S(2)}, u32[]{:S(2)}) collective-permute-start(f32[16,2048]{1,0:T(8,128)S(1)} %shard_map.80), channel_id=1, source_target_pairs={{0,28},{4,0},{8,4},{12,8},{16,12},{20,16},{24,20},{28,24},{1,29},{... | collective-permute-start | bytes 393224 | tf_op jit(solution)/shard_map/ppermute | solution.py:16
  17.6 7.5 %collective-permute-start.4 = (f32[16,2048]{1,0:T(8,128)S(1)}, f32[16,2048]{1,0:T(8,128)S(1)}, u32[]{:S(2)}, u32[]{:S(2)}) collective-permute-start(f32[16,2048]{1,0:T(8,128)S(1)} %get-tuple-element.15), channel_id=1, source_target_pairs={{0,16},{4,20},{8,24},{12,28},{16,0},{20,4},{24,8},{28,12},{1,17},{... | collective-permute-start | bytes 393224 | tf_op jit(solution)/shard_map/ppermute | solution.py:16

commit v9 on v8

--- a/solution.py
+++ b/solution.py
@@ -229,7 +229,7 @@
         leaf_inverse,
         preferred_element_type=F32,
     ).reshape(vectors, rows)
-    return diag + out_half + out_below
+    return diag + out_below + out_half
 
 
 def solution(mesh):

time: 25.9 us -> 22.1 us (0.85)
  the two profiles are of different devices: /device:TPU:0 before, /device:TPU:24 now
where the time goes in v9:
time: 22.1 us; the launch traced here: 22 us
  waiting for transfers between devices  12.7 us (57%)
  starting transfers between devices  5.53 us (25%)
  Pallas kernels  2.58 us (12%)
  other arithmetic  0.68 us (3%)
  matrix products  0.37 us (2%)
    ppermute x2, waiting for transfers between devices, shifted(): lax.ppermute(value, axis, [(source, (source + distance) % size) for sourc...  7.52 us
    ppermute x2, waiting for transfers between devices, across(): lax.ppermute(value, 'bf', [(n, n ^ 1 << bit) for n in range(lax.axis_size...  4.44 us
    ppermute x2, starting transfers between devices, across(): lax.ppermute(value, 'bf', [(n, n ^ 1 << bit) for n in range(lax.axis_size...  3.17 us
    pallas_call x8, Pallas kernels, call(): pl.pallas_call(body, out_shape=shapes, in_specs=specs, out_specs=jax.tree...  2.58 us
    ppermute x2, starting transfers between devices, shifted(): lax.ppermute(value, axis, [(source, (source + distance) % size) for sourc...  1.77 us
    ppermute x2, waiting for transfers between devices, swapped(): lax.ppermute(value, 'bf', [(n, n ^ 1) for n in range(lax.axis_size('bf'))])  0.77 us
    add x1, other arithmetic, shards(): return diag + out_below + out_half  0.68 us
    ppermute x2, starting transfers between devices, swapped(): lax.ppermute(value, 'bf', [(n, n ^ 1) for n in range(lax.axis_size('bf'))])  0.58 us
  transfers between devices with their start and end apart: 6, of which 5 were waited for; matrix products, arithmetic and copies ran while one was open for 2% of the time, Pallas kernels for 2%

profile of v9, /device:TPU:24, one launch (start us, length us, event | category | flops | bytes accessed | tf_op | source)
XLA Modules:
  0.0 22.0 jit_solution(6275403447253787376)
XLA Ops:
  0.0 0.0 copy-start
  0.0 0.0 copy-start.1
  0.0 0.0 copy-start.2
  0.0 1.4 %shard_map.73 = (bf16[16,2048]{1,0:T(8,128)(2,1)S(1)}, bf16[128,2048]{1,0:T(8,128)(2,1)S(1)}, f32[3,128,128]{2,1,0:T(8,128)S(1)}, f32[1,128,128]{2,1,0:T(8,128)S(1)}) custom-call(f32[16,2048]{1,0:T(8,128)} %field_hbm.1, bf16[128,2048]{1,0:T(8,128)(2,1)} %bitcast.15, bf16[2,4,2,64,64]{4,3,2,1,0:T(8,128)(2,1)} %bitcast.17, s32[2,64]{1,0:T(2,128)} %perm_hbm.1), custom_call_target="tpu_custom_call" | custom-call | flops 16777216 | bytes 786432 | tf_op jit(solution)/shard_map/pallas_call | solution.py:28
  1.4 0.1 collective-permute-start.1
  1.5 0.2 %shard_map.74.refs_0_ = f32[16,128]{1,0:T(8,128)S(1)} custom-call(bf16[16,2048]{1,0:T(8,128)(2,1)S(1)} %get-tuple-element.11.xb_ref, bf16[128,2048]{1,0:T(8,128)(2,1)S(1)} %get-tuple-element.12.col_ref), custom_call_target="tpu_custom_call" | custom-call | flops 8388608 | bytes 786432 | tf_op jit(solution)/shard_map/pallas_call | solution.py:28
  1.7 0.5 %collective-permute-start = (f32[16,128]{1,0:T(8,128)S(1)}, f32[16,128]{1,0:T(8,128)S(1)}, u32[]{:S(2)}, u32[]{:S(2)}) collective-permute-start(f32[16,128]{1,0:T(8,128)S(1)} %shard_map.74.refs_0_), channel_id=1, source_target_pairs={{0,1},{1,0},{2,3},{3,2},{4,5},{5,4},{6,7},{7,6},{8,9},{9,8},{10,11... | collective-permute-start | bytes 24584 | tf_op jit(solution)/shard_map/ppermute | solution.py:20
  2.3 0.6 %collective-permute-done.1.refs_0_ = f32[3,128,128]{2,1,0:T(8,128)S(1)} collective-permute-done((f32[3,128,128]{2,1,0:T(8,128)S(1)}, f32[3,128,128]{2,1,0:T(8,128)S(1)}, u32[]{:S(2)}, u32[]{:S(2)}) %collective-permute-start.1) | collective-permute-done | bytes 196640 | tf_op jit(solution)/shard_map/ppermute | solution.py:20
  2.9 0.1 collective-permute-done.refs_1_
  3.1 0.1 shard_map.77.refs_0_
  3.2 1.6 %collective-permute-start.2 = (f32[2,16,128]{2,1,0:T(8,128)S(1)}, f32[2,16,128]{2,1,0:T(8,128)S(1)}, u32[]{:S(2)}, u32[]{:S(2)}) collective-permute-start(f32[2,16,128]{2,1,0:T(8,128)S(1)} %shard_map.77.refs_0_), channel_id=1, source_target_pairs={{0,2},{1,3},{2,0},{3,1},{4,6},{5,7},{6,4},{7,5},{8,10},{9,11},{10,... | collective-permute-start | bytes 49160 | tf_op jit(solution)/shard_map/ppermute | solution.py:24
  4.8 2.2 %collective-permute-done.2.refs_1_ = f32[2,16,128]{2,1,0:T(8,128)S(1)} collective-permute-done((f32[2,16,128]{2,1,0:T(8,128)S(1)}, f32[2,16,128]{2,1,0:T(8,128)S(1)}, u32[]{:S(2)}, u32[]{:S(2)}) %collective-permute-start.2) | collective-permute-done | bytes 16416 | tf_op jit(solution)/shard_map/ppermute | solution.py:24
  7.0 0.3 %shard_map.78.refs_0_ = f32[2,16,128]{2,1,0:T(8,128)S(1)} custom-call(f32[2,16,128]{2,1,0:T(8,128)S(1)} %shard_map.77.refs_0_, f32[2,16,128]{2,1,0:T(8,128)S(1)} %collective-permute-done.2.refs_1_, bf16[4,256,128]{2,1,0:T(8,128)(2,1)S(1)} %shard_map.75.refs_2_, bf16[3,256,128]{2,1,0:T(8,128)(2,1)S(1)} %shard_map.76.refs_3_), custom_call_target="tpu_custom_call" | custom-call | flops 6291456 | bytes 131072 | tf_op jit(solution)/shard_map/pallas_call | solution.py:28
  7.3 1.6 %collective-permute-start.3 = (f32[2,16,128]{2,1,0:T(8,128)S(1)}, f32[2,16,128]{2,1,0:T(8,128)S(1)}, u32[]{:S(2)}, u32[]{:S(2)}) collective-permute-start(f32[2,16,128]{2,1,0:T(8,128)S(1)} %shard_map.78.refs_0_), channel_id=1, source_target_pairs={{0,2},{1,3},{2,0},{3,1},{4,6},{5,7},{6,4},{7,5},{8,10},{9,11},{10,... | collective-permute-start | bytes 49160 | tf_op jit(solution)/shard_map/ppermute | solution.py:24
  8.9 2.2 %collective-permute-done.3.refs_1_ = f32[2,16,128]{2,1,0:T(8,128)S(1)} collective-permute-done((f32[2,16,128]{2,1,0:T(8,128)S(1)}, f32[2,16,128]{2,1,0:T(8,128)S(1)}, u32[]{:S(2)}, u32[]{:S(2)}) %collective-permute-start.3) | collective-permute-done | bytes 16416 | tf_op jit(solution)/shard_map/ppermute | solution.py:24
  11.1 0.0 copy-done.1
  11.1 0.0 copy-done.2
  11.1 0.3 %shard_map.79 = (f32[16,128]{1,0:T(8,128)S(1)}, f32[16,2048]{1,0:T(8,128)S(1)}) custom-call(f32[2,16,128]{2,1,0:T(8,128)S(1)} %shard_map.78.refs_0_, f32[2,16,128]{2,1,0:T(8,128)S(1)} %collective-permute-done.3.refs_1_, bf16[4,256,128]{2,1,0:T(8,128)(2,1)S(1)} %shard_map.75.refs_2_, bf16[3,256,128]{2,1,0:T(8,128)(2,1)S(1)} %shard_map.76.refs_3_, ...), custom_call_target="tpu_custom_call" | custom-call | flops 8388608 | bytes 1048576 | tf_op jit(solution)/shard_map/pallas_call | solution.py:28
  11.4 0.4 %collective-permute-start.5 = (f32[16,2048]{1,0:T(8,128)S(1)}, f32[16,2048]{1,0:T(8,128)S(1)}, u32[]{:S(2)}, u32[]{:S(2)}) collective-permute-start(f32[16,2048]{1,0:T(8,128)S(1)} %get-tuple-element.16), channel_id=1, source_target_pairs={{0,16},{4,20},{8,24},{12,28},{16,0},{20,4},{24,8},{28,12},{1,17},{... | collective-permute-start | bytes 393224 | tf_op jit(solution)/shard_map/ppermute | solution.py:16
  11.8 0.2 shard_map.80
  12.0 1.4 %collective-permute-start.4 = (f32[16,2048]{1,0:T(8,128)S(1)}, f32[16,2048]{1,0:T(8,128)S(1)}, u32[]{:S(2)}, u32[]{:S(2)}) collective-permute-start(f32[16,2048]{1,0:T(8,128)S(1)} %shard_map.80), channel_id=1, source_target_pairs={{0,28},{4,0},{8,4},{12,8},{16,12},{20,16},{24,20},{28,24},{1,29},{... | collective-permute-start | bytes 393224 | tf_op jit(solution)/shard_map/ppermute | solution.py:16
  13.4 0.0 copy-done
  13.4 0.4 %convolution_bitcast_fusion = f32[4,2,8,512]{3,2,1,0:T(8,128)S(1)} fusion(bf16[4,512,512]{2,1,0:T(8,128)(2,1)S(1)} %copy-done, bf16[2,4,8,512]{3,2,1,0:T(8,128)(2,1)S(1)} %bitcast.14), kind=kOutput, calls=%fused_computation | convolution fusion | flops 33554432 | bytes 2293760 | tf_op jit(solution)/shard_map/rnl,nlm->rnm/dot_general | solution.py:226
  13.8 7.5 %collective-permute-done.5 = f32[16,2048]{1,0:T(8,128)S(1)} collective-permute-done((f32[16,2048]{1,0:T(8,128)S(1)}, f32[16,2048]{1,0:T(8,128)S(1)}, u32[]{:S(2)}, u32[]{:S(2)}) %collective-permute-start.5) | collective-permute-done | bytes 131104 | tf_op jit(solution)/shard_map/ppermute | solution.py:16
  21.3 0.0 collective-permute-done.4
  21.3 0.7 %add_add_fusion = f32[16,2048]{1,0:T(8,128)} fusion(f32[16,2048]{1,0:T(8,128)S(1)} %collective-permute-done.5, f32[16,2048]{1,0:T(8,128)S(1)} %bitcast.16, f32[16,2048]{1,0:T(8,128)S(1)} %collective-permute-done.4), kind=kLoop, calls=%fused_computation.1 | loop fusion | flops 65536 | bytes 524288 | tf_op jit(solution)/shard_map/add | solution.py:232
  (3 shorter events, 0.1 us)
Async XLA Ops:
  0.0 13.4 %copy-start = (bf16[4,512,512]{2,1,0:T(8,128)(2,1)S(1)}, bf16[4,512,512]{2,1,0:T(8,128)(2,1)}, u32[]{:S(2)}) copy-start(bf16[4,512,512]{2,1,0:T(8,128)(2,1)} %param.8) | copy-start | bytes 6291460
  0.0 11.1 %copy-start.1 = (bf16[2,64,2048]{2,1,0:T(8,128)(2,1)S(1)}, bf16[2,64,2048]{2,1,0:T(8,128)(2,1)}, u32[]{:S(2)}) copy-start(bf16[2,64,2048]{2,1,0:T(8,128)(2,1)} %param.10) | copy-start | bytes 1572868
  0.0 11.1 %copy-start.2 = (s32[2,8]{1,0:T(2,128)S(1)}, s32[2,8]{1,0:T(2,128)}, u32[]{:S(2)}) copy-start(s32[2,8]{1,0:T(2,128)} %refs_2_.1) | copy-start | bytes 196
  1.4 1.5 %collective-permute-start.1 = (f32[3,128,128]{2,1,0:T(8,128)S(1)}, f32[3,128,128]{2,1,0:T(8,128)S(1)}, u32[]{:S(2)}, u32[]{:S(2)}) collective-permute-start(f32[3,128,128]{2,1,0:T(8,128)S(1)} %get-tuple-element.13.refs_0_), channel_id=1, source_target_pairs={{0,1},{1,0},{2,3},{3,2},{4,5},{5,4},{6,7},{7,6},{8,9},{9,8},{10,11... | collective-permute-start | bytes 589832 | tf_op jit(solution)/shard_map/ppermute | solution.py:20
  1.7 1.3 %collective-permute-start = (f32[16,128]{1,0:T(8,128)S(1)}, f32[16,128]{1,0:T(8,128)S(1)}, u32[]{:S(2)}, u32[]{:S(2)}) collective-permute-start(f32[16,128]{1,0:T(8,128)S(1)} %shard_map.74.refs_0_), channel_id=1, source_target_pairs={{0,1},{1,0},{2,3},{3,2},{4,5},{5,4},{6,7},{7,6},{8,9},{9,8},{10,11... | collective-permute-start | bytes 24584 | tf_op jit(solution)/shard_map/ppermute | solution.py:20
  3.2 3.8 %collective-permute-start.2 = (f32[2,16,128]{2,1,0:T(8,128)S(1)}, f32[2,16,128]{2,1,0:T(8,128)S(1)}, u32[]{:S(2)}, u32[]{:S(2)}) collective-permute-start(f32[2,16,128]{2,1,0:T(8,128)S(1)} %shard_map.77.refs_0_), channel_id=1, source_target_pairs={{0,2},{1,3},{2,0},{3,1},{4,6},{5,7},{6,4},{7,5},{8,10},{9,11},{10,... | collective-permute-start | bytes 49160 | tf_op jit(solution)/shard_map/ppermute | solution.py:24
  7.3 3.8 %collective-permute-start.3 = (f32[2,16,128]{2,1,0:T(8,128)S(1)}, f32[2,16,128]{2,1,0:T(8,128)S(1)}, u32[]{:S(2)}, u32[]{:S(2)}) collective-permute-start(f32[2,16,128]{2,1,0:T(8,128)S(1)} %shard_map.78.refs_0_), channel_id=1, source_target_pairs={{0,2},{1,3},{2,0},{3,1},{4,6},{5,7},{6,4},{7,5},{8,10},{9,11},{10,... | collective-permute-start | bytes 49160 | tf_op jit(solution)/shard_map/ppermute | solution.py:24
  11.4 9.9 %collective-permute-start.5 = (f32[16,2048]{1,0:T(8,128)S(1)}, f32[16,2048]{1,0:T(8,128)S(1)}, u32[]{:S(2)}, u32[]{:S(2)}) collective-permute-start(f32[16,2048]{1,0:T(8,128)S(1)} %get-tuple-element.16), channel_id=1, source_target_pairs={{0,16},{4,20},{8,24},{12,28},{16,0},{20,4},{24,8},{28,12},{1,17},{... | collective-permute-start | bytes 393224 | tf_op jit(solution)/shard_map/ppermute | solution.py:16
  12.0 9.3 %collective-permute-start.4 = (f32[16,2048]{1,0:T(8,128)S(1)}, f32[16,2048]{1,0:T(8,128)S(1)}, u32[]{:S(2)}, u32[]{:S(2)}) collective-permute-start(f32[16,2048]{1,0:T(8,128)S(1)} %shard_map.80), channel_id=1, source_target_pairs={{0,28},{4,0},{8,4},{12,8},{16,12},{20,16},{24,20},{28,24},{1,29},{... | collective-permute-start | bytes 393224 | tf_op jit(solution)/shard_map/ppermute | solution.py:16

commit v10 on v9

--- a/solution.py
+++ b/solution.py
@@ -21,7 +21,7 @@
 
 
 def across(value, bit):
-    return lax.ppermute(value, "bf", [(n, n ^ 1 << bit) for n in range(lax.axis_size("bf"))])
+    return lax.ppermute(value, "bf", [(n, n ^ (1 << bit | 1)) for n in range(lax.axis_size("bf"))])
 
 
 def call(body, shapes, specs, flops, moved, *operands, scratch=()):
@@ -114,7 +114,7 @@
     weights = (mine_ref, theirs_ref)
     if sections[0]:
         states_ref, other_ref = first_refs
-        states, others = [states_ref[0], states_ref[1]], [other_ref[0], other_ref[1]]
+        states, others = [states_ref[0], states_ref[1]], [other_ref[1], other_ref[0]]
     else:
         states = [ref[...] for ref in first_refs]
         others = states[::-1]

time: 22.1 us -> 23.5 us (1.063); the launches traced: 22 us -> 23.1 us
  waiting for transfers between devices: 12.7 us -> 14 us
    ppermute x2, waiting for transfers between devices: 7.52 us -> 9.82 us  [shifted(): lax.ppermute(value, axis, [(source, (source + distance) % size) for sourc...]
    ppermute x2, waiting for transfers between devices: 4.44 us -> 3.39 us  [across(): lax.ppermute(value, 'bf', [(n, n ^ (1 << bit | 1)) for n in range(lax.axi...]
where the time goes in v10:
time: 23.5 us; the launch traced here: 23.1 us
  waiting for transfers between devices  14 us (60%)
  starting transfers between devices  5.42 us (23%)
  Pallas kernels  2.58 us (11%)
  other arithmetic  0.68 us (3%)
  matrix products  0.37 us (2%)
    ppermute x2, waiting for transfers between devices, shifted(): lax.ppermute(value, axis, [(source, (source + distance) % size) for sourc...  9.82 us
    ppermute x2, waiting for transfers between devices, across(): lax.ppermute(value, 'bf', [(n, n ^ (1 << bit | 1)) for n in range(lax.axi...  3.39 us
    ppermute x2, starting transfers between devices, across(): lax.ppermute(value, 'bf', [(n, n ^ (1 << bit | 1)) for n in range(lax.axi...  3.07 us
    pallas_call x8, Pallas kernels, call(): pl.pallas_call(body, out_shape=shapes, in_specs=specs, out_specs=jax.tree...  2.58 us
    ppermute x2, starting transfers between devices, shifted(): lax.ppermute(value, axis, [(source, (source + distance) % size) for sourc...  1.77 us
    ppermute x2, waiting for transfers between devices, swapped(): lax.ppermute(value, 'bf', [(n, n ^ 1) for n in range(lax.axis_size('bf'))])  0.77 us
    add x1, other arithmetic, shards(): return diag + out_below + out_half  0.68 us
    ppermute x2, starting transfers between devices, swapped(): lax.ppermute(value, 'bf', [(n, n ^ 1) for n in range(lax.axis_size('bf'))])  0.58 us
  transfers between devices with their start and end apart: 6, of which 5 were waited for; matrix products, arithmetic and copies ran while one was open for 2% of the time, Pallas kernels for 2%

profile of v10, /device:TPU:24, one launch (start us, length us, event | category | flops | bytes accessed | tf_op | source)
XLA Modules:
  0.0 23.1 jit_solution(11125826018361997681)
XLA Ops:
  0.0 0.0 copy-start
  0.0 0.0 copy-start.1
  0.0 0.0 copy-start.2
  0.0 1.4 %shard_map.73 = (bf16[16,2048]{1,0:T(8,128)(2,1)S(1)}, bf16[128,2048]{1,0:T(8,128)(2,1)S(1)}, f32[3,128,128]{2,1,0:T(8,128)S(1)}, f32[1,128,128]{2,1,0:T(8,128)S(1)}) custom-call(f32[16,2048]{1,0:T(8,128)} %field_hbm.1, bf16[128,2048]{1,0:T(8,128)(2,1)} %bitcast.15, bf16[2,4,2,64,64]{4,3,2,1,0:T(8,128)(2,1)} %bitcast.17, s32[2,64]{1,0:T(2,128)} %perm_hbm.1), custom_call_target="tpu_custom_call" | custom-call | flops 16777216 | bytes 786432 | tf_op jit(solution)/shard_map/pallas_call | solution.py:28
  1.4 0.1 collective-permute-start.1
  1.5 0.2 %shard_map.74.refs_0_ = f32[16,128]{1,0:T(8,128)S(1)} custom-call(bf16[16,2048]{1,0:T(8,128)(2,1)S(1)} %get-tuple-element.11.xb_ref, bf16[128,2048]{1,0:T(8,128)(2,1)S(1)} %get-tuple-element.12.col_ref), custom_call_target="tpu_custom_call" | custom-call | flops 8388608 | bytes 786432 | tf_op jit(solution)/shard_map/pallas_call | solution.py:28
  1.7 0.5 %collective-permute-start = (f32[16,128]{1,0:T(8,128)S(1)}, f32[16,128]{1,0:T(8,128)S(1)}, u32[]{:S(2)}, u32[]{:S(2)}) collective-permute-start(f32[16,128]{1,0:T(8,128)S(1)} %shard_map.74.refs_0_), channel_id=1, source_target_pairs={{0,1},{1,0},{2,3},{3,2},{4,5},{5,4},{6,7},{7,6},{8,9},{9,8},{10,11... | collective-permute-start | bytes 24584 | tf_op jit(solution)/shard_map/ppermute | solution.py:20
  2.3 0.6 %collective-permute-done.1.refs_0_ = f32[3,128,128]{2,1,0:T(8,128)S(1)} collective-permute-done((f32[3,128,128]{2,1,0:T(8,128)S(1)}, f32[3,128,128]{2,1,0:T(8,128)S(1)}, u32[]{:S(2)}, u32[]{:S(2)}) %collective-permute-start.1) | collective-permute-done | bytes 196640 | tf_op jit(solution)/shard_map/ppermute | solution.py:20
  2.9 0.1 collective-permute-done.refs_1_
  3.1 0.1 shard_map.77.refs_0_
  3.2 1.5 %collective-permute-start.2 = (f32[2,16,128]{2,1,0:T(8,128)S(1)}, f32[2,16,128]{2,1,0:T(8,128)S(1)}, u32[]{:S(2)}, u32[]{:S(2)}) collective-permute-start(f32[2,16,128]{2,1,0:T(8,128)S(1)} %shard_map.77.refs_0_), channel_id=1, source_target_pairs={{0,3},{1,2},{2,1},{3,0},{4,7},{5,6},{6,5},{7,4},{8,11},{9,10},{10,... | collective-permute-start | bytes 49160 | tf_op jit(solution)/shard_map/ppermute | solution.py:24
  4.7 1.7 %collective-permute-done.2.refs_1_ = f32[2,16,128]{2,1,0:T(8,128)S(1)} collective-permute-done((f32[2,16,128]{2,1,0:T(8,128)S(1)}, f32[2,16,128]{2,1,0:T(8,128)S(1)}, u32[]{:S(2)}, u32[]{:S(2)}) %collective-permute-start.2) | collective-permute-done | bytes 16416 | tf_op jit(solution)/shard_map/ppermute | solution.py:24
  6.4 0.3 %shard_map.78.refs_0_ = f32[2,16,128]{2,1,0:T(8,128)S(1)} custom-call(f32[2,16,128]{2,1,0:T(8,128)S(1)} %shard_map.77.refs_0_, f32[2,16,128]{2,1,0:T(8,128)S(1)} %collective-permute-done.2.refs_1_, bf16[4,256,128]{2,1,0:T(8,128)(2,1)S(1)} %shard_map.75.refs_2_, bf16[3,256,128]{2,1,0:T(8,128)(2,1)S(1)} %shard_map.76.refs_3_), custom_call_target="tpu_custom_call" | custom-call | flops 6291456 | bytes 131072 | tf_op jit(solution)/shard_map/pallas_call | solution.py:28
  6.7 1.5 %collective-permute-start.3 = (f32[2,16,128]{2,1,0:T(8,128)S(1)}, f32[2,16,128]{2,1,0:T(8,128)S(1)}, u32[]{:S(2)}, u32[]{:S(2)}) collective-permute-start(f32[2,16,128]{2,1,0:T(8,128)S(1)} %shard_map.78.refs_0_), channel_id=1, source_target_pairs={{0,3},{1,2},{2,1},{3,0},{4,7},{5,6},{6,5},{7,4},{8,11},{9,10},{10,... | collective-permute-start | bytes 49160 | tf_op jit(solution)/shard_map/ppermute | solution.py:24
  8.3 1.7 %collective-permute-done.3.refs_1_ = f32[2,16,128]{2,1,0:T(8,128)S(1)} collective-permute-done((f32[2,16,128]{2,1,0:T(8,128)S(1)}, f32[2,16,128]{2,1,0:T(8,128)S(1)}, u32[]{:S(2)}, u32[]{:S(2)}) %collective-permute-start.3) | collective-permute-done | bytes 16416 | tf_op jit(solution)/shard_map/ppermute | solution.py:24
  9.9 0.0 copy-done.1
  10.0 0.0 copy-done.2
  10.0 0.3 %shard_map.79 = (f32[16,128]{1,0:T(8,128)S(1)}, f32[16,2048]{1,0:T(8,128)S(1)}) custom-call(f32[2,16,128]{2,1,0:T(8,128)S(1)} %shard_map.78.refs_0_, f32[2,16,128]{2,1,0:T(8,128)S(1)} %collective-permute-done.3.refs_1_, bf16[4,256,128]{2,1,0:T(8,128)(2,1)S(1)} %shard_map.75.refs_2_, bf16[3,256,128]{2,1,0:T(8,128)(2,1)S(1)} %shard_map.76.refs_3_, ...), custom_call_target="tpu_custom_call" | custom-call | flops 8388608 | bytes 1048576 | tf_op jit(solution)/shard_map/pallas_call | solution.py:28
  10.3 0.4 %collective-permute-start.5 = (f32[16,2048]{1,0:T(8,128)S(1)}, f32[16,2048]{1,0:T(8,128)S(1)}, u32[]{:S(2)}, u32[]{:S(2)}) collective-permute-start(f32[16,2048]{1,0:T(8,128)S(1)} %get-tuple-element.16), channel_id=1, source_target_pairs={{0,16},{4,20},{8,24},{12,28},{16,0},{20,4},{24,8},{28,12},{1,17},{... | collective-permute-start | bytes 393224 | tf_op jit(solution)/shard_map/ppermute | solution.py:16
  10.6 0.2 shard_map.80
  10.8 1.4 %collective-permute-start.4 = (f32[16,2048]{1,0:T(8,128)S(1)}, f32[16,2048]{1,0:T(8,128)S(1)}, u32[]{:S(2)}, u32[]{:S(2)}) collective-permute-start(f32[16,2048]{1,0:T(8,128)S(1)} %shard_map.80), channel_id=1, source_target_pairs={{0,28},{4,0},{8,4},{12,8},{16,12},{20,16},{24,20},{28,24},{1,29},{... | collective-permute-start | bytes 393224 | tf_op jit(solution)/shard_map/ppermute | solution.py:16
  12.2 0.0 copy-done
  12.2 0.4 %convolution_bitcast_fusion = f32[4,2,8,512]{3,2,1,0:T(8,128)S(1)} fusion(bf16[4,512,512]{2,1,0:T(8,128)(2,1)S(1)} %copy-done, bf16[2,4,8,512]{3,2,1,0:T(8,128)(2,1)S(1)} %bitcast.14), kind=kOutput, calls=%fused_computation | convolution fusion | flops 33554432 | bytes 2293760 | tf_op jit(solution)/shard_map/rnl,nlm->rnm/dot_general | solution.py:226
  12.6 9.8 %collective-permute-done.5 = f32[16,2048]{1,0:T(8,128)S(1)} collective-permute-done((f32[16,2048]{1,0:T(8,128)S(1)}, f32[16,2048]{1,0:T(8,128)S(1)}, u32[]{:S(2)}, u32[]{:S(2)}) %collective-permute-start.5) | collective-permute-done | bytes 131104 | tf_op jit(solution)/shard_map/ppermute | solution.py:16
  22.4 0.0 collective-permute-done.4
  22.4 0.7 %add_add_fusion = f32[16,2048]{1,0:T(8,128)} fusion(f32[16,2048]{1,0:T(8,128)S(1)} %collective-permute-done.5, f32[16,2048]{1,0:T(8,128)S(1)} %bitcast.16, f32[16,2048]{1,0:T(8,128)S(1)} %collective-permute-done.4), kind=kLoop, calls=%fused_computation.1 | loop fusion | flops 65536 | bytes 524288 | tf_op jit(solution)/shard_map/add | solution.py:232
  (3 shorter events, 0.1 us)
Async XLA Ops:
  0.0 12.2 %copy-start = (bf16[4,512,512]{2,1,0:T(8,128)(2,1)S(1)}, bf16[4,512,512]{2,1,0:T(8,128)(2,1)}, u32[]{:S(2)}) copy-start(bf16[4,512,512]{2,1,0:T(8,128)(2,1)} %param.8) | copy-start | bytes 6291460
  0.0 9.9 %copy-start.1 = (bf16[2,64,2048]{2,1,0:T(8,128)(2,1)S(1)}, bf16[2,64,2048]{2,1,0:T(8,128)(2,1)}, u32[]{:S(2)}) copy-start(bf16[2,64,2048]{2,1,0:T(8,128)(2,1)} %param.10) | copy-start | bytes 1572868
  0.0 9.9 %copy-start.2 = (s32[2,8]{1,0:T(2,128)S(1)}, s32[2,8]{1,0:T(2,128)}, u32[]{:S(2)}) copy-start(s32[2,8]{1,0:T(2,128)} %refs_2_.1) | copy-start | bytes 196
  1.4 1.5 %collective-permute-start.1 = (f32[3,128,128]{2,1,0:T(8,128)S(1)}, f32[3,128,128]{2,1,0:T(8,128)S(1)}, u32[]{:S(2)}, u32[]{:S(2)}) collective-permute-start(f32[3,128,128]{2,1,0:T(8,128)S(1)} %get-tuple-element.13.refs_0_), channel_id=1, source_target_pairs={{0,1},{1,0},{2,3},{3,2},{4,5},{5,4},{6,7},{7,6},{8,9},{9,8},{10,11... | collective-permute-start | bytes 589832 | tf_op jit(solution)/shard_map/ppermute | solution.py:20
  1.7 1.3 %collective-permute-start = (f32[16,128]{1,0:T(8,128)S(1)}, f32[16,128]{1,0:T(8,128)S(1)}, u32[]{:S(2)}, u32[]{:S(2)}) collective-permute-start(f32[16,128]{1,0:T(8,128)S(1)} %shard_map.74.refs_0_), channel_id=1, source_target_pairs={{0,1},{1,0},{2,3},{3,2},{4,5},{5,4},{6,7},{7,6},{8,9},{9,8},{10,11... | collective-permute-start | bytes 24584 | tf_op jit(solution)/shard_map/ppermute | solution.py:20
  3.2 3.2 %collective-permute-start.2 = (f32[2,16,128]{2,1,0:T(8,128)S(1)}, f32[2,16,128]{2,1,0:T(8,128)S(1)}, u32[]{:S(2)}, u32[]{:S(2)}) collective-permute-start(f32[2,16,128]{2,1,0:T(8,128)S(1)} %shard_map.77.refs_0_), channel_id=1, source_target_pairs={{0,3},{1,2},{2,1},{3,0},{4,7},{5,6},{6,5},{7,4},{8,11},{9,10},{10,... | collective-permute-start | bytes 49160 | tf_op jit(solution)/shard_map/ppermute | solution.py:24
  6.7 3.2 %collective-permute-start.3 = (f32[2,16,128]{2,1,0:T(8,128)S(1)}, f32[2,16,128]{2,1,0:T(8,128)S(1)}, u32[]{:S(2)}, u32[]{:S(2)}) collective-permute-start(f32[2,16,128]{2,1,0:T(8,128)S(1)} %shard_map.78.refs_0_), channel_id=1, source_target_pairs={{0,3},{1,2},{2,1},{3,0},{4,7},{5,6},{6,5},{7,4},{8,11},{9,10},{10,... | collective-permute-start | bytes 49160 | tf_op jit(solution)/shard_map/ppermute | solution.py:24
  10.3 12.2 %collective-permute-start.5 = (f32[16,2048]{1,0:T(8,128)S(1)}, f32[16,2048]{1,0:T(8,128)S(1)}, u32[]{:S(2)}, u32[]{:S(2)}) collective-permute-start(f32[16,2048]{1,0:T(8,128)S(1)} %get-tuple-element.16), channel_id=1, source_target_pairs={{0,16},{4,20},{8,24},{12,28},{16,0},{20,4},{24,8},{28,12},{1,17},{... | collective-permute-start | bytes 393224 | tf_op jit(solution)/shard_map/ppermute | solution.py:16
  10.8 11.6 %collective-permute-start.4 = (f32[16,2048]{1,0:T(8,128)S(1)}, f32[16,2048]{1,0:T(8,128)S(1)}, u32[]{:S(2)}, u32[]{:S(2)}) collective-permute-start(f32[16,2048]{1,0:T(8,128)S(1)} %shard_map.80), channel_id=1, source_target_pairs={{0,28},{4,0},{8,4},{12,8},{16,12},{20,16},{24,20},{28,24},{1,29},{... | collective-permute-start | bytes 393224 | tf_op jit(solution)/shard_map/ppermute | solution.py:16

commit v11 on v9

--- a/solution.py
+++ b/solution.py
@@ -24,12 +24,12 @@
     return lax.ppermute(value, "bf", [(n, n ^ 1 << bit) for n in range(lax.axis_size("bf"))])
 
 
-def call(body, shapes, specs, flops, moved, *operands, scratch=()):
+def call(body, shapes, specs, flops, moved, *operands, scratch=(), out=VMEM):
     return pl.pallas_call(
         body,
         out_shape=shapes,
         in_specs=specs,
-        out_specs=jax.tree.map(lambda _: VMEM, shapes),
+        out_specs=jax.tree.map(lambda _: out, shapes),
         scratch_shapes=scratch,
         cost_estimate=pl.CostEstimate(flops=flops, bytes_accessed=moved, transcendentals=0),
         compiler_params=pltpu.CompilerParams(vmem_limit_bytes=16 * 2**20),
@@ -138,16 +138,32 @@
     return (jnp.where(chosen, state, 0.0) if half else jnp.where(chosen, 0.0, state)).astype(BF16)
 
 
-def last_step(sections, final, rank_size, half_shift, first_ref, second_ref, mine_ref, theirs_ref, row_ref, owner_ref, state_ref, half_ref):
+def last_step(sections, final, rank_size, half_shift, first_ref, second_ref, mine_ref, theirs_ref, row_ref, owner_ref, state_ref, *half_refs):
     state = run_sections(sections, final, (first_ref, second_ref), mine_ref, theirs_ref, None)
     state_ref[...] = state
     rank = level_rank(state, rank_size, half_shift, owner_ref, True)
-    half_ref[...] = jnp.dot(rank, row_ref[...], preferred_element_type=F32)
+    outs = jnp.dot(rank, row_ref[...], preferred_element_type=F32)
+    count = half_refs[0].shape[0]
+    for n, half_ref in enumerate(half_refs):
+        half_ref[...] = outs[n * count : (n + 1) * count]
 
 
 def expand_below(rank_size, half_shift, state_ref, row_ref, owner_ref, below_ref):
     rank = level_rank(state_ref[...], rank_size, half_shift, owner_ref, False)
     below_ref[...] = jnp.dot(rank, row_ref[...], preferred_element_type=F32)
+
+
+def combine(diag_ref, below_ref, *refs):
+    *half_refs, out_hbm, sum_ref, sems = refs
+    count = half_refs[0].shape[0]
+    copies = []
+    for n, half_ref in enumerate(half_refs):
+        part = pl.ds(n * count, count)
+        sum_ref[part, :] = diag_ref[part, :] + below_ref[part, :] + half_ref[...]
+        copies.append(pltpu.make_async_copy(sum_ref.at[part, :], out_hbm.at[part, :], sems.at[n]))
+        copies[-1].start()
+    for copy in copies:
+        copy.wait()
 
 
 def shards(field, leaf_inverse, col_factor, row_factor, mixing, row_owner, rank_perm):
@@ -212,16 +228,17 @@
         first_states = (states, across(states, (run[-1] + 1) % bits))
     expand_cost = (2 * vectors * width * rows, 4 * width * rows)
     expand = row_factor.reshape(width, rows)
-    state, out_half = call(
+    parts = 2
+    state, *out_half = call(
         lambda *refs: last_step(runs[-1], final, rank_size, groups // 2, *refs),
-        [array(vectors, width), array(vectors, rows)],
+        [array(vectors, width)] + [array(vectors // parts, rows)] * parts,
         [VMEM] * 6, *expand_cost, *first_states, mine, theirs, expand, row_owner,
     )
     out_below = call(
         lambda *refs: expand_below(rank_size, groups // 2, *refs), array(vectors, rows),
         [VMEM] * 3, *expand_cost, state, expand, row_owner,
     )
-    out_half = shifted(out_half, "grp", groups // 2)
+    out_half = [shifted(part, "grp", groups // 2) for part in out_half]
     out_below = shifted(out_below, "grp", groups - 1)
     diag = jnp.einsum(
         "rnl,nlm->rnm",
@@ -229,7 +246,11 @@
         leaf_inverse,
         preferred_element_type=F32,
     ).reshape(vectors, rows)
-    return diag + out_below + out_half
+    return call(
+        combine, array(vectors, rows), [VMEM] * (2 + parts), 2 * vectors * rows, 16 * vectors * rows,
+        diag, out_below, *out_half,
+        scratch=[pltpu.VMEM((vectors, rows), F32), pltpu.SemaphoreType.DMA((parts,))], out=HBM,
+    )
 
 
 def solution(mesh):

time: 22.1 us -> 23.9 us (1.081)
  the two profiles are of different devices: /device:TPU:24 before, /device:TPU:0 now
where the time goes in v11:
time: 23.9 us; the launch traced here: 23.8 us
  starting transfers between devices  13.4 us (56%)
  waiting for transfers between devices  6.61 us (28%)
  Pallas kernels  3.26 us (14%)
  matrix products  0.37 us (2%)
    ppermute x3, starting transfers between devices, shifted(): lax.ppermute(value, axis, [(source, (source + distance) % size) for sourc...  8.01 us
    ppermute x2, starting transfers between devices, across(): lax.ppermute(value, 'bf', [(n, n ^ 1 << bit) for n in range(lax.axis_size...  4.83 us
    ppermute x2, waiting for transfers between devices, across(): lax.ppermute(value, 'bf', [(n, n ^ 1 << bit) for n in range(lax.axis_size...  3.44 us
    pallas_call x9, Pallas kernels, call(): pl.pallas_call(body, out_shape=shapes, in_specs=specs, out_specs=jax.tree...  3.26 us
    ppermute x3, waiting for transfers between devices, shifted(): lax.ppermute(value, axis, [(source, (source + distance) % size) for sourc...  2.11 us
    ppermute x2, waiting for transfers between devices, swapped(): lax.ppermute(value, 'bf', [(n, n ^ 1) for n in range(lax.axis_size('bf'))])  1.06 us
    ppermute x2, starting transfers between devices, swapped(): lax.ppermute(value, 'bf', [(n, n ^ 1) for n in range(lax.axis_size('bf'))])  0.59 us
  transfers between devices with their start and end apart: 7, of which 6 were waited for; matrix products, arithmetic and copies ran while one was open for 2% of the time, Pallas kernels for 2%

profile of v11, /device:TPU:0, one launch (start us, length us, event | category | flops | bytes accessed | tf_op | source)
XLA Modules:
  0.0 23.8 jit_solution(10666224990964020702)
XLA Ops:
  0.0 0.0 copy-start
  0.0 0.0 copy-start.2
  0.0 0.0 copy-start.1
  0.0 1.4 %shard_map.73 = (bf16[16,2048]{1,0:T(8,128)(2,1)S(1)}, bf16[128,2048]{1,0:T(8,128)(2,1)S(1)}, f32[3,128,128]{2,1,0:T(8,128)S(1)}, f32[1,128,128]{2,1,0:T(8,128)S(1)}) custom-call(f32[16,2048]{1,0:T(8,128)} %field_hbm.1, bf16[128,2048]{1,0:T(8,128)(2,1)} %bitcast.16, bf16[2,4,2,64,64]{4,3,2,1,0:T(8,128)(2,1)} %bitcast.17, s32[2,64]{1,0:T(2,128)} %perm_hbm.1), custom_call_target="tpu_custom_call" | custom-call | flops 16777216 | bytes 786432 | tf_op jit(solution)/shard_map/pallas_call | solution.py:28
  1.4 0.5 %collective-permute-start.1 = (f32[3,128,128]{2,1,0:T(8,128)S(1)}, f32[3,128,128]{2,1,0:T(8,128)S(1)}, u32[]{:S(2)}, u32[]{:S(2)}) collective-permute-start(f32[3,128,128]{2,1,0:T(8,128)S(1)} %get-tuple-element.14.refs_0_), channel_id=1, source_target_pairs={{0,1},{1,0},{2,3},{3,2},{4,5},{5,4},{6,7},{7,6},{8,9},{9,8},{10,11... | collective-permute-start | bytes 589832 | tf_op jit(solution)/shard_map/ppermute | solution.py:20
  1.9 0.2 shard_map.74.refs_0_
  2.2 0.1 collective-permute-start
  2.3 0.7 %collective-permute-done.1.refs_0_ = f32[3,128,128]{2,1,0:T(8,128)S(1)} collective-permute-done((f32[3,128,128]{2,1,0:T(8,128)S(1)}, f32[3,128,128]{2,1,0:T(8,128)S(1)}, u32[]{:S(2)}, u32[]{:S(2)}) %collective-permute-start.1) | collective-permute-done | bytes 196640 | tf_op jit(solution)/shard_map/ppermute | solution.py:20
  3.0 0.3 %collective-permute-done.refs_1_ = f32[16,128]{1,0:T(8,128)S(1)} collective-permute-done((f32[16,128]{1,0:T(8,128)S(1)}, f32[16,128]{1,0:T(8,128)S(1)}, u32[]{:S(2)}, u32[]{:S(2)}) %collective-permute-start) | collective-permute-done | bytes 8224 | tf_op jit(solution)/shard_map/ppermute | solution.py:20
  3.3 0.1 shard_map.77.refs_0_
  3.5 2.7 %collective-permute-start.2 = (f32[2,16,128]{2,1,0:T(8,128)S(1)}, f32[2,16,128]{2,1,0:T(8,128)S(1)}, u32[]{:S(2)}, u32[]{:S(2)}) collective-permute-start(f32[2,16,128]{2,1,0:T(8,128)S(1)} %shard_map.77.refs_0_), channel_id=1, source_target_pairs={{0,2},{1,3},{2,0},{3,1},{4,6},{5,7},{6,4},{7,5},{8,10},{9,11},{10,... | collective-permute-start | bytes 49160 | tf_op jit(solution)/shard_map/ppermute | solution.py:24
  6.2 1.7 %collective-permute-done.2.refs_1_ = f32[2,16,128]{2,1,0:T(8,128)S(1)} collective-permute-done((f32[2,16,128]{2,1,0:T(8,128)S(1)}, f32[2,16,128]{2,1,0:T(8,128)S(1)}, u32[]{:S(2)}, u32[]{:S(2)}) %collective-permute-start.2) | collective-permute-done | bytes 16416 | tf_op jit(solution)/shard_map/ppermute | solution.py:24
  8.0 0.3 %shard_map.78.refs_0_ = f32[2,16,128]{2,1,0:T(8,128)S(1)} custom-call(f32[2,16,128]{2,1,0:T(8,128)S(1)} %shard_map.77.refs_0_, f32[2,16,128]{2,1,0:T(8,128)S(1)} %collective-permute-done.2.refs_1_, bf16[4,256,128]{2,1,0:T(8,128)(2,1)S(1)} %shard_map.75.refs_2_, bf16[3,256,128]{2,1,0:T(8,128)(2,1)S(1)} %shard_map.76.refs_3_), custom_call_target="tpu_custom_call" | custom-call | flops 6291456 | bytes 131072 | tf_op jit(solution)/shard_map/pallas_call | solution.py:28
  8.2 2.1 %collective-permute-start.3 = (f32[2,16,128]{2,1,0:T(8,128)S(1)}, f32[2,16,128]{2,1,0:T(8,128)S(1)}, u32[]{:S(2)}, u32[]{:S(2)}) collective-permute-start(f32[2,16,128]{2,1,0:T(8,128)S(1)} %shard_map.78.refs_0_), channel_id=1, source_target_pairs={{0,2},{1,3},{2,0},{3,1},{4,6},{5,7},{6,4},{7,5},{8,10},{9,11},{10,... | collective-permute-start | bytes 49160 | tf_op jit(solution)/shard_map/ppermute | solution.py:24
  10.3 1.7 %collective-permute-done.3.refs_1_ = f32[2,16,128]{2,1,0:T(8,128)S(1)} collective-permute-done((f32[2,16,128]{2,1,0:T(8,128)S(1)}, f32[2,16,128]{2,1,0:T(8,128)S(1)}, u32[]{:S(2)}, u32[]{:S(2)}) %collective-permute-start.3) | collective-permute-done | bytes 16416 | tf_op jit(solution)/shard_map/ppermute | solution.py:24
  12.0 0.0 copy-done.2
  12.0 0.0 copy-done.1
  12.1 0.3 %shard_map.79 = (f32[16,128]{1,0:T(8,128)S(1)}, f32[8,2048]{1,0:T(8,128)S(1)}, f32[8,2048]{1,0:T(8,128)S(1)}) custom-call(f32[2,16,128]{2,1,0:T(8,128)S(1)} %shard_map.78.refs_0_, f32[2,16,128]{2,1,0:T(8,128)S(1)} %collective-permute-done.3.refs_1_, bf16[4,256,128]{2,1,0:T(8,128)(2,1)S(1)} %shard_map.75.refs_2_, bf16[3,256,128]{2,1,0:T(8,128)(2,1)S(1)} %shard_map.76.refs_3_, ...), custom_call_target="tpu_custom_call" | custom-call | flops 8388608 | bytes 1048576 | tf_op jit(solution)/shard_map/pallas_call | solution.py:28
  12.4 3.1 %collective-permute-start.5 = (f32[8,2048]{1,0:T(8,128)S(1)}, f32[8,2048]{1,0:T(8,128)S(1)}, u32[]{:S(2)}, u32[]{:S(2)}) collective-permute-start(f32[8,2048]{1,0:T(8,128)S(1)} %get-tuple-element.17), channel_id=1, source_target_pairs={{0,16},{4,20},{8,24},{12,28},{16,0},{20,4},{24,8},{28,12},{1,17},{... | collective-permute-start | bytes 196616 | tf_op jit(solution)/shard_map/ppermute | solution.py:16
  15.5 0.1 collective-permute-start.6
  15.6 0.2 shard_map.80
  15.8 4.8 %collective-permute-start.4 = (f32[16,2048]{1,0:T(8,128)S(1)}, f32[16,2048]{1,0:T(8,128)S(1)}, u32[]{:S(2)}, u32[]{:S(2)}) collective-permute-start(f32[16,2048]{1,0:T(8,128)S(1)} %shard_map.80), channel_id=1, source_target_pairs={{0,28},{4,0},{8,4},{12,8},{16,12},{20,16},{24,20},{28,24},{1,29},{... | collective-permute-start | bytes 393224 | tf_op jit(solution)/shard_map/ppermute | solution.py:16
  20.6 0.0 copy-done
  20.6 0.4 %convolution_bitcast_fusion = f32[4,2,8,512]{3,2,1,0:T(8,128)S(1)} fusion(bf16[4,512,512]{2,1,0:T(8,128)(2,1)S(1)} %copy-done, bf16[2,4,8,512]{3,2,1,0:T(8,128)(2,1)S(1)} %bitcast.15), kind=kOutput, calls=%fused_computation | convolution fusion | flops 33554432 | bytes 2293760 | tf_op jit(solution)/shard_map/rnl,nlm->rnm/dot_general | solution.py:243
  21.0 0.0 collective-permute-done.5.refs_0_
  21.0 1.1 %collective-permute-done.6.refs_1_ = f32[8,2048]{1,0:T(8,128)S(1)} collective-permute-done((f32[8,2048]{1,0:T(8,128)S(1)}, f32[8,2048]{1,0:T(8,128)S(1)}, u32[]{:S(2)}, u32[]{:S(2)}) %collective-permute-start.6) | collective-permute-done | bytes 65568 | tf_op jit(solution)/shard_map/ppermute | solution.py:16
  22.1 1.0 %collective-permute-done.4.below_ref = f32[16,2048]{1,0:T(8,128)S(1)} collective-permute-done((f32[16,2048]{1,0:T(8,128)S(1)}, f32[16,2048]{1,0:T(8,128)S(1)}, u32[]{:S(2)}, u32[]{:S(2)}) %collective-permute-start.4) | collective-permute-done | bytes 131104 | tf_op jit(solution)/shard_map/ppermute | solution.py:16
  23.1 0.7 %shard_map.81 = f32[16,2048]{1,0:T(8,128)} custom-call(f32[16,2048]{1,0:T(8,128)S(1)} %bitcast.14, f32[16,2048]{1,0:T(8,128)S(1)} %collective-permute-done.4.below_ref, f32[8,2048]{1,0:T(8,128)S(1)} %collective-permute-done.5.refs_0_, f32[8,2048]{1,0:T(8,128)S(1)} %collective-permute-done.6.refs_1_), custom_call_target="tpu_custom_call" | custom-call | flops 65536 | bytes 524288 | tf_op jit(solution)/shard_map/pallas_call | solution.py:28
  (3 shorter events, 0.1 us)
Async XLA Ops:
  0.0 20.6 %copy-start = (bf16[4,512,512]{2,1,0:T(8,128)(2,1)S(1)}, bf16[4,512,512]{2,1,0:T(8,128)(2,1)}, u32[]{:S(2)}) copy-start(bf16[4,512,512]{2,1,0:T(8,128)(2,1)} %param.8) | copy-start | bytes 6291460
  0.0 12.0 %copy-start.2 = (s32[2,8]{1,0:T(2,128)S(1)}, s32[2,8]{1,0:T(2,128)}, u32[]{:S(2)}) copy-start(s32[2,8]{1,0:T(2,128)} %refs_2_.1) | copy-start | bytes 196
  0.0 12.0 %copy-start.1 = (bf16[2,64,2048]{2,1,0:T(8,128)(2,1)S(1)}, bf16[2,64,2048]{2,1,0:T(8,128)(2,1)}, u32[]{:S(2)}) copy-start(bf16[2,64,2048]{2,1,0:T(8,128)(2,1)} %param.10) | copy-start | bytes 1572868
  1.4 1.6 %collective-permute-start.1 = (f32[3,128,128]{2,1,0:T(8,128)S(1)}, f32[3,128,128]{2,1,0:T(8,128)S(1)}, u32[]{:S(2)}, u32[]{:S(2)}) collective-permute-start(f32[3,128,128]{2,1,0:T(8,128)S(1)} %get-tuple-element.14.refs_0_), channel_id=1, source_target_pairs={{0,1},{1,0},{2,3},{3,2},{4,5},{5,4},{6,7},{7,6},{8,9},{9,8},{10,11... | collective-permute-start | bytes 589832 | tf_op jit(solution)/shard_map/ppermute | solution.py:20
  2.2 1.2 %collective-permute-start = (f32[16,128]{1,0:T(8,128)S(1)}, f32[16,128]{1,0:T(8,128)S(1)}, u32[]{:S(2)}, u32[]{:S(2)}) collective-permute-start(f32[16,128]{1,0:T(8,128)S(1)} %shard_map.74.refs_0_), channel_id=1, source_target_pairs={{0,1},{1,0},{2,3},{3,2},{4,5},{5,4},{6,7},{7,6},{8,9},{9,8},{10,11... | collective-permute-start | bytes 24584 | tf_op jit(solution)/shard_map/ppermute | solution.py:20
  3.5 4.5 %collective-permute-start.2 = (f32[2,16,128]{2,1,0:T(8,128)S(1)}, f32[2,16,128]{2,1,0:T(8,128)S(1)}, u32[]{:S(2)}, u32[]{:S(2)}) collective-permute-start(f32[2,16,128]{2,1,0:T(8,128)S(1)} %shard_map.77.refs_0_), channel_id=1, source_target_pairs={{0,2},{1,3},{2,0},{3,1},{4,6},{5,7},{6,4},{7,5},{8,10},{9,11},{10,... | collective-permute-start | bytes 49160 | tf_op jit(solution)/shard_map/ppermute | solution.py:24
  8.2 3.8 %collective-permute-start.3 = (f32[2,16,128]{2,1,0:T(8,128)S(1)}, f32[2,16,128]{2,1,0:T(8,128)S(1)}, u32[]{:S(2)}, u32[]{:S(2)}) collective-permute-start(f32[2,16,128]{2,1,0:T(8,128)S(1)} %shard_map.78.refs_0_), channel_id=1, source_target_pairs={{0,2},{1,3},{2,0},{3,1},{4,6},{5,7},{6,4},{7,5},{8,10},{9,11},{10,... | collective-permute-start | bytes 49160 | tf_op jit(solution)/shard_map/ppermute | solution.py:24
  12.4 8.6 %collective-permute-start.5 = (f32[8,2048]{1,0:T(8,128)S(1)}, f32[8,2048]{1,0:T(8,128)S(1)}, u32[]{:S(2)}, u32[]{:S(2)}) collective-permute-start(f32[8,2048]{1,0:T(8,128)S(1)} %get-tuple-element.17), channel_id=1, source_target_pairs={{0,16},{4,20},{8,24},{12,28},{16,0},{20,4},{24,8},{28,12},{1,17},{... | collective-permute-start | bytes 196616 | tf_op jit(solution)/shard_map/ppermute | solution.py:16
  15.5 6.6 %collective-permute-start.6 = (f32[8,2048]{1,0:T(8,128)S(1)}, f32[8,2048]{1,0:T(8,128)S(1)}, u32[]{:S(2)}, u32[]{:S(2)}) collective-permute-start(f32[8,2048]{1,0:T(8,128)S(1)} %get-tuple-element.18), channel_id=1, source_target_pairs={{0,16},{4,20},{8,24},{12,28},{16,0},{20,4},{24,8},{28,12},{1,17},{... | collective-permute-start | bytes 196616 | tf_op jit(solution)/shard_map/ppermute | solution.py:16
  15.8 7.3 %collective-permute-start.4 = (f32[16,2048]{1,0:T(8,128)S(1)}, f32[16,2048]{1,0:T(8,128)S(1)}, u32[]{:S(2)}, u32[]{:S(2)}) collective-permute-start(f32[16,2048]{1,0:T(8,128)S(1)} %shard_map.80), channel_id=1, source_target_pairs={{0,28},{4,0},{8,4},{12,8},{16,12},{20,16},{24,20},{28,24},{1,29},{... | collective-permute-start | bytes 393224 | tf_op jit(solution)/shard_map/ppermute | solution.py:16

commit v12 on v9

--- a/solution.py
+++ b/solution.py
@@ -14,6 +14,23 @@
 def shifted(value, axis, distance):
     size = lax.axis_size(axis)
     return lax.ppermute(value, axis, [(source, (source + distance) % size) for source in range(size)])
+
+
+def below_in_half(value):
+    half = lax.axis_size("grp") // 2
+    pairs = [(g, g - 1 if g % half else g + half - 1) for g in range(2 * half)]
+    return lax.ppermute(value, "grp", pairs)
+
+
+def between_halves(value):
+    size, places = lax.axis_size("grp"), lax.axis_size("bf")
+    half = size // 2
+    pairs = []
+    for g in range(size):
+        for b in range(places):
+            target = ((g + half) % size, b) if g % half == half - 1 else (g, b ^ 2)
+            pairs.append((g * places + b, target[0] * places + target[1]))
+    return lax.ppermute(value, ("grp", "bf"), pairs)
 
 
 def swapped(value):
@@ -138,16 +155,16 @@
     return (jnp.where(chosen, state, 0.0) if half else jnp.where(chosen, 0.0, state)).astype(BF16)
 
 
-def last_step(sections, final, rank_size, half_shift, first_ref, second_ref, mine_ref, theirs_ref, row_ref, owner_ref, state_ref, half_ref):
+def last_step(sections, final, rank_size, half_shift, first_ref, second_ref, mine_ref, theirs_ref, row_ref, owner_ref, state_ref, below_ref):
     state = run_sections(sections, final, (first_ref, second_ref), mine_ref, theirs_ref, None)
     state_ref[...] = state
-    rank = level_rank(state, rank_size, half_shift, owner_ref, True)
+    rank = level_rank(state, rank_size, half_shift, owner_ref, False)
+    below_ref[...] = jnp.dot(rank, row_ref[...], preferred_element_type=F32)
+
+
+def expand_half(rank_size, half_shift, state_ref, row_ref, owner_ref, half_ref):
+    rank = level_rank(state_ref[...], rank_size, half_shift, owner_ref, True)
     half_ref[...] = jnp.dot(rank, row_ref[...], preferred_element_type=F32)
-
-
-def expand_below(rank_size, half_shift, state_ref, row_ref, owner_ref, below_ref):
-    rank = level_rank(state_ref[...], rank_size, half_shift, owner_ref, False)
-    below_ref[...] = jnp.dot(rank, row_ref[...], preferred_element_type=F32)
 
 
 def shards(field, leaf_inverse, col_factor, row_factor, mixing, row_owner, rank_perm):
@@ -212,24 +229,26 @@
         first_states = (states, across(states, (run[-1] + 1) % bits))
     expand_cost = (2 * vectors * width * rows, 4 * width * rows)
     expand = row_factor.reshape(width, rows)
-    state, out_half = call(
+    state, out_below = call(
         lambda *refs: last_step(runs[-1], final, rank_size, groups // 2, *refs),
         [array(vectors, width), array(vectors, rows)],
         [VMEM] * 6, *expand_cost, *first_states, mine, theirs, expand, row_owner,
     )
-    out_below = call(
-        lambda *refs: expand_below(rank_size, groups // 2, *refs), array(vectors, rows),
+    out_half = call(
+        lambda *refs: expand_half(rank_size, groups // 2, *refs), array(vectors, rows),
         [VMEM] * 3, *expand_cost, state, expand, row_owner,
     )
     out_half = shifted(out_half, "grp", groups // 2)
-    out_below = shifted(out_below, "grp", groups - 1)
+    turned = below_in_half(out_below)
+    crossed = between_halves(turned)
+    highest = lax.rem(lax.axis_index("grp"), groups // 2) == groups // 2 - 1
     diag = jnp.einsum(
         "rnl,nlm->rnm",
         xb.reshape(vectors, rows // order, order),
         leaf_inverse,
         preferred_element_type=F32,
     ).reshape(vectors, rows)
-    return diag + out_below + out_half
+    return diag + out_half + jnp.where(highest, crossed, turned)
 
 
 def solution(mesh):

time: 22.1 us -> 25 us (1.13)
  the two profiles are of different devices: /device:TPU:24 before, /device:TPU:10 now
where the time goes in v12:
time: 25 us; the launch traced here: 24.9 us
  waiting for transfers between devices  12.2 us (49%)
  starting transfers between devices  8.89 us (36%)
  Pallas kernels  2.58 us (10%)
  other arithmetic  0.68 us (3%)
  matrix products  0.37 us (1%)
    ppermute x2, waiting for transfers between devices, across(): lax.ppermute(value, 'bf', [(n, n ^ 1 << bit) for n in range(lax.axis_size...  4.44 us
    ppermute x1, waiting for transfers between devices, below_in_half(): return lax.ppermute(value, 'grp', pairs)  3.53 us
    ppermute x1, waiting for transfers between devices, between_halves(): return lax.ppermute(value, ('grp', 'bf'), pairs)  3.49 us
    ppermute x2, starting transfers between devices, across(): lax.ppermute(value, 'bf', [(n, n ^ 1 << bit) for n in range(lax.axis_size...  3.17 us
    ppermute x1, starting transfers between devices, shifted(): lax.ppermute(value, axis, [(source, (source + distance) % size) for sourc...  2.63 us
    pallas_call x8, Pallas kernels, call(): pl.pallas_call(body, out_shape=shapes, in_specs=specs, out_specs=jax.tree...  2.58 us
    ppermute x1, starting transfers between devices, between_halves(): return lax.ppermute(value, ('grp', 'bf'), pairs)  1.95 us
    ppermute x2, waiting for transfers between devices, swapped(): lax.ppermute(value, 'bf', [(n, n ^ 1) for n in range(lax.axis_size('bf'))])  0.77 us
  transfers between devices with their start and end apart: 7, of which 6 were waited for; matrix products, arithmetic and copies ran while one was open for 2% of the time, Pallas kernels for 2%

profile of v12, /device:TPU:10, one launch (start us, length us, event | category | flops | bytes accessed | tf_op | source)
XLA Modules:
  0.0 24.9 jit_solution(5656415940534816462)
XLA Ops:
  0.0 0.0 copy-start
  0.0 0.0 copy-start.1
  0.0 0.0 copy-start.2
  0.0 1.4 %shard_map.73 = (bf16[16,2048]{1,0:T(8,128)(2,1)S(1)}, bf16[128,2048]{1,0:T(8,128)(2,1)S(1)}, f32[3,128,128]{2,1,0:T(8,128)S(1)}, f32[1,128,128]{2,1,0:T(8,128)S(1)}) custom-call(f32[16,2048]{1,0:T(8,128)} %field_hbm.1, bf16[128,2048]{1,0:T(8,128)(2,1)} %bitcast.15, bf16[2,4,2,64,64]{4,3,2,1,0:T(8,128)(2,1)} %bitcast.17, s32[2,64]{1,0:T(2,128)} %perm_hbm.1), custom_call_target="tpu_custom_call" | custom-call | flops 16777216 | bytes 786432 | tf_op jit(solution)/shard_map/pallas_call | solution.py:45
  1.4 0.1 collective-permute-start.1
  1.5 0.2 shard_map.74.refs_0_
  1.7 0.5 %collective-permute-start = (f32[16,128]{1,0:T(8,128)S(1)}, f32[16,128]{1,0:T(8,128)S(1)}, u32[]{:S(2)}, u32[]{:S(2)}) collective-permute-start(f32[16,128]{1,0:T(8,128)S(1)} %shard_map.74.refs_0_), channel_id=1, source_target_pairs={{0,1},{1,0},{2,3},{3,2},{4,5},{5,4},{6,7},{7,6},{8,9},{9,8},{10,11... | collective-permute-start | bytes 24584 | tf_op jit(solution)/shard_map/ppermute | solution.py:37
  2.3 0.6 %collective-permute-done.1.refs_0_ = f32[3,128,128]{2,1,0:T(8,128)S(1)} collective-permute-done((f32[3,128,128]{2,1,0:T(8,128)S(1)}, f32[3,128,128]{2,1,0:T(8,128)S(1)}, u32[]{:S(2)}, u32[]{:S(2)}) %collective-permute-start.1) | collective-permute-done | bytes 196640 | tf_op jit(solution)/shard_map/ppermute | solution.py:37
  2.9 0.1 collective-permute-done.refs_1_
  3.1 0.1 shard_map.77.refs_0_
  3.2 1.6 %collective-permute-start.2 = (f32[2,16,128]{2,1,0:T(8,128)S(1)}, f32[2,16,128]{2,1,0:T(8,128)S(1)}, u32[]{:S(2)}, u32[]{:S(2)}) collective-permute-start(f32[2,16,128]{2,1,0:T(8,128)S(1)} %shard_map.77.refs_0_), channel_id=1, source_target_pairs={{0,2},{1,3},{2,0},{3,1},{4,6},{5,7},{6,4},{7,5},{8,10},{9,11},{10,... | collective-permute-start | bytes 49160 | tf_op jit(solution)/shard_map/ppermute | solution.py:41
  4.8 2.2 %collective-permute-done.2.refs_1_ = f32[2,16,128]{2,1,0:T(8,128)S(1)} collective-permute-done((f32[2,16,128]{2,1,0:T(8,128)S(1)}, f32[2,16,128]{2,1,0:T(8,128)S(1)}, u32[]{:S(2)}, u32[]{:S(2)}) %collective-permute-start.2) | collective-permute-done | bytes 16416 | tf_op jit(solution)/shard_map/ppermute | solution.py:41
  7.0 0.3 %shard_map.78.refs_0_ = f32[2,16,128]{2,1,0:T(8,128)S(1)} custom-call(f32[2,16,128]{2,1,0:T(8,128)S(1)} %shard_map.77.refs_0_, f32[2,16,128]{2,1,0:T(8,128)S(1)} %collective-permute-done.2.refs_1_, bf16[4,256,128]{2,1,0:T(8,128)(2,1)S(1)} %shard_map.75.refs_2_, bf16[3,256,128]{2,1,0:T(8,128)(2,1)S(1)} %shard_map.76.refs_3_), custom_call_target="tpu_custom_call" | custom-call | flops 6291456 | bytes 131072 | tf_op jit(solution)/shard_map/pallas_call | solution.py:45
  7.3 1.6 %collective-permute-start.3 = (f32[2,16,128]{2,1,0:T(8,128)S(1)}, f32[2,16,128]{2,1,0:T(8,128)S(1)}, u32[]{:S(2)}, u32[]{:S(2)}) collective-permute-start(f32[2,16,128]{2,1,0:T(8,128)S(1)} %shard_map.78.refs_0_), channel_id=1, source_target_pairs={{0,2},{1,3},{2,0},{3,1},{4,6},{5,7},{6,4},{7,5},{8,10},{9,11},{10,... | collective-permute-start | bytes 49160 | tf_op jit(solution)/shard_map/ppermute | solution.py:41
  8.9 2.2 %collective-permute-done.3.refs_1_ = f32[2,16,128]{2,1,0:T(8,128)S(1)} collective-permute-done((f32[2,16,128]{2,1,0:T(8,128)S(1)}, f32[2,16,128]{2,1,0:T(8,128)S(1)}, u32[]{:S(2)}, u32[]{:S(2)}) %collective-permute-start.3) | collective-permute-done | bytes 16416 | tf_op jit(solution)/shard_map/ppermute | solution.py:41
  11.1 0.0 copy-done.1
  11.1 0.0 copy-done.2
  11.1 0.3 %shard_map.79 = (f32[16,128]{1,0:T(8,128)S(1)}, f32[16,2048]{1,0:T(8,128)S(1)}) custom-call(f32[2,16,128]{2,1,0:T(8,128)S(1)} %shard_map.78.refs_0_, f32[2,16,128]{2,1,0:T(8,128)S(1)} %collective-permute-done.3.refs_1_, bf16[4,256,128]{2,1,0:T(8,128)(2,1)S(1)} %shard_map.75.refs_2_, bf16[3,256,128]{2,1,0:T(8,128)(2,1)S(1)} %shard_map.76.refs_3_, ...), custom_call_target="tpu_custom_call" | custom-call | flops 8388608 | bytes 1048576 | tf_op jit(solution)/shard_map/pallas_call | solution.py:45
  11.4 0.6 %collective-permute-start.5 = (f32[16,2048]{1,0:T(8,128)S(1)}, f32[16,2048]{1,0:T(8,128)S(1)}, u32[]{:S(2)}, u32[]{:S(2)}) collective-permute-start(f32[16,2048]{1,0:T(8,128)S(1)} %get-tuple-element.16), channel_id=1, source_target_pairs={{0,12},{4,0},{8,4},{12,8},{16,28},{20,16},{24,20},{28,24},{1,13},{... | collective-permute-start | bytes 393224 | tf_op jit(solution)/shard_map/ppermute | solution.py:22
  12.0 0.2 shard_map.80
  12.2 2.6 %collective-permute-start.4 = (f32[16,2048]{1,0:T(8,128)S(1)}, f32[16,2048]{1,0:T(8,128)S(1)}, u32[]{:S(2)}, u32[]{:S(2)}) collective-permute-start(f32[16,2048]{1,0:T(8,128)S(1)} %shard_map.80), channel_id=1, source_target_pairs={{0,16},{4,20},{8,24},{12,28},{16,0},{20,4},{24,8},{28,12},{1,17},{... | collective-permute-start | bytes 393224 | tf_op jit(solution)/shard_map/ppermute | solution.py:16
  14.8 3.5 %collective-permute-done.5 = f32[16,2048]{1,0:T(8,128)S(1)} collective-permute-done((f32[16,2048]{1,0:T(8,128)S(1)}, f32[16,2048]{1,0:T(8,128)S(1)}, u32[]{:S(2)}, u32[]{:S(2)}) %collective-permute-start.5) | collective-permute-done | bytes 131104 | tf_op jit(solution)/shard_map/ppermute | solution.py:22
  18.3 2.0 %collective-permute-start.6 = (f32[16,2048]{1,0:T(8,128)S(1)}, f32[16,2048]{1,0:T(8,128)S(1)}, u32[]{:S(2)}, u32[]{:S(2)}) collective-permute-start(f32[16,2048]{1,0:T(8,128)S(1)} %collective-permute-done.5), channel_id=1, source_target_pairs={{0,2},{1,3},{2,0},{3,1},{4,6},{5,7},{6,4},{7,5},{8,10},{9,11},{10,... | collective-permute-start | bytes 393224 | tf_op jit(solution)/shard_map/ppermute | solution.py:33
  20.3 0.0 copy-done
  20.3 0.4 %convolution_bitcast_fusion = f32[4,2,8,512]{3,2,1,0:T(8,128)S(1)} fusion(bf16[4,512,512]{2,1,0:T(8,128)(2,1)S(1)} %copy-done, bf16[2,4,8,512]{3,2,1,0:T(8,128)(2,1)S(1)} %bitcast.14), kind=kOutput, calls=%fused_computation | convolution fusion | flops 33554432 | bytes 2293760 | tf_op jit(solution)/shard_map/rnl,nlm->rnm/dot_general | solution.py:245
  20.7 0.0 collective-permute-done.4
  20.7 3.5 %collective-permute-done.6 = f32[16,2048]{1,0:T(8,128)S(1)} collective-permute-done((f32[16,2048]{1,0:T(8,128)S(1)}, f32[16,2048]{1,0:T(8,128)S(1)}, u32[]{:S(2)}, u32[]{:S(2)}) %collective-permute-start.6) | collective-permute-done | bytes 131104 | tf_op jit(solution)/shard_map/ppermute | solution.py:33
  24.2 0.7 %select_add_fusion = f32[16,2048]{1,0:T(8,128)} fusion(f32[16,2048]{1,0:T(8,128)S(1)} %collective-permute-done.6, f32[16,2048]{1,0:T(8,128)S(1)} %collective-permute-done.5, f32[16,2048]{1,0:T(8,128)S(1)} %bitcast.16, f32[16,2048]{1,0:T(8,128)S(1)} %collective-permute-done.4, pred[]{:T(512)S(6)} %eq.3), kind=kLoop, calls=%fused_computation.1 | loop fusion | flops 98304 | bytes 655361 | tf_op jit(solution)/shard_map/add | solution.py:251
  (3 shorter events, 0.1 us)
Async XLA Ops:
  0.0 20.3 %copy-start = (bf16[4,512,512]{2,1,0:T(8,128)(2,1)S(1)}, bf16[4,512,512]{2,1,0:T(8,128)(2,1)}, u32[]{:S(2)}) copy-start(bf16[4,512,512]{2,1,0:T(8,128)(2,1)} %param.8) | copy-start | bytes 6291460
  0.0 11.1 %copy-start.1 = (bf16[2,64,2048]{2,1,0:T(8,128)(2,1)S(1)}, bf16[2,64,2048]{2,1,0:T(8,128)(2,1)}, u32[]{:S(2)}) copy-start(bf16[2,64,2048]{2,1,0:T(8,128)(2,1)} %param.10) | copy-start | bytes 1572868
  0.0 11.1 %copy-start.2 = (s32[2,8]{1,0:T(2,128)S(1)}, s32[2,8]{1,0:T(2,128)}, u32[]{:S(2)}) copy-start(s32[2,8]{1,0:T(2,128)} %refs_2_.1) | copy-start | bytes 196
  1.4 1.5 %collective-permute-start.1 = (f32[3,128,128]{2,1,0:T(8,128)S(1)}, f32[3,128,128]{2,1,0:T(8,128)S(1)}, u32[]{:S(2)}, u32[]{:S(2)}) collective-permute-start(f32[3,128,128]{2,1,0:T(8,128)S(1)} %get-tuple-element.13.refs_0_), channel_id=1, source_target_pairs={{0,1},{1,0},{2,3},{3,2},{4,5},{5,4},{6,7},{7,6},{8,9},{9,8},{10,11... | collective-permute-start | bytes 589832 | tf_op jit(solution)/shard_map/ppermute | solution.py:37
  1.7 1.3 %collective-permute-start = (f32[16,128]{1,0:T(8,128)S(1)}, f32[16,128]{1,0:T(8,128)S(1)}, u32[]{:S(2)}, u32[]{:S(2)}) collective-permute-start(f32[16,128]{1,0:T(8,128)S(1)} %shard_map.74.refs_0_), channel_id=1, source_target_pairs={{0,1},{1,0},{2,3},{3,2},{4,5},{5,4},{6,7},{7,6},{8,9},{9,8},{10,11... | collective-permute-start | bytes 24584 | tf_op jit(solution)/shard_map/ppermute | solution.py:37
  3.2 3.8 %collective-permute-start.2 = (f32[2,16,128]{2,1,0:T(8,128)S(1)}, f32[2,16,128]{2,1,0:T(8,128)S(1)}, u32[]{:S(2)}, u32[]{:S(2)}) collective-permute-start(f32[2,16,128]{2,1,0:T(8,128)S(1)} %shard_map.77.refs_0_), channel_id=1, source_target_pairs={{0,2},{1,3},{2,0},{3,1},{4,6},{5,7},{6,4},{7,5},{8,10},{9,11},{10,... | collective-permute-start | bytes 49160 | tf_op jit(solution)/shard_map/ppermute | solution.py:41
  7.3 3.8 %collective-permute-start.3 = (f32[2,16,128]{2,1,0:T(8,128)S(1)}, f32[2,16,128]{2,1,0:T(8,128)S(1)}, u32[]{:S(2)}, u32[]{:S(2)}) collective-permute-start(f32[2,16,128]{2,1,0:T(8,128)S(1)} %shard_map.78.refs_0_), channel_id=1, source_target_pairs={{0,2},{1,3},{2,0},{3,1},{4,6},{5,7},{6,4},{7,5},{8,10},{9,11},{10,... | collective-permute-start | bytes 49160 | tf_op jit(solution)/shard_map/ppermute | solution.py:41
  11.4 6.9 %collective-permute-start.5 = (f32[16,2048]{1,0:T(8,128)S(1)}, f32[16,2048]{1,0:T(8,128)S(1)}, u32[]{:S(2)}, u32[]{:S(2)}) collective-permute-start(f32[16,2048]{1,0:T(8,128)S(1)} %get-tuple-element.16), channel_id=1, source_target_pairs={{0,12},{4,0},{8,4},{12,8},{16,28},{20,16},{24,20},{28,24},{1,13},{... | collective-permute-start | bytes 393224 | tf_op jit(solution)/shard_map/ppermute | solution.py:22
  12.2 8.5 %collective-permute-start.4 = (f32[16,2048]{1,0:T(8,128)S(1)}, f32[16,2048]{1,0:T(8,128)S(1)}, u32[]{:S(2)}, u32[]{:S(2)}) collective-permute-start(f32[16,2048]{1,0:T(8,128)S(1)} %shard_map.80), channel_id=1, source_target_pairs={{0,16},{4,20},{8,24},{12,28},{16,0},{20,4},{24,8},{28,12},{1,17},{... | collective-permute-start | bytes 393224 | tf_op jit(solution)/shard_map/ppermute | solution.py:16
  18.3 5.9 %collective-permute-start.6 = (f32[16,2048]{1,0:T(8,128)S(1)}, f32[16,2048]{1,0:T(8,128)S(1)}, u32[]{:S(2)}, u32[]{:S(2)}) collective-permute-start(f32[16,2048]{1,0:T(8,128)S(1)} %collective-permute-done.5), channel_id=1, source_target_pairs={{0,2},{1,3},{2,0},{3,1},{4,6},{5,7},{6,4},{7,5},{8,10},{9,11},{10,... | collective-permute-start | bytes 393224 | tf_op jit(solution)/shard_map/ppermute | solution.py:33

commit v13 on v9

--- a/solution.py
+++ b/solution.py
@@ -24,12 +24,12 @@
     return lax.ppermute(value, "bf", [(n, n ^ 1 << bit) for n in range(lax.axis_size("bf"))])
 
 
-def call(body, shapes, specs, flops, moved, *operands, scratch=()):
+def call(body, shapes, specs, flops, moved, *operands, scratch=(), out=VMEM):
     return pl.pallas_call(
         body,
         out_shape=shapes,
         in_specs=specs,
-        out_specs=jax.tree.map(lambda _: VMEM, shapes),
+        out_specs=jax.tree.map(lambda _: out, shapes),
         scratch_shapes=scratch,
         cost_estimate=pl.CostEstimate(flops=flops, bytes_accessed=moved, transcendentals=0),
         compiler_params=pltpu.CompilerParams(vmem_limit_bytes=16 * 2**20),
@@ -57,14 +57,22 @@
     return jnp.concatenate([mixing_ref[level, section, side].astype(F32) for level in range(levels)], axis=1)
 
 
+def split_rows(source, target, parts):
+    count = source.shape[0] // parts
+    return [(source.at[pl.ds(n * count, count)], target.at[pl.ds(n * count, count)]) for n in range(parts)]
+
+
 def load(field_hbm, col_hbm, mixing_hbm, perm_hbm, xb_ref, col_ref, sent_ref, kept_ref, field_ref, mixing_ref, perm_ref, sems):
-    pairs = [(mixing_hbm, mixing_ref), (perm_hbm, perm_ref), (field_hbm, field_ref), (col_hbm, col_ref)]
-    copies = [pltpu.make_async_copy(source, target, sems.at[n]) for n, (source, target) in enumerate(pairs)]
+    levels, sections, _, k, _ = mixing_ref.shape
+    first = [(perm_hbm, perm_ref)]
+    first += [(mixing_hbm.at[level], mixing_ref.at[level]) for level in range(levels)]
+    second = split_rows(field_hbm, field_ref, 2)
+    third = split_rows(col_hbm, col_ref, 4)
+    copies = [pltpu.make_async_copy(*pair, sems.at[n]) for n, pair in enumerate(first + second + third)]
     for copy in copies:
         copy.start()
-    copies[0].wait()
-    copies[1].wait()
-    levels, sections, _, k, _ = mixing_ref.shape
+    for copy in copies[: len(first)]:
+        copy.wait()
     row = lax.broadcasted_iota(jnp.int32, (k, k), 0)
     picks = jnp.concatenate([(row == perm_ref[level : level + 1, :]).astype(F32) for level in range(levels)], axis=1)
     picks = block_diagonal(picks, levels).astype(BF16)
@@ -78,9 +86,11 @@
                 sent_ref[section, side * k : (side + 1) * k, :] = mats
             else:
                 kept_ref[0, side * k : (side + 1) * k, :] = mats
-    copies[2].wait()
+    for copy in copies[len(first) : -len(third)]:
+        copy.wait()
     xb_ref[...] = field_ref[...].astype(BF16)
-    copies[3].wait()
+    for copy in copies[-len(third) :]:
+        copy.wait()
 
 
 def project(xb_ref, col_ref, out_ref):
@@ -148,6 +158,33 @@
 def expand_below(rank_size, half_shift, state_ref, row_ref, owner_ref, below_ref):
     rank = level_rank(state_ref[...], rank_size, half_shift, owner_ref, False)
     below_ref[...] = jnp.dot(rank, row_ref[...], preferred_element_type=F32)
+
+
+def diagonal(xb_ref, leaf_hbm, out_ref, leaf_ref, sems):
+    blocks, order, _ = leaf_hbm.shape
+    copies = []
+    for n in range(blocks):
+        for source, target in split_rows(leaf_hbm.at[n], leaf_ref.at[n], 2):
+            copies.append(pltpu.make_async_copy(source, target, sems.at[len(copies)]))
+            copies[-1].start()
+    for n in range(blocks):
+        copies[2 * n].wait()
+        copies[2 * n + 1].wait()
+        part = pl.ds(n * order, order)
+        out_ref[:, part] = jnp.dot(xb_ref[:, part], leaf_ref[n], preferred_element_type=F32)
+
+
+def combine(half_ref, below_ref, diag_ref, out_hbm, sum_ref, sems):
+    parts = sems.shape[0]
+    count = sum_ref.shape[1] // parts
+    copies = []
+    for n in range(parts):
+        part = pl.ds(n * count, count)
+        sum_ref[:, part] = diag_ref[:, part] + below_ref[:, part] + half_ref[:, part]
+        copies.append(pltpu.make_async_copy(sum_ref.at[:, part], out_hbm.at[:, part], sems.at[n]))
+        copies[-1].start()
+    for copy in copies:
+        copy.wait()
 
 
 def shards(field, leaf_inverse, col_factor, row_factor, mixing, row_owner, rank_perm):
@@ -179,7 +216,7 @@
             pltpu.VMEM(field.shape, F32),
             pltpu.VMEM(mixing.shape[1:], BF16),
             pltpu.VMEM(rank_perm.shape, jnp.int32),
-            pltpu.SemaphoreType.DMA((4,)),
+            pltpu.SemaphoreType.DMA((1 + levels + 2 + 4,)),
         ],
     )
     received = swapped(sent)
@@ -223,13 +260,15 @@
     )
     out_half = shifted(out_half, "grp", groups // 2)
     out_below = shifted(out_below, "grp", groups - 1)
-    diag = jnp.einsum(
-        "rnl,nlm->rnm",
-        xb.reshape(vectors, rows // order, order),
-        leaf_inverse,
-        preferred_element_type=F32,
-    ).reshape(vectors, rows)
-    return diag + out_below + out_half
+    diag = call(
+        diagonal, array(vectors, rows), [VMEM, HBM], 2 * vectors * rows * order, 2 * rows * order,
+        xb, pltpu.with_memory_space_constraint(leaf_inverse, pltpu.HBM),
+        scratch=[pltpu.VMEM(leaf_inverse.shape, BF16), pltpu.SemaphoreType.DMA((2 * leaf_inverse.shape[0],))],
+    )
+    return call(
+        combine, array(vectors, rows), [VMEM] * 3, 2 * vectors * rows, 16 * vectors * rows, out_half, out_below, diag,
+        scratch=[pltpu.VMEM((vectors, rows), F32), pltpu.SemaphoreType.DMA((4,))], out=HBM,
+    )
 
 
 def solution(mesh):

time: 22.1 us -> 22.1 us (level)
  Pallas kernels: 2.58 us -> 5.11 us
  waiting for transfers between devices: 12.7 us -> 11.3 us
  other arithmetic: 0.68 us -> 0 us
  matrix products: 0.37 us -> 0 us
    pallas_call x8 -> x10, Pallas kernels: 2.58 us -> 5.11 us  [call(): pl.pallas_call(body, out_shape=shapes, in_specs=specs, out_specs=jax.tree...]
    ppermute x2, waiting for transfers between devices: 7.52 us -> 6.08 us  [shifted(): lax.ppermute(value, axis, [(source, (source + distance) % size) for sourc...]
    add x1 -> x0, other arithmetic: 0.68 us -> none  [shards(): return diag + out_below + out_half]
    dot_general x1 -> x0, matrix products: 0.37 us -> none  [shards(): jnp.einsum('rnl,nlm->rnm', xb.reshape(vectors, rows // order, order), lea...]
  transfers between devices with their start and end apart: 6 -> 6, of which waited for: 5 -> 5; matrix products, arithmetic and copies ran while one was open for 2% -> 0% of each run, Pallas kernels for 2% -> 11%
where the time goes in v13:
time: 22.1 us; the launch traced here: 22 us
  waiting for transfers between devices  11.3 us (51%)
  starting transfers between devices  5.53 us (25%)
  Pallas kernels  5.11 us (23%)
    ppermute x2, waiting for transfers between devices, shifted(): lax.ppermute(value, axis, [(source, (source + distance) % size) for sourc...  6.08 us
    pallas_call x10, Pallas kernels, call(): pl.pallas_call(body, out_shape=shapes, in_specs=specs, out_specs=jax.tree...  5.11 us
    ppermute x2, waiting for transfers between devices, across(): lax.ppermute(value, 'bf', [(n, n ^ 1 << bit) for n in range(lax.axis_size...  4.44 us
    ppermute x2, starting transfers between devices, across(): lax.ppermute(value, 'bf', [(n, n ^ 1 << bit) for n in range(lax.axis_size...  3.17 us
    ppermute x2, starting transfers between devices, shifted(): lax.ppermute(value, axis, [(source, (source + distance) % size) for sourc...  1.77 us
    ppermute x2, waiting for transfers between devices, swapped(): lax.ppermute(value, 'bf', [(n, n ^ 1) for n in range(lax.axis_size('bf'))])  0.77 us
    ppermute x2, starting transfers between devices, swapped(): lax.ppermute(value, 'bf', [(n, n ^ 1) for n in range(lax.axis_size('bf'))])  0.58 us
  transfers between devices with their start and end apart: 6, of which 5 were waited for; matrix products, arithmetic and copies ran while one was open for 0% of the time, Pallas kernels for 11%

profile of v13, /device:TPU:24, one launch (start us, length us, event | category | flops | bytes accessed | tf_op | source)
XLA Modules:
  0.0 22.0 jit_solution(16452020558026741197)
XLA Ops:
  0.0 0.0 copy-start
  0.0 0.0 copy-start.1
  0.0 1.4 %shard_map.73 = (bf16[16,2048]{1,0:T(8,128)(2,1)S(1)}, bf16[128,2048]{1,0:T(8,128)(2,1)S(1)}, f32[3,128,128]{2,1,0:T(8,128)S(1)}, f32[1,128,128]{2,1,0:T(8,128)S(1)}) custom-call(f32[16,2048]{1,0:T(8,128)} %field_hbm.1, bf16[128,2048]{1,0:T(8,128)(2,1)} %bitcast.5, bf16[2,4,2,64,64]{4,3,2,1,0:T(8,128)(2,1)} %bitcast.6, s32[2,64]{1,0:T(2,128)} %perm_hbm.1), custom_call_target="tpu_custom_call" | custom-call | flops 16777216 | bytes 786432 | tf_op jit(solution)/shard_map/pallas_call | solution.py:28
  1.4 0.1 collective-permute-start.1
  1.5 0.2 %shard_map.74.refs_0_ = f32[16,128]{1,0:T(8,128)S(1)} custom-call(bf16[16,2048]{1,0:T(8,128)(2,1)S(1)} %get-tuple-element.11.xb_ref, bf16[128,2048]{1,0:T(8,128)(2,1)S(1)} %get-tuple-element.12.col_ref), custom_call_target="tpu_custom_call" | custom-call | flops 8388608 | bytes 786432 | tf_op jit(solution)/shard_map/pallas_call | solution.py:28
  1.7 0.5 %collective-permute-start = (f32[16,128]{1,0:T(8,128)S(1)}, f32[16,128]{1,0:T(8,128)S(1)}, u32[]{:S(2)}, u32[]{:S(2)}) collective-permute-start(f32[16,128]{1,0:T(8,128)S(1)} %shard_map.74.refs_0_), channel_id=1, source_target_pairs={{0,1},{1,0},{2,3},{3,2},{4,5},{5,4},{6,7},{7,6},{8,9},{9,8},{10,11... | collective-permute-start | bytes 24584 | tf_op jit(solution)/shard_map/ppermute | solution.py:20
  2.3 0.6 %collective-permute-done.1.refs_0_ = f32[3,128,128]{2,1,0:T(8,128)S(1)} collective-permute-done((f32[3,128,128]{2,1,0:T(8,128)S(1)}, f32[3,128,128]{2,1,0:T(8,128)S(1)}, u32[]{:S(2)}, u32[]{:S(2)}) %collective-permute-start.1) | collective-permute-done | bytes 196640 | tf_op jit(solution)/shard_map/ppermute | solution.py:20
  2.9 0.1 collective-permute-done.refs_1_
  3.1 0.1 shard_map.77.refs_0_
  3.2 1.6 %collective-permute-start.2 = (f32[2,16,128]{2,1,0:T(8,128)S(1)}, f32[2,16,128]{2,1,0:T(8,128)S(1)}, u32[]{:S(2)}, u32[]{:S(2)}) collective-permute-start(f32[2,16,128]{2,1,0:T(8,128)S(1)} %shard_map.77.refs_0_), channel_id=1, source_target_pairs={{0,2},{1,3},{2,0},{3,1},{4,6},{5,7},{6,4},{7,5},{8,10},{9,11},{10,... | collective-permute-start | bytes 49160 | tf_op jit(solution)/shard_map/ppermute | solution.py:24
  4.8 2.2 %collective-permute-done.2.refs_1_ = f32[2,16,128]{2,1,0:T(8,128)S(1)} collective-permute-done((f32[2,16,128]{2,1,0:T(8,128)S(1)}, f32[2,16,128]{2,1,0:T(8,128)S(1)}, u32[]{:S(2)}, u32[]{:S(2)}) %collective-permute-start.2) | collective-permute-done | bytes 16416 | tf_op jit(solution)/shard_map/ppermute | solution.py:24
  7.0 0.3 %shard_map.78.refs_0_ = f32[2,16,128]{2,1,0:T(8,128)S(1)} custom-call(f32[2,16,128]{2,1,0:T(8,128)S(1)} %shard_map.77.refs_0_, f32[2,16,128]{2,1,0:T(8,128)S(1)} %collective-permute-done.2.refs_1_, bf16[4,256,128]{2,1,0:T(8,128)(2,1)S(1)} %shard_map.75.refs_2_, bf16[3,256,128]{2,1,0:T(8,128)(2,1)S(1)} %shard_map.76.refs_3_), custom_call_target="tpu_custom_call" | custom-call | flops 6291456 | bytes 131072 | tf_op jit(solution)/shard_map/pallas_call | solution.py:28
  7.3 1.6 %collective-permute-start.3 = (f32[2,16,128]{2,1,0:T(8,128)S(1)}, f32[2,16,128]{2,1,0:T(8,128)S(1)}, u32[]{:S(2)}, u32[]{:S(2)}) collective-permute-start(f32[2,16,128]{2,1,0:T(8,128)S(1)} %shard_map.78.refs_0_), channel_id=1, source_target_pairs={{0,2},{1,3},{2,0},{3,1},{4,6},{5,7},{6,4},{7,5},{8,10},{9,11},{10,... | collective-permute-start | bytes 49160 | tf_op jit(solution)/shard_map/ppermute | solution.py:24
  8.9 2.2 %collective-permute-done.3.refs_1_ = f32[2,16,128]{2,1,0:T(8,128)S(1)} collective-permute-done((f32[2,16,128]{2,1,0:T(8,128)S(1)}, f32[2,16,128]{2,1,0:T(8,128)S(1)}, u32[]{:S(2)}, u32[]{:S(2)}) %collective-permute-start.3) | collective-permute-done | bytes 16416 | tf_op jit(solution)/shard_map/ppermute | solution.py:24
  11.1 0.0 copy-done
  11.1 0.0 copy-done.1
  11.1 0.3 %shard_map.79 = (f32[16,128]{1,0:T(8,128)S(1)}, f32[16,2048]{1,0:T(8,128)S(1)}) custom-call(f32[2,16,128]{2,1,0:T(8,128)S(1)} %shard_map.78.refs_0_, f32[2,16,128]{2,1,0:T(8,128)S(1)} %collective-permute-done.3.refs_1_, bf16[4,256,128]{2,1,0:T(8,128)(2,1)S(1)} %shard_map.75.refs_2_, bf16[3,256,128]{2,1,0:T(8,128)(2,1)S(1)} %shard_map.76.refs_3_, ...), custom_call_target="tpu_custom_call" | custom-call | flops 8388608 | bytes 1048576 | tf_op jit(solution)/shard_map/pallas_call | solution.py:28
  11.4 0.4 %collective-permute-start.4 = (f32[16,2048]{1,0:T(8,128)S(1)}, f32[16,2048]{1,0:T(8,128)S(1)}, u32[]{:S(2)}, u32[]{:S(2)}) collective-permute-start(f32[16,2048]{1,0:T(8,128)S(1)} %get-tuple-element.15), channel_id=1, source_target_pairs={{0,16},{4,20},{8,24},{12,28},{16,0},{20,4},{24,8},{28,12},{1,17},{... | collective-permute-start | bytes 393224 | tf_op jit(solution)/shard_map/ppermute | solution.py:16
  11.8 0.2 shard_map.80
  12.0 1.4 %collective-permute-start.5 = (f32[16,2048]{1,0:T(8,128)S(1)}, f32[16,2048]{1,0:T(8,128)S(1)}, u32[]{:S(2)}, u32[]{:S(2)}) collective-permute-start(f32[16,2048]{1,0:T(8,128)S(1)} %shard_map.80), channel_id=1, source_target_pairs={{0,28},{4,0},{8,4},{12,8},{16,12},{20,16},{24,20},{28,24},{1,29},{... | collective-permute-start | bytes 393224 | tf_op jit(solution)/shard_map/ppermute | solution.py:16
  13.4 1.8 %shard_map.81.diag_ref = f32[16,2048]{1,0:T(8,128)S(1)} custom-call(bf16[16,2048]{1,0:T(8,128)(2,1)S(1)} %get-tuple-element.11.xb_ref, bf16[4,512,512]{2,1,0:T(8,128)(2,1)} %leaf_hbm.1), custom_call_target="tpu_custom_call" | custom-call | flops 33554432 | bytes 2097152 | tf_op jit(solution)/shard_map/pallas_call | solution.py:28
  15.2 6.1 %collective-permute-done.4.half_ref = f32[16,2048]{1,0:T(8,128)S(1)} collective-permute-done((f32[16,2048]{1,0:T(8,128)S(1)}, f32[16,2048]{1,0:T(8,128)S(1)}, u32[]{:S(2)}, u32[]{:S(2)}) %collective-permute-start.4) | collective-permute-done | bytes 131104 | tf_op jit(solution)/shard_map/ppermute | solution.py:16
  21.3 0.0 collective-permute-done.5.below_ref
  21.3 0.7 %shard_map.82 = f32[16,2048]{1,0:T(8,128)} custom-call(f32[16,2048]{1,0:T(8,128)S(1)} %collective-permute-done.4.half_ref, f32[16,2048]{1,0:T(8,128)S(1)} %collective-permute-done.5.below_ref, f32[16,2048]{1,0:T(8,128)S(1)} %shard_map.81.diag_ref), custom_call_target="tpu_custom_call" | custom-call | flops 65536 | bytes 524288 | tf_op jit(solution)/shard_map/pallas_call | solution.py:28
  (2 shorter events, 0.1 us)
Async XLA Ops:
  0.0 11.1 %copy-start = (bf16[2,64,2048]{2,1,0:T(8,128)(2,1)S(1)}, bf16[2,64,2048]{2,1,0:T(8,128)(2,1)}, u32[]{:S(2)}) copy-start(bf16[2,64,2048]{2,1,0:T(8,128)(2,1)} %param.10) | copy-start | bytes 1572868
  0.0 11.1 %copy-start.1 = (s32[2,8]{1,0:T(2,128)S(1)}, s32[2,8]{1,0:T(2,128)}, u32[]{:S(2)}) copy-start(s32[2,8]{1,0:T(2,128)} %refs_2_.1) | copy-start | bytes 196
  1.4 1.5 %collective-permute-start.1 = (f32[3,128,128]{2,1,0:T(8,128)S(1)}, f32[3,128,128]{2,1,0:T(8,128)S(1)}, u32[]{:S(2)}, u32[]{:S(2)}) collective-permute-start(f32[3,128,128]{2,1,0:T(8,128)S(1)} %get-tuple-element.13.refs_0_), channel_id=1, source_target_pairs={{0,1},{1,0},{2,3},{3,2},{4,5},{5,4},{6,7},{7,6},{8,9},{9,8},{10,11... | collective-permute-start | bytes 589832 | tf_op jit(solution)/shard_map/ppermute | solution.py:20
  1.7 1.3 %collective-permute-start = (f32[16,128]{1,0:T(8,128)S(1)}, f32[16,128]{1,0:T(8,128)S(1)}, u32[]{:S(2)}, u32[]{:S(2)}) collective-permute-start(f32[16,128]{1,0:T(8,128)S(1)} %shard_map.74.refs_0_), channel_id=1, source_target_pairs={{0,1},{1,0},{2,3},{3,2},{4,5},{5,4},{6,7},{7,6},{8,9},{9,8},{10,11... | collective-permute-start | bytes 24584 | tf_op jit(solution)/shard_map/ppermute | solution.py:20
  3.2 3.8 %collective-permute-start.2 = (f32[2,16,128]{2,1,0:T(8,128)S(1)}, f32[2,16,128]{2,1,0:T(8,128)S(1)}, u32[]{:S(2)}, u32[]{:S(2)}) collective-permute-start(f32[2,16,128]{2,1,0:T(8,128)S(1)} %shard_map.77.refs_0_), channel_id=1, source_target_pairs={{0,2},{1,3},{2,0},{3,1},{4,6},{5,7},{6,4},{7,5},{8,10},{9,11},{10,... | collective-permute-start | bytes 49160 | tf_op jit(solution)/shard_map/ppermute | solution.py:24
  7.3 3.8 %collective-permute-start.3 = (f32[2,16,128]{2,1,0:T(8,128)S(1)}, f32[2,16,128]{2,1,0:T(8,128)S(1)}, u32[]{:S(2)}, u32[]{:S(2)}) collective-permute-start(f32[2,16,128]{2,1,0:T(8,128)S(1)} %shard_map.78.refs_0_), channel_id=1, source_target_pairs={{0,2},{1,3},{2,0},{3,1},{4,6},{5,7},{6,4},{7,5},{8,10},{9,11},{10,... | collective-permute-start | bytes 49160 | tf_op jit(solution)/shard_map/ppermute | solution.py:24
  11.4 9.9 %collective-permute-start.4 = (f32[16,2048]{1,0:T(8,128)S(1)}, f32[16,2048]{1,0:T(8,128)S(1)}, u32[]{:S(2)}, u32[]{:S(2)}) collective-permute-start(f32[16,2048]{1,0:T(8,128)S(1)} %get-tuple-element.15), channel_id=1, source_target_pairs={{0,16},{4,20},{8,24},{12,28},{16,0},{20,4},{24,8},{28,12},{1,17},{... | collective-permute-start | bytes 393224 | tf_op jit(solution)/shard_map/ppermute | solution.py:16
  12.0 9.3 %collective-permute-start.5 = (f32[16,2048]{1,0:T(8,128)S(1)}, f32[16,2048]{1,0:T(8,128)S(1)}, u32[]{:S(2)}, u32[]{:S(2)}) collective-permute-start(f32[16,2048]{1,0:T(8,128)S(1)} %shard_map.80), channel_id=1, source_target_pairs={{0,28},{4,0},{8,4},{12,8},{16,12},{20,16},{24,20},{28,24},{1,29},{... | collective-permute-start | bytes 393224 | tf_op jit(solution)/shard_map/ppermute | solution.py:16

commit v14 on v13

--- a/solution.py
+++ b/solution.py
@@ -62,7 +62,8 @@
     return [(source.at[pl.ds(n * count, count)], target.at[pl.ds(n * count, count)]) for n in range(parts)]
 
 
-def load(field_hbm, col_hbm, mixing_hbm, perm_hbm, xb_ref, col_ref, sent_ref, kept_ref, field_ref, mixing_ref, perm_ref, sems):
+def load(groups, field_hbm, col_hbm, mixing_hbm, perm_hbm, xb_ref, col_ref, *refs):
+    *out_refs, field_ref, mixing_ref, perm_ref, sems = refs
     levels, sections, _, k, _ = mixing_ref.shape
     first = [(perm_hbm, perm_ref)]
     first += [(mixing_hbm.at[level], mixing_ref.at[level]) for level in range(levels)]
@@ -82,10 +83,9 @@
             if section == 0:
                 mats = jnp.dot(picks, block_diagonal(mats, levels).astype(BF16), preferred_element_type=F32)
                 mats = sum(mats[level * k : (level + 1) * k] for level in range(levels))
-            if section < sections - 1:
-                sent_ref[section, side * k : (side + 1) * k, :] = mats
-            else:
-                kept_ref[0, side * k : (side + 1) * k, :] = mats
+            for group, out_ref in zip(groups, out_refs):
+                if section in group:
+                    out_ref[group.index(section), side * k : (side + 1) * k, :] = mats
     for copy in copies[len(first) : -len(third)]:
         copy.wait()
     xb_ref[...] = field_ref[...].astype(BF16)
@@ -97,13 +97,9 @@
     out_ref[...] = lax.dot_general(xb_ref[...], col_ref[...], NT, preferred_element_type=F32)
 
 
-def build_weights(levels, *refs):
-    *compact_refs, weights_ref = refs
-    n = 0
-    for compact_ref in compact_refs:
-        for section in range(compact_ref.shape[0]):
-            weights_ref[n] = section_weights(compact_ref[section], levels)
-            n += 1
+def build_weights(levels, chosen, *refs):
+    for n, (operand, place) in enumerate(chosen):
+        refs[-1][n] = section_weights(refs[operand][place], levels)
 
 
 def exact_dot(value, factor):
@@ -141,6 +137,14 @@
     run_sections(sections, final, (first_ref, second_ref), mine_ref, theirs_ref, out_ref)
 
 
+def first_step(first_ref, second_ref, mine_ref, theirs_ref, received_ref, out_ref):
+    count = first_ref.shape[0]
+    mine, theirs = first_ref[...], second_ref[...]
+    out_ref[:count, :] = section_product(mine, theirs, mine_ref[0])
+    out_ref[count : 2 * count, :] = section_product(theirs, mine, theirs_ref[0])
+    out_ref[2 * count :, :] = received_ref[1]
+
+
 def level_rank(state, rank_size, half_shift, owner_ref, half):
     first_is_half = jnp.broadcast_to(owner_ref[0:1, 0:1], state.shape) == half_shift
     lane = lax.broadcasted_iota(jnp.int32, state.shape, 1)
@@ -148,11 +152,29 @@
     return (jnp.where(chosen, state, 0.0) if half else jnp.where(chosen, 0.0, state)).astype(BF16)
 
 
-def last_step(sections, final, rank_size, half_shift, first_ref, second_ref, mine_ref, theirs_ref, row_ref, owner_ref, state_ref, half_ref):
-    state = run_sections(sections, final, (first_ref, second_ref), mine_ref, theirs_ref, None)
+def finish(state, rank_size, half_shift, row_ref, owner_ref, state_ref, half_ref):
     state_ref[...] = state
     rank = level_rank(state, rank_size, half_shift, owner_ref, True)
     half_ref[...] = jnp.dot(rank, row_ref[...], preferred_element_type=F32)
+
+
+def last_step(sections, final, rank_size, half_shift, first_ref, second_ref, mine_ref, theirs_ref, *refs):
+    state = run_sections(sections, final, (first_ref, second_ref), mine_ref, theirs_ref, None)
+    finish(state, rank_size, half_shift, *refs)
+
+
+def last_sections(levels, rank_size, half_shift, pair_ref, other_ref, mine_ref, theirs_ref, far_ref, *refs):
+    count = (pair_ref.shape[0] - 2 * rank_size) // 2
+    mine, theirs = pair_ref[:count, :], pair_ref[count : 2 * count, :]
+    far, cross = other_ref[:count, :], other_ref[count : 2 * count, :]
+    mine, theirs, far, cross = (
+        section_product(mine, far, mine_ref[1]),
+        section_product(theirs, cross, theirs_ref[1]),
+        section_product(far, mine, far_ref[0]),
+        section_product(cross, theirs, section_weights(other_ref[2 * count :, :], levels)),
+    )
+    mine, far = section_product(mine, theirs, mine_ref[2]), section_product(far, cross, far_ref[1])
+    finish(section_product(mine, far, mine_ref[3]), rank_size, half_shift, *refs)
 
 
 def expand_below(rank_size, half_shift, state_ref, row_ref, owner_ref, below_ref):
@@ -203,14 +225,12 @@
         pltpu.with_memory_space_constraint(x, pltpu.HBM)
         for x in (field, col_factor.reshape(width, rows), mixing[0], rank_perm)
     ]
-    xb, col_here, sent, kept = call(
-        load,
-        [
-            array(vectors, rows, kind=BF16),
-            array(width, rows, kind=BF16),
-            array(sections - 1, 2 * rank_size, width),
-            array(1, 2 * rank_size, width),
-        ],
+    one_round = bits == 2 and sections == 4
+    sent_groups = [(0, 1), (1, 2), (3,)] if one_round else [tuple(range(sections - 1)), (sections - 1,)]
+    xb, col_here, sent, *kept = call(
+        lambda *refs: load(sent_groups, *refs),
+        [array(vectors, rows, kind=BF16), array(width, rows, kind=BF16)]
+        + [array(len(group), 2 * rank_size, width) for group in sent_groups],
         [HBM] * 4, 8 * width**3, 3 * rows * width, *in_hbm,
         scratch=[
             pltpu.VMEM(field.shape, F32),
@@ -219,40 +239,57 @@
             pltpu.SemaphoreType.DMA((1 + levels + 2 + 4,)),
         ],
     )
+
+    def weights(chosen, *compacts):
+        return call(
+            lambda *refs: build_weights(levels, chosen, *refs), array(len(chosen), 2 * width, width, kind=BF16),
+            [VMEM] * len(compacts), 4 * width * width * sections, 8 * width * width * sections, *compacts,
+        )
+
     received = swapped(sent)
+    if one_round:
+        received_far = across(kept[0], 1)
     state = call(
         project, array(vectors, width), [VMEM, VMEM], 2 * vectors * rows * width, 3 * rows * width, xb, col_here
     )
     first_states = (state, swapped(state))
-    weight_cost = (4 * width * width * sections, 8 * width * width * sections)
-    mine, theirs = [
-        call(
-            lambda *refs: build_weights(levels, *refs),
-            array(sum(x.shape[0] for x in compacts), 2 * width, width, kind=BF16),
-            [VMEM] * len(compacts), *weight_cost, *compacts,
-        )
-        for compacts in ((sent, kept), (received,))
-    ]
-    runs = []
-    for section in range(sections):
-        if section % bits or not section:
-            runs.append([section])
-        else:
-            runs[-1].append(section)
     step_cost = (24 * vectors * width * width, 8 * width * width)
     final = sections - 1
-    for run in runs[:-1]:
+    if one_round:
+        mine = weights([(0, 0), (0, 1), (1, 1), (2, 0)], sent, *kept)
+    else:
+        mine = weights([(0, n) for n in range(final)] + [(1, 0)], sent, *kept)
+        runs = []
+        for section in range(sections):
+            if section % bits or not section:
+                runs.append([section])
+            else:
+                runs[-1].append(section)
+    theirs = weights([(0, n) for n in range(sent.shape[0])], received)
+    if one_round:
+        states = call(
+            first_step, array(2 * (vectors + rank_size), width), [VMEM] * 5, *step_cost,
+            *first_states, mine, theirs, received,
+        )
+        first_states = (states, across(states, 1))
+    for run in [] if one_round else runs[:-1]:
         states = call(
             lambda *refs, run=run: step(run, final, *refs), array(2, vectors, width), [VMEM] * 4, *step_cost,
             *first_states, mine, theirs,
         )
         first_states = (states, across(states, (run[-1] + 1) % bits))
+    if one_round:
+        last_body = lambda *refs: last_sections(levels, *refs)
+        last_weights = (mine, theirs, weights([(0, 0), (0, 1)], received_far))
+    else:
+        last_body = lambda *refs: last_step(runs[-1], final, *refs)
+        last_weights = (mine, theirs)
     expand_cost = (2 * vectors * width * rows, 4 * width * rows)
     expand = row_factor.reshape(width, rows)
     state, out_half = call(
-        lambda *refs: last_step(runs[-1], final, rank_size, groups // 2, *refs),
+        lambda *refs: last_body(rank_size, groups // 2, *refs),
         [array(vectors, width), array(vectors, rows)],
-        [VMEM] * 6, *expand_cost, *first_states, mine, theirs, expand, row_owner,
+        [VMEM] * (4 + len(last_weights)), *expand_cost, *first_states, *last_weights, expand, row_owner,
     )
     out_below = call(
         lambda *refs: expand_below(rank_size, groups // 2, *refs), array(vectors, rows),

time: 22.1 us -> 22.3 us (level)
  the two profiles are of different devices: /device:TPU:24 before, /device:TPU:29 now
where the time goes in v14:
time: 22.3 us; the launch traced here: 22.1 us
  waiting for transfers between devices  13.1 us (59%)
  Pallas kernels  5.14 us (23%)
  starting transfers between devices  3.86 us (17%)
    ppermute x2, waiting for transfers between devices, shifted(): lax.ppermute(value, axis, [(source, (source + distance) % size) for sourc...  8.61 us
    pallas_call x10, Pallas kernels, call(): pl.pallas_call(body, out_shape=shapes, in_specs=specs, out_specs=jax.tree...  5.14 us
    ppermute x2, waiting for transfers between devices, across(): lax.ppermute(value, 'bf', [(n, n ^ 1 << bit) for n in range(lax.axis_size...  3.69 us
    ppermute x2, starting transfers between devices, across(): lax.ppermute(value, 'bf', [(n, n ^ 1 << bit) for n in range(lax.axis_size...  1.55 us
    ppermute x2, starting transfers between devices, shifted(): lax.ppermute(value, axis, [(source, (source + distance) % size) for sourc...  1.21 us
    ppermute x2, starting transfers between devices, swapped(): lax.ppermute(value, 'bf', [(n, n ^ 1) for n in range(lax.axis_size('bf'))])  1.1 us
    ppermute x2, waiting for transfers between devices, swapped(): lax.ppermute(value, 'bf', [(n, n ^ 1) for n in range(lax.axis_size('bf'))])  0.77 us
  transfers between devices with their start and end apart: 6, of which 5 were waited for; matrix products, arithmetic and copies ran while one was open for 0% of the time, Pallas kernels for 11%

profile of v14, /device:TPU:29, one launch (start us, length us, event | category | flops | bytes accessed | tf_op | source)
XLA Modules:
  0.0 22.1 jit_solution(6608544415457335677)
XLA Ops:
  0.0 0.0 copy-start
  0.0 0.0 copy-start.1
  0.0 1.4 %shard_map.73 = (bf16[16,2048]{1,0:T(8,128)(2,1)S(1)}, bf16[128,2048]{1,0:T(8,128)(2,1)S(1)}, f32[2,128,128]{2,1,0:T(8,128)S(1)}, f32[2,128,128]{2,1,0:T(8,128)S(1)}, f32[1,128,128]{2,1,0:T(8,128)S(1)}) custom-call(f32[16,2048]{1,0:T(8,128)} %refs_0_.1, bf16[128,2048]{1,0:T(8,128)(2,1)} %bitcast.5, bf16[2,4,2,64,64]{4,3,2,1,0:T(8,128)(2,1)} %bitcast.6, ...), custom_call_target="tpu_custom_call" | custom-call | flops 16777216 | bytes 786432 | tf_op jit(solution)/shard_map/pallas_call | solution.py:28
  1.4 0.7 %collective-permute-start.1 = (f32[2,128,128]{2,1,0:T(8,128)S(1)}, f32[2,128,128]{2,1,0:T(8,128)S(1)}, u32[]{:S(2)}, u32[]{:S(2)}) collective-permute-start(f32[2,128,128]{2,1,0:T(8,128)S(1)} %get-tuple-element.14.refs_0_), channel_id=1, source_target_pairs={{0,1},{1,0},{2,3},{3,2},{4,5},{5,4},{6,7},{7,6},{8,9},{9,8},{10,11... | collective-permute-start | bytes 393224 | tf_op jit(solution)/shard_map/ppermute | solution.py:20
  2.1 0.2 %collective-permute-start.3 = (f32[2,128,128]{2,1,0:T(8,128)S(1)}, f32[2,128,128]{2,1,0:T(8,128)S(1)}, u32[]{:S(2)}, u32[]{:S(2)}) collective-permute-start(f32[2,128,128]{2,1,0:T(8,128)S(1)} %get-tuple-element.15.refs_1_), channel_id=1, source_target_pairs={{0,2},{1,3},{2,0},{3,1},{4,6},{5,7},{6,4},{7,5},{8,10},{9,11},{10,... | collective-permute-start | bytes 393224 | tf_op jit(solution)/shard_map/ppermute | solution.py:24
  2.4 0.2 %shard_map.74.first_ref = f32[16,128]{1,0:T(8,128)S(1)} custom-call(bf16[16,2048]{1,0:T(8,128)(2,1)S(1)} %get-tuple-element.12.xb_ref, bf16[128,2048]{1,0:T(8,128)(2,1)S(1)} %get-tuple-element.13.col_ref), custom_call_target="tpu_custom_call" | custom-call | flops 8388608 | bytes 786432 | tf_op jit(solution)/shard_map/pallas_call | solution.py:28
  2.6 0.4 %collective-permute-start = (f32[16,128]{1,0:T(8,128)S(1)}, f32[16,128]{1,0:T(8,128)S(1)}, u32[]{:S(2)}, u32[]{:S(2)}) collective-permute-start(f32[16,128]{1,0:T(8,128)S(1)} %shard_map.74.first_ref), channel_id=1, source_target_pairs={{0,1},{1,0},{2,3},{3,2},{4,5},{5,4},{6,7},{7,6},{8,9},{9,8},{10,11... | collective-permute-start | bytes 24584 | tf_op jit(solution)/shard_map/ppermute | solution.py:20
  3.0 0.1 collective-permute-done.1.refs_0_.received_ref
  3.1 0.7 %collective-permute-done.second_ref = f32[16,128]{1,0:T(8,128)S(1)} collective-permute-done((f32[16,128]{1,0:T(8,128)S(1)}, f32[16,128]{1,0:T(8,128)S(1)}, u32[]{:S(2)}, u32[]{:S(2)}) %collective-permute-start) | collective-permute-done | bytes 8224 | tf_op jit(solution)/shard_map/ppermute | solution.py:20
  3.8 0.1 shard_map.77.refs_0_
  4.0 1.3 %collective-permute-start.2 = (f32[160,128]{1,0:T(8,128)S(1)}, f32[160,128]{1,0:T(8,128)S(1)}, u32[]{:S(2)}, u32[]{:S(2)}) collective-permute-start(f32[160,128]{1,0:T(8,128)S(1)} %shard_map.77.refs_0_), channel_id=1, source_target_pairs={{0,2},{1,3},{2,0},{3,1},{4,6},{5,7},{6,4},{7,5},{8,10},{9,11},{10,... | collective-permute-start | bytes 245768 | tf_op jit(solution)/shard_map/ppermute | solution.py:24
  5.3 2.0 %collective-permute-done.3.refs_0_ = f32[2,128,128]{2,1,0:T(8,128)S(1)} collective-permute-done((f32[2,128,128]{2,1,0:T(8,128)S(1)}, f32[2,128,128]{2,1,0:T(8,128)S(1)}, u32[]{:S(2)}, u32[]{:S(2)}) %collective-permute-start.3) | collective-permute-done | bytes 131104 | tf_op jit(solution)/shard_map/ppermute | solution.py:24
  7.2 1.7 %collective-permute-done.2.refs_1_ = f32[160,128]{1,0:T(8,128)S(1)} collective-permute-done((f32[160,128]{1,0:T(8,128)S(1)}, f32[160,128]{1,0:T(8,128)S(1)}, u32[]{:S(2)}, u32[]{:S(2)}) %collective-permute-start.2) | collective-permute-done | bytes 81952 | tf_op jit(solution)/shard_map/ppermute | solution.py:24
  9.0 0.0 copy-done
  9.0 0.0 copy-done.1
  9.0 0.6 %shard_map.79 = (f32[16,128]{1,0:T(8,128)S(1)}, f32[16,2048]{1,0:T(8,128)S(1)}) custom-call(f32[160,128]{1,0:T(8,128)S(1)} %shard_map.77.refs_0_, f32[160,128]{1,0:T(8,128)S(1)} %collective-permute-done.2.refs_1_, bf16[4,256,128]{2,1,0:T(8,128)(2,1)S(1)} %shard_map.75.mine_ref.refs_2_, bf16[2,256,128]{2,1,0:T(8,128)(2,1)S(1)} %shard_map.76.theirs_ref.refs_3_, ...), custom_call_target="tpu_custom_call" | custom-call | flops 8388608 | bytes 1048576 | tf_op jit(solution)/shard_map/pallas_call | solution.py:28
  9.6 0.1 collective-permute-start.4
  9.7 0.2 shard_map.80
  9.9 1.1 %collective-permute-start.5 = (f32[16,2048]{1,0:T(8,128)S(1)}, f32[16,2048]{1,0:T(8,128)S(1)}, u32[]{:S(2)}, u32[]{:S(2)}) collective-permute-start(f32[16,2048]{1,0:T(8,128)S(1)} %shard_map.80), channel_id=1, source_target_pairs={{0,28},{4,0},{8,4},{12,8},{16,12},{20,16},{24,20},{28,24},{1,29},{... | collective-permute-start | bytes 393224 | tf_op jit(solution)/shard_map/ppermute | solution.py:16
  11.0 1.8 %shard_map.81.diag_ref = f32[16,2048]{1,0:T(8,128)S(1)} custom-call(bf16[16,2048]{1,0:T(8,128)(2,1)S(1)} %get-tuple-element.12.xb_ref, bf16[4,512,512]{2,1,0:T(8,128)(2,1)} %leaf_hbm.1), custom_call_target="tpu_custom_call" | custom-call | flops 33554432 | bytes 2097152 | tf_op jit(solution)/shard_map/pallas_call | solution.py:28
  12.8 8.6 %collective-permute-done.4.half_ref = f32[16,2048]{1,0:T(8,128)S(1)} collective-permute-done((f32[16,2048]{1,0:T(8,128)S(1)}, f32[16,2048]{1,0:T(8,128)S(1)}, u32[]{:S(2)}, u32[]{:S(2)}) %collective-permute-start.4) | collective-permute-done | bytes 131104 | tf_op jit(solution)/shard_map/ppermute | solution.py:16
  21.4 0.0 collective-permute-done.5.below_ref
  21.4 0.7 %shard_map.82 = f32[16,2048]{1,0:T(8,128)} custom-call(f32[16,2048]{1,0:T(8,128)S(1)} %collective-permute-done.4.half_ref, f32[16,2048]{1,0:T(8,128)S(1)} %collective-permute-done.5.below_ref, f32[16,2048]{1,0:T(8,128)S(1)} %shard_map.81.diag_ref), custom_call_target="tpu_custom_call" | custom-call | flops 65536 | bytes 524288 | tf_op jit(solution)/shard_map/pallas_call | solution.py:28
  (3 shorter events, 0.1 us)
Async XLA Ops:
  0.0 9.0 %copy-start = (bf16[2,64,2048]{2,1,0:T(8,128)(2,1)S(1)}, bf16[2,64,2048]{2,1,0:T(8,128)(2,1)}, u32[]{:S(2)}) copy-start(bf16[2,64,2048]{2,1,0:T(8,128)(2,1)} %param.10) | copy-start | bytes 1572868
  0.0 9.0 %copy-start.1 = (s32[2,8]{1,0:T(2,128)S(1)}, s32[2,8]{1,0:T(2,128)}, u32[]{:S(2)}) copy-start(s32[2,8]{1,0:T(2,128)} %refs_2_.1) | copy-start | bytes 196
  1.4 1.7 %collective-permute-start.1 = (f32[2,128,128]{2,1,0:T(8,128)S(1)}, f32[2,128,128]{2,1,0:T(8,128)S(1)}, u32[]{:S(2)}, u32[]{:S(2)}) collective-permute-start(f32[2,128,128]{2,1,0:T(8,128)S(1)} %get-tuple-element.14.refs_0_), channel_id=1, source_target_pairs={{0,1},{1,0},{2,3},{3,2},{4,5},{5,4},{6,7},{7,6},{8,9},{9,8},{10,11... | collective-permute-start | bytes 393224 | tf_op jit(solution)/shard_map/ppermute | solution.py:20
  2.1 5.1 %collective-permute-start.3 = (f32[2,128,128]{2,1,0:T(8,128)S(1)}, f32[2,128,128]{2,1,0:T(8,128)S(1)}, u32[]{:S(2)}, u32[]{:S(2)}) collective-permute-start(f32[2,128,128]{2,1,0:T(8,128)S(1)} %get-tuple-element.15.refs_1_), channel_id=1, source_target_pairs={{0,2},{1,3},{2,0},{3,1},{4,6},{5,7},{6,4},{7,5},{8,10},{9,11},{10,... | collective-permute-start | bytes 393224 | tf_op jit(solution)/shard_map/ppermute | solution.py:24
  2.6 1.2 %collective-permute-start = (f32[16,128]{1,0:T(8,128)S(1)}, f32[16,128]{1,0:T(8,128)S(1)}, u32[]{:S(2)}, u32[]{:S(2)}) collective-permute-start(f32[16,128]{1,0:T(8,128)S(1)} %shard_map.74.first_ref), channel_id=1, source_target_pairs={{0,1},{1,0},{2,3},{3,2},{4,5},{5,4},{6,7},{7,6},{8,9},{9,8},{10,11... | collective-permute-start | bytes 24584 | tf_op jit(solution)/shard_map/ppermute | solution.py:20
  4.0 5.0 %collective-permute-start.2 = (f32[160,128]{1,0:T(8,128)S(1)}, f32[160,128]{1,0:T(8,128)S(1)}, u32[]{:S(2)}, u32[]{:S(2)}) collective-permute-start(f32[160,128]{1,0:T(8,128)S(1)} %shard_map.77.refs_0_), channel_id=1, source_target_pairs={{0,2},{1,3},{2,0},{3,1},{4,6},{5,7},{6,4},{7,5},{8,10},{9,11},{10,... | collective-permute-start | bytes 245768 | tf_op jit(solution)/shard_map/ppermute | solution.py:24
  9.6 11.9 %collective-permute-start.4 = (f32[16,2048]{1,0:T(8,128)S(1)}, f32[16,2048]{1,0:T(8,128)S(1)}, u32[]{:S(2)}, u32[]{:S(2)}) collective-permute-start(f32[16,2048]{1,0:T(8,128)S(1)} %get-tuple-element.17), channel_id=1, source_target_pairs={{0,16},{4,20},{8,24},{12,28},{16,0},{20,4},{24,8},{28,12},{1,17},{... | collective-permute-start | bytes 393224 | tf_op jit(solution)/shard_map/ppermute | solution.py:16
  9.9 11.6 %collective-permute-start.5 = (f32[16,2048]{1,0:T(8,128)S(1)}, f32[16,2048]{1,0:T(8,128)S(1)}, u32[]{:S(2)}, u32[]{:S(2)}) collective-permute-start(f32[16,2048]{1,0:T(8,128)S(1)} %shard_map.80), channel_id=1, source_target_pairs={{0,28},{4,0},{8,4},{12,8},{16,12},{20,16},{24,20},{28,24},{1,29},{... | collective-permute-start | bytes 393224 | tf_op jit(solution)/shard_map/ppermute | solution.py:16

commit v15 on v14

--- a/solution.py
+++ b/solution.py
@@ -62,9 +62,10 @@
     return [(source.at[pl.ds(n * count, count)], target.at[pl.ds(n * count, count)]) for n in range(parts)]
 
 
-def load(groups, field_hbm, col_hbm, mixing_hbm, perm_hbm, xb_ref, col_ref, *refs):
-    *out_refs, field_ref, mixing_ref, perm_ref, sems = refs
+def load(groups, field_hbm, col_hbm, mixing_hbm, perm_hbm, xb_ref, sent_ref, *refs):
+    *out_refs, field_ref, col_ref, mixing_ref, perm_ref, sems = refs
     levels, sections, _, k, _ = mixing_ref.shape
+    vectors = field_ref.shape[0]
     first = [(perm_hbm, perm_ref)]
     first += [(mixing_hbm.at[level], mixing_ref.at[level]) for level in range(levels)]
     second = split_rows(field_hbm, field_ref, 2)
@@ -83,23 +84,32 @@
             if section == 0:
                 mats = jnp.dot(picks, block_diagonal(mats, levels).astype(BF16), preferred_element_type=F32)
                 mats = sum(mats[level * k : (level + 1) * k] for level in range(levels))
-            for group, out_ref in zip(groups, out_refs):
+            for n, (group, out_ref) in enumerate(zip(groups, (sent_ref, *out_refs))):
                 if section in group:
-                    out_ref[group.index(section), side * k : (side + 1) * k, :] = mats
-    for copy in copies[len(first) : -len(third)]:
+                    start = (0 if n else vectors) + (2 * group.index(section) + side) * k
+                    out_ref[start : start + k, :] = mats
+    for copy in copies[len(first) :]:
         copy.wait()
-    xb_ref[...] = field_ref[...].astype(BF16)
-    for copy in copies[-len(third) :]:
-        copy.wait()
-
-
-def project(xb_ref, col_ref, out_ref):
-    out_ref[...] = lax.dot_general(xb_ref[...], col_ref[...], NT, preferred_element_type=F32)
+    xb = field_ref[...].astype(BF16)
+    xb_ref[...] = xb
+    sent_ref[:vectors, :] = lax.dot_general(xb, col_ref[...], NT, preferred_element_type=F32)
 
 
 def build_weights(levels, chosen, *refs):
-    for n, (operand, place) in enumerate(chosen):
-        refs[-1][n] = section_weights(refs[operand][place], levels)
+    *compact_refs, weights_ref = refs
+    size = 2 * weights_ref.shape[2] // levels
+    for n, (operand, start) in enumerate(chosen):
+        weights_ref[n] = section_weights(compact_refs[operand][start : start + size, :], levels)
+
+
+def build_pair_weights(levels, start, mine_ref, far_ref, weights_ref):
+    k = far_ref.shape[0] // 2
+    width = levels * k
+    for n, (ref, first) in enumerate(((mine_ref, start), (far_ref, 0))):
+        for side in range(2):
+            mats = block_diagonal(ref[first + side * k : first + (side + 1) * k, :], levels).astype(BF16)
+            row = (n + side) % 2 * width
+            weights_ref[row : row + width, n * width : (n + 1) * width] = mats
 
 
 def exact_dot(value, factor):
@@ -122,7 +132,7 @@
         states_ref, other_ref = first_refs
         states, others = [states_ref[0], states_ref[1]], [other_ref[0], other_ref[1]]
     else:
-        states = [ref[...] for ref in first_refs]
+        states = [ref[: out_ref.shape[1], :] for ref in first_refs]
         others = states[::-1]
     for section in sections:
         count = 1 if section == final else 2
@@ -137,12 +147,13 @@
     run_sections(sections, final, (first_ref, second_ref), mine_ref, theirs_ref, out_ref)
 
 
-def first_step(first_ref, second_ref, mine_ref, theirs_ref, received_ref, out_ref):
-    count = first_ref.shape[0]
-    mine, theirs = first_ref[...], second_ref[...]
+def first_step(sent_ref, received_ref, mine_ref, theirs_ref, kept_ref, out_ref):
+    size = kept_ref.shape[0] // 2
+    count = (out_ref.shape[0] - size) // 2
+    mine, theirs = sent_ref[:count, :], received_ref[:count, :]
     out_ref[:count, :] = section_product(mine, theirs, mine_ref[0])
     out_ref[count : 2 * count, :] = section_product(theirs, mine, theirs_ref[0])
-    out_ref[2 * count :, :] = received_ref[1]
+    out_ref[2 * count :, :] = kept_ref[:size, :]
 
 
 def level_rank(state, rank_size, half_shift, owner_ref, half):
@@ -163,18 +174,17 @@
     finish(state, rank_size, half_shift, *refs)
 
 
-def last_sections(levels, rank_size, half_shift, pair_ref, other_ref, mine_ref, theirs_ref, far_ref, *refs):
+def last_sections(levels, rank_size, half_shift, pair_ref, other_ref, mine_ref, near_ref, cross_ref, *refs):
+    width = levels * rank_size
     count = (pair_ref.shape[0] - 2 * rank_size) // 2
-    mine, theirs = pair_ref[:count, :], pair_ref[count : 2 * count, :]
-    far, cross = other_ref[:count, :], other_ref[count : 2 * count, :]
-    mine, theirs, far, cross = (
-        section_product(mine, far, mine_ref[1]),
-        section_product(theirs, cross, theirs_ref[1]),
-        section_product(far, mine, far_ref[0]),
-        section_product(cross, theirs, section_weights(other_ref[2 * count :, :], levels)),
-    )
-    mine, far = section_product(mine, theirs, mine_ref[2]), section_product(far, cross, far_ref[1])
-    finish(section_product(mine, far, mine_ref[3]), rank_size, half_shift, *refs)
+    own, pair = [
+        exact_dot(jnp.concatenate([pair_ref[rows, :], other_ref[rows, :]], axis=1), weights_ref[...])
+        for rows, weights_ref in ((pl.ds(0, count), near_ref), (pl.ds(count, count), cross_ref))
+    ]
+    far_weights = section_weights(other_ref[2 * count :, :], levels)
+    mine = section_product(own[:, :width], pair[:, :width], mine_ref[1])
+    far = section_product(own[:, width:], pair[:, width:], far_weights)
+    finish(section_product(mine, far, mine_ref[2]), rank_size, half_shift, *refs)
 
 
 def expand_below(rank_size, half_shift, state_ref, row_ref, owner_ref, below_ref):
@@ -225,63 +235,65 @@
         pltpu.with_memory_space_constraint(x, pltpu.HBM)
         for x in (field, col_factor.reshape(width, rows), mixing[0], rank_perm)
     ]
-    one_round = bits == 2 and sections == 4
-    sent_groups = [(0, 1), (1, 2), (3,)] if one_round else [tuple(range(sections - 1)), (sections - 1,)]
-    xb, col_here, sent, *kept = call(
-        lambda *refs: load(sent_groups, *refs),
-        [array(vectors, rows, kind=BF16), array(width, rows, kind=BF16)]
-        + [array(len(group), 2 * rank_size, width) for group in sent_groups],
-        [HBM] * 4, 8 * width**3, 3 * rows * width, *in_hbm,
+    size = 2 * rank_size
+    one_round = bits == 2 and sections == 4 and levels == 2
+    groups_sent = [(0, 1), (1,), (2, 3)] if one_round else [tuple(range(sections - 1)), (sections - 1,)]
+    xb, sent, *kept = call(
+        lambda *refs: load(groups_sent, *refs),
+        [array(vectors, rows, kind=BF16)]
+        + [array(len(group) * size + (0 if n else vectors), width) for n, group in enumerate(groups_sent)],
+        [HBM] * 4, 2 * vectors * rows * width, 3 * rows * width, *in_hbm,
         scratch=[
             pltpu.VMEM(field.shape, F32),
+            pltpu.VMEM((width, rows), BF16),
             pltpu.VMEM(mixing.shape[1:], BF16),
             pltpu.VMEM(rank_perm.shape, jnp.int32),
             pltpu.SemaphoreType.DMA((1 + levels + 2 + 4,)),
         ],
     )
+    weight_cost = (4 * width * width * sections, 8 * width * width * sections)
 
     def weights(chosen, *compacts):
         return call(
             lambda *refs: build_weights(levels, chosen, *refs), array(len(chosen), 2 * width, width, kind=BF16),
-            [VMEM] * len(compacts), 4 * width * width * sections, 8 * width * width * sections, *compacts,
+            [VMEM] * len(compacts), *weight_cost, *compacts,
         )
 
+    def pair_weights(start, mine, far):
+        return call(
+            lambda *refs: build_pair_weights(levels, start, *refs), array(2 * width, 2 * width, kind=BF16),
+            [VMEM] * 2, *weight_cost, mine, far,
+        )
+
     received = swapped(sent)
-    if one_round:
-        received_far = across(kept[0], 1)
-    state = call(
-        project, array(vectors, width), [VMEM, VMEM], 2 * vectors * rows * width, 3 * rows * width, xb, col_here
-    )
-    first_states = (state, swapped(state))
     step_cost = (24 * vectors * width * width, 8 * width * width)
     final = sections - 1
     if one_round:
-        mine = weights([(0, 0), (0, 1), (1, 1), (2, 0)], sent, *kept)
+        far = across(kept[0], 1)
+        mine = weights([(0, vectors), (1, 0), (1, size)], sent, kept[1])
+        states = call(
+            first_step, array(2 * vectors + size, width), [VMEM] * 5, *step_cost,
+            sent, received, mine, weights([(0, vectors)], received), kept[1],
+        )
+        first_states = (states, across(states, 1))
+        last_body = lambda *refs: last_sections(levels, *refs)
+        last_weights = (mine, pair_weights(vectors + size, sent, far), pair_weights(vectors + size, received, swapped(far)))
     else:
-        mine = weights([(0, n) for n in range(final)] + [(1, 0)], sent, *kept)
+        starts = [(0, vectors + n * size) for n in range(final)]
+        mine, theirs = weights(starts + [(1, 0)], sent, *kept), weights(starts, received)
         runs = []
         for section in range(sections):
             if section % bits or not section:
                 runs.append([section])
             else:
                 runs[-1].append(section)
-    theirs = weights([(0, n) for n in range(sent.shape[0])], received)
-    if one_round:
-        states = call(
-            first_step, array(2 * (vectors + rank_size), width), [VMEM] * 5, *step_cost,
-            *first_states, mine, theirs, received,
-        )
-        first_states = (states, across(states, 1))
-    for run in [] if one_round else runs[:-1]:
-        states = call(
-            lambda *refs, run=run: step(run, final, *refs), array(2, vectors, width), [VMEM] * 4, *step_cost,
-            *first_states, mine, theirs,
-        )
-        first_states = (states, across(states, (run[-1] + 1) % bits))
-    if one_round:
-        last_body = lambda *refs: last_sections(levels, *refs)
-        last_weights = (mine, theirs, weights([(0, 0), (0, 1)], received_far))
-    else:
+        first_states = (sent, received)
+        for run in runs[:-1]:
+            states = call(
+                lambda *refs, run=run: step(run, final, *refs), array(2, vectors, width), [VMEM] * 4, *step_cost,
+                *first_states, mine, theirs,
+            )
+            first_states = (states, across(states, (run[-1] + 1) % bits))
         last_body = lambda *refs: last_step(runs[-1], final, *refs)
         last_weights = (mine, theirs)
     expand_cost = (2 * vectors * width * rows, 4 * width * rows)

time: 22.3 us -> 21.4 us (0.960)
  waiting for transfers between devices: 13.1 us -> 12.1 us
    ppermute x2, waiting for transfers between devices: 3.69 us -> 1.92 us  [across(): lax.ppermute(value, 'bf', [(n, n ^ 1 << bit) for n in range(lax.axis_size...]
    ppermute x2, waiting for transfers between devices: 0.77 us -> 1.6 us  [swapped(): lax.ppermute(value, 'bf', [(n, n ^ 1) for n in range(lax.axis_size('bf'))])]
    ppermute x2, starting transfers between devices: 1.1 us -> 1.82 us  [swapped(): lax.ppermute(value, 'bf', [(n, n ^ 1) for n in range(lax.axis_size('bf'))])]
    ppermute x2, starting transfers between devices: 1.55 us -> 0.83 us  [across(): lax.ppermute(value, 'bf', [(n, n ^ 1 << bit) for n in range(lax.axis_size...]
  transfers between devices with their start and end apart: 6 -> 6, of which waited for: 5 -> 4; matrix products, arithmetic and copies ran while one was open for 0% -> 0% of each run, Pallas kernels for 11% -> 11%
where the time goes in v15:
time: 21.4 us; the launch traced here: 21.2 us
  waiting for transfers between devices  12.1 us (57%)
  Pallas kernels  5.18 us (24%)
  starting transfers between devices  3.86 us (18%)
    ppermute x2, waiting for transfers between devices, shifted(): lax.ppermute(value, axis, [(source, (source + distance) % size) for sourc...  8.61 us
    pallas_call x10, Pallas kernels, call(): pl.pallas_call(body, out_shape=shapes, in_specs=specs, out_specs=jax.tree...  5.18 us
    ppermute x2, waiting for transfers between devices, across(): lax.ppermute(value, 'bf', [(n, n ^ 1 << bit) for n in range(lax.axis_size...  1.92 us
    ppermute x2, starting transfers between devices, swapped(): lax.ppermute(value, 'bf', [(n, n ^ 1) for n in range(lax.axis_size('bf'))])  1.82 us
    ppermute x2, waiting for transfers between devices, swapped(): lax.ppermute(value, 'bf', [(n, n ^ 1) for n in range(lax.axis_size('bf'))])  1.6 us
    ppermute x2, starting transfers between devices, shifted(): lax.ppermute(value, axis, [(source, (source + distance) % size) for sourc...  1.21 us
    ppermute x2, starting transfers between devices, across(): lax.ppermute(value, 'bf', [(n, n ^ 1 << bit) for n in range(lax.axis_size...  0.83 us
  transfers between devices with their start and end apart: 6, of which 4 were waited for; matrix products, arithmetic and copies ran while one was open for 0% of the time, Pallas kernels for 11%

profile of v15, /device:TPU:29, one launch (start us, length us, event | category | flops | bytes accessed | tf_op | source)
XLA Modules:
  0.0 21.2 jit_solution(1555081843986687182)
XLA Ops:
  0.0 0.0 copy-start
  0.0 0.0 copy-start.1
  0.0 1.6 %shard_map.73 = (bf16[16,2048]{1,0:T(8,128)(2,1)S(1)}, f32[272,128]{1,0:T(8,128)S(1)}, f32[128,128]{1,0:T(8,128)S(1)}, f32[256,128]{1,0:T(8,128)S(1)}) custom-call(f32[16,2048]{1,0:T(8,128)} %refs_0_.1, bf16[128,2048]{1,0:T(8,128)(2,1)} %bitcast.5, bf16[2,4,2,64,64]{4,3,2,1,0:T(8,128)(2,1)} %bitcast.6, s32[2,64]{1,0:T(2,128)} %refs_3_.1), custom_call_target="tpu_custom_call" | custom-call | flops 8388608 | bytes 786432 | tf_op jit(solution)/shard_map/pallas_call | solution.py:28
  1.7 0.7 %collective-permute-start = (f32[272,128]{1,0:T(8,128)S(1)}, f32[272,128]{1,0:T(8,128)S(1)}, u32[]{:S(2)}, u32[]{:S(2)}) collective-permute-start(f32[272,128]{1,0:T(8,128)S(1)} %get-tuple-element.11.refs_0_.sent_ref), channel_id=1, source_target_pairs={{0,1},{1,0},{2,3},{3,2},{4,5},{5,4},{6,7},{7,6},{8,9},{9,8},{10,11... | collective-permute-start | bytes 417800 | tf_op jit(solution)/shard_map/ppermute | solution.py:20
  2.4 0.2 %collective-permute-start.2 = (f32[128,128]{1,0:T(8,128)S(1)}, f32[128,128]{1,0:T(8,128)S(1)}, u32[]{:S(2)}, u32[]{:S(2)}) collective-permute-start(f32[128,128]{1,0:T(8,128)S(1)} %get-tuple-element.13), channel_id=1, source_target_pairs={{0,2},{1,3},{2,0},{3,1},{4,6},{5,7},{6,4},{7,5},{8,10},{9,11},{10,... | collective-permute-start | bytes 196616 | tf_op jit(solution)/shard_map/ppermute | solution.py:24
  2.7 0.7 %collective-permute-done.refs_0_.received_ref = f32[272,128]{1,0:T(8,128)S(1)} collective-permute-done((f32[272,128]{1,0:T(8,128)S(1)}, f32[272,128]{1,0:T(8,128)S(1)}, u32[]{:S(2)}, u32[]{:S(2)}) %collective-permute-start) | collective-permute-done | bytes 139296 | tf_op jit(solution)/shard_map/ppermute | solution.py:20
  3.4 0.1 shard_map.76.refs_0_
  3.6 0.6 %collective-permute-start.1 = (f32[160,128]{1,0:T(8,128)S(1)}, f32[160,128]{1,0:T(8,128)S(1)}, u32[]{:S(2)}, u32[]{:S(2)}) collective-permute-start(f32[160,128]{1,0:T(8,128)S(1)} %shard_map.76.refs_0_), channel_id=1, source_target_pairs={{0,2},{1,3},{2,0},{3,1},{4,6},{5,7},{6,4},{7,5},{8,10},{9,11},{10,... | collective-permute-start | bytes 245768 | tf_op jit(solution)/shard_map/ppermute | solution.py:24
  4.1 1.9 %collective-permute-done.2.refs_1_ = f32[128,128]{1,0:T(8,128)S(1)} collective-permute-done((f32[128,128]{1,0:T(8,128)S(1)}, f32[128,128]{1,0:T(8,128)S(1)}, u32[]{:S(2)}, u32[]{:S(2)}) %collective-permute-start.2) | collective-permute-done | bytes 65568 | tf_op jit(solution)/shard_map/ppermute | solution.py:24
  6.1 1.1 %collective-permute-start.3 = (f32[128,128]{1,0:T(8,128)S(1)}, f32[128,128]{1,0:T(8,128)S(1)}, u32[]{:S(2)}, u32[]{:S(2)}) collective-permute-start(f32[128,128]{1,0:T(8,128)S(1)} %collective-permute-done.2.refs_1_), channel_id=1, source_target_pairs={{0,1},{1,0},{2,3},{3,2},{4,5},{5,4},{6,7},{7,6},{8,9},{9,8},{10,11... | collective-permute-start | bytes 196616 | tf_op jit(solution)/shard_map/ppermute | solution.py:20
  7.2 0.9 %collective-permute-done.3.refs_1_ = f32[128,128]{1,0:T(8,128)S(1)} collective-permute-done((f32[128,128]{1,0:T(8,128)S(1)}, f32[128,128]{1,0:T(8,128)S(1)}, u32[]{:S(2)}, u32[]{:S(2)}) %collective-permute-start.3) | collective-permute-done | bytes 65568 | tf_op jit(solution)/shard_map/ppermute | solution.py:20
  8.1 0.0 collective-permute-done.1.refs_1_
  8.1 0.0 copy-done
  8.1 0.0 copy-done.1
  8.1 0.6 %shard_map.79 = (f32[16,128]{1,0:T(8,128)S(1)}, f32[16,2048]{1,0:T(8,128)S(1)}) custom-call(f32[160,128]{1,0:T(8,128)S(1)} %shard_map.76.refs_0_, f32[160,128]{1,0:T(8,128)S(1)} %collective-permute-done.1.refs_1_, bf16[3,256,128]{2,1,0:T(8,128)(2,1)S(1)} %shard_map.74.mine_ref.refs_2_, bf16[256,256]{1,0:T(8,128)(2,1)S(1)} %shard_map.77.refs_3_, ...), custom_call_target="tpu_custom_call" | custom-call | flops 8388608 | bytes 1048576 | tf_op jit(solution)/shard_map/pallas_call | solution.py:28
  8.7 0.1 collective-permute-start.4
  8.8 0.2 shard_map.80
  9.0 1.1 %collective-permute-start.5 = (f32[16,2048]{1,0:T(8,128)S(1)}, f32[16,2048]{1,0:T(8,128)S(1)}, u32[]{:S(2)}, u32[]{:S(2)}) collective-permute-start(f32[16,2048]{1,0:T(8,128)S(1)} %shard_map.80), channel_id=1, source_target_pairs={{0,28},{4,0},{8,4},{12,8},{16,12},{20,16},{24,20},{28,24},{1,29},{... | collective-permute-start | bytes 393224 | tf_op jit(solution)/shard_map/ppermute | solution.py:16
  10.1 1.8 %shard_map.81.diag_ref = f32[16,2048]{1,0:T(8,128)S(1)} custom-call(bf16[16,2048]{1,0:T(8,128)(2,1)S(1)} %get-tuple-element.16.xb_ref, bf16[4,512,512]{2,1,0:T(8,128)(2,1)} %leaf_hbm.1), custom_call_target="tpu_custom_call" | custom-call | flops 33554432 | bytes 2097152 | tf_op jit(solution)/shard_map/pallas_call | solution.py:28
  11.9 8.6 %collective-permute-done.4.half_ref = f32[16,2048]{1,0:T(8,128)S(1)} collective-permute-done((f32[16,2048]{1,0:T(8,128)S(1)}, f32[16,2048]{1,0:T(8,128)S(1)}, u32[]{:S(2)}, u32[]{:S(2)}) %collective-permute-start.4) | collective-permute-done | bytes 131104 | tf_op jit(solution)/shard_map/ppermute | solution.py:16
  20.6 0.0 collective-permute-done.5.below_ref
  20.6 0.7 %shard_map.82 = f32[16,2048]{1,0:T(8,128)} custom-call(f32[16,2048]{1,0:T(8,128)S(1)} %collective-permute-done.4.half_ref, f32[16,2048]{1,0:T(8,128)S(1)} %collective-permute-done.5.below_ref, f32[16,2048]{1,0:T(8,128)S(1)} %shard_map.81.diag_ref), custom_call_target="tpu_custom_call" | custom-call | flops 65536 | bytes 524288 | tf_op jit(solution)/shard_map/pallas_call | solution.py:28
  (4 shorter events, 0.1 us)
Async XLA Ops:
  0.0 8.1 %copy-start = (bf16[2,64,2048]{2,1,0:T(8,128)(2,1)S(1)}, bf16[2,64,2048]{2,1,0:T(8,128)(2,1)}, u32[]{:S(2)}) copy-start(bf16[2,64,2048]{2,1,0:T(8,128)(2,1)} %param.10) | copy-start | bytes 1572868
  0.0 8.1 %copy-start.1 = (s32[2,8]{1,0:T(2,128)S(1)}, s32[2,8]{1,0:T(2,128)}, u32[]{:S(2)}) copy-start(s32[2,8]{1,0:T(2,128)} %refs_2_.1) | copy-start | bytes 196
  1.7 1.7 %collective-permute-start = (f32[272,128]{1,0:T(8,128)S(1)}, f32[272,128]{1,0:T(8,128)S(1)}, u32[]{:S(2)}, u32[]{:S(2)}) collective-permute-start(f32[272,128]{1,0:T(8,128)S(1)} %get-tuple-element.11.refs_0_.sent_ref), channel_id=1, source_target_pairs={{0,1},{1,0},{2,3},{3,2},{4,5},{5,4},{6,7},{7,6},{8,9},{9,8},{10,11... | collective-permute-start | bytes 417800 | tf_op jit(solution)/shard_map/ppermute | solution.py:20
  2.4 3.7 %collective-permute-start.2 = (f32[128,128]{1,0:T(8,128)S(1)}, f32[128,128]{1,0:T(8,128)S(1)}, u32[]{:S(2)}, u32[]{:S(2)}) collective-permute-start(f32[128,128]{1,0:T(8,128)S(1)} %get-tuple-element.13), channel_id=1, source_target_pairs={{0,2},{1,3},{2,0},{3,1},{4,6},{5,7},{6,4},{7,5},{8,10},{9,11},{10,... | collective-permute-start | bytes 196616 | tf_op jit(solution)/shard_map/ppermute | solution.py:24
  3.6 4.5 %collective-permute-start.1 = (f32[160,128]{1,0:T(8,128)S(1)}, f32[160,128]{1,0:T(8,128)S(1)}, u32[]{:S(2)}, u32[]{:S(2)}) collective-permute-start(f32[160,128]{1,0:T(8,128)S(1)} %shard_map.76.refs_0_), channel_id=1, source_target_pairs={{0,2},{1,3},{2,0},{3,1},{4,6},{5,7},{6,4},{7,5},{8,10},{9,11},{10,... | collective-permute-start | bytes 245768 | tf_op jit(solution)/shard_map/ppermute | solution.py:24
  6.1 2.0 %collective-permute-start.3 = (f32[128,128]{1,0:T(8,128)S(1)}, f32[128,128]{1,0:T(8,128)S(1)}, u32[]{:S(2)}, u32[]{:S(2)}) collective-permute-start(f32[128,128]{1,0:T(8,128)S(1)} %collective-permute-done.2.refs_1_), channel_id=1, source_target_pairs={{0,1},{1,0},{2,3},{3,2},{4,5},{5,4},{6,7},{7,6},{8,9},{9,8},{10,11... | collective-permute-start | bytes 196616 | tf_op jit(solution)/shard_map/ppermute | solution.py:20
  8.7 11.9 %collective-permute-start.4 = (f32[16,2048]{1,0:T(8,128)S(1)}, f32[16,2048]{1,0:T(8,128)S(1)}, u32[]{:S(2)}, u32[]{:S(2)}) collective-permute-start(f32[16,2048]{1,0:T(8,128)S(1)} %get-tuple-element.14), channel_id=1, source_target_pairs={{0,16},{4,20},{8,24},{12,28},{16,0},{20,4},{24,8},{28,12},{1,17},{... | collective-permute-start | bytes 393224 | tf_op jit(solution)/shard_map/ppermute | solution.py:16
  9.0 11.6 %collective-permute-start.5 = (f32[16,2048]{1,0:T(8,128)S(1)}, f32[16,2048]{1,0:T(8,128)S(1)}, u32[]{:S(2)}, u32[]{:S(2)}) collective-permute-start(f32[16,2048]{1,0:T(8,128)S(1)} %shard_map.80), channel_id=1, source_target_pairs={{0,28},{4,0},{8,4},{12,8},{16,12},{20,16},{24,20},{28,24},{1,29},{... | collective-permute-start | bytes 393224 | tf_op jit(solution)/shard_map/ppermute | solution.py:16

commit v16 on v15

--- a/solution.py
+++ b/solution.py
@@ -18,6 +18,10 @@
 
 def swapped(value):
     return lax.ppermute(value, "bf", [(n, n ^ 1) for n in range(lax.axis_size("bf"))])
+
+
+def crossed(value):
+    return lax.ppermute(value, "bf", [(n, n ^ 3) for n in range(lax.axis_size("bf"))])
 
 
 def across(value, bit):
@@ -57,9 +61,10 @@
     return jnp.concatenate([mixing_ref[level, section, side].astype(F32) for level in range(levels)], axis=1)
 
 
-def split_rows(source, target, parts):
-    count = source.shape[0] // parts
-    return [(source.at[pl.ds(n * count, count)], target.at[pl.ds(n * count, count)]) for n in range(parts)]
+def split(source, target, parts, axis):
+    count = source.shape[axis] // parts
+    places = [(slice(None),) * axis + (pl.ds(n * count, count),) for n in range(parts)]
+    return [(source.at[place], target.at[place]) for place in places]
 
 
 def load(groups, field_hbm, col_hbm, mixing_hbm, perm_hbm, xb_ref, sent_ref, *refs):
@@ -68,8 +73,9 @@
     vectors = field_ref.shape[0]
     first = [(perm_hbm, perm_ref)]
     first += [(mixing_hbm.at[level], mixing_ref.at[level]) for level in range(levels)]
-    second = split_rows(field_hbm, field_ref, 2)
-    third = split_rows(col_hbm, col_ref, 4)
+    parts = 4
+    second = split(field_hbm, field_ref, parts, 1)
+    third = split(col_hbm, col_ref, parts, 1)
     copies = [pltpu.make_async_copy(*pair, sems.at[n]) for n, pair in enumerate(first + second + third)]
     for copy in copies:
         copy.start()
@@ -88,11 +94,17 @@
                 if section in group:
                     start = (0 if n else vectors) + (2 * group.index(section) + side) * k
                     out_ref[start : start + k, :] = mats
-    for copy in copies[len(first) :]:
-        copy.wait()
-    xb = field_ref[...].astype(BF16)
-    xb_ref[...] = xb
-    sent_ref[:vectors, :] = lax.dot_general(xb, col_ref[...], NT, preferred_element_type=F32)
+    count = field_ref.shape[1] // parts
+    state = None
+    for n in range(parts):
+        copies[len(first) + n].wait()
+        copies[len(first) + parts + n].wait()
+        part = pl.ds(n * count, count)
+        xb = field_ref[:, part].astype(BF16)
+        xb_ref[:, part] = xb
+        term = lax.dot_general(xb, col_ref[:, part], NT, preferred_element_type=F32)
+        state = term if state is None else state + term
+    sent_ref[:vectors, :] = state
 
 
 def build_weights(levels, chosen, *refs):
@@ -147,13 +159,12 @@
     run_sections(sections, final, (first_ref, second_ref), mine_ref, theirs_ref, out_ref)
 
 
-def first_step(sent_ref, received_ref, mine_ref, theirs_ref, kept_ref, out_ref):
-    size = kept_ref.shape[0] // 2
+def first_step(size, sent_ref, received_ref, mine_ref, theirs_ref, out_ref):
     count = (out_ref.shape[0] - size) // 2
     mine, theirs = sent_ref[:count, :], received_ref[:count, :]
     out_ref[:count, :] = section_product(mine, theirs, mine_ref[0])
     out_ref[count : 2 * count, :] = section_product(theirs, mine, theirs_ref[0])
-    out_ref[2 * count :, :] = kept_ref[:size, :]
+    out_ref[2 * count :, :] = received_ref[-size:, :]
 
 
 def level_rank(state, rank_size, half_shift, owner_ref, half):
@@ -163,10 +174,11 @@
     return (jnp.where(chosen, state, 0.0) if half else jnp.where(chosen, 0.0, state)).astype(BF16)
 
 
-def finish(state, rank_size, half_shift, row_ref, owner_ref, state_ref, half_ref):
-    state_ref[...] = state
-    rank = level_rank(state, rank_size, half_shift, owner_ref, True)
-    half_ref[...] = jnp.dot(rank, row_ref[...], preferred_element_type=F32)
+def finish(state, rank_size, half_shift, row_ref, owner_ref, half_ref, below_ref):
+    ranks = [level_rank(state, rank_size, half_shift, owner_ref, half) for half in (True, False)]
+    outs = jnp.dot(jnp.concatenate(ranks, axis=0), row_ref[...], preferred_element_type=F32)
+    half_ref[...] = outs[: state.shape[0]]
+    below_ref[...] = outs[state.shape[0] :]
 
 
 def last_step(sections, final, rank_size, half_shift, first_ref, second_ref, mine_ref, theirs_ref, *refs):
@@ -178,8 +190,11 @@
     width = levels * rank_size
     count = (pair_ref.shape[0] - 2 * rank_size) // 2
     own, pair = [
-        exact_dot(jnp.concatenate([pair_ref[rows, :], other_ref[rows, :]], axis=1), weights_ref[...])
-        for rows, weights_ref in ((pl.ds(0, count), near_ref), (pl.ds(count, count), cross_ref))
+        exact_dot(jnp.concatenate([pair_ref[here, :], other_ref[there, :]], axis=1), weights_ref[...])
+        for here, there, weights_ref in (
+            (pl.ds(0, count), pl.ds(count, count), near_ref),
+            (pl.ds(count, count), pl.ds(0, count), cross_ref),
+        )
     ]
     far_weights = section_weights(other_ref[2 * count :, :], levels)
     mine = section_product(own[:, :width], pair[:, :width], mine_ref[1])
@@ -187,16 +202,11 @@
     finish(section_product(mine, far, mine_ref[2]), rank_size, half_shift, *refs)
 
 
-def expand_below(rank_size, half_shift, state_ref, row_ref, owner_ref, below_ref):
-    rank = level_rank(state_ref[...], rank_size, half_shift, owner_ref, False)
-    below_ref[...] = jnp.dot(rank, row_ref[...], preferred_element_type=F32)
-
-
 def diagonal(xb_ref, leaf_hbm, out_ref, leaf_ref, sems):
     blocks, order, _ = leaf_hbm.shape
     copies = []
     for n in range(blocks):
-        for source, target in split_rows(leaf_hbm.at[n], leaf_ref.at[n], 2):
+        for source, target in split(leaf_hbm.at[n], leaf_ref.at[n], 2, 0):
             copies.append(pltpu.make_async_copy(source, target, sems.at[len(copies)]))
             copies[-1].start()
     for n in range(blocks):
@@ -237,7 +247,7 @@
     ]
     size = 2 * rank_size
     one_round = bits == 2 and sections == 4 and levels == 2
-    groups_sent = [(0, 1), (1,), (2, 3)] if one_round else [tuple(range(sections - 1)), (sections - 1,)]
+    groups_sent = [(0, 1, 2), (1,), (2, 3)] if one_round else [tuple(range(sections - 1)), (sections - 1,)]
     xb, sent, *kept = call(
         lambda *refs: load(groups_sent, *refs),
         [array(vectors, rows, kind=BF16)]
@@ -248,7 +258,7 @@
             pltpu.VMEM((width, rows), BF16),
             pltpu.VMEM(mixing.shape[1:], BF16),
             pltpu.VMEM(rank_perm.shape, jnp.int32),
-            pltpu.SemaphoreType.DMA((1 + levels + 2 + 4,)),
+            pltpu.SemaphoreType.DMA((1 + levels + 4 + 4,)),
         ],
     )
     weight_cost = (4 * width * width * sections, 8 * width * width * sections)
@@ -269,15 +279,15 @@
     step_cost = (24 * vectors * width * width, 8 * width * width)
     final = sections - 1
     if one_round:
-        far = across(kept[0], 1)
+        cross = crossed(kept[0])
         mine = weights([(0, vectors), (1, 0), (1, size)], sent, kept[1])
         states = call(
-            first_step, array(2 * vectors + size, width), [VMEM] * 5, *step_cost,
-            sent, received, mine, weights([(0, vectors)], received), kept[1],
+            lambda *refs: first_step(size, *refs), array(2 * vectors + size, width), [VMEM] * 4, *step_cost,
+            sent, received, mine, weights([(0, vectors)], received),
         )
-        first_states = (states, across(states, 1))
+        first_states = (states, crossed(states))
         last_body = lambda *refs: last_sections(levels, *refs)
-        last_weights = (mine, pair_weights(vectors + size, sent, far), pair_weights(vectors + size, received, swapped(far)))
+        last_weights = (mine, pair_weights(vectors + size, sent, swapped(cross)), pair_weights(vectors + size, received, cross))
     else:
         starts = [(0, vectors + n * size) for n in range(final)]
         mine, theirs = weights(starts + [(1, 0)], sent, *kept), weights(starts, received)
@@ -298,14 +308,9 @@
         last_weights = (mine, theirs)
     expand_cost = (2 * vectors * width * rows, 4 * width * rows)
     expand = row_factor.reshape(width, rows)
-    state, out_half = call(
-        lambda *refs: last_body(rank_size, groups // 2, *refs),
-        [array(vectors, width), array(vectors, rows)],
+    out_half, out_below = call(
+        lambda *refs: last_body(rank_size, groups // 2, *refs), [array(vectors, rows)] * 2,
         [VMEM] * (4 + len(last_weights)), *expand_cost, *first_states, *last_weights, expand, row_owner,
-    )
-    out_below = call(
-        lambda *refs: expand_below(rank_size, groups // 2, *refs), array(vectors, rows),
-        [VMEM] * 3, *expand_cost, state, expand, row_owner,
     )
     out_half = shifted(out_half, "grp", groups // 2)
     out_below = shifted(out_below, "grp", groups - 1)

time: 21.4 us -> 22 us (1.028)
  the two profiles are of different devices: /device:TPU:29 before, /device:TPU:24 now
where the time goes in v16:
time: 22 us; the launch traced here: 21.7 us
  waiting for transfers between devices  11.4 us (52%)
  Pallas kernels  5.27 us (24%)
  starting transfers between devices  4.96 us (23%)
    ppermute x2, waiting for transfers between devices, shifted(): lax.ppermute(value, axis, [(source, (source + distance) % size) for sourc...  8.36 us
    pallas_call x9, Pallas kernels, call(): pl.pallas_call(body, out_shape=shapes, in_specs=specs, out_specs=jax.tree...  5.27 us
    ppermute x2, starting transfers between devices, crossed(): lax.ppermute(value, 'bf', [(n, n ^ 3) for n in range(lax.axis_size('bf'))])  2.72 us
    ppermute x2, waiting for transfers between devices, crossed(): lax.ppermute(value, 'bf', [(n, n ^ 3) for n in range(lax.axis_size('bf'))])  2.12 us
    ppermute x2, starting transfers between devices, shifted(): lax.ppermute(value, axis, [(source, (source + distance) % size) for sourc...  1.77 us
    ppermute x2, waiting for transfers between devices, swapped(): lax.ppermute(value, 'bf', [(n, n ^ 1) for n in range(lax.axis_size('bf'))])  0.9 us
    ppermute x2, starting transfers between devices, swapped(): lax.ppermute(value, 'bf', [(n, n ^ 1) for n in range(lax.axis_size('bf'))])  0.46 us
  transfers between devices with their start and end apart: 6, of which 4 were waited for; matrix products, arithmetic and copies ran while one was open for 0% of the time, Pallas kernels for 10%

profile of v16, /device:TPU:24, one launch (start us, length us, event | category | flops | bytes accessed | tf_op | source)
XLA Modules:
  0.0 21.7 jit_solution(6386482780886103826)
XLA Ops:
  0.0 0.0 copy-start
  0.0 0.0 copy-start.1
  0.0 1.9 %shard_map.73 = (bf16[16,2048]{1,0:T(8,128)(2,1)S(1)}, f32[400,128]{1,0:T(8,128)S(1)}, f32[128,128]{1,0:T(8,128)S(1)}, f32[256,128]{1,0:T(8,128)S(1)}) custom-call(f32[16,2048]{1,0:T(8,128)} %refs_0_.1, bf16[128,2048]{1,0:T(8,128)(2,1)} %bitcast.4, bf16[2,4,2,64,64]{4,3,2,1,0:T(8,128)(2,1)} %bitcast.5, s32[2,64]{1,0:T(2,128)} %refs_3_.1), custom_call_target="tpu_custom_call" | custom-call | flops 8388608 | bytes 786432 | tf_op jit(solution)/shard_map/pallas_call | solution.py:32
  1.9 0.1 collective-permute-start
  2.0 1.6 %collective-permute-start.2 = (f32[128,128]{1,0:T(8,128)S(1)}, f32[128,128]{1,0:T(8,128)S(1)}, u32[]{:S(2)}, u32[]{:S(2)}) collective-permute-start(f32[128,128]{1,0:T(8,128)S(1)} %get-tuple-element.13), channel_id=1, source_target_pairs={{0,3},{1,2},{2,1},{3,0},{4,7},{5,6},{6,5},{7,4},{8,11},{9,10},{10,... | collective-permute-start | bytes 196616 | tf_op jit(solution)/shard_map/ppermute | solution.py:24
  3.7 0.0 collective-permute-done.refs_0_.refs_1_
  3.7 0.1 shard_map.76.refs_0_
  3.8 1.1 %collective-permute-start.1 = (f32[160,128]{1,0:T(8,128)S(1)}, f32[160,128]{1,0:T(8,128)S(1)}, u32[]{:S(2)}, u32[]{:S(2)}) collective-permute-start(f32[160,128]{1,0:T(8,128)S(1)} %shard_map.76.refs_0_), channel_id=1, source_target_pairs={{0,3},{1,2},{2,1},{3,0},{4,7},{5,6},{6,5},{7,4},{8,11},{9,10},{10,... | collective-permute-start | bytes 245768 | tf_op jit(solution)/shard_map/ppermute | solution.py:24
  4.9 1.0 %collective-permute-done.2.refs_1_ = f32[128,128]{1,0:T(8,128)S(1)} collective-permute-done((f32[128,128]{1,0:T(8,128)S(1)}, f32[128,128]{1,0:T(8,128)S(1)}, u32[]{:S(2)}, u32[]{:S(2)}) %collective-permute-start.2) | collective-permute-done | bytes 65568 | tf_op jit(solution)/shard_map/ppermute | solution.py:24
  5.9 0.4 %collective-permute-start.3 = (f32[128,128]{1,0:T(8,128)S(1)}, f32[128,128]{1,0:T(8,128)S(1)}, u32[]{:S(2)}, u32[]{:S(2)}) collective-permute-start(f32[128,128]{1,0:T(8,128)S(1)} %collective-permute-done.2.refs_1_), channel_id=1, source_target_pairs={{0,1},{1,0},{2,3},{3,2},{4,5},{5,4},{6,7},{7,6},{8,9},{9,8},{10,11... | collective-permute-start | bytes 196616 | tf_op jit(solution)/shard_map/ppermute | solution.py:20
  6.3 0.9 %collective-permute-done.3.refs_1_ = f32[128,128]{1,0:T(8,128)S(1)} collective-permute-done((f32[128,128]{1,0:T(8,128)S(1)}, f32[128,128]{1,0:T(8,128)S(1)}, u32[]{:S(2)}, u32[]{:S(2)}) %collective-permute-start.3) | collective-permute-done | bytes 65568 | tf_op jit(solution)/shard_map/ppermute | solution.py:20
  7.2 1.2 %collective-permute-done.1.refs_1_ = f32[160,128]{1,0:T(8,128)S(1)} collective-permute-done((f32[160,128]{1,0:T(8,128)S(1)}, f32[160,128]{1,0:T(8,128)S(1)}, u32[]{:S(2)}, u32[]{:S(2)}) %collective-permute-start.1) | collective-permute-done | bytes 81952 | tf_op jit(solution)/shard_map/ppermute | solution.py:24
  8.4 0.0 copy-done
  8.4 0.0 copy-done.1
  8.4 0.6 %shard_map.79 = (f32[16,2048]{1,0:T(8,128)S(1)}, f32[16,2048]{1,0:T(8,128)S(1)}) custom-call(f32[160,128]{1,0:T(8,128)S(1)} %shard_map.76.refs_0_, f32[160,128]{1,0:T(8,128)S(1)} %collective-permute-done.1.refs_1_, bf16[3,256,128]{2,1,0:T(8,128)(2,1)S(1)} %shard_map.74.refs_2_, bf16[256,256]{1,0:T(8,128)(2,1)S(1)} %shard_map.77.refs_3_, ...), custom_call_target="tpu_custom_call" | custom-call | flops 8388608 | bytes 1048576 | tf_op jit(solution)/shard_map/pallas_call | solution.py:32
  9.0 0.4 %collective-permute-start.4 = (f32[16,2048]{1,0:T(8,128)S(1)}, f32[16,2048]{1,0:T(8,128)S(1)}, u32[]{:S(2)}, u32[]{:S(2)}) collective-permute-start(f32[16,2048]{1,0:T(8,128)S(1)} %get-tuple-element.14), channel_id=1, source_target_pairs={{0,16},{4,20},{8,24},{12,28},{16,0},{20,4},{24,8},{28,12},{1,17},{... | collective-permute-start | bytes 393224 | tf_op jit(solution)/shard_map/ppermute | solution.py:16
  9.4 1.4 %collective-permute-start.5 = (f32[16,2048]{1,0:T(8,128)S(1)}, f32[16,2048]{1,0:T(8,128)S(1)}, u32[]{:S(2)}, u32[]{:S(2)}) collective-permute-start(f32[16,2048]{1,0:T(8,128)S(1)} %get-tuple-element.15), channel_id=1, source_target_pairs={{0,28},{4,0},{8,4},{12,8},{16,12},{20,16},{24,20},{28,24},{1,29},{... | collective-permute-start | bytes 393224 | tf_op jit(solution)/shard_map/ppermute | solution.py:16
  10.8 1.8 %shard_map.80.diag_ref = f32[16,2048]{1,0:T(8,128)S(1)} custom-call(bf16[16,2048]{1,0:T(8,128)(2,1)S(1)} %get-tuple-element.16.xb_ref, bf16[4,512,512]{2,1,0:T(8,128)(2,1)} %leaf_hbm.1), custom_call_target="tpu_custom_call" | custom-call | flops 33554432 | bytes 2097152 | tf_op jit(solution)/shard_map/pallas_call | solution.py:32
  12.6 8.4 %collective-permute-done.4.half_ref = f32[16,2048]{1,0:T(8,128)S(1)} collective-permute-done((f32[16,2048]{1,0:T(8,128)S(1)}, f32[16,2048]{1,0:T(8,128)S(1)}, u32[]{:S(2)}, u32[]{:S(2)}) %collective-permute-start.4) | collective-permute-done | bytes 131104 | tf_op jit(solution)/shard_map/ppermute | solution.py:16
  21.0 0.0 collective-permute-done.5.below_ref
  21.0 0.7 %shard_map.81 = f32[16,2048]{1,0:T(8,128)} custom-call(f32[16,2048]{1,0:T(8,128)S(1)} %collective-permute-done.4.half_ref, f32[16,2048]{1,0:T(8,128)S(1)} %collective-permute-done.5.below_ref, f32[16,2048]{1,0:T(8,128)S(1)} %shard_map.80.diag_ref), custom_call_target="tpu_custom_call" | custom-call | flops 65536 | bytes 524288 | tf_op jit(solution)/shard_map/pallas_call | solution.py:32
  (4 shorter events, 0.1 us)
Async XLA Ops:
  0.0 8.4 %copy-start = (bf16[2,64,2048]{2,1,0:T(8,128)(2,1)S(1)}, bf16[2,64,2048]{2,1,0:T(8,128)(2,1)}, u32[]{:S(2)}) copy-start(bf16[2,64,2048]{2,1,0:T(8,128)(2,1)} %param.10) | copy-start | bytes 1572868
  0.0 8.4 %copy-start.1 = (s32[2,8]{1,0:T(2,128)S(1)}, s32[2,8]{1,0:T(2,128)}, u32[]{:S(2)}) copy-start(s32[2,8]{1,0:T(2,128)} %refs_6_.1) | copy-start | bytes 196
  1.9 1.7 %collective-permute-start = (f32[400,128]{1,0:T(8,128)S(1)}, f32[400,128]{1,0:T(8,128)S(1)}, u32[]{:S(2)}, u32[]{:S(2)}) collective-permute-start(f32[400,128]{1,0:T(8,128)S(1)} %get-tuple-element.11.refs_0_), channel_id=1, source_target_pairs={{0,1},{1,0},{2,3},{3,2},{4,5},{5,4},{6,7},{7,6},{8,9},{9,8},{10,11... | collective-permute-start | bytes 614408 | tf_op jit(solution)/shard_map/ppermute | solution.py:20
  2.0 3.9 %collective-permute-start.2 = (f32[128,128]{1,0:T(8,128)S(1)}, f32[128,128]{1,0:T(8,128)S(1)}, u32[]{:S(2)}, u32[]{:S(2)}) collective-permute-start(f32[128,128]{1,0:T(8,128)S(1)} %get-tuple-element.13), channel_id=1, source_target_pairs={{0,3},{1,2},{2,1},{3,0},{4,7},{5,6},{6,5},{7,4},{8,11},{9,10},{10,... | collective-permute-start | bytes 196616 | tf_op jit(solution)/shard_map/ppermute | solution.py:24
  3.8 4.6 %collective-permute-start.1 = (f32[160,128]{1,0:T(8,128)S(1)}, f32[160,128]{1,0:T(8,128)S(1)}, u32[]{:S(2)}, u32[]{:S(2)}) collective-permute-start(f32[160,128]{1,0:T(8,128)S(1)} %shard_map.76.refs_0_), channel_id=1, source_target_pairs={{0,3},{1,2},{2,1},{3,0},{4,7},{5,6},{6,5},{7,4},{8,11},{9,10},{10,... | collective-permute-start | bytes 245768 | tf_op jit(solution)/shard_map/ppermute | solution.py:24
  5.9 1.3 %collective-permute-start.3 = (f32[128,128]{1,0:T(8,128)S(1)}, f32[128,128]{1,0:T(8,128)S(1)}, u32[]{:S(2)}, u32[]{:S(2)}) collective-permute-start(f32[128,128]{1,0:T(8,128)S(1)} %collective-permute-done.2.refs_1_), channel_id=1, source_target_pairs={{0,1},{1,0},{2,3},{3,2},{4,5},{5,4},{6,7},{7,6},{8,9},{9,8},{10,11... | collective-permute-start | bytes 196616 | tf_op jit(solution)/shard_map/ppermute | solution.py:20
  9.0 12.0 %collective-permute-start.4 = (f32[16,2048]{1,0:T(8,128)S(1)}, f32[16,2048]{1,0:T(8,128)S(1)}, u32[]{:S(2)}, u32[]{:S(2)}) collective-permute-start(f32[16,2048]{1,0:T(8,128)S(1)} %get-tuple-element.14), channel_id=1, source_target_pairs={{0,16},{4,20},{8,24},{12,28},{16,0},{20,4},{24,8},{28,12},{1,17},{... | collective-permute-start | bytes 393224 | tf_op jit(solution)/shard_map/ppermute | solution.py:16
  9.4 11.6 %collective-permute-start.5 = (f32[16,2048]{1,0:T(8,128)S(1)}, f32[16,2048]{1,0:T(8,128)S(1)}, u32[]{:S(2)}, u32[]{:S(2)}) collective-permute-start(f32[16,2048]{1,0:T(8,128)S(1)} %get-tuple-element.15), channel_id=1, source_target_pairs={{0,28},{4,0},{8,4},{12,8},{16,12},{20,16},{24,20},{28,24},{1,29},{... | collective-permute-start | bytes 393224 | tf_op jit(solution)/shard_map/ppermute | solution.py:16

commit v17 on v16

--- a/solution.py
+++ b/solution.py
@@ -73,9 +73,8 @@
     vectors = field_ref.shape[0]
     first = [(perm_hbm, perm_ref)]
     first += [(mixing_hbm.at[level], mixing_ref.at[level]) for level in range(levels)]
-    parts = 4
-    second = split(field_hbm, field_ref, parts, 1)
-    third = split(col_hbm, col_ref, parts, 1)
+    second = split(field_hbm, field_ref, 2, 0)
+    third = split(col_hbm, col_ref, 4, 0)
     copies = [pltpu.make_async_copy(*pair, sems.at[n]) for n, pair in enumerate(first + second + third)]
     for copy in copies:
         copy.start()
@@ -94,17 +93,11 @@
                 if section in group:
                     start = (0 if n else vectors) + (2 * group.index(section) + side) * k
                     out_ref[start : start + k, :] = mats
-    count = field_ref.shape[1] // parts
-    state = None
-    for n in range(parts):
-        copies[len(first) + n].wait()
-        copies[len(first) + parts + n].wait()
-        part = pl.ds(n * count, count)
-        xb = field_ref[:, part].astype(BF16)
-        xb_ref[:, part] = xb
-        term = lax.dot_general(xb, col_ref[:, part], NT, preferred_element_type=F32)
-        state = term if state is None else state + term
-    sent_ref[:vectors, :] = state
+    for copy in copies[len(first) :]:
+        copy.wait()
+    xb = field_ref[...].astype(BF16)
+    xb_ref[...] = xb
+    sent_ref[:vectors, :] = lax.dot_general(xb, col_ref[...], NT, preferred_element_type=F32)
 
 
 def build_weights(levels, chosen, *refs):
@@ -159,12 +152,12 @@
     run_sections(sections, final, (first_ref, second_ref), mine_ref, theirs_ref, out_ref)
 
 
-def first_step(size, sent_ref, received_ref, mine_ref, theirs_ref, out_ref):
+def first_step(size, sent_ref, received_ref, mine_ref, theirs_ref, kept_ref, out_ref):
     count = (out_ref.shape[0] - size) // 2
     mine, theirs = sent_ref[:count, :], received_ref[:count, :]
     out_ref[:count, :] = section_product(mine, theirs, mine_ref[0])
     out_ref[count : 2 * count, :] = section_product(theirs, mine, theirs_ref[0])
-    out_ref[2 * count :, :] = received_ref[-size:, :]
+    out_ref[2 * count :, :] = kept_ref[:size, :]
 
 
 def level_rank(state, rank_size, half_shift, owner_ref, half):
@@ -190,11 +183,8 @@
     width = levels * rank_size
     count = (pair_ref.shape[0] - 2 * rank_size) // 2
     own, pair = [
-        exact_dot(jnp.concatenate([pair_ref[here, :], other_ref[there, :]], axis=1), weights_ref[...])
-        for here, there, weights_ref in (
-            (pl.ds(0, count), pl.ds(count, count), near_ref),
-            (pl.ds(count, count), pl.ds(0, count), cross_ref),
-        )
+        exact_dot(jnp.concatenate([pair_ref[rows, :], other_ref[rows, :]], axis=1), weights_ref[...])
+        for rows, weights_ref in ((pl.ds(0, count), near_ref), (pl.ds(count, count), cross_ref))
     ]
     far_weights = section_weights(other_ref[2 * count :, :], levels)
     mine = section_product(own[:, :width], pair[:, :width], mine_ref[1])
@@ -247,7 +237,7 @@
     ]
     size = 2 * rank_size
     one_round = bits == 2 and sections == 4 and levels == 2
-    groups_sent = [(0, 1, 2), (1,), (2, 3)] if one_round else [tuple(range(sections - 1)), (sections - 1,)]
+    groups_sent = [(0, 1), (1,), (2, 3)] if one_round else [tuple(range(sections - 1)), (sections - 1,)]
     xb, sent, *kept = call(
         lambda *refs: load(groups_sent, *refs),
         [array(vectors, rows, kind=BF16)]
@@ -258,7 +248,7 @@
             pltpu.VMEM((width, rows), BF16),
             pltpu.VMEM(mixing.shape[1:], BF16),
             pltpu.VMEM(rank_perm.shape, jnp.int32),
-            pltpu.SemaphoreType.DMA((1 + levels + 4 + 4,)),
+            pltpu.SemaphoreType.DMA((1 + levels + 2 + 4,)),
         ],
     )
     weight_cost = (4 * width * width * sections, 8 * width * width * sections)
@@ -282,10 +272,10 @@
         cross = crossed(kept[0])
         mine = weights([(0, vectors), (1, 0), (1, size)], sent, kept[1])
         states = call(
-            lambda *refs: first_step(size, *refs), array(2 * vectors + size, width), [VMEM] * 4, *step_cost,
-            sent, received, mine, weights([(0, vectors)], received),
+            lambda *refs: first_step(size, *refs), array(2 * vectors + size, width), [VMEM] * 5, *step_cost,
+            sent, received, mine, weights([(0, vectors)], received), kept[1],
         )
-        first_states = (states, crossed(states))
+        first_states = (states, across(states, 1))
         last_body = lambda *refs: last_sections(levels, *refs)
         last_weights = (mine, pair_weights(vectors + size, sent, swapped(cross)), pair_weights(vectors + size, received, cross))
     else:

time: 22 us -> 21.1 us (0.959)
  the two profiles are of different devices: /device:TPU:24 before, /device:TPU:29 now
where the time goes in v17:
time: 21.1 us; the launch traced here: 20.9 us
  waiting for transfers between devices  13.1 us (62%)
  Pallas kernels  5.02 us (24%)
  starting transfers between devices  2.69 us (13%)
    ppermute x2, waiting for transfers between devices, shifted(): lax.ppermute(value, axis, [(source, (source + distance) % size) for sourc...  8.81 us
    pallas_call x9, Pallas kernels, call(): pl.pallas_call(body, out_shape=shapes, in_specs=specs, out_specs=jax.tree...  5.02 us
    ppermute x1, waiting for transfers between devices, crossed(): lax.ppermute(value, 'bf', [(n, n ^ 3) for n in range(lax.axis_size('bf'))])  2.27 us
    ppermute x2, waiting for transfers between devices, swapped(): lax.ppermute(value, 'bf', [(n, n ^ 1) for n in range(lax.axis_size('bf'))])  2.03 us
    ppermute x2, starting transfers between devices, shifted(): lax.ppermute(value, axis, [(source, (source + distance) % size) for sourc...  1.22 us
    ppermute x2, starting transfers between devices, swapped(): lax.ppermute(value, 'bf', [(n, n ^ 1) for n in range(lax.axis_size('bf'))])  0.74 us
    ppermute x1, starting transfers between devices, across(): lax.ppermute(value, 'bf', [(n, n ^ 1 << bit) for n in range(lax.axis_size...  0.54 us
  transfers between devices with their start and end apart: 6, of which 4 were waited for; matrix products, arithmetic and copies ran while one was open for 0% of the time, Pallas kernels for 10%

profile of v17, /device:TPU:29, one launch (start us, length us, event | category | flops | bytes accessed | tf_op | source)
XLA Modules:
  0.0 20.9 jit_solution(17457512914321973303)
XLA Ops:
  0.0 0.0 copy-start
  0.0 0.0 copy-start.1
  0.0 1.6 %shard_map.73 = (bf16[16,2048]{1,0:T(8,128)(2,1)S(1)}, f32[272,128]{1,0:T(8,128)S(1)}, f32[128,128]{1,0:T(8,128)S(1)}, f32[256,128]{1,0:T(8,128)S(1)}) custom-call(f32[16,2048]{1,0:T(8,128)} %refs_0_.1, bf16[128,2048]{1,0:T(8,128)(2,1)} %bitcast.4, bf16[2,4,2,64,64]{4,3,2,1,0:T(8,128)(2,1)} %bitcast.5, s32[2,64]{1,0:T(2,128)} %refs_3_.1), custom_call_target="tpu_custom_call" | custom-call | flops 8388608 | bytes 786432 | tf_op jit(solution)/shard_map/pallas_call | solution.py:32
  1.7 0.7 %collective-permute-start = (f32[272,128]{1,0:T(8,128)S(1)}, f32[272,128]{1,0:T(8,128)S(1)}, u32[]{:S(2)}, u32[]{:S(2)}) collective-permute-start(f32[272,128]{1,0:T(8,128)S(1)} %get-tuple-element.11.refs_0_), channel_id=1, source_target_pairs={{0,1},{1,0},{2,3},{3,2},{4,5},{5,4},{6,7},{7,6},{8,9},{9,8},{10,11... | collective-permute-start | bytes 417800 | tf_op jit(solution)/shard_map/ppermute | solution.py:20
  2.4 0.2 collective-permute-start.2
  2.6 0.8 %collective-permute-done.refs_0_.refs_1_ = f32[272,128]{1,0:T(8,128)S(1)} collective-permute-done((f32[272,128]{1,0:T(8,128)S(1)}, f32[272,128]{1,0:T(8,128)S(1)}, u32[]{:S(2)}, u32[]{:S(2)}) %collective-permute-start) | collective-permute-done | bytes 139296 | tf_op jit(solution)/shard_map/ppermute | solution.py:20
  3.4 0.1 shard_map.76.refs_0_
  3.6 0.5 %collective-permute-start.1 = (f32[160,128]{1,0:T(8,128)S(1)}, f32[160,128]{1,0:T(8,128)S(1)}, u32[]{:S(2)}, u32[]{:S(2)}) collective-permute-start(f32[160,128]{1,0:T(8,128)S(1)} %shard_map.76.refs_0_), channel_id=1, source_target_pairs={{0,2},{1,3},{2,0},{3,1},{4,6},{5,7},{6,4},{7,5},{8,10},{9,11},{10,... | collective-permute-start | bytes 245768 | tf_op jit(solution)/shard_map/ppermute | solution.py:28
  4.1 2.3 %collective-permute-done.2.refs_1_ = f32[128,128]{1,0:T(8,128)S(1)} collective-permute-done((f32[128,128]{1,0:T(8,128)S(1)}, f32[128,128]{1,0:T(8,128)S(1)}, u32[]{:S(2)}, u32[]{:S(2)}) %collective-permute-start.2) | collective-permute-done | bytes 65568 | tf_op jit(solution)/shard_map/ppermute | solution.py:24
  6.4 0.0 collective-permute-start.3
  6.4 1.3 %collective-permute-done.3.refs_1_ = f32[128,128]{1,0:T(8,128)S(1)} collective-permute-done((f32[128,128]{1,0:T(8,128)S(1)}, f32[128,128]{1,0:T(8,128)S(1)}, u32[]{:S(2)}, u32[]{:S(2)}) %collective-permute-start.3) | collective-permute-done | bytes 65568 | tf_op jit(solution)/shard_map/ppermute | solution.py:20
  7.7 0.0 collective-permute-done.1.refs_1_
  7.7 0.0 copy-done
  7.7 0.0 copy-done.1
  7.7 0.6 %shard_map.79 = (f32[16,2048]{1,0:T(8,128)S(1)}, f32[16,2048]{1,0:T(8,128)S(1)}) custom-call(f32[160,128]{1,0:T(8,128)S(1)} %shard_map.76.refs_0_, f32[160,128]{1,0:T(8,128)S(1)} %collective-permute-done.1.refs_1_, bf16[3,256,128]{2,1,0:T(8,128)(2,1)S(1)} %shard_map.74.refs_2_, bf16[256,256]{1,0:T(8,128)(2,1)S(1)} %shard_map.77.refs_3_, ...), custom_call_target="tpu_custom_call" | custom-call | flops 8388608 | bytes 1048576 | tf_op jit(solution)/shard_map/pallas_call | solution.py:32
  8.3 0.1 collective-permute-start.4
  8.4 1.1 %collective-permute-start.5 = (f32[16,2048]{1,0:T(8,128)S(1)}, f32[16,2048]{1,0:T(8,128)S(1)}, u32[]{:S(2)}, u32[]{:S(2)}) collective-permute-start(f32[16,2048]{1,0:T(8,128)S(1)} %get-tuple-element.15), channel_id=1, source_target_pairs={{0,28},{4,0},{8,4},{12,8},{16,12},{20,16},{24,20},{28,24},{1,29},{... | collective-permute-start | bytes 393224 | tf_op jit(solution)/shard_map/ppermute | solution.py:16
  9.6 1.8 %shard_map.80.diag_ref = f32[16,2048]{1,0:T(8,128)S(1)} custom-call(bf16[16,2048]{1,0:T(8,128)(2,1)S(1)} %get-tuple-element.16.xb_ref, bf16[4,512,512]{2,1,0:T(8,128)(2,1)} %leaf_hbm.1), custom_call_target="tpu_custom_call" | custom-call | flops 33554432 | bytes 2097152 | tf_op jit(solution)/shard_map/pallas_call | solution.py:32
  11.4 8.8 %collective-permute-done.4.half_ref = f32[16,2048]{1,0:T(8,128)S(1)} collective-permute-done((f32[16,2048]{1,0:T(8,128)S(1)}, f32[16,2048]{1,0:T(8,128)S(1)}, u32[]{:S(2)}, u32[]{:S(2)}) %collective-permute-start.4) | collective-permute-done | bytes 131104 | tf_op jit(solution)/shard_map/ppermute | solution.py:16
  20.2 0.0 collective-permute-done.5.below_ref
  20.2 0.7 %shard_map.81 = f32[16,2048]{1,0:T(8,128)} custom-call(f32[16,2048]{1,0:T(8,128)S(1)} %collective-permute-done.4.half_ref, f32[16,2048]{1,0:T(8,128)S(1)} %collective-permute-done.5.below_ref, f32[16,2048]{1,0:T(8,128)S(1)} %shard_map.80.diag_ref), custom_call_target="tpu_custom_call" | custom-call | flops 65536 | bytes 524288 | tf_op jit(solution)/shard_map/pallas_call | solution.py:32
  (4 shorter events, 0.1 us)
Async XLA Ops:
  0.0 7.7 %copy-start = (bf16[2,64,2048]{2,1,0:T(8,128)(2,1)S(1)}, bf16[2,64,2048]{2,1,0:T(8,128)(2,1)}, u32[]{:S(2)}) copy-start(bf16[2,64,2048]{2,1,0:T(8,128)(2,1)} %param.10) | copy-start | bytes 1572868
  0.0 7.7 %copy-start.1 = (s32[2,8]{1,0:T(2,128)S(1)}, s32[2,8]{1,0:T(2,128)}, u32[]{:S(2)}) copy-start(s32[2,8]{1,0:T(2,128)} %refs_6_.1) | copy-start | bytes 196
  1.7 1.7 %collective-permute-start = (f32[272,128]{1,0:T(8,128)S(1)}, f32[272,128]{1,0:T(8,128)S(1)}, u32[]{:S(2)}, u32[]{:S(2)}) collective-permute-start(f32[272,128]{1,0:T(8,128)S(1)} %get-tuple-element.11.refs_0_), channel_id=1, source_target_pairs={{0,1},{1,0},{2,3},{3,2},{4,5},{5,4},{6,7},{7,6},{8,9},{9,8},{10,11... | collective-permute-start | bytes 417800 | tf_op jit(solution)/shard_map/ppermute | solution.py:20
  2.4 4.0 %collective-permute-start.2 = (f32[128,128]{1,0:T(8,128)S(1)}, f32[128,128]{1,0:T(8,128)S(1)}, u32[]{:S(2)}, u32[]{:S(2)}) collective-permute-start(f32[128,128]{1,0:T(8,128)S(1)} %get-tuple-element.13), channel_id=1, source_target_pairs={{0,3},{1,2},{2,1},{3,0},{4,7},{5,6},{6,5},{7,4},{8,11},{9,10},{10,... | collective-permute-start | bytes 196616 | tf_op jit(solution)/shard_map/ppermute | solution.py:24
  3.6 4.1 %collective-permute-start.1 = (f32[160,128]{1,0:T(8,128)S(1)}, f32[160,128]{1,0:T(8,128)S(1)}, u32[]{:S(2)}, u32[]{:S(2)}) collective-permute-start(f32[160,128]{1,0:T(8,128)S(1)} %shard_map.76.refs_0_), channel_id=1, source_target_pairs={{0,2},{1,3},{2,0},{3,1},{4,6},{5,7},{6,4},{7,5},{8,10},{9,11},{10,... | collective-permute-start | bytes 245768 | tf_op jit(solution)/shard_map/ppermute | solution.py:28
  6.4 1.3 %collective-permute-start.3 = (f32[128,128]{1,0:T(8,128)S(1)}, f32[128,128]{1,0:T(8,128)S(1)}, u32[]{:S(2)}, u32[]{:S(2)}) collective-permute-start(f32[128,128]{1,0:T(8,128)S(1)} %collective-permute-done.2.refs_1_), channel_id=1, source_target_pairs={{0,1},{1,0},{2,3},{3,2},{4,5},{5,4},{6,7},{7,6},{8,9},{9,8},{10,11... | collective-permute-start | bytes 196616 | tf_op jit(solution)/shard_map/ppermute | solution.py:20
  8.3 11.9 %collective-permute-start.4 = (f32[16,2048]{1,0:T(8,128)S(1)}, f32[16,2048]{1,0:T(8,128)S(1)}, u32[]{:S(2)}, u32[]{:S(2)}) collective-permute-start(f32[16,2048]{1,0:T(8,128)S(1)} %get-tuple-element.14), channel_id=1, source_target_pairs={{0,16},{4,20},{8,24},{12,28},{16,0},{20,4},{24,8},{28,12},{1,17},{... | collective-permute-start | bytes 393224 | tf_op jit(solution)/shard_map/ppermute | solution.py:16
  8.4 11.8 %collective-permute-start.5 = (f32[16,2048]{1,0:T(8,128)S(1)}, f32[16,2048]{1,0:T(8,128)S(1)}, u32[]{:S(2)}, u32[]{:S(2)}) collective-permute-start(f32[16,2048]{1,0:T(8,128)S(1)} %get-tuple-element.15), channel_id=1, source_target_pairs={{0,28},{4,0},{8,4},{12,8},{16,12},{20,16},{24,20},{28,24},{1,29},{... | collective-permute-start | bytes 393224 | tf_op jit(solution)/shard_map/ppermute | solution.py:16

commit v18 on v17

--- a/solution.py
+++ b/solution.py
@@ -18,10 +18,6 @@
 
 def swapped(value):
     return lax.ppermute(value, "bf", [(n, n ^ 1) for n in range(lax.axis_size("bf"))])
-
-
-def crossed(value):
-    return lax.ppermute(value, "bf", [(n, n ^ 3) for n in range(lax.axis_size("bf"))])
 
 
 def across(value, bit):
@@ -107,24 +103,48 @@
         weights_ref[n] = section_weights(compact_refs[operand][start : start + size, :], levels)
 
 
-def build_pair_weights(levels, start, mine_ref, far_ref, weights_ref):
-    k = far_ref.shape[0] // 2
-    width = levels * k
-    for n, (ref, first) in enumerate(((mine_ref, start), (far_ref, 0))):
-        for side in range(2):
-            mats = block_diagonal(ref[first + side * k : first + (side + 1) * k, :], levels).astype(BF16)
-            row = (n + side) % 2 * width
-            weights_ref[row : row + width, n * width : (n + 1) * width] = mats
-
-
-def exact_dot(value, factor):
-    count = value.shape[0]
+def build_own(levels, chosen, *refs):
+    *operand_refs, weights_ref, compact_ref = refs
+    build_weights(levels, chosen, *operand_refs, weights_ref)
+    width = weights_ref.shape[2]
+    compact_ref[...] = compact_product(levels, weights_ref[1, width:, :], weights_ref[2, :width, :])
+
+
+def compact_product(levels, left, right):
+    k = left.shape[0] // levels
+    product = jnp.dot(left, right, preferred_element_type=F32)
+    return sum(product[level * k : (level + 1) * k] for level in range(levels))
+
+
+def three_terms(value):
     high = value.astype(BF16)
     rest = value - high.astype(F32)
     middle = rest.astype(BF16)
-    low = (rest - middle.astype(F32)).astype(BF16)
-    terms = jnp.dot(jnp.concatenate([high, middle, low], axis=0), factor, preferred_element_type=F32)
-    return terms[:count] + (terms[count : 2 * count] + terms[2 * count :])
+    return high, middle, (rest - middle.astype(F32)).astype(BF16)
+
+
+def factor_terms(levels, compact):
+    return three_terms(block_diagonal(compact, levels))
+
+
+def build_terms(levels, compact_ref, *refs):
+    *message_refs, terms_ref = refs
+    k, width = compact_ref.shape
+    parts = [compact_ref[...]] + [ref[-k:, :] for ref in message_refs]
+    for row, part in enumerate(parts):
+        for n, term in enumerate(factor_terms(levels, part)):
+            terms_ref[n, row * width : (row + 1) * width, :] = term
+
+
+def terms_dot(value, terms):
+    count = value.shape[0]
+    stacked = jnp.concatenate(three_terms(value), axis=0)
+    sums = sum(jnp.dot(stacked, term, preferred_element_type=F32) for term in reversed(terms))
+    return sums[:count] + (sums[count : 2 * count] + sums[2 * count :])
+
+
+def exact_dot(value, factor):
+    return terms_dot(value, [factor])
 
 
 def section_product(own, other, weights):
@@ -152,12 +172,17 @@
     run_sections(sections, final, (first_ref, second_ref), mine_ref, theirs_ref, out_ref)
 
 
-def first_step(size, sent_ref, received_ref, mine_ref, theirs_ref, kept_ref, out_ref):
-    count = (out_ref.shape[0] - size) // 2
+def first_step(levels, sent_ref, received_ref, mine_ref, theirs_ref, out_ref):
+    width = out_ref.shape[1]
+    k = width // levels
+    count = (out_ref.shape[0] - k) // 3
     mine, theirs = sent_ref[:count, :], received_ref[:count, :]
-    out_ref[:count, :] = section_product(mine, theirs, mine_ref[0])
-    out_ref[count : 2 * count, :] = section_product(theirs, mine, theirs_ref[0])
-    out_ref[2 * count :, :] = kept_ref[:size, :]
+    mine, theirs = section_product(mine, theirs, mine_ref[0]), section_product(theirs, mine, theirs_ref[0])
+    out_ref[:count, :] = mine
+    out_ref[count : 2 * count, :] = theirs
+    mine, theirs = exact_dot(mine, mine_ref[1, :width, :]), exact_dot(theirs, theirs_ref[1, :width, :])
+    out_ref[2 * count : 3 * count, :] = section_product(mine, theirs, mine_ref[2])
+    out_ref[3 * count :, :] = compact_product(levels, theirs_ref[1, width:, :], mine_ref[2, width:, :])
 
 
 def level_rank(state, rank_size, half_shift, owner_ref, half):
@@ -179,17 +204,15 @@
     finish(state, rank_size, half_shift, *refs)
 
 
-def last_sections(levels, rank_size, half_shift, pair_ref, other_ref, mine_ref, near_ref, cross_ref, *refs):
-    width = levels * rank_size
-    count = (pair_ref.shape[0] - 2 * rank_size) // 2
-    own, pair = [
-        exact_dot(jnp.concatenate([pair_ref[rows, :], other_ref[rows, :]], axis=1), weights_ref[...])
-        for rows, weights_ref in ((pl.ds(0, count), near_ref), (pl.ds(count, count), cross_ref))
-    ]
-    far_weights = section_weights(other_ref[2 * count :, :], levels)
-    mine = section_product(own[:, :width], pair[:, :width], mine_ref[1])
-    far = section_product(own[:, width:], pair[:, width:], far_weights)
-    finish(section_product(mine, far, mine_ref[2]), rank_size, half_shift, *refs)
+def last_sections(levels, rank_size, half_shift, here_ref, there_ref, mine_ref, terms_ref, far_ref, *refs):
+    count = (here_ref.shape[0] - rank_size) // 3
+    here = jnp.concatenate([here_ref[:count, :], here_ref[count : 2 * count, :]], axis=1)
+    there = jnp.concatenate([there_ref[:count, :], there_ref[count : 2 * count, :]], axis=1)
+    mine = here_ref[2 * count : 3 * count, :] + terms_dot(there, [terms_ref[n] for n in range(3)])
+    behind = factor_terms(levels, there_ref[3 * count :, :])
+    far_terms = [jnp.concatenate([far_ref[n], behind[n]], axis=0) for n in range(3)]
+    far = there_ref[2 * count : 3 * count, :] + terms_dot(here, far_terms)
+    finish(section_product(mine, far, mine_ref[3]), rank_size, half_shift, *refs)
 
 
 def diagonal(xb_ref, leaf_hbm, out_ref, leaf_ref, sems):
@@ -237,7 +260,7 @@
     ]
     size = 2 * rank_size
     one_round = bits == 2 and sections == 4 and levels == 2
-    groups_sent = [(0, 1), (1,), (2, 3)] if one_round else [tuple(range(sections - 1)), (sections - 1,)]
+    groups_sent = [(0, 1), (2, 3)] if one_round else [tuple(range(sections - 1)), (sections - 1,)]
     xb, sent, *kept = call(
         lambda *refs: load(groups_sent, *refs),
         [array(vectors, rows, kind=BF16)]
@@ -259,25 +282,30 @@
             [VMEM] * len(compacts), *weight_cost, *compacts,
         )
 
-    def pair_weights(start, mine, far):
+    def terms(*compacts):
         return call(
-            lambda *refs: build_pair_weights(levels, start, *refs), array(2 * width, 2 * width, kind=BF16),
-            [VMEM] * 2, *weight_cost, mine, far,
+            lambda *refs: build_terms(levels, *refs), array(3, len(compacts) * width, width, kind=BF16),
+            [VMEM] * len(compacts), *weight_cost, *compacts,
         )
 
     received = swapped(sent)
     step_cost = (24 * vectors * width * width, 8 * width * width)
     final = sections - 1
     if one_round:
-        cross = crossed(kept[0])
-        mine = weights([(0, vectors), (1, 0), (1, size)], sent, kept[1])
+        chosen = [(0, vectors), (0, vectors + size), (1, 0), (1, size)]
+        mine, factor = call(
+            lambda *refs: build_own(levels, chosen, *refs),
+            [array(sections, 2 * width, width, kind=BF16), array(rank_size, width)],
+            [VMEM] * 2, *weight_cost, sent, kept[0],
+        )
+        far_factor = across(factor, 1)
         states = call(
-            lambda *refs: first_step(size, *refs), array(2 * vectors + size, width), [VMEM] * 5, *step_cost,
-            sent, received, mine, weights([(0, vectors)], received), kept[1],
+            lambda *refs: first_step(levels, *refs), array(3 * vectors + rank_size, width), [VMEM] * 4, *step_cost,
+            sent, received, mine, weights(chosen[:2], received),
         )
         first_states = (states, across(states, 1))
         last_body = lambda *refs: last_sections(levels, *refs)
-        last_weights = (mine, pair_weights(vectors + size, sent, swapped(cross)), pair_weights(vectors + size, received, cross))
+        last_weights = (mine, terms(factor, states), terms(far_factor))
     else:
         starts = [(0, vectors + n * size) for n in range(final)]
         mine, theirs = weights(starts + [(1, 0)], sent, *kept), weights(starts, received)

time: 21.1 us -> 21.5 us (1.019)
  the two profiles are of different devices: /device:TPU:29 before, /device:TPU:24 now
where the time goes in v18:
time: 21.5 us; the launch traced here: 21.3 us
  waiting for transfers between devices  12 us (56%)
  Pallas kernels  5.31 us (25%)
  starting transfers between devices  3.94 us (18%)
    ppermute x2, waiting for transfers between devices, shifted(): lax.ppermute(value, axis, [(source, (source + distance) % size) for sourc...  7.37 us
    pallas_call x9, Pallas kernels, call(): pl.pallas_call(body, out_shape=shapes, in_specs=specs, out_specs=jax.tree...  5.31 us
    ppermute x2, waiting for transfers between devices, across(): lax.ppermute(value, 'bf', [(n, n ^ 1 << bit) for n in range(lax.axis_size...  3.42 us
    ppermute x2, starting transfers between devices, across(): lax.ppermute(value, 'bf', [(n, n ^ 1 << bit) for n in range(lax.axis_size...  2.09 us
    ppermute x2, starting transfers between devices, shifted(): lax.ppermute(value, axis, [(source, (source + distance) % size) for sourc...  1.77 us
    ppermute x1, waiting for transfers between devices, swapped(): lax.ppermute(value, 'bf', [(n, n ^ 1) for n in range(lax.axis_size('bf'))])  1.19 us
  transfers between devices with their start and end apart: 5, of which 3 were waited for; matrix products, arithmetic and copies ran while one was open for 0% of the time, Pallas kernels for 10%

profile of v18, /device:TPU:24, one launch (start us, length us, event | category | flops | bytes accessed | tf_op | source)
XLA Modules:
  0.0 21.3 jit_solution(16525721370941819434)
XLA Ops:
  0.0 0.0 copy-start
  0.0 0.0 copy-start.1
  0.0 1.6 %shard_map.73 = (bf16[16,2048]{1,0:T(8,128)(2,1)S(1)}, f32[272,128]{1,0:T(8,128)S(1)}, f32[256,128]{1,0:T(8,128)S(1)}) custom-call(f32[16,2048]{1,0:T(8,128)} %refs_0_.1, bf16[128,2048]{1,0:T(8,128)(2,1)} %bitcast.4, bf16[2,4,2,64,64]{4,3,2,1,0:T(8,128)(2,1)} %bitcast.5, s32[2,64]{1,0:T(2,128)} %refs_3_.1), custom_call_target="tpu_custom_call" | custom-call | flops 8388608 | bytes 786432 | tf_op jit(solution)/shard_map/pallas_call | solution.py:28
  1.7 0.1 collective-permute-start
  1.7 0.2 shard_map.74
  1.9 1.2 %collective-permute-done.refs_0_.refs_1_ = f32[272,128]{1,0:T(8,128)S(1)} collective-permute-done((f32[272,128]{1,0:T(8,128)S(1)}, f32[272,128]{1,0:T(8,128)S(1)}, u32[]{:S(2)}, u32[]{:S(2)}) %collective-permute-start) | collective-permute-done | bytes 139296 | tf_op jit(solution)/shard_map/ppermute | solution.py:20
  3.1 0.4 %shard_map.76.refs_1_.refs_0_ = f32[112,128]{1,0:T(8,128)S(1)} custom-call(f32[272,128]{1,0:T(8,128)S(1)} %get-tuple-element.12.refs_0_, f32[272,128]{1,0:T(8,128)S(1)} %collective-permute-done.refs_0_.refs_1_, bf16[4,256,128]{2,1,0:T(8,128)(2,1)S(1)} %get-tuple-element.14.refs_2_, bf16[2,256,128]{2,1,0:T(8,128)(2,1)S(1)} %shard_map.75.refs_3_), custom_call_target="tpu_custom_call" | custom-call | flops 6291456 | bytes 131072 | tf_op jit(solution)/shard_map/pallas_call | solution.py:28
  3.5 1.6 %collective-permute-start.1 = (f32[112,128]{1,0:T(8,128)S(1)}, f32[112,128]{1,0:T(8,128)S(1)}, u32[]{:S(2)}, u32[]{:S(2)}) collective-permute-start(f32[112,128]{1,0:T(8,128)S(1)} %shard_map.76.refs_1_.refs_0_), channel_id=1, source_target_pairs={{0,2},{1,3},{2,0},{3,1},{4,6},{5,7},{6,4},{7,5},{8,10},{9,11},{10,... | collective-permute-start | bytes 172040 | tf_op jit(solution)/shard_map/ppermute | solution.py:24
  5.1 0.5 %collective-permute-start.2 = (f32[64,128]{1,0:T(8,128)S(1)}, f32[64,128]{1,0:T(8,128)S(1)}, u32[]{:S(2)}, u32[]{:S(2)}) collective-permute-start(f32[64,128]{1,0:T(8,128)S(1)} %get-tuple-element.15.refs_0_), channel_id=1, source_target_pairs={{0,2},{1,3},{2,0},{3,1},{4,6},{5,7},{6,4},{7,5},{8,10},{9,11},{10,... | collective-permute-start | bytes 98312 | tf_op jit(solution)/shard_map/ppermute | solution.py:24
  5.6 3.4 %collective-permute-done.2.refs_0_ = f32[64,128]{1,0:T(8,128)S(1)} collective-permute-done((f32[64,128]{1,0:T(8,128)S(1)}, f32[64,128]{1,0:T(8,128)S(1)}, u32[]{:S(2)}, u32[]{:S(2)}) %collective-permute-start.2) | collective-permute-done | bytes 32800 | tf_op jit(solution)/shard_map/ppermute | solution.py:24
  9.1 0.0 collective-permute-done.1.refs_1_
  9.1 0.0 copy-done
  9.1 0.0 copy-done.1
  9.1 0.5 %shard_map.79 = (f32[16,2048]{1,0:T(8,128)S(1)}, f32[16,2048]{1,0:T(8,128)S(1)}) custom-call(f32[112,128]{1,0:T(8,128)S(1)} %shard_map.76.refs_1_.refs_0_, f32[112,128]{1,0:T(8,128)S(1)} %collective-permute-done.1.refs_1_, bf16[4,256,128]{2,1,0:T(8,128)(2,1)S(1)} %get-tuple-element.14.refs_2_, bf16[3,256,128]{2,1,0:T(8,128)(2,1)S(1)} %shard_map.77.refs_3_, ...), custom_call_target="tpu_custom_call" | custom-call | flops 8388608 | bytes 1048576 | tf_op jit(solution)/shard_map/pallas_call | solution.py:28
  9.6 0.4 %collective-permute-start.3 = (f32[16,2048]{1,0:T(8,128)S(1)}, f32[16,2048]{1,0:T(8,128)S(1)}, u32[]{:S(2)}, u32[]{:S(2)}) collective-permute-start(f32[16,2048]{1,0:T(8,128)S(1)} %get-tuple-element.16), channel_id=1, source_target_pairs={{0,16},{4,20},{8,24},{12,28},{16,0},{20,4},{24,8},{28,12},{1,17},{... | collective-permute-start | bytes 393224 | tf_op jit(solution)/shard_map/ppermute | solution.py:16
  10.0 1.4 %collective-permute-start.4 = (f32[16,2048]{1,0:T(8,128)S(1)}, f32[16,2048]{1,0:T(8,128)S(1)}, u32[]{:S(2)}, u32[]{:S(2)}) collective-permute-start(f32[16,2048]{1,0:T(8,128)S(1)} %get-tuple-element.17), channel_id=1, source_target_pairs={{0,28},{4,0},{8,4},{12,8},{16,12},{20,16},{24,20},{28,24},{1,29},{... | collective-permute-start | bytes 393224 | tf_op jit(solution)/shard_map/ppermute | solution.py:16
  11.4 1.8 %shard_map.80.diag_ref = f32[16,2048]{1,0:T(8,128)S(1)} custom-call(bf16[16,2048]{1,0:T(8,128)(2,1)S(1)} %get-tuple-element.18.xb_ref, bf16[4,512,512]{2,1,0:T(8,128)(2,1)} %leaf_hbm.1), custom_call_target="tpu_custom_call" | custom-call | flops 33554432 | bytes 2097152 | tf_op jit(solution)/shard_map/pallas_call | solution.py:28
  13.3 7.4 %collective-permute-done.3.half_ref = f32[16,2048]{1,0:T(8,128)S(1)} collective-permute-done((f32[16,2048]{1,0:T(8,128)S(1)}, f32[16,2048]{1,0:T(8,128)S(1)}, u32[]{:S(2)}, u32[]{:S(2)}) %collective-permute-start.3) | collective-permute-done | bytes 131104 | tf_op jit(solution)/shard_map/ppermute | solution.py:16
  20.6 0.0 collective-permute-done.4.below_ref
  20.6 0.7 %shard_map.81 = f32[16,2048]{1,0:T(8,128)} custom-call(f32[16,2048]{1,0:T(8,128)S(1)} %collective-permute-done.3.half_ref, f32[16,2048]{1,0:T(8,128)S(1)} %collective-permute-done.4.below_ref, f32[16,2048]{1,0:T(8,128)S(1)} %shard_map.80.diag_ref), custom_call_target="tpu_custom_call" | custom-call | flops 65536 | bytes 524288 | tf_op jit(solution)/shard_map/pallas_call | solution.py:28
  (3 shorter events, 0.1 us)
Async XLA Ops:
  0.0 9.1 %copy-start = (bf16[2,64,2048]{2,1,0:T(8,128)(2,1)S(1)}, bf16[2,64,2048]{2,1,0:T(8,128)(2,1)}, u32[]{:S(2)}) copy-start(bf16[2,64,2048]{2,1,0:T(8,128)(2,1)} %param.10) | copy-start | bytes 1572868
  0.0 9.1 %copy-start.1 = (s32[2,8]{1,0:T(2,128)S(1)}, s32[2,8]{1,0:T(2,128)}, u32[]{:S(2)}) copy-start(s32[2,8]{1,0:T(2,128)} %refs_6_.1) | copy-start | bytes 196
  1.7 1.4 %collective-permute-start = (f32[272,128]{1,0:T(8,128)S(1)}, f32[272,128]{1,0:T(8,128)S(1)}, u32[]{:S(2)}, u32[]{:S(2)}) collective-permute-start(f32[272,128]{1,0:T(8,128)S(1)} %get-tuple-element.12.refs_0_), channel_id=1, source_target_pairs={{0,1},{1,0},{2,3},{3,2},{4,5},{5,4},{6,7},{7,6},{8,9},{9,8},{10,11... | collective-permute-start | bytes 417800 | tf_op jit(solution)/shard_map/ppermute | solution.py:20
  3.5 5.6 %collective-permute-start.1 = (f32[112,128]{1,0:T(8,128)S(1)}, f32[112,128]{1,0:T(8,128)S(1)}, u32[]{:S(2)}, u32[]{:S(2)}) collective-permute-start(f32[112,128]{1,0:T(8,128)S(1)} %shard_map.76.refs_1_.refs_0_), channel_id=1, source_target_pairs={{0,2},{1,3},{2,0},{3,1},{4,6},{5,7},{6,4},{7,5},{8,10},{9,11},{10,... | collective-permute-start | bytes 172040 | tf_op jit(solution)/shard_map/ppermute | solution.py:24
  5.1 3.9 %collective-permute-start.2 = (f32[64,128]{1,0:T(8,128)S(1)}, f32[64,128]{1,0:T(8,128)S(1)}, u32[]{:S(2)}, u32[]{:S(2)}) collective-permute-start(f32[64,128]{1,0:T(8,128)S(1)} %get-tuple-element.15.refs_0_), channel_id=1, source_target_pairs={{0,2},{1,3},{2,0},{3,1},{4,6},{5,7},{6,4},{7,5},{8,10},{9,11},{10,... | collective-permute-start | bytes 98312 | tf_op jit(solution)/shard_map/ppermute | solution.py:24
  9.6 11.0 %collective-permute-start.3 = (f32[16,2048]{1,0:T(8,128)S(1)}, f32[16,2048]{1,0:T(8,128)S(1)}, u32[]{:S(2)}, u32[]{:S(2)}) collective-permute-start(f32[16,2048]{1,0:T(8,128)S(1)} %get-tuple-element.16), channel_id=1, source_target_pairs={{0,16},{4,20},{8,24},{12,28},{16,0},{20,4},{24,8},{28,12},{1,17},{... | collective-permute-start | bytes 393224 | tf_op jit(solution)/shard_map/ppermute | solution.py:16
  10.0 10.6 %collective-permute-start.4 = (f32[16,2048]{1,0:T(8,128)S(1)}, f32[16,2048]{1,0:T(8,128)S(1)}, u32[]{:S(2)}, u32[]{:S(2)}) collective-permute-start(f32[16,2048]{1,0:T(8,128)S(1)} %get-tuple-element.17), channel_id=1, source_target_pairs={{0,28},{4,0},{8,4},{12,8},{16,12},{20,16},{24,20},{28,24},{1,29},{... | collective-permute-start | bytes 393224 | tf_op jit(solution)/shard_map/ppermute | solution.py:16

commit v19 on v18

--- a/solution.py
+++ b/solution.py
@@ -65,6 +65,7 @@
 
 def load(groups, field_hbm, col_hbm, mixing_hbm, perm_hbm, xb_ref, sent_ref, *refs):
     *out_refs, field_ref, col_ref, mixing_ref, perm_ref, sems = refs
+    compact = {}
     levels, sections, _, k, _ = mixing_ref.shape
     vectors = field_ref.shape[0]
     first = [(perm_hbm, perm_ref)]
@@ -85,10 +86,14 @@
             if section == 0:
                 mats = jnp.dot(picks, block_diagonal(mats, levels).astype(BF16), preferred_element_type=F32)
                 mats = sum(mats[level * k : (level + 1) * k] for level in range(levels))
+            compact[section, side] = mats
             for n, (group, out_ref) in enumerate(zip(groups, (sent_ref, *out_refs))):
                 if section in group:
                     start = (0 if n else vectors) + (2 * group.index(section) + side) * k
                     out_ref[start : start + k, :] = mats
+    if len(out_refs) == len(groups):
+        left, right = [block_diagonal(compact[which], levels).astype(BF16) for which in ((1, 1), (2, 0))]
+        out_refs[-1][...] = compact_product(levels, left, right)
     for copy in copies[len(first) :]:
         copy.wait()
     xb = field_ref[...].astype(BF16)
@@ -101,13 +106,6 @@
     size = 2 * weights_ref.shape[2] // levels
     for n, (operand, start) in enumerate(chosen):
         weights_ref[n] = section_weights(compact_refs[operand][start : start + size, :], levels)
-
-
-def build_own(levels, chosen, *refs):
-    *operand_refs, weights_ref, compact_ref = refs
-    build_weights(levels, chosen, *operand_refs, weights_ref)
-    width = weights_ref.shape[2]
-    compact_ref[...] = compact_product(levels, weights_ref[1, width:, :], weights_ref[2, :width, :])
 
 
 def compact_product(levels, left, right):
@@ -264,7 +262,8 @@
     xb, sent, *kept = call(
         lambda *refs: load(groups_sent, *refs),
         [array(vectors, rows, kind=BF16)]
-        + [array(len(group) * size + (0 if n else vectors), width) for n, group in enumerate(groups_sent)],
+        + [array(len(group) * size + (0 if n else vectors), width) for n, group in enumerate(groups_sent)]
+        + [array(rank_size, width)] * one_round,
         [HBM] * 4, 2 * vectors * rows * width, 3 * rows * width, *in_hbm,
         scratch=[
             pltpu.VMEM(field.shape, F32),
@@ -282,10 +281,10 @@
             [VMEM] * len(compacts), *weight_cost, *compacts,
         )
 
-    def terms(*compacts):
+    def terms(*compacts, scale=1):
         return call(
             lambda *refs: build_terms(levels, *refs), array(3, len(compacts) * width, width, kind=BF16),
-            [VMEM] * len(compacts), *weight_cost, *compacts,
+            [VMEM] * len(compacts), *[scale * cost for cost in weight_cost], *compacts,
         )
 
     received = swapped(sent)
@@ -293,11 +292,7 @@
     final = sections - 1
     if one_round:
         chosen = [(0, vectors), (0, vectors + size), (1, 0), (1, size)]
-        mine, factor = call(
-            lambda *refs: build_own(levels, chosen, *refs),
-            [array(sections, 2 * width, width, kind=BF16), array(rank_size, width)],
-            [VMEM] * 2, *weight_cost, sent, kept[0],
-        )
+        mine, factor = weights(chosen, sent, kept[0]), kept[1]
         far_factor = across(factor, 1)
         states = call(
             lambda *refs: first_step(levels, *refs), array(3 * vectors + rank_size, width), [VMEM] * 4, *step_cost,
@@ -305,7 +300,7 @@
         )
         first_states = (states, across(states, 1))
         last_body = lambda *refs: last_sections(levels, *refs)
-        last_weights = (mine, terms(factor, states), terms(far_factor))
+        last_weights = (mine, terms(factor, states), terms(far_factor, scale=1000))
     else:
         starts = [(0, vectors + n * size) for n in range(final)]
         mine, theirs = weights(starts + [(1, 0)], sent, *kept), weights(starts, received)

time: 21.5 us -> 20.3 us (0.944)
  waiting for transfers between devices: 12 us -> 10.1 us
  starting transfers between devices: 3.94 us -> 4.73 us
    ppermute x1, waiting for transfers between devices: 1.19 us -> 0.01 us  [swapped(): lax.ppermute(value, 'bf', [(n, n ^ 1) for n in range(lax.axis_size('bf'))])]
    ppermute x2, starting transfers between devices: 2.09 us -> 2.88 us  [across(): lax.ppermute(value, 'bf', [(n, n ^ 1 << bit) for n in range(lax.axis_size...]
    ppermute x2, waiting for transfers between devices: 3.42 us -> 2.88 us  [across(): lax.ppermute(value, 'bf', [(n, n ^ 1 << bit) for n in range(lax.axis_size...]
  transfers between devices with their start and end apart: 5 -> 5, of which waited for: 3 -> 3; matrix products, arithmetic and copies ran while one was open for 0% -> 0% of each run, Pallas kernels for 10% -> 12%
where the time goes in v19:
time: 20.3 us; the launch traced here: 20.2 us
  waiting for transfers between devices  10.1 us (50%)
  Pallas kernels  5.22 us (26%)
  starting transfers between devices  4.73 us (23%)
    ppermute x2, waiting for transfers between devices, shifted(): lax.ppermute(value, axis, [(source, (source + distance) % size) for sourc...  7.26 us
    pallas_call x9, Pallas kernels, call(): pl.pallas_call(body, out_shape=shapes, in_specs=specs, out_specs=jax.tree...  5.22 us
    ppermute x2, starting transfers between devices, across(): lax.ppermute(value, 'bf', [(n, n ^ 1 << bit) for n in range(lax.axis_size...  2.88 us
    ppermute x2, waiting for transfers between devices, across(): lax.ppermute(value, 'bf', [(n, n ^ 1 << bit) for n in range(lax.axis_size...  2.88 us
    ppermute x2, starting transfers between devices, shifted(): lax.ppermute(value, axis, [(source, (source + distance) % size) for sourc...  1.77 us
  transfers between devices with their start and end apart: 5, of which 3 were waited for; matrix products, arithmetic and copies ran while one was open for 0% of the time, Pallas kernels for 12%

profile of v19, /device:TPU:24, one launch (start us, length us, event | category | flops | bytes accessed | tf_op | source)
XLA Modules:
  0.0 20.2 jit_solution(11950744407669037287)
XLA Ops:
  0.0 0.0 copy-start
  0.0 0.0 copy-start.1
  0.0 1.7 %shard_map.73 = (bf16[16,2048]{1,0:T(8,128)(2,1)S(1)}, f32[272,128]{1,0:T(8,128)S(1)}, f32[256,128]{1,0:T(8,128)S(1)}, f32[64,128]{1,0:T(8,128)S(1)}) custom-call(f32[16,2048]{1,0:T(8,128)} %refs_0_.1, bf16[128,2048]{1,0:T(8,128)(2,1)} %bitcast.4, bf16[2,4,2,64,64]{4,3,2,1,0:T(8,128)(2,1)} %bitcast.5, s32[2,64]{1,0:T(2,128)} %refs_3_.1), custom_call_target="tpu_custom_call" | custom-call | flops 8388608 | bytes 786432 | tf_op jit(solution)/shard_map/pallas_call | solution.py:28
  1.7 0.1 collective-permute-start
  1.8 1.6 %collective-permute-start.2 = (f32[64,128]{1,0:T(8,128)S(1)}, f32[64,128]{1,0:T(8,128)S(1)}, u32[]{:S(2)}, u32[]{:S(2)}) collective-permute-start(f32[64,128]{1,0:T(8,128)S(1)} %get-tuple-element.13.refs_0_), channel_id=1, source_target_pairs={{0,2},{1,3},{2,0},{3,1},{4,6},{5,7},{6,4},{7,5},{8,10},{9,11},{10,... | collective-permute-start | bytes 98312 | tf_op jit(solution)/shard_map/ppermute | solution.py:24
  3.4 0.0 collective-permute-done.refs_0_.refs_1_
  3.4 0.4 %shard_map.76.refs_1_.refs_0_ = f32[112,128]{1,0:T(8,128)S(1)} custom-call(f32[272,128]{1,0:T(8,128)S(1)} %get-tuple-element.11.refs_0_, f32[272,128]{1,0:T(8,128)S(1)} %collective-permute-done.refs_0_.refs_1_, bf16[4,256,128]{2,1,0:T(8,128)(2,1)S(1)} %shard_map.74.refs_2_, bf16[2,256,128]{2,1,0:T(8,128)(2,1)S(1)} %shard_map.75.refs_3_), custom_call_target="tpu_custom_call" | custom-call | flops 6291456 | bytes 131072 | tf_op jit(solution)/shard_map/pallas_call | solution.py:28
  3.8 1.3 %collective-permute-start.1 = (f32[112,128]{1,0:T(8,128)S(1)}, f32[112,128]{1,0:T(8,128)S(1)}, u32[]{:S(2)}, u32[]{:S(2)}) collective-permute-start(f32[112,128]{1,0:T(8,128)S(1)} %shard_map.76.refs_1_.refs_0_), channel_id=1, source_target_pairs={{0,2},{1,3},{2,0},{3,1},{4,6},{5,7},{6,4},{7,5},{8,10},{9,11},{10,... | collective-permute-start | bytes 172040 | tf_op jit(solution)/shard_map/ppermute | solution.py:24
  5.1 0.6 %collective-permute-done.2.refs_0_ = f32[64,128]{1,0:T(8,128)S(1)} collective-permute-done((f32[64,128]{1,0:T(8,128)S(1)}, f32[64,128]{1,0:T(8,128)S(1)}, u32[]{:S(2)}, u32[]{:S(2)}) %collective-permute-start.2) | collective-permute-done | bytes 32800 | tf_op jit(solution)/shard_map/ppermute | solution.py:24
  5.8 2.3 %collective-permute-done.1.refs_1_ = f32[112,128]{1,0:T(8,128)S(1)} collective-permute-done((f32[112,128]{1,0:T(8,128)S(1)}, f32[112,128]{1,0:T(8,128)S(1)}, u32[]{:S(2)}, u32[]{:S(2)}) %collective-permute-start.1) | collective-permute-done | bytes 57376 | tf_op jit(solution)/shard_map/ppermute | solution.py:24
  8.1 0.0 copy-done
  8.1 0.0 copy-done.1
  8.1 0.5 %shard_map.79 = (f32[16,2048]{1,0:T(8,128)S(1)}, f32[16,2048]{1,0:T(8,128)S(1)}) custom-call(f32[112,128]{1,0:T(8,128)S(1)} %shard_map.76.refs_1_.refs_0_, f32[112,128]{1,0:T(8,128)S(1)} %collective-permute-done.1.refs_1_, bf16[4,256,128]{2,1,0:T(8,128)(2,1)S(1)} %shard_map.74.refs_2_, bf16[3,256,128]{2,1,0:T(8,128)(2,1)S(1)} %shard_map.77.refs_3_, ...), custom_call_target="tpu_custom_call" | custom-call | flops 8388608 | bytes 1048576 | tf_op jit(solution)/shard_map/pallas_call | solution.py:28
  8.6 0.4 %collective-permute-start.3 = (f32[16,2048]{1,0:T(8,128)S(1)}, f32[16,2048]{1,0:T(8,128)S(1)}, u32[]{:S(2)}, u32[]{:S(2)}) collective-permute-start(f32[16,2048]{1,0:T(8,128)S(1)} %get-tuple-element.14), channel_id=1, source_target_pairs={{0,16},{4,20},{8,24},{12,28},{16,0},{20,4},{24,8},{28,12},{1,17},{... | collective-permute-start | bytes 393224 | tf_op jit(solution)/shard_map/ppermute | solution.py:16
  9.0 1.4 %collective-permute-start.4 = (f32[16,2048]{1,0:T(8,128)S(1)}, f32[16,2048]{1,0:T(8,128)S(1)}, u32[]{:S(2)}, u32[]{:S(2)}) collective-permute-start(f32[16,2048]{1,0:T(8,128)S(1)} %get-tuple-element.15), channel_id=1, source_target_pairs={{0,28},{4,0},{8,4},{12,8},{16,12},{20,16},{24,20},{28,24},{1,29},{... | collective-permute-start | bytes 393224 | tf_op jit(solution)/shard_map/ppermute | solution.py:16
  10.4 1.8 %shard_map.80.diag_ref = f32[16,2048]{1,0:T(8,128)S(1)} custom-call(bf16[16,2048]{1,0:T(8,128)(2,1)S(1)} %get-tuple-element.16.xb_ref, bf16[4,512,512]{2,1,0:T(8,128)(2,1)} %leaf_hbm.1), custom_call_target="tpu_custom_call" | custom-call | flops 33554432 | bytes 2097152 | tf_op jit(solution)/shard_map/pallas_call | solution.py:28
  12.2 7.3 %collective-permute-done.3.half_ref = f32[16,2048]{1,0:T(8,128)S(1)} collective-permute-done((f32[16,2048]{1,0:T(8,128)S(1)}, f32[16,2048]{1,0:T(8,128)S(1)}, u32[]{:S(2)}, u32[]{:S(2)}) %collective-permute-start.3) | collective-permute-done | bytes 131104 | tf_op jit(solution)/shard_map/ppermute | solution.py:16
  19.5 0.0 collective-permute-done.4.below_ref
  19.5 0.7 %shard_map.81 = f32[16,2048]{1,0:T(8,128)} custom-call(f32[16,2048]{1,0:T(8,128)S(1)} %collective-permute-done.3.half_ref, f32[16,2048]{1,0:T(8,128)S(1)} %collective-permute-done.4.below_ref, f32[16,2048]{1,0:T(8,128)S(1)} %shard_map.80.diag_ref), custom_call_target="tpu_custom_call" | custom-call | flops 65536 | bytes 524288 | tf_op jit(solution)/shard_map/pallas_call | solution.py:28
  (4 shorter events, 0.1 us)
Async XLA Ops:
  0.0 8.1 %copy-start = (bf16[2,64,2048]{2,1,0:T(8,128)(2,1)S(1)}, bf16[2,64,2048]{2,1,0:T(8,128)(2,1)}, u32[]{:S(2)}) copy-start(bf16[2,64,2048]{2,1,0:T(8,128)(2,1)} %param.10) | copy-start | bytes 1572868
  0.0 8.1 %copy-start.1 = (s32[2,8]{1,0:T(2,128)S(1)}, s32[2,8]{1,0:T(2,128)}, u32[]{:S(2)}) copy-start(s32[2,8]{1,0:T(2,128)} %refs_6_.1) | copy-start | bytes 196
  1.7 1.7 %collective-permute-start = (f32[272,128]{1,0:T(8,128)S(1)}, f32[272,128]{1,0:T(8,128)S(1)}, u32[]{:S(2)}, u32[]{:S(2)}) collective-permute-start(f32[272,128]{1,0:T(8,128)S(1)} %get-tuple-element.11.refs_0_), channel_id=1, source_target_pairs={{0,1},{1,0},{2,3},{3,2},{4,5},{5,4},{6,7},{7,6},{8,9},{9,8},{10,11... | collective-permute-start | bytes 417800 | tf_op jit(solution)/shard_map/ppermute | solution.py:20
  1.8 4.0 %collective-permute-start.2 = (f32[64,128]{1,0:T(8,128)S(1)}, f32[64,128]{1,0:T(8,128)S(1)}, u32[]{:S(2)}, u32[]{:S(2)}) collective-permute-start(f32[64,128]{1,0:T(8,128)S(1)} %get-tuple-element.13.refs_0_), channel_id=1, source_target_pairs={{0,2},{1,3},{2,0},{3,1},{4,6},{5,7},{6,4},{7,5},{8,10},{9,11},{10,... | collective-permute-start | bytes 98312 | tf_op jit(solution)/shard_map/ppermute | solution.py:24
  3.8 4.2 %collective-permute-start.1 = (f32[112,128]{1,0:T(8,128)S(1)}, f32[112,128]{1,0:T(8,128)S(1)}, u32[]{:S(2)}, u32[]{:S(2)}) collective-permute-start(f32[112,128]{1,0:T(8,128)S(1)} %shard_map.76.refs_1_.refs_0_), channel_id=1, source_target_pairs={{0,2},{1,3},{2,0},{3,1},{4,6},{5,7},{6,4},{7,5},{8,10},{9,11},{10,... | collective-permute-start | bytes 172040 | tf_op jit(solution)/shard_map/ppermute | solution.py:24
  8.6 10.9 %collective-permute-start.3 = (f32[16,2048]{1,0:T(8,128)S(1)}, f32[16,2048]{1,0:T(8,128)S(1)}, u32[]{:S(2)}, u32[]{:S(2)}) collective-permute-start(f32[16,2048]{1,0:T(8,128)S(1)} %get-tuple-element.14), channel_id=1, source_target_pairs={{0,16},{4,20},{8,24},{12,28},{16,0},{20,4},{24,8},{28,12},{1,17},{... | collective-permute-start | bytes 393224 | tf_op jit(solution)/shard_map/ppermute | solution.py:16
  9.0 10.5 %collective-permute-start.4 = (f32[16,2048]{1,0:T(8,128)S(1)}, f32[16,2048]{1,0:T(8,128)S(1)}, u32[]{:S(2)}, u32[]{:S(2)}) collective-permute-start(f32[16,2048]{1,0:T(8,128)S(1)} %get-tuple-element.15), channel_id=1, source_target_pairs={{0,28},{4,0},{8,4},{12,8},{16,12},{20,16},{24,20},{28,24},{1,29},{... | collective-permute-start | bytes 393224 | tf_op jit(solution)/shard_map/ppermute | solution.py:16

commit v20 on v19

--- a/solution.py
+++ b/solution.py
@@ -68,15 +68,17 @@
     compact = {}
     levels, sections, _, k, _ = mixing_ref.shape
     vectors = field_ref.shape[0]
-    first = [(perm_hbm, perm_ref)]
-    first += [(mixing_hbm.at[level], mixing_ref.at[level]) for level in range(levels)]
-    second = split(field_hbm, field_ref, 2, 0)
-    third = split(col_hbm, col_ref, 4, 0)
-    copies = [pltpu.make_async_copy(*pair, sems.at[n]) for n, pair in enumerate(first + second + third)]
+    pairs = split(col_hbm, col_ref, 4, 0) + split(field_hbm, field_ref, 2, 0)
+    pairs += [(mixing_hbm.at[level], mixing_ref.at[level]) for level in range(levels)]
+    pairs.append((perm_hbm, perm_ref))
+    copies = [pltpu.make_async_copy(*pair, sems.at[n]) for n, pair in enumerate(pairs)]
     for copy in copies:
         copy.start()
-    for copy in copies[: len(first)]:
+    for copy in copies:
         copy.wait()
+    xb = field_ref[...].astype(BF16)
+    xb_ref[...] = xb
+    sent_ref[:vectors, :] = lax.dot_general(xb, col_ref[...], NT, preferred_element_type=F32)
     row = lax.broadcasted_iota(jnp.int32, (k, k), 0)
     picks = jnp.concatenate([(row == perm_ref[level : level + 1, :]).astype(F32) for level in range(levels)], axis=1)
     picks = block_diagonal(picks, levels).astype(BF16)
@@ -94,11 +96,6 @@
     if len(out_refs) == len(groups):
         left, right = [block_diagonal(compact[which], levels).astype(BF16) for which in ((1, 1), (2, 0))]
         out_refs[-1][...] = compact_product(levels, left, right)
-    for copy in copies[len(first) :]:
-        copy.wait()
-    xb = field_ref[...].astype(BF16)
-    xb_ref[...] = xb
-    sent_ref[:vectors, :] = lax.dot_general(xb, col_ref[...], NT, preferred_element_type=F32)
 
 
 def build_weights(levels, chosen, *refs):

time: 20.3 us -> 20.3 us (level)
  no operation moved by 1% of the time
where the time goes in v20:
time: 20.3 us; the launch traced here: 20.2 us
  waiting for transfers between devices  10.1 us (50%)
  Pallas kernels  5.21 us (26%)
  starting transfers between devices  4.73 us (23%)
    ppermute x2, waiting for transfers between devices, shifted(): lax.ppermute(value, axis, [(source, (source + distance) % size) for sourc...  7.26 us
    pallas_call x9, Pallas kernels, call(): pl.pallas_call(body, out_shape=shapes, in_specs=specs, out_specs=jax.tree...  5.21 us
    ppermute x2, starting transfers between devices, across(): lax.ppermute(value, 'bf', [(n, n ^ 1 << bit) for n in range(lax.axis_size...  2.88 us
    ppermute x2, waiting for transfers between devices, across(): lax.ppermute(value, 'bf', [(n, n ^ 1 << bit) for n in range(lax.axis_size...  2.88 us
    ppermute x2, starting transfers between devices, shifted(): lax.ppermute(value, axis, [(source, (source + distance) % size) for sourc...  1.77 us
  transfers between devices with their start and end apart: 5, of which 3 were waited for; matrix products, arithmetic and copies ran while one was open for 0% of the time, Pallas kernels for 12%

profile of v20, /device:TPU:24, one launch (start us, length us, event | category | flops | bytes accessed | tf_op | source)
XLA Modules:
  0.0 20.2 jit_solution(8120856031043468410)
XLA Ops:
  0.0 0.0 copy-start
  0.0 0.0 copy-start.1
  0.0 1.7 %shard_map.73 = (bf16[16,2048]{1,0:T(8,128)(2,1)S(1)}, f32[272,128]{1,0:T(8,128)S(1)}, f32[256,128]{1,0:T(8,128)S(1)}, f32[64,128]{1,0:T(8,128)S(1)}) custom-call(f32[16,2048]{1,0:T(8,128)} %refs_0_.1, bf16[128,2048]{1,0:T(8,128)(2,1)} %bitcast.4, bf16[2,4,2,64,64]{4,3,2,1,0:T(8,128)(2,1)} %bitcast.5, s32[2,64]{1,0:T(2,128)} %refs_3_.1), custom_call_target="tpu_custom_call" | custom-call | flops 8388608 | bytes 786432 | tf_op jit(solution)/shard_map/pallas_call | solution.py:28
  1.7 0.1 collective-permute-start
  1.8 1.6 %collective-permute-start.2 = (f32[64,128]{1,0:T(8,128)S(1)}, f32[64,128]{1,0:T(8,128)S(1)}, u32[]{:S(2)}, u32[]{:S(2)}) collective-permute-start(f32[64,128]{1,0:T(8,128)S(1)} %get-tuple-element.13.refs_0_), channel_id=1, source_target_pairs={{0,2},{1,3},{2,0},{3,1},{4,6},{5,7},{6,4},{7,5},{8,10},{9,11},{10,... | collective-permute-start | bytes 98312 | tf_op jit(solution)/shard_map/ppermute | solution.py:24
  3.4 0.0 collective-permute-done.refs_0_.refs_1_
  3.4 0.4 %shard_map.76.refs_1_.refs_0_ = f32[112,128]{1,0:T(8,128)S(1)} custom-call(f32[272,128]{1,0:T(8,128)S(1)} %get-tuple-element.11.refs_0_, f32[272,128]{1,0:T(8,128)S(1)} %collective-permute-done.refs_0_.refs_1_, bf16[4,256,128]{2,1,0:T(8,128)(2,1)S(1)} %shard_map.74.refs_2_, bf16[2,256,128]{2,1,0:T(8,128)(2,1)S(1)} %shard_map.75.refs_3_), custom_call_target="tpu_custom_call" | custom-call | flops 6291456 | bytes 131072 | tf_op jit(solution)/shard_map/pallas_call | solution.py:28
  3.8 1.3 %collective-permute-start.1 = (f32[112,128]{1,0:T(8,128)S(1)}, f32[112,128]{1,0:T(8,128)S(1)}, u32[]{:S(2)}, u32[]{:S(2)}) collective-permute-start(f32[112,128]{1,0:T(8,128)S(1)} %shard_map.76.refs_1_.refs_0_), channel_id=1, source_target_pairs={{0,2},{1,3},{2,0},{3,1},{4,6},{5,7},{6,4},{7,5},{8,10},{9,11},{10,... | collective-permute-start | bytes 172040 | tf_op jit(solution)/shard_map/ppermute | solution.py:24
  5.1 0.6 %collective-permute-done.2.refs_0_ = f32[64,128]{1,0:T(8,128)S(1)} collective-permute-done((f32[64,128]{1,0:T(8,128)S(1)}, f32[64,128]{1,0:T(8,128)S(1)}, u32[]{:S(2)}, u32[]{:S(2)}) %collective-permute-start.2) | collective-permute-done | bytes 32800 | tf_op jit(solution)/shard_map/ppermute | solution.py:24
  5.8 2.3 %collective-permute-done.1.refs_1_ = f32[112,128]{1,0:T(8,128)S(1)} collective-permute-done((f32[112,128]{1,0:T(8,128)S(1)}, f32[112,128]{1,0:T(8,128)S(1)}, u32[]{:S(2)}, u32[]{:S(2)}) %collective-permute-start.1) | collective-permute-done | bytes 57376 | tf_op jit(solution)/shard_map/ppermute | solution.py:24
  8.1 0.0 copy-done
  8.1 0.0 copy-done.1
  8.1 0.5 %shard_map.79 = (f32[16,2048]{1,0:T(8,128)S(1)}, f32[16,2048]{1,0:T(8,128)S(1)}) custom-call(f32[112,128]{1,0:T(8,128)S(1)} %shard_map.76.refs_1_.refs_0_, f32[112,128]{1,0:T(8,128)S(1)} %collective-permute-done.1.refs_1_, bf16[4,256,128]{2,1,0:T(8,128)(2,1)S(1)} %shard_map.74.refs_2_, bf16[3,256,128]{2,1,0:T(8,128)(2,1)S(1)} %shard_map.77.refs_3_, ...), custom_call_target="tpu_custom_call" | custom-call | flops 8388608 | bytes 1048576 | tf_op jit(solution)/shard_map/pallas_call | solution.py:28
  8.6 0.4 %collective-permute-start.3 = (f32[16,2048]{1,0:T(8,128)S(1)}, f32[16,2048]{1,0:T(8,128)S(1)}, u32[]{:S(2)}, u32[]{:S(2)}) collective-permute-start(f32[16,2048]{1,0:T(8,128)S(1)} %get-tuple-element.14), channel_id=1, source_target_pairs={{0,16},{4,20},{8,24},{12,28},{16,0},{20,4},{24,8},{28,12},{1,17},{... | collective-permute-start | bytes 393224 | tf_op jit(solution)/shard_map/ppermute | solution.py:16
  9.0 1.4 %collective-permute-start.4 = (f32[16,2048]{1,0:T(8,128)S(1)}, f32[16,2048]{1,0:T(8,128)S(1)}, u32[]{:S(2)}, u32[]{:S(2)}) collective-permute-start(f32[16,2048]{1,0:T(8,128)S(1)} %get-tuple-element.15), channel_id=1, source_target_pairs={{0,28},{4,0},{8,4},{12,8},{16,12},{20,16},{24,20},{28,24},{1,29},{... | collective-permute-start | bytes 393224 | tf_op jit(solution)/shard_map/ppermute | solution.py:16
  10.4 1.8 %shard_map.80.diag_ref = f32[16,2048]{1,0:T(8,128)S(1)} custom-call(bf16[16,2048]{1,0:T(8,128)(2,1)S(1)} %get-tuple-element.16.xb_ref, bf16[4,512,512]{2,1,0:T(8,128)(2,1)} %leaf_hbm.1), custom_call_target="tpu_custom_call" | custom-call | flops 33554432 | bytes 2097152 | tf_op jit(solution)/shard_map/pallas_call | solution.py:28
  12.2 7.3 %collective-permute-done.3.half_ref = f32[16,2048]{1,0:T(8,128)S(1)} collective-permute-done((f32[16,2048]{1,0:T(8,128)S(1)}, f32[16,2048]{1,0:T(8,128)S(1)}, u32[]{:S(2)}, u32[]{:S(2)}) %collective-permute-start.3) | collective-permute-done | bytes 131104 | tf_op jit(solution)/shard_map/ppermute | solution.py:16
  19.5 0.0 collective-permute-done.4.below_ref
  19.5 0.7 %shard_map.81 = f32[16,2048]{1,0:T(8,128)} custom-call(f32[16,2048]{1,0:T(8,128)S(1)} %collective-permute-done.3.half_ref, f32[16,2048]{1,0:T(8,128)S(1)} %collective-permute-done.4.below_ref, f32[16,2048]{1,0:T(8,128)S(1)} %shard_map.80.diag_ref), custom_call_target="tpu_custom_call" | custom-call | flops 65536 | bytes 524288 | tf_op jit(solution)/shard_map/pallas_call | solution.py:28
  (4 shorter events, 0.1 us)
Async XLA Ops:
  0.0 8.1 %copy-start = (bf16[2,64,2048]{2,1,0:T(8,128)(2,1)S(1)}, bf16[2,64,2048]{2,1,0:T(8,128)(2,1)}, u32[]{:S(2)}) copy-start(bf16[2,64,2048]{2,1,0:T(8,128)(2,1)} %param.10) | copy-start | bytes 1572868
  0.0 8.1 %copy-start.1 = (s32[2,8]{1,0:T(2,128)S(1)}, s32[2,8]{1,0:T(2,128)}, u32[]{:S(2)}) copy-start(s32[2,8]{1,0:T(2,128)} %refs_6_.1) | copy-start | bytes 196
  1.7 1.7 %collective-permute-start = (f32[272,128]{1,0:T(8,128)S(1)}, f32[272,128]{1,0:T(8,128)S(1)}, u32[]{:S(2)}, u32[]{:S(2)}) collective-permute-start(f32[272,128]{1,0:T(8,128)S(1)} %get-tuple-element.11.refs_0_), channel_id=1, source_target_pairs={{0,1},{1,0},{2,3},{3,2},{4,5},{5,4},{6,7},{7,6},{8,9},{9,8},{10,11... | collective-permute-start | bytes 417800 | tf_op jit(solution)/shard_map/ppermute | solution.py:20
  1.8 4.0 %collective-permute-start.2 = (f32[64,128]{1,0:T(8,128)S(1)}, f32[64,128]{1,0:T(8,128)S(1)}, u32[]{:S(2)}, u32[]{:S(2)}) collective-permute-start(f32[64,128]{1,0:T(8,128)S(1)} %get-tuple-element.13.refs_0_), channel_id=1, source_target_pairs={{0,2},{1,3},{2,0},{3,1},{4,6},{5,7},{6,4},{7,5},{8,10},{9,11},{10,... | collective-permute-start | bytes 98312 | tf_op jit(solution)/shard_map/ppermute | solution.py:24
  3.8 4.2 %collective-permute-start.1 = (f32[112,128]{1,0:T(8,128)S(1)}, f32[112,128]{1,0:T(8,128)S(1)}, u32[]{:S(2)}, u32[]{:S(2)}) collective-permute-start(f32[112,128]{1,0:T(8,128)S(1)} %shard_map.76.refs_1_.refs_0_), channel_id=1, source_target_pairs={{0,2},{1,3},{2,0},{3,1},{4,6},{5,7},{6,4},{7,5},{8,10},{9,11},{10,... | collective-permute-start | bytes 172040 | tf_op jit(solution)/shard_map/ppermute | solution.py:24
  8.6 10.9 %collective-permute-start.3 = (f32[16,2048]{1,0:T(8,128)S(1)}, f32[16,2048]{1,0:T(8,128)S(1)}, u32[]{:S(2)}, u32[]{:S(2)}) collective-permute-start(f32[16,2048]{1,0:T(8,128)S(1)} %get-tuple-element.14), channel_id=1, source_target_pairs={{0,16},{4,20},{8,24},{12,28},{16,0},{20,4},{24,8},{28,12},{1,17},{... | collective-permute-start | bytes 393224 | tf_op jit(solution)/shard_map/ppermute | solution.py:16
  9.0 10.5 %collective-permute-start.4 = (f32[16,2048]{1,0:T(8,128)S(1)}, f32[16,2048]{1,0:T(8,128)S(1)}, u32[]{:S(2)}, u32[]{:S(2)}) collective-permute-start(f32[16,2048]{1,0:T(8,128)S(1)} %get-tuple-element.15), channel_id=1, source_target_pairs={{0,28},{4,0},{8,4},{12,8},{16,12},{20,16},{24,20},{28,24},{1,29},{... | collective-permute-start | bytes 393224 | tf_op jit(solution)/shard_map/ppermute | solution.py:16

commit v21 on v20

--- a/solution.py
+++ b/solution.py
@@ -78,7 +78,7 @@
         copy.wait()
     xb = field_ref[...].astype(BF16)
     xb_ref[...] = xb
-    sent_ref[:vectors, :] = lax.dot_general(xb, col_ref[...], NT, preferred_element_type=F32)
+    sent_ref[:vectors, :] = lax.dot_general(col_ref[...], xb, NT, preferred_element_type=F32).T
     row = lax.broadcasted_iota(jnp.int32, (k, k), 0)
     picks = jnp.concatenate([(row == perm_ref[level : level + 1, :]).astype(F32) for level in range(levels)], axis=1)
     picks = block_diagonal(picks, levels).astype(BF16)

time: 20.3 us -> 20.4 us (level)
  no operation moved by 1% of the time
where the time goes in v21:
time: 20.4 us; the launch traced here: 20.2 us
  waiting for transfers between devices  10.1 us (50%)
  Pallas kernels  5.27 us (26%)
  starting transfers between devices  4.72 us (23%)
    ppermute x2, waiting for transfers between devices, shifted(): lax.ppermute(value, axis, [(source, (source + distance) % size) for sourc...  7.27 us
    pallas_call x9, Pallas kernels, call(): pl.pallas_call(body, out_shape=shapes, in_specs=specs, out_specs=jax.tree...  5.27 us
    ppermute x2, waiting for transfers between devices, across(): lax.ppermute(value, 'bf', [(n, n ^ 1 << bit) for n in range(lax.axis_size...  2.88 us
    ppermute x2, starting transfers between devices, across(): lax.ppermute(value, 'bf', [(n, n ^ 1 << bit) for n in range(lax.axis_size...  2.88 us
    ppermute x2, starting transfers between devices, shifted(): lax.ppermute(value, axis, [(source, (source + distance) % size) for sourc...  1.77 us
  transfers between devices with their start and end apart: 5, of which 3 were waited for; matrix products, arithmetic and copies ran while one was open for 0% of the time, Pallas kernels for 12%

profile of v21, /device:TPU:24, one launch (start us, length us, event | category | flops | bytes accessed | tf_op | source)
XLA Modules:
  0.0 20.2 jit_solution(4083310854485245000)
XLA Ops:
  0.0 0.0 copy-start
  0.0 0.0 copy-start.1
  0.0 1.7 %shard_map.73 = (bf16[16,2048]{1,0:T(8,128)(2,1)S(1)}, f32[272,128]{1,0:T(8,128)S(1)}, f32[256,128]{1,0:T(8,128)S(1)}, f32[64,128]{1,0:T(8,128)S(1)}) custom-call(f32[16,2048]{1,0:T(8,128)} %refs_0_.1, bf16[128,2048]{1,0:T(8,128)(2,1)} %bitcast.4, bf16[2,4,2,64,64]{4,3,2,1,0:T(8,128)(2,1)} %bitcast.5, s32[2,64]{1,0:T(2,128)} %refs_3_.1), custom_call_target="tpu_custom_call" | custom-call | flops 8388608 | bytes 786432 | tf_op jit(solution)/shard_map/pallas_call | solution.py:28
  1.7 0.1 collective-permute-start
  1.8 1.6 %collective-permute-start.2 = (f32[64,128]{1,0:T(8,128)S(1)}, f32[64,128]{1,0:T(8,128)S(1)}, u32[]{:S(2)}, u32[]{:S(2)}) collective-permute-start(f32[64,128]{1,0:T(8,128)S(1)} %get-tuple-element.13.refs_0_), channel_id=1, source_target_pairs={{0,2},{1,3},{2,0},{3,1},{4,6},{5,7},{6,4},{7,5},{8,10},{9,11},{10,... | collective-permute-start | bytes 98312 | tf_op jit(solution)/shard_map/ppermute | solution.py:24
  3.4 0.0 collective-permute-done.refs_0_.refs_1_
  3.5 0.4 %shard_map.76.refs_1_.refs_0_ = f32[112,128]{1,0:T(8,128)S(1)} custom-call(f32[272,128]{1,0:T(8,128)S(1)} %get-tuple-element.11.refs_0_, f32[272,128]{1,0:T(8,128)S(1)} %collective-permute-done.refs_0_.refs_1_, bf16[4,256,128]{2,1,0:T(8,128)(2,1)S(1)} %shard_map.74.refs_2_, bf16[2,256,128]{2,1,0:T(8,128)(2,1)S(1)} %shard_map.75.refs_3_), custom_call_target="tpu_custom_call" | custom-call | flops 6291456 | bytes 131072 | tf_op jit(solution)/shard_map/pallas_call | solution.py:28
  3.9 1.3 %collective-permute-start.1 = (f32[112,128]{1,0:T(8,128)S(1)}, f32[112,128]{1,0:T(8,128)S(1)}, u32[]{:S(2)}, u32[]{:S(2)}) collective-permute-start(f32[112,128]{1,0:T(8,128)S(1)} %shard_map.76.refs_1_.refs_0_), channel_id=1, source_target_pairs={{0,2},{1,3},{2,0},{3,1},{4,6},{5,7},{6,4},{7,5},{8,10},{9,11},{10,... | collective-permute-start | bytes 172040 | tf_op jit(solution)/shard_map/ppermute | solution.py:24
  5.2 0.6 %collective-permute-done.2.refs_0_ = f32[64,128]{1,0:T(8,128)S(1)} collective-permute-done((f32[64,128]{1,0:T(8,128)S(1)}, f32[64,128]{1,0:T(8,128)S(1)}, u32[]{:S(2)}, u32[]{:S(2)}) %collective-permute-start.2) | collective-permute-done | bytes 32800 | tf_op jit(solution)/shard_map/ppermute | solution.py:24
  5.9 2.2 %collective-permute-done.1.refs_1_ = f32[112,128]{1,0:T(8,128)S(1)} collective-permute-done((f32[112,128]{1,0:T(8,128)S(1)}, f32[112,128]{1,0:T(8,128)S(1)}, u32[]{:S(2)}, u32[]{:S(2)}) %collective-permute-start.1) | collective-permute-done | bytes 57376 | tf_op jit(solution)/shard_map/ppermute | solution.py:24
  8.1 0.0 copy-done
  8.1 0.0 copy-done.1
  8.1 0.5 %shard_map.79 = (f32[16,2048]{1,0:T(8,128)S(1)}, f32[16,2048]{1,0:T(8,128)S(1)}) custom-call(f32[112,128]{1,0:T(8,128)S(1)} %shard_map.76.refs_1_.refs_0_, f32[112,128]{1,0:T(8,128)S(1)} %collective-permute-done.1.refs_1_, bf16[4,256,128]{2,1,0:T(8,128)(2,1)S(1)} %shard_map.74.refs_2_, bf16[3,256,128]{2,1,0:T(8,128)(2,1)S(1)} %shard_map.77.refs_3_, ...), custom_call_target="tpu_custom_call" | custom-call | flops 8388608 | bytes 1048576 | tf_op jit(solution)/shard_map/pallas_call | solution.py:28
  8.6 0.4 %collective-permute-start.3 = (f32[16,2048]{1,0:T(8,128)S(1)}, f32[16,2048]{1,0:T(8,128)S(1)}, u32[]{:S(2)}, u32[]{:S(2)}) collective-permute-start(f32[16,2048]{1,0:T(8,128)S(1)} %get-tuple-element.14), channel_id=1, source_target_pairs={{0,16},{4,20},{8,24},{12,28},{16,0},{20,4},{24,8},{28,12},{1,17},{... | collective-permute-start | bytes 393224 | tf_op jit(solution)/shard_map/ppermute | solution.py:16
  9.0 1.4 %collective-permute-start.4 = (f32[16,2048]{1,0:T(8,128)S(1)}, f32[16,2048]{1,0:T(8,128)S(1)}, u32[]{:S(2)}, u32[]{:S(2)}) collective-permute-start(f32[16,2048]{1,0:T(8,128)S(1)} %get-tuple-element.15), channel_id=1, source_target_pairs={{0,28},{4,0},{8,4},{12,8},{16,12},{20,16},{24,20},{28,24},{1,29},{... | collective-permute-start | bytes 393224 | tf_op jit(solution)/shard_map/ppermute | solution.py:16
  10.4 1.8 %shard_map.80.diag_ref = f32[16,2048]{1,0:T(8,128)S(1)} custom-call(bf16[16,2048]{1,0:T(8,128)(2,1)S(1)} %get-tuple-element.16.xb_ref, bf16[4,512,512]{2,1,0:T(8,128)(2,1)} %leaf_hbm.1), custom_call_target="tpu_custom_call" | custom-call | flops 33554432 | bytes 2097152 | tf_op jit(solution)/shard_map/pallas_call | solution.py:28
  12.3 7.3 %collective-permute-done.3.half_ref = f32[16,2048]{1,0:T(8,128)S(1)} collective-permute-done((f32[16,2048]{1,0:T(8,128)S(1)}, f32[16,2048]{1,0:T(8,128)S(1)}, u32[]{:S(2)}, u32[]{:S(2)}) %collective-permute-start.3) | collective-permute-done | bytes 131104 | tf_op jit(solution)/shard_map/ppermute | solution.py:16
  19.5 0.0 collective-permute-done.4.below_ref
  19.5 0.7 %shard_map.81 = f32[16,2048]{1,0:T(8,128)} custom-call(f32[16,2048]{1,0:T(8,128)S(1)} %collective-permute-done.3.half_ref, f32[16,2048]{1,0:T(8,128)S(1)} %collective-permute-done.4.below_ref, f32[16,2048]{1,0:T(8,128)S(1)} %shard_map.80.diag_ref), custom_call_target="tpu_custom_call" | custom-call | flops 65536 | bytes 524288 | tf_op jit(solution)/shard_map/pallas_call | solution.py:28
  (4 shorter events, 0.1 us)
Async XLA Ops:
  0.0 8.1 %copy-start = (bf16[2,64,2048]{2,1,0:T(8,128)(2,1)S(1)}, bf16[2,64,2048]{2,1,0:T(8,128)(2,1)}, u32[]{:S(2)}) copy-start(bf16[2,64,2048]{2,1,0:T(8,128)(2,1)} %param.10) | copy-start | bytes 1572868
  0.0 8.1 %copy-start.1 = (s32[2,8]{1,0:T(2,128)S(1)}, s32[2,8]{1,0:T(2,128)}, u32[]{:S(2)}) copy-start(s32[2,8]{1,0:T(2,128)} %refs_6_.1) | copy-start | bytes 196
  1.7 1.7 %collective-permute-start = (f32[272,128]{1,0:T(8,128)S(1)}, f32[272,128]{1,0:T(8,128)S(1)}, u32[]{:S(2)}, u32[]{:S(2)}) collective-permute-start(f32[272,128]{1,0:T(8,128)S(1)} %get-tuple-element.11.refs_0_), channel_id=1, source_target_pairs={{0,1},{1,0},{2,3},{3,2},{4,5},{5,4},{6,7},{7,6},{8,9},{9,8},{10,11... | collective-permute-start | bytes 417800 | tf_op jit(solution)/shard_map/ppermute | solution.py:20
  1.8 4.0 %collective-permute-start.2 = (f32[64,128]{1,0:T(8,128)S(1)}, f32[64,128]{1,0:T(8,128)S(1)}, u32[]{:S(2)}, u32[]{:S(2)}) collective-permute-start(f32[64,128]{1,0:T(8,128)S(1)} %get-tuple-element.13.refs_0_), channel_id=1, source_target_pairs={{0,2},{1,3},{2,0},{3,1},{4,6},{5,7},{6,4},{7,5},{8,10},{9,11},{10,... | collective-permute-start | bytes 98312 | tf_op jit(solution)/shard_map/ppermute | solution.py:24
  3.9 4.2 %collective-permute-start.1 = (f32[112,128]{1,0:T(8,128)S(1)}, f32[112,128]{1,0:T(8,128)S(1)}, u32[]{:S(2)}, u32[]{:S(2)}) collective-permute-start(f32[112,128]{1,0:T(8,128)S(1)} %shard_map.76.refs_1_.refs_0_), channel_id=1, source_target_pairs={{0,2},{1,3},{2,0},{3,1},{4,6},{5,7},{6,4},{7,5},{8,10},{9,11},{10,... | collective-permute-start | bytes 172040 | tf_op jit(solution)/shard_map/ppermute | solution.py:24
  8.6 10.9 %collective-permute-start.3 = (f32[16,2048]{1,0:T(8,128)S(1)}, f32[16,2048]{1,0:T(8,128)S(1)}, u32[]{:S(2)}, u32[]{:S(2)}) collective-permute-start(f32[16,2048]{1,0:T(8,128)S(1)} %get-tuple-element.14), channel_id=1, source_target_pairs={{0,16},{4,20},{8,24},{12,28},{16,0},{20,4},{24,8},{28,12},{1,17},{... | collective-permute-start | bytes 393224 | tf_op jit(solution)/shard_map/ppermute | solution.py:16
  9.0 10.5 %collective-permute-start.4 = (f32[16,2048]{1,0:T(8,128)S(1)}, f32[16,2048]{1,0:T(8,128)S(1)}, u32[]{:S(2)}, u32[]{:S(2)}) collective-permute-start(f32[16,2048]{1,0:T(8,128)S(1)} %get-tuple-element.15), channel_id=1, source_target_pairs={{0,28},{4,0},{8,4},{12,8},{16,12},{20,16},{24,20},{28,24},{1,29},{... | collective-permute-start | bytes 393224 | tf_op jit(solution)/shard_map/ppermute | solution.py:16

commit v22 on v20

--- a/solution.py
+++ b/solution.py
@@ -14,6 +14,23 @@
 def shifted(value, axis, distance):
     size = lax.axis_size(axis)
     return lax.ppermute(value, axis, [(source, (source + distance) % size) for source in range(size)])
+
+
+def swapped_groups(value):
+    return lax.ppermute(value, "grp", [(g, g ^ 1) for g in range(lax.axis_size("grp"))])
+
+
+def rest_below(value):
+    size, places = lax.axis_size("grp"), lax.axis_size("bf")
+    pairs = []
+    for g in range(size):
+        for b in range(places):
+            if b % 2:
+                target = ((g - 2) % size, b) if g % 2 else (g, b ^ 2)
+            else:
+                target = (g ^ 1, b) if g % 2 else ((g - 1) % size, b)
+            pairs.append((g * places + b, target[0] * places + target[1]))
+    return lax.ppermute(value, ("grp", "bf"), pairs)
 
 
 def swapped(value):
@@ -224,13 +241,19 @@
         out_ref[:, part] = jnp.dot(xb_ref[:, part], leaf_ref[n], preferred_element_type=F32)
 
 
-def combine(half_ref, below_ref, diag_ref, out_hbm, sum_ref, sems):
+def arrived(half_ref, out_ref):
+    out_ref[...] = half_ref[: out_ref.shape[0], : out_ref.shape[1]]
+
+
+def combine(half_ref, near_ref, rest_ref, diag_ref, _, out_hbm, sum_ref, sems):
     parts = sems.shape[0]
     count = sum_ref.shape[1] // parts
+    odd = jnp.broadcast_to(lax.rem(lax.axis_index("grp"), 2), (sum_ref.shape[0], count)) == 1
     copies = []
     for n in range(parts):
         part = pl.ds(n * count, count)
-        sum_ref[:, part] = diag_ref[:, part] + below_ref[:, part] + half_ref[:, part]
+        below = jnp.where(odd, rest_ref[:, part], near_ref[:, part])
+        sum_ref[:, part] = diag_ref[:, part] + below + half_ref[:, part]
         copies.append(pltpu.make_async_copy(sum_ref.at[:, part], out_hbm.at[:, part], sems.at[n]))
         copies[-1].start()
     for copy in copies:
@@ -323,14 +346,16 @@
         [VMEM] * (4 + len(last_weights)), *expand_cost, *first_states, *last_weights, expand, row_owner,
     )
     out_half = shifted(out_half, "grp", groups // 2)
-    out_below = shifted(out_below, "grp", groups - 1)
+    near = swapped_groups(out_below)
+    rest = rest_below(jnp.where(lax.axis_index("bf") % 2 == 1, near, out_below))
     diag = call(
         diagonal, array(vectors, rows), [VMEM, HBM], 2 * vectors * rows * order, 2 * rows * order,
         xb, pltpu.with_memory_space_constraint(leaf_inverse, pltpu.HBM),
         scratch=[pltpu.VMEM(leaf_inverse.shape, BF16), pltpu.SemaphoreType.DMA((2 * leaf_inverse.shape[0],))],
     )
+    token = call(arrived, array(8, 128), [VMEM], *[1000 * cost for cost in weight_cost], out_half)
     return call(
-        combine, array(vectors, rows), [VMEM] * 3, 2 * vectors * rows, 16 * vectors * rows, out_half, out_below, diag,
+        combine, array(vectors, rows), [VMEM] * 5, 2 * vectors * rows, 16 * vectors * rows, out_half, near, rest, diag, token,
         scratch=[pltpu.VMEM((vectors, rows), F32), pltpu.SemaphoreType.DMA((4,))], out=HBM,
     )
 

time: 20.3 us -> 23 us (1.13)
  the two profiles are of different devices: /device:TPU:24 before, /device:TPU:0 now
where the time goes in v22:
time: 23 us; the launch traced here: 22.9 us
  starting transfers between devices  13.1 us (57%)
  Pallas kernels  5.22 us (23%)
  waiting for transfers between devices  4.43 us (19%)
    pallas_call x10, Pallas kernels, call(): pl.pallas_call(body, out_shape=shapes, in_specs=specs, out_specs=jax.tree...  5.22 us
    ppermute x1, starting transfers between devices, rest_below(): return lax.ppermute(value, ('grp', 'bf'), pairs)  4.58 us
    ppermute x2, starting transfers between devices, across(): lax.ppermute(value, 'bf', [(n, n ^ 1 << bit) for n in range(lax.axis_size...  3.89 us
    ppermute x2, waiting for transfers between devices, across(): lax.ppermute(value, 'bf', [(n, n ^ 1 << bit) for n in range(lax.axis_size...  2.88 us
    ppermute x1, starting transfers between devices, shifted(): lax.ppermute(value, axis, [(source, (source + distance) % size) for sourc...  2.58 us
    ppermute x1, starting transfers between devices, swapped_groups(): lax.ppermute(value, 'grp', [(g, g ^ 1) for g in range(lax.axis_size('grp'...  1.56 us
    ppermute x1, waiting for transfers between devices, swapped_groups(): lax.ppermute(value, 'grp', [(g, g ^ 1) for g in range(lax.axis_size('grp'...  0.89 us
    ppermute x1, waiting for transfers between devices, rest_below(): return lax.ppermute(value, ('grp', 'bf'), pairs)  0.65 us
  transfers between devices with their start and end apart: 6, of which 4 were waited for; matrix products, arithmetic and copies ran while one was open for 0% of the time, Pallas kernels for 10%

profile of v22, /device:TPU:0, one launch (start us, length us, event | category | flops | bytes accessed | tf_op | source)
XLA Modules:
  0.0 22.9 jit_solution(7462983371854881970)
XLA Ops:
  0.0 0.0 copy-start
  0.0 0.0 copy-start.1
  0.0 1.7 %shard_map.73 = (bf16[16,2048]{1,0:T(8,128)(2,1)S(1)}, f32[272,128]{1,0:T(8,128)S(1)}, f32[256,128]{1,0:T(8,128)S(1)}, f32[64,128]{1,0:T(8,128)S(1)}) custom-call(f32[16,2048]{1,0:T(8,128)} %refs_0_.1, bf16[128,2048]{1,0:T(8,128)(2,1)} %bitcast.4, bf16[2,4,2,64,64]{4,3,2,1,0:T(8,128)(2,1)} %bitcast.5, s32[2,64]{1,0:T(2,128)} %refs_3_.1), custom_call_target="tpu_custom_call" | custom-call | flops 8388608 | bytes 786432 | tf_op jit(solution)/shard_map/pallas_call | solution.py:45
  1.7 0.5 %collective-permute-start = (f32[272,128]{1,0:T(8,128)S(1)}, f32[272,128]{1,0:T(8,128)S(1)}, u32[]{:S(2)}, u32[]{:S(2)}) collective-permute-start(f32[272,128]{1,0:T(8,128)S(1)} %get-tuple-element.11.refs_0_), channel_id=1, source_target_pairs={{0,1},{1,0},{2,3},{3,2},{4,5},{5,4},{6,7},{7,6},{8,9},{9,8},{10,11... | collective-permute-start | bytes 417800 | tf_op jit(solution)/shard_map/ppermute | solution.py:37
  2.2 2.6 %collective-permute-start.2 = (f32[64,128]{1,0:T(8,128)S(1)}, f32[64,128]{1,0:T(8,128)S(1)}, u32[]{:S(2)}, u32[]{:S(2)}) collective-permute-start(f32[64,128]{1,0:T(8,128)S(1)} %get-tuple-element.13.refs_0_), channel_id=1, source_target_pairs={{0,2},{1,3},{2,0},{3,1},{4,6},{5,7},{6,4},{7,5},{8,10},{9,11},{10,... | collective-permute-start | bytes 98312 | tf_op jit(solution)/shard_map/ppermute | solution.py:41
  4.8 0.0 collective-permute-done.refs_0_.refs_1_
  4.9 0.4 %shard_map.76.refs_1_.refs_0_ = f32[112,128]{1,0:T(8,128)S(1)} custom-call(f32[272,128]{1,0:T(8,128)S(1)} %get-tuple-element.11.refs_0_, f32[272,128]{1,0:T(8,128)S(1)} %collective-permute-done.refs_0_.refs_1_, bf16[4,256,128]{2,1,0:T(8,128)(2,1)S(1)} %shard_map.74.refs_2_, bf16[2,256,128]{2,1,0:T(8,128)(2,1)S(1)} %shard_map.75.refs_3_), custom_call_target="tpu_custom_call" | custom-call | flops 6291456 | bytes 131072 | tf_op jit(solution)/shard_map/pallas_call | solution.py:45
  5.3 1.3 %collective-permute-start.1 = (f32[112,128]{1,0:T(8,128)S(1)}, f32[112,128]{1,0:T(8,128)S(1)}, u32[]{:S(2)}, u32[]{:S(2)}) collective-permute-start(f32[112,128]{1,0:T(8,128)S(1)} %shard_map.76.refs_1_.refs_0_), channel_id=1, source_target_pairs={{0,2},{1,3},{2,0},{3,1},{4,6},{5,7},{6,4},{7,5},{8,10},{9,11},{10,... | collective-permute-start | bytes 172040 | tf_op jit(solution)/shard_map/ppermute | solution.py:41
  6.6 0.2 collective-permute-done.2.refs_0_
  6.8 2.7 %collective-permute-done.1.refs_1_ = f32[112,128]{1,0:T(8,128)S(1)} collective-permute-done((f32[112,128]{1,0:T(8,128)S(1)}, f32[112,128]{1,0:T(8,128)S(1)}, u32[]{:S(2)}, u32[]{:S(2)}) %collective-permute-start.1) | collective-permute-done | bytes 57376 | tf_op jit(solution)/shard_map/ppermute | solution.py:41
  9.5 0.0 copy-done
  9.5 0.0 copy-done.1
  9.5 0.5 %shard_map.79 = (f32[16,2048]{1,0:T(8,128)S(1)}, f32[16,2048]{1,0:T(8,128)S(1)}) custom-call(f32[112,128]{1,0:T(8,128)S(1)} %shard_map.76.refs_1_.refs_0_, f32[112,128]{1,0:T(8,128)S(1)} %collective-permute-done.1.refs_1_, bf16[4,256,128]{2,1,0:T(8,128)(2,1)S(1)} %shard_map.74.refs_2_, bf16[3,256,128]{2,1,0:T(8,128)(2,1)S(1)} %shard_map.77.refs_3_, ...), custom_call_target="tpu_custom_call" | custom-call | flops 8388608 | bytes 1048576 | tf_op jit(solution)/shard_map/pallas_call | solution.py:45
  10.0 1.6 %collective-permute-start.4 = (f32[16,2048]{1,0:T(8,128)S(1)}, f32[16,2048]{1,0:T(8,128)S(1)}, u32[]{:S(2)}, u32[]{:S(2)}) collective-permute-start(f32[16,2048]{1,0:T(8,128)S(1)} %get-tuple-element.15), channel_id=1, source_target_pairs={{0,4},{4,0},{8,12},{12,8},{16,20},{20,16},{24,28},{28,24},{1,5},{5... | collective-permute-start | bytes 393224 | tf_op jit(solution)/shard_map/ppermute | solution.py:20
  11.6 2.6 %collective-permute-start.3 = (f32[16,2048]{1,0:T(8,128)S(1)}, f32[16,2048]{1,0:T(8,128)S(1)}, u32[]{:S(2)}, u32[]{:S(2)}) collective-permute-start(f32[16,2048]{1,0:T(8,128)S(1)} %get-tuple-element.14), channel_id=1, source_target_pairs={{0,16},{4,20},{8,24},{12,28},{16,0},{20,4},{24,8},{28,12},{1,17},{... | collective-permute-start | bytes 393224 | tf_op jit(solution)/shard_map/ppermute | solution.py:16
  14.2 0.9 %collective-permute-done.4.near_ref = f32[16,2048]{1,0:T(8,128)S(1)} collective-permute-done((f32[16,2048]{1,0:T(8,128)S(1)}, f32[16,2048]{1,0:T(8,128)S(1)}, u32[]{:S(2)}, u32[]{:S(2)}) %collective-permute-start.4) | collective-permute-done | bytes 131104 | tf_op jit(solution)/shard_map/ppermute | solution.py:20
  15.1 4.6 %collective-permute-start.5 = (f32[16,2048]{1,0:T(8,128)S(1)}, f32[16,2048]{1,0:T(8,128)S(1)}, u32[]{:S(2)}, u32[]{:S(2)}) collective-permute-start(f32[16,2048]{1,0:T(8,128)S(1)} %broadcast_select_fusion), channel_id=1, source_target_pairs={{0,28},{1,3},{2,30},{3,1},{4,0},{5,29},{6,2},{7,31},{8,4},{9,11},{... | collective-permute-start | bytes 393224 | tf_op jit(solution)/shard_map/ppermute | solution.py:33
  19.7 1.8 %shard_map.80.diag_ref = f32[16,2048]{1,0:T(8,128)S(1)} custom-call(bf16[16,2048]{1,0:T(8,128)(2,1)S(1)} %get-tuple-element.16.xb_ref, bf16[4,512,512]{2,1,0:T(8,128)(2,1)} %leaf_hbm.1), custom_call_target="tpu_custom_call" | custom-call | flops 33554432 | bytes 2097152 | tf_op jit(solution)/shard_map/pallas_call | solution.py:45
  21.5 0.0 collective-permute-done.3.half_ref
  21.5 0.7 %collective-permute-done.5.rest_ref = f32[16,2048]{1,0:T(8,128)S(1)} collective-permute-done((f32[16,2048]{1,0:T(8,128)S(1)}, f32[16,2048]{1,0:T(8,128)S(1)}, u32[]{:S(2)}, u32[]{:S(2)}) %collective-permute-start.5) | collective-permute-done | bytes 131104 | tf_op jit(solution)/shard_map/ppermute | solution.py:33
  22.2 0.7 %shard_map.82 = f32[16,2048]{1,0:T(8,128)} custom-call(f32[16,2048]{1,0:T(8,128)S(1)} %collective-permute-done.3.half_ref, f32[16,2048]{1,0:T(8,128)S(1)} %collective-permute-done.4.near_ref, f32[16,2048]{1,0:T(8,128)S(1)} %collective-permute-done.5.rest_ref, f32[16,2048]{1,0:T(8,128)S(1)} %shard_map.80.diag_ref, f32[8,128]{1,0:T(8,128)S(1)} %shard_map.81._), custom_call_target="tpu_custom_call" | custom-call | flops 65536 | bytes 524288 | tf_op jit(solution)/shard_map/pallas_call | solution.py:45
  (6 shorter events, 0.1 us)
Async XLA Ops:
  0.0 9.5 %copy-start = (bf16[2,64,2048]{2,1,0:T(8,128)(2,1)S(1)}, bf16[2,64,2048]{2,1,0:T(8,128)(2,1)}, u32[]{:S(2)}) copy-start(bf16[2,64,2048]{2,1,0:T(8,128)(2,1)} %param.10) | copy-start | bytes 1572868
  0.0 9.5 %copy-start.1 = (s32[2,8]{1,0:T(2,128)S(1)}, s32[2,8]{1,0:T(2,128)}, u32[]{:S(2)}) copy-start(s32[2,8]{1,0:T(2,128)} %refs_6_.1) | copy-start | bytes 196
  1.7 3.1 %collective-permute-start = (f32[272,128]{1,0:T(8,128)S(1)}, f32[272,128]{1,0:T(8,128)S(1)}, u32[]{:S(2)}, u32[]{:S(2)}) collective-permute-start(f32[272,128]{1,0:T(8,128)S(1)} %get-tuple-element.11.refs_0_), channel_id=1, source_target_pairs={{0,1},{1,0},{2,3},{3,2},{4,5},{5,4},{6,7},{7,6},{8,9},{9,8},{10,11... | collective-permute-start | bytes 417800 | tf_op jit(solution)/shard_map/ppermute | solution.py:37
  2.2 4.6 %collective-permute-start.2 = (f32[64,128]{1,0:T(8,128)S(1)}, f32[64,128]{1,0:T(8,128)S(1)}, u32[]{:S(2)}, u32[]{:S(2)}) collective-permute-start(f32[64,128]{1,0:T(8,128)S(1)} %get-tuple-element.13.refs_0_), channel_id=1, source_target_pairs={{0,2},{1,3},{2,0},{3,1},{4,6},{5,7},{6,4},{7,5},{8,10},{9,11},{10,... | collective-permute-start | bytes 98312 | tf_op jit(solution)/shard_map/ppermute | solution.py:41
  5.3 4.2 %collective-permute-start.1 = (f32[112,128]{1,0:T(8,128)S(1)}, f32[112,128]{1,0:T(8,128)S(1)}, u32[]{:S(2)}, u32[]{:S(2)}) collective-permute-start(f32[112,128]{1,0:T(8,128)S(1)} %shard_map.76.refs_1_.refs_0_), channel_id=1, source_target_pairs={{0,2},{1,3},{2,0},{3,1},{4,6},{5,7},{6,4},{7,5},{8,10},{9,11},{10,... | collective-permute-start | bytes 172040 | tf_op jit(solution)/shard_map/ppermute | solution.py:41
  10.0 5.0 %collective-permute-start.4 = (f32[16,2048]{1,0:T(8,128)S(1)}, f32[16,2048]{1,0:T(8,128)S(1)}, u32[]{:S(2)}, u32[]{:S(2)}) collective-permute-start(f32[16,2048]{1,0:T(8,128)S(1)} %get-tuple-element.15), channel_id=1, source_target_pairs={{0,4},{4,0},{8,12},{12,8},{16,20},{20,16},{24,28},{28,24},{1,5},{5... | collective-permute-start | bytes 393224 | tf_op jit(solution)/shard_map/ppermute | solution.py:20
  11.6 9.9 %collective-permute-start.3 = (f32[16,2048]{1,0:T(8,128)S(1)}, f32[16,2048]{1,0:T(8,128)S(1)}, u32[]{:S(2)}, u32[]{:S(2)}) collective-permute-start(f32[16,2048]{1,0:T(8,128)S(1)} %get-tuple-element.14), channel_id=1, source_target_pairs={{0,16},{4,20},{8,24},{12,28},{16,0},{20,4},{24,8},{28,12},{1,17},{... | collective-permute-start | bytes 393224 | tf_op jit(solution)/shard_map/ppermute | solution.py:16
  15.1 7.1 %collective-permute-start.5 = (f32[16,2048]{1,0:T(8,128)S(1)}, f32[16,2048]{1,0:T(8,128)S(1)}, u32[]{:S(2)}, u32[]{:S(2)}) collective-permute-start(f32[16,2048]{1,0:T(8,128)S(1)} %broadcast_select_fusion), channel_id=1, source_target_pairs={{0,28},{1,3},{2,30},{3,1},{4,0},{5,29},{6,2},{7,31},{8,4},{9,11},{... | collective-permute-start | bytes 393224 | tf_op jit(solution)/shard_map/ppermute | solution.py:33

commit v23 on v22

--- a/solution.py
+++ b/solution.py
@@ -20,15 +20,17 @@
     return lax.ppermute(value, "grp", [(g, g ^ 1) for g in range(lax.axis_size("grp"))])
 
 
-def rest_below(value):
+def below_from_even(value, step, parity):
     size, places = lax.axis_size("grp"), lax.axis_size("bf")
     pairs = []
     for g in range(size):
         for b in range(places):
-            if b % 2:
-                target = ((g - 2) % size, b) if g % 2 else (g, b ^ 2)
+            if b % 2 != parity:
+                target = (g, b ^ 2)
+            elif g % 2 == step - 1:
+                target = ((g - step) % size, b)
             else:
-                target = (g ^ 1, b) if g % 2 else ((g - 1) % size, b)
+                target = (g ^ 1, b) if step == 1 else (g, b ^ 2)
             pairs.append((g * places + b, target[0] * places + target[1]))
     return lax.ppermute(value, ("grp", "bf"), pairs)
 
@@ -245,14 +247,17 @@
     out_ref[...] = half_ref[: out_ref.shape[0], : out_ref.shape[1]]
 
 
-def combine(half_ref, near_ref, rest_ref, diag_ref, _, out_hbm, sum_ref, sems):
+def combine(half_ref, near_ref, straight_ref, onward_ref, diag_ref, _, out_hbm, sum_ref, sems):
     parts = sems.shape[0]
     count = sum_ref.shape[1] // parts
-    odd = jnp.broadcast_to(lax.rem(lax.axis_index("grp"), 2), (sum_ref.shape[0], count)) == 1
+    shape = (sum_ref.shape[0], count)
+    odd = jnp.broadcast_to(lax.rem(lax.axis_index("grp"), 2), shape) == 1
+    first = jnp.broadcast_to(lax.rem(lax.axis_index("bf"), 2), shape) == 0
     copies = []
     for n in range(parts):
         part = pl.ds(n * count, count)
-        below = jnp.where(odd, rest_ref[:, part], near_ref[:, part])
+        rest = jnp.where(first, straight_ref[:, part], onward_ref[:, part])
+        below = jnp.where(odd, rest, near_ref[:, part])
         sum_ref[:, part] = diag_ref[:, part] + below + half_ref[:, part]
         copies.append(pltpu.make_async_copy(sum_ref.at[:, part], out_hbm.at[:, part], sems.at[n]))
         copies[-1].start()
@@ -347,7 +352,8 @@
     )
     out_half = shifted(out_half, "grp", groups // 2)
     near = swapped_groups(out_below)
-    rest = rest_below(jnp.where(lax.axis_index("bf") % 2 == 1, near, out_below))
+    straight = below_from_even(out_below, 1, 0)
+    onward = below_from_even(near, 2, 1)
     diag = call(
         diagonal, array(vectors, rows), [VMEM, HBM], 2 * vectors * rows * order, 2 * rows * order,
         xb, pltpu.with_memory_space_constraint(leaf_inverse, pltpu.HBM),
@@ -355,7 +361,7 @@
     )
     token = call(arrived, array(8, 128), [VMEM], *[1000 * cost for cost in weight_cost], out_half)
     return call(
-        combine, array(vectors, rows), [VMEM] * 5, 2 * vectors * rows, 16 * vectors * rows, out_half, near, rest, diag, token,
+        combine, array(vectors, rows), [VMEM] * 6, 2 * vectors * rows, 16 * vectors * rows, out_half, near, straight, onward, diag, token,
         scratch=[pltpu.VMEM((vectors, rows), F32), pltpu.SemaphoreType.DMA((4,))], out=HBM,
     )
 

time: 23 us -> 21.3 us (0.926)
  starting transfers between devices: 13.1 us -> 11.1 us
  waiting for transfers between devices: 4.43 us -> 4.77 us
    ppermute x1 -> x2, starting transfers between devices: 4.58 us -> 2.55 us  [below_from_even(): return lax.ppermute(value, ('grp', 'bf'), pairs)]
    ppermute x1, waiting for transfers between devices: 0.01 us -> 0.96 us  [shifted(): lax.ppermute(value, axis, [(source, (source + distance) % size) for sourc...]
    ppermute x1, waiting for transfers between devices: 0.89 us -> 0.01 us  [swapped_groups(): lax.ppermute(value, 'grp', [(g, g ^ 1) for g in range(lax.axis_size('grp'...]
    ppermute x1 -> x2, waiting for transfers between devices: 0.65 us -> 0.93 us  [below_from_even(): return lax.ppermute(value, ('grp', 'bf'), pairs)]
  transfers between devices with their start and end apart: 6 -> 7, of which waited for: 4 -> 4; matrix products, arithmetic and copies ran while one was open for 0% -> 0% of each run, Pallas kernels for 10% -> 11%
where the time goes in v23:
time: 21.3 us; the launch traced here: 21.2 us
  starting transfers between devices  11.1 us (52%)
  Pallas kernels  5.22 us (25%)
  waiting for transfers between devices  4.77 us (22%)
    pallas_call x10, Pallas kernels, call(): pl.pallas_call(body, out_shape=shapes, in_specs=specs, out_specs=jax.tree...  5.22 us
    ppermute x2, starting transfers between devices, across(): lax.ppermute(value, 'bf', [(n, n ^ 1 << bit) for n in range(lax.axis_size...  3.89 us
    ppermute x2, waiting for transfers between devices, across(): lax.ppermute(value, 'bf', [(n, n ^ 1 << bit) for n in range(lax.axis_size...  2.88 us
    ppermute x1, starting transfers between devices, shifted(): lax.ppermute(value, axis, [(source, (source + distance) % size) for sourc...  2.58 us
    ppermute x2, starting transfers between devices, below_from_even(): return lax.ppermute(value, ('grp', 'bf'), pairs)  2.55 us
    ppermute x1, starting transfers between devices, swapped_groups(): lax.ppermute(value, 'grp', [(g, g ^ 1) for g in range(lax.axis_size('grp'...  1.56 us
    ppermute x1, waiting for transfers between devices, shifted(): lax.ppermute(value, axis, [(source, (source + distance) % size) for sourc...  0.96 us
    ppermute x2, waiting for transfers between devices, below_from_even(): return lax.ppermute(value, ('grp', 'bf'), pairs)  0.93 us
  transfers between devices with their start and end apart: 7, of which 4 were waited for; matrix products, arithmetic and copies ran while one was open for 0% of the time, Pallas kernels for 11%

profile of v23, /device:TPU:0, one launch (start us, length us, event | category | flops | bytes accessed | tf_op | source)
XLA Modules:
  0.0 21.2 jit_solution(1814508195981140258)
XLA Ops:
  0.0 0.0 copy-start
  0.0 0.0 copy-start.1
  0.0 1.7 %shard_map.73 = (bf16[16,2048]{1,0:T(8,128)(2,1)S(1)}, f32[272,128]{1,0:T(8,128)S(1)}, f32[256,128]{1,0:T(8,128)S(1)}, f32[64,128]{1,0:T(8,128)S(1)}) custom-call(f32[16,2048]{1,0:T(8,128)} %refs_0_.1, bf16[128,2048]{1,0:T(8,128)(2,1)} %bitcast.4, bf16[2,4,2,64,64]{4,3,2,1,0:T(8,128)(2,1)} %bitcast.5, s32[2,64]{1,0:T(2,128)} %refs_3_.1), custom_call_target="tpu_custom_call" | custom-call | flops 8388608 | bytes 786432 | tf_op jit(solution)/shard_map/pallas_call | solution.py:47
  1.7 0.5 %collective-permute-start = (f32[272,128]{1,0:T(8,128)S(1)}, f32[272,128]{1,0:T(8,128)S(1)}, u32[]{:S(2)}, u32[]{:S(2)}) collective-permute-start(f32[272,128]{1,0:T(8,128)S(1)} %get-tuple-element.11.refs_0_), channel_id=1, source_target_pairs={{0,1},{1,0},{2,3},{3,2},{4,5},{5,4},{6,7},{7,6},{8,9},{9,8},{10,11... | collective-permute-start | bytes 417800 | tf_op jit(solution)/shard_map/ppermute | solution.py:39
  2.2 2.6 %collective-permute-start.2 = (f32[64,128]{1,0:T(8,128)S(1)}, f32[64,128]{1,0:T(8,128)S(1)}, u32[]{:S(2)}, u32[]{:S(2)}) collective-permute-start(f32[64,128]{1,0:T(8,128)S(1)} %get-tuple-element.13.refs_0_), channel_id=1, source_target_pairs={{0,2},{1,3},{2,0},{3,1},{4,6},{5,7},{6,4},{7,5},{8,10},{9,11},{10,... | collective-permute-start | bytes 98312 | tf_op jit(solution)/shard_map/ppermute | solution.py:43
  4.8 0.0 collective-permute-done.refs_0_.refs_1_
  4.9 0.4 %shard_map.76.refs_1_.refs_0_ = f32[112,128]{1,0:T(8,128)S(1)} custom-call(f32[272,128]{1,0:T(8,128)S(1)} %get-tuple-element.11.refs_0_, f32[272,128]{1,0:T(8,128)S(1)} %collective-permute-done.refs_0_.refs_1_, bf16[4,256,128]{2,1,0:T(8,128)(2,1)S(1)} %shard_map.74.refs_2_, bf16[2,256,128]{2,1,0:T(8,128)(2,1)S(1)} %shard_map.75.refs_3_), custom_call_target="tpu_custom_call" | custom-call | flops 6291456 | bytes 131072 | tf_op jit(solution)/shard_map/pallas_call | solution.py:47
  5.3 1.3 %collective-permute-start.1 = (f32[112,128]{1,0:T(8,128)S(1)}, f32[112,128]{1,0:T(8,128)S(1)}, u32[]{:S(2)}, u32[]{:S(2)}) collective-permute-start(f32[112,128]{1,0:T(8,128)S(1)} %shard_map.76.refs_1_.refs_0_), channel_id=1, source_target_pairs={{0,2},{1,3},{2,0},{3,1},{4,6},{5,7},{6,4},{7,5},{8,10},{9,11},{10,... | collective-permute-start | bytes 172040 | tf_op jit(solution)/shard_map/ppermute | solution.py:43
  6.6 0.2 %collective-permute-done.2.refs_0_ = f32[64,128]{1,0:T(8,128)S(1)} collective-permute-done((f32[64,128]{1,0:T(8,128)S(1)}, f32[64,128]{1,0:T(8,128)S(1)}, u32[]{:S(2)}, u32[]{:S(2)}) %collective-permute-start.2) | collective-permute-done | bytes 32800 | tf_op jit(solution)/shard_map/ppermute | solution.py:43
  6.8 2.7 %collective-permute-done.1.refs_1_ = f32[112,128]{1,0:T(8,128)S(1)} collective-permute-done((f32[112,128]{1,0:T(8,128)S(1)}, f32[112,128]{1,0:T(8,128)S(1)}, u32[]{:S(2)}, u32[]{:S(2)}) %collective-permute-start.1) | collective-permute-done | bytes 57376 | tf_op jit(solution)/shard_map/ppermute | solution.py:43
  9.5 0.0 copy-done
  9.5 0.0 copy-done.1
  9.5 0.5 %shard_map.79 = (f32[16,2048]{1,0:T(8,128)S(1)}, f32[16,2048]{1,0:T(8,128)S(1)}) custom-call(f32[112,128]{1,0:T(8,128)S(1)} %shard_map.76.refs_1_.refs_0_, f32[112,128]{1,0:T(8,128)S(1)} %collective-permute-done.1.refs_1_, bf16[4,256,128]{2,1,0:T(8,128)(2,1)S(1)} %shard_map.74.refs_2_, bf16[3,256,128]{2,1,0:T(8,128)(2,1)S(1)} %shard_map.77.refs_3_, ...), custom_call_target="tpu_custom_call" | custom-call | flops 8388608 | bytes 1048576 | tf_op jit(solution)/shard_map/pallas_call | solution.py:47
  10.0 1.6 %collective-permute-start.4 = (f32[16,2048]{1,0:T(8,128)S(1)}, f32[16,2048]{1,0:T(8,128)S(1)}, u32[]{:S(2)}, u32[]{:S(2)}) collective-permute-start(f32[16,2048]{1,0:T(8,128)S(1)} %get-tuple-element.15), channel_id=1, source_target_pairs={{0,4},{4,0},{8,12},{12,8},{16,20},{20,16},{24,28},{28,24},{1,5},{5... | collective-permute-start | bytes 393224 | tf_op jit(solution)/shard_map/ppermute | solution.py:20
  11.6 2.6 %collective-permute-start.3 = (f32[16,2048]{1,0:T(8,128)S(1)}, f32[16,2048]{1,0:T(8,128)S(1)}, u32[]{:S(2)}, u32[]{:S(2)}) collective-permute-start(f32[16,2048]{1,0:T(8,128)S(1)} %get-tuple-element.14), channel_id=1, source_target_pairs={{0,16},{4,20},{8,24},{12,28},{16,0},{20,4},{24,8},{28,12},{1,17},{... | collective-permute-start | bytes 393224 | tf_op jit(solution)/shard_map/ppermute | solution.py:16
  14.2 1.3 %collective-permute-start.5 = (f32[16,2048]{1,0:T(8,128)S(1)}, f32[16,2048]{1,0:T(8,128)S(1)}, u32[]{:S(2)}, u32[]{:S(2)}) collective-permute-start(f32[16,2048]{1,0:T(8,128)S(1)} %get-tuple-element.15), channel_id=1, source_target_pairs={{0,28},{1,3},{2,30},{3,1},{4,0},{5,7},{6,2},{7,5},{8,4},{9,11},{10... | collective-permute-start | bytes 393224 | tf_op jit(solution)/shard_map/ppermute | solution.py:35
  15.5 0.0 collective-permute-done.4.near_ref
  15.5 1.2 %collective-permute-start.6 = (f32[16,2048]{1,0:T(8,128)S(1)}, f32[16,2048]{1,0:T(8,128)S(1)}, u32[]{:S(2)}, u32[]{:S(2)}) collective-permute-start(f32[16,2048]{1,0:T(8,128)S(1)} %collective-permute-done.4.near_ref), channel_id=1, source_target_pairs={{0,2},{1,3},{2,0},{3,1},{4,6},{5,29},{6,4},{7,31},{8,10},{9,11},{1... | collective-permute-start | bytes 393224 | tf_op jit(solution)/shard_map/ppermute | solution.py:35
  16.7 1.8 %shard_map.80.diag_ref = f32[16,2048]{1,0:T(8,128)S(1)} custom-call(bf16[16,2048]{1,0:T(8,128)(2,1)S(1)} %get-tuple-element.16.xb_ref, bf16[4,512,512]{2,1,0:T(8,128)(2,1)} %leaf_hbm.1), custom_call_target="tpu_custom_call" | custom-call | flops 33554432 | bytes 2097152 | tf_op jit(solution)/shard_map/pallas_call | solution.py:47
  18.6 1.0 %collective-permute-done.3.half_ref = f32[16,2048]{1,0:T(8,128)S(1)} collective-permute-done((f32[16,2048]{1,0:T(8,128)S(1)}, f32[16,2048]{1,0:T(8,128)S(1)}, u32[]{:S(2)}, u32[]{:S(2)}) %collective-permute-start.3) | collective-permute-done | bytes 131104 | tf_op jit(solution)/shard_map/ppermute | solution.py:16
  19.5 0.0 collective-permute-done.5.straight_ref
  19.5 0.9 %collective-permute-done.6.onward_ref = f32[16,2048]{1,0:T(8,128)S(1)} collective-permute-done((f32[16,2048]{1,0:T(8,128)S(1)}, f32[16,2048]{1,0:T(8,128)S(1)}, u32[]{:S(2)}, u32[]{:S(2)}) %collective-permute-start.6) | collective-permute-done | bytes 131104 | tf_op jit(solution)/shard_map/ppermute | solution.py:35
  20.5 0.7 %shard_map.82 = f32[16,2048]{1,0:T(8,128)} custom-call(f32[16,2048]{1,0:T(8,128)S(1)} %collective-permute-done.3.half_ref, f32[16,2048]{1,0:T(8,128)S(1)} %collective-permute-done.4.near_ref, f32[16,2048]{1,0:T(8,128)S(1)} %collective-permute-done.5.straight_ref, f32[16,2048]{1,0:T(8,128)S(1)} %collective-permute-done.6.onward_ref, ...), custom_call_target="tpu_custom_call" | custom-call | flops 65536 | bytes 524288 | tf_op jit(solution)/shard_map/pallas_call | solution.py:47
  (5 shorter events, 0.1 us)
Async XLA Ops:
  0.0 9.5 %copy-start = (bf16[2,64,2048]{2,1,0:T(8,128)(2,1)S(1)}, bf16[2,64,2048]{2,1,0:T(8,128)(2,1)}, u32[]{:S(2)}) copy-start(bf16[2,64,2048]{2,1,0:T(8,128)(2,1)} %param.10) | copy-start | bytes 1572868
  0.0 9.5 %copy-start.1 = (s32[2,8]{1,0:T(2,128)S(1)}, s32[2,8]{1,0:T(2,128)}, u32[]{:S(2)}) copy-start(s32[2,8]{1,0:T(2,128)} %refs_6_.1) | copy-start | bytes 196
  1.7 3.1 %collective-permute-start = (f32[272,128]{1,0:T(8,128)S(1)}, f32[272,128]{1,0:T(8,128)S(1)}, u32[]{:S(2)}, u32[]{:S(2)}) collective-permute-start(f32[272,128]{1,0:T(8,128)S(1)} %get-tuple-element.11.refs_0_), channel_id=1, source_target_pairs={{0,1},{1,0},{2,3},{3,2},{4,5},{5,4},{6,7},{7,6},{8,9},{9,8},{10,11... | collective-permute-start | bytes 417800 | tf_op jit(solution)/shard_map/ppermute | solution.py:39
  2.2 4.6 %collective-permute-start.2 = (f32[64,128]{1,0:T(8,128)S(1)}, f32[64,128]{1,0:T(8,128)S(1)}, u32[]{:S(2)}, u32[]{:S(2)}) collective-permute-start(f32[64,128]{1,0:T(8,128)S(1)} %get-tuple-element.13.refs_0_), channel_id=1, source_target_pairs={{0,2},{1,3},{2,0},{3,1},{4,6},{5,7},{6,4},{7,5},{8,10},{9,11},{10,... | collective-permute-start | bytes 98312 | tf_op jit(solution)/shard_map/ppermute | solution.py:43
  5.3 4.2 %collective-permute-start.1 = (f32[112,128]{1,0:T(8,128)S(1)}, f32[112,128]{1,0:T(8,128)S(1)}, u32[]{:S(2)}, u32[]{:S(2)}) collective-permute-start(f32[112,128]{1,0:T(8,128)S(1)} %shard_map.76.refs_1_.refs_0_), channel_id=1, source_target_pairs={{0,2},{1,3},{2,0},{3,1},{4,6},{5,7},{6,4},{7,5},{8,10},{9,11},{10,... | collective-permute-start | bytes 172040 | tf_op jit(solution)/shard_map/ppermute | solution.py:43
  10.0 5.5 %collective-permute-start.4 = (f32[16,2048]{1,0:T(8,128)S(1)}, f32[16,2048]{1,0:T(8,128)S(1)}, u32[]{:S(2)}, u32[]{:S(2)}) collective-permute-start(f32[16,2048]{1,0:T(8,128)S(1)} %get-tuple-element.15), channel_id=1, source_target_pairs={{0,4},{4,0},{8,12},{12,8},{16,20},{20,16},{24,28},{28,24},{1,5},{5... | collective-permute-start | bytes 393224 | tf_op jit(solution)/shard_map/ppermute | solution.py:20
  11.6 7.9 %collective-permute-start.3 = (f32[16,2048]{1,0:T(8,128)S(1)}, f32[16,2048]{1,0:T(8,128)S(1)}, u32[]{:S(2)}, u32[]{:S(2)}) collective-permute-start(f32[16,2048]{1,0:T(8,128)S(1)} %get-tuple-element.14), channel_id=1, source_target_pairs={{0,16},{4,20},{8,24},{12,28},{16,0},{20,4},{24,8},{28,12},{1,17},{... | collective-permute-start | bytes 393224 | tf_op jit(solution)/shard_map/ppermute | solution.py:16
  14.2 5.4 %collective-permute-start.5 = (f32[16,2048]{1,0:T(8,128)S(1)}, f32[16,2048]{1,0:T(8,128)S(1)}, u32[]{:S(2)}, u32[]{:S(2)}) collective-permute-start(f32[16,2048]{1,0:T(8,128)S(1)} %get-tuple-element.15), channel_id=1, source_target_pairs={{0,28},{1,3},{2,30},{3,1},{4,0},{5,7},{6,2},{7,5},{8,4},{9,11},{10... | collective-permute-start | bytes 393224 | tf_op jit(solution)/shard_map/ppermute | solution.py:35
  15.5 5.0 %collective-permute-start.6 = (f32[16,2048]{1,0:T(8,128)S(1)}, f32[16,2048]{1,0:T(8,128)S(1)}, u32[]{:S(2)}, u32[]{:S(2)}) collective-permute-start(f32[16,2048]{1,0:T(8,128)S(1)} %collective-permute-done.4.near_ref), channel_id=1, source_target_pairs={{0,2},{1,3},{2,0},{3,1},{4,6},{5,29},{6,4},{7,31},{8,10},{9,11},{1... | collective-permute-start | bytes 393224 | tf_op jit(solution)/shard_map/ppermute | solution.py:35

commit v24 on v20

--- a/solution.py
+++ b/solution.py
@@ -63,10 +63,12 @@
     return [(source.at[place], target.at[place]) for place in places]
 
 
-def load(groups, field_hbm, col_hbm, mixing_hbm, perm_hbm, xb_ref, sent_ref, *refs):
-    *out_refs, field_ref, col_ref, mixing_ref, perm_ref, sems = refs
-    compact = {}
-    levels, sections, _, k, _ = mixing_ref.shape
+def section_factors(mixing_ref, section, side):
+    return jnp.concatenate([mixing_ref[level, section, side].astype(F32) for level in range(mixing_ref.shape[0])], axis=1)
+
+
+def load(count, field_hbm, col_hbm, mixing_hbm, perm_hbm, xb_ref, sent_ref, mixing_ref, field_ref, col_ref, perm_ref, sems):
+    levels, _, _, k, _ = mixing_ref.shape
     vectors = field_ref.shape[0]
     pairs = split(col_hbm, col_ref, 4, 0) + split(field_hbm, field_ref, 2, 0)
     pairs += [(mixing_hbm.at[level], mixing_ref.at[level]) for level in range(levels)]
@@ -82,20 +84,27 @@
     row = lax.broadcasted_iota(jnp.int32, (k, k), 0)
     picks = jnp.concatenate([(row == perm_ref[level : level + 1, :]).astype(F32) for level in range(levels)], axis=1)
     picks = block_diagonal(picks, levels).astype(BF16)
-    for section in range(sections):
+    for section in range(count):
         for side in range(2):
-            mats = jnp.concatenate([mixing_ref[level, section, side].astype(F32) for level in range(levels)], axis=1)
+            mats = section_factors(mixing_ref, section, side)
             if section == 0:
                 mats = jnp.dot(picks, block_diagonal(mats, levels).astype(BF16), preferred_element_type=F32)
                 mats = sum(mats[level * k : (level + 1) * k] for level in range(levels))
-            compact[section, side] = mats
-            for n, (group, out_ref) in enumerate(zip(groups, (sent_ref, *out_refs))):
-                if section in group:
-                    start = (0 if n else vectors) + (2 * group.index(section) + side) * k
-                    out_ref[start : start + k, :] = mats
-    if len(out_refs) == len(groups):
-        left, right = [block_diagonal(compact[which], levels).astype(BF16) for which in ((1, 1), (2, 0))]
-        out_refs[-1][...] = compact_product(levels, left, right)
+            start = vectors + (2 * section + side) * k
+            sent_ref[start : start + k, :] = mats
+
+
+def keep(first, mixing_ref, kept_ref, *factor_refs):
+    levels, sections, _, k, _ = mixing_ref.shape
+    for section in range(first, sections):
+        for side in range(2):
+            start = (2 * (section - first) + side) * k
+            kept_ref[start : start + k, :] = section_factors(mixing_ref, section, side)
+    for factor_ref in factor_refs:
+        left, right = [
+            block_diagonal(section_factors(mixing_ref, *which), levels).astype(BF16) for which in ((1, 1), (2, 0))
+        ]
+        factor_ref[...] = compact_product(levels, left, right)
 
 
 def build_weights(levels, chosen, *refs):
@@ -255,17 +264,18 @@
     ]
     size = 2 * rank_size
     one_round = bits == 2 and sections == 4 and levels == 2
-    groups_sent = [(0, 1), (2, 3)] if one_round else [tuple(range(sections - 1)), (sections - 1,)]
-    xb, sent, *kept = call(
-        lambda *refs: load(groups_sent, *refs),
-        [array(vectors, rows, kind=BF16)]
-        + [array(len(group) * size + (0 if n else vectors), width) for n, group in enumerate(groups_sent)]
-        + [array(rank_size, width)] * one_round,
+    ahead = 2 if one_round else sections - 1
+    xb, sent, mixing_here = call(
+        lambda *refs: load(ahead, *refs),
+        [
+            array(vectors, rows, kind=BF16),
+            array(vectors + ahead * size, width),
+            array(*mixing.shape[1:], kind=BF16),
+        ],
         [HBM] * 4, 2 * vectors * rows * width, 3 * rows * width, *in_hbm,
         scratch=[
             pltpu.VMEM(field.shape, F32),
             pltpu.VMEM((width, rows), BF16),
-            pltpu.VMEM(mixing.shape[1:], BF16),
             pltpu.VMEM(rank_perm.shape, jnp.int32),
             pltpu.SemaphoreType.DMA((1 + levels + 2 + 4,)),
         ],
@@ -285,6 +295,11 @@
         )
 
     received = swapped(sent)
+    kept = call(
+        lambda *refs: keep(ahead, *refs),
+        [array((sections - ahead) * size, width)] + [array(rank_size, width)] * one_round,
+        [VMEM], *weight_cost, mixing_here,
+    )
     step_cost = (24 * vectors * width * width, 8 * width * width)
     final = sections - 1
     if one_round:

time: 20.3 us -> 20.5 us (level)
  starting transfers between devices: 4.73 us -> 4.52 us
  Pallas kernels: 5.21 us -> 5.42 us
    pallas_call x9 -> x10, Pallas kernels: 5.21 us -> 5.42 us  [call(): pl.pallas_call(body, out_shape=shapes, in_specs=specs, out_specs=jax.tree...]
  transfers between devices with their start and end apart: 5 -> 5, of which waited for: 3 -> 3; matrix products, arithmetic and copies ran while one was open for 0% -> 0% of each run, Pallas kernels for 12% -> 13%
where the time goes in v24:
time: 20.5 us; the launch traced here: 20.3 us
  waiting for transfers between devices  10.3 us (50%)
  Pallas kernels  5.42 us (26%)
  starting transfers between devices  4.52 us (22%)
    ppermute x2, waiting for transfers between devices, shifted(): lax.ppermute(value, axis, [(source, (source + distance) % size) for sourc...  7.31 us
    pallas_call x10, Pallas kernels, call(): pl.pallas_call(body, out_shape=shapes, in_specs=specs, out_specs=jax.tree...  5.42 us
    ppermute x2, waiting for transfers between devices, across(): lax.ppermute(value, 'bf', [(n, n ^ 1 << bit) for n in range(lax.axis_size...  3.02 us
    ppermute x2, starting transfers between devices, across(): lax.ppermute(value, 'bf', [(n, n ^ 1 << bit) for n in range(lax.axis_size...  2.68 us
    ppermute x2, starting transfers between devices, shifted(): lax.ppermute(value, axis, [(source, (source + distance) % size) for sourc...  1.77 us
  transfers between devices with their start and end apart: 5, of which 3 were waited for; matrix products, arithmetic and copies ran while one was open for 0% of the time, Pallas kernels for 13%

profile of v24, /device:TPU:24, one launch (start us, length us, event | category | flops | bytes accessed | tf_op | source)
XLA Modules:
  0.0 20.3 jit_solution(17327779322097321716)
XLA Ops:
  0.0 0.0 copy-start
  0.0 0.0 copy-start.1
  0.0 1.7 %shard_map.73 = (bf16[16,2048]{1,0:T(8,128)(2,1)S(1)}, f32[272,128]{1,0:T(8,128)S(1)}, bf16[2,4,2,64,64]{4,3,2,1,0:T(8,128)(2,1)S(1)}) custom-call(f32[16,2048]{1,0:T(8,128)} %refs_0_.1, bf16[128,2048]{1,0:T(8,128)(2,1)} %bitcast.4, bf16[2,4,2,64,64]{4,3,2,1,0:T(8,128)(2,1)} %bitcast.5, s32[2,64]{1,0:T(2,128)} %refs_3_.1), custom_call_target="tpu_custom_call" | custom-call | flops 8388608 | bytes 786432 | tf_op jit(solution)/shard_map/pallas_call | solution.py:28
  1.7 0.1 collective-permute-start
  1.8 0.2 %shard_map.74 = (f32[256,128]{1,0:T(8,128)S(1)}, f32[64,128]{1,0:T(8,128)S(1)}) custom-call(bf16[2,4,2,64,64]{4,3,2,1,0:T(8,128)(2,1)S(1)} %get-tuple-element.13.refs_0_), custom_call_target="tpu_custom_call" | custom-call | flops 262144 | bytes 524288 | tf_op jit(solution)/shard_map/pallas_call | solution.py:28
  2.0 1.5 %collective-permute-start.2 = (f32[64,128]{1,0:T(8,128)S(1)}, f32[64,128]{1,0:T(8,128)S(1)}, u32[]{:S(2)}, u32[]{:S(2)}) collective-permute-start(f32[64,128]{1,0:T(8,128)S(1)} %get-tuple-element.15.refs_0_), channel_id=1, source_target_pairs={{0,2},{1,3},{2,0},{3,1},{4,6},{5,7},{6,4},{7,5},{8,10},{9,11},{10,... | collective-permute-start | bytes 98312 | tf_op jit(solution)/shard_map/ppermute | solution.py:24
  3.5 0.0 collective-permute-done.refs_0_.refs_1_
  3.6 0.4 %shard_map.77.refs_1_.refs_0_ = f32[112,128]{1,0:T(8,128)S(1)} custom-call(f32[272,128]{1,0:T(8,128)S(1)} %get-tuple-element.12.refs_0_, f32[272,128]{1,0:T(8,128)S(1)} %collective-permute-done.refs_0_.refs_1_, bf16[4,256,128]{2,1,0:T(8,128)(2,1)S(1)} %shard_map.75.refs_2_, bf16[2,256,128]{2,1,0:T(8,128)(2,1)S(1)} %shard_map.76.refs_3_), custom_call_target="tpu_custom_call" | custom-call | flops 6291456 | bytes 131072 | tf_op jit(solution)/shard_map/pallas_call | solution.py:28
  4.0 1.2 %collective-permute-start.1 = (f32[112,128]{1,0:T(8,128)S(1)}, f32[112,128]{1,0:T(8,128)S(1)}, u32[]{:S(2)}, u32[]{:S(2)}) collective-permute-start(f32[112,128]{1,0:T(8,128)S(1)} %shard_map.77.refs_1_.refs_0_), channel_id=1, source_target_pairs={{0,2},{1,3},{2,0},{3,1},{4,6},{5,7},{6,4},{7,5},{8,10},{9,11},{10,... | collective-permute-start | bytes 172040 | tf_op jit(solution)/shard_map/ppermute | solution.py:24
  5.1 0.8 %collective-permute-done.2.refs_0_ = f32[64,128]{1,0:T(8,128)S(1)} collective-permute-done((f32[64,128]{1,0:T(8,128)S(1)}, f32[64,128]{1,0:T(8,128)S(1)}, u32[]{:S(2)}, u32[]{:S(2)}) %collective-permute-start.2) | collective-permute-done | bytes 32800 | tf_op jit(solution)/shard_map/ppermute | solution.py:24
  5.9 2.3 %collective-permute-done.1.refs_1_ = f32[112,128]{1,0:T(8,128)S(1)} collective-permute-done((f32[112,128]{1,0:T(8,128)S(1)}, f32[112,128]{1,0:T(8,128)S(1)}, u32[]{:S(2)}, u32[]{:S(2)}) %collective-permute-start.1) | collective-permute-done | bytes 57376 | tf_op jit(solution)/shard_map/ppermute | solution.py:24
  8.2 0.0 copy-done
  8.2 0.0 copy-done.1
  8.2 0.5 %shard_map.80 = (f32[16,2048]{1,0:T(8,128)S(1)}, f32[16,2048]{1,0:T(8,128)S(1)}) custom-call(f32[112,128]{1,0:T(8,128)S(1)} %shard_map.77.refs_1_.refs_0_, f32[112,128]{1,0:T(8,128)S(1)} %collective-permute-done.1.refs_1_, bf16[4,256,128]{2,1,0:T(8,128)(2,1)S(1)} %shard_map.75.refs_2_, bf16[3,256,128]{2,1,0:T(8,128)(2,1)S(1)} %shard_map.78.refs_3_, ...), custom_call_target="tpu_custom_call" | custom-call | flops 8388608 | bytes 1048576 | tf_op jit(solution)/shard_map/pallas_call | solution.py:28
  8.7 0.4 %collective-permute-start.3 = (f32[16,2048]{1,0:T(8,128)S(1)}, f32[16,2048]{1,0:T(8,128)S(1)}, u32[]{:S(2)}, u32[]{:S(2)}) collective-permute-start(f32[16,2048]{1,0:T(8,128)S(1)} %get-tuple-element.16), channel_id=1, source_target_pairs={{0,16},{4,20},{8,24},{12,28},{16,0},{20,4},{24,8},{28,12},{1,17},{... | collective-permute-start | bytes 393224 | tf_op jit(solution)/shard_map/ppermute | solution.py:16
  9.1 1.4 %collective-permute-start.4 = (f32[16,2048]{1,0:T(8,128)S(1)}, f32[16,2048]{1,0:T(8,128)S(1)}, u32[]{:S(2)}, u32[]{:S(2)}) collective-permute-start(f32[16,2048]{1,0:T(8,128)S(1)} %get-tuple-element.17), channel_id=1, source_target_pairs={{0,28},{4,0},{8,4},{12,8},{16,12},{20,16},{24,20},{28,24},{1,29},{... | collective-permute-start | bytes 393224 | tf_op jit(solution)/shard_map/ppermute | solution.py:16
  10.5 1.8 %shard_map.81.diag_ref = f32[16,2048]{1,0:T(8,128)S(1)} custom-call(bf16[16,2048]{1,0:T(8,128)(2,1)S(1)} %get-tuple-element.18.xb_ref, bf16[4,512,512]{2,1,0:T(8,128)(2,1)} %leaf_hbm.1), custom_call_target="tpu_custom_call" | custom-call | flops 33554432 | bytes 2097152 | tf_op jit(solution)/shard_map/pallas_call | solution.py:28
  12.3 7.3 %collective-permute-done.3.half_ref = f32[16,2048]{1,0:T(8,128)S(1)} collective-permute-done((f32[16,2048]{1,0:T(8,128)S(1)}, f32[16,2048]{1,0:T(8,128)S(1)}, u32[]{:S(2)}, u32[]{:S(2)}) %collective-permute-start.3) | collective-permute-done | bytes 131104 | tf_op jit(solution)/shard_map/ppermute | solution.py:16
  19.7 0.0 collective-permute-done.4.below_ref
  19.7 0.7 %shard_map.82 = f32[16,2048]{1,0:T(8,128)} custom-call(f32[16,2048]{1,0:T(8,128)S(1)} %collective-permute-done.3.half_ref, f32[16,2048]{1,0:T(8,128)S(1)} %collective-permute-done.4.below_ref, f32[16,2048]{1,0:T(8,128)S(1)} %shard_map.81.diag_ref), custom_call_target="tpu_custom_call" | custom-call | flops 65536 | bytes 524288 | tf_op jit(solution)/shard_map/pallas_call | solution.py:28
  (4 shorter events, 0.1 us)
Async XLA Ops:
  0.0 8.2 %copy-start = (bf16[2,64,2048]{2,1,0:T(8,128)(2,1)S(1)}, bf16[2,64,2048]{2,1,0:T(8,128)(2,1)}, u32[]{:S(2)}) copy-start(bf16[2,64,2048]{2,1,0:T(8,128)(2,1)} %param.10) | copy-start | bytes 1572868
  0.0 8.2 %copy-start.1 = (s32[2,8]{1,0:T(2,128)S(1)}, s32[2,8]{1,0:T(2,128)}, u32[]{:S(2)}) copy-start(s32[2,8]{1,0:T(2,128)} %refs_6_.1) | copy-start | bytes 196
  1.7 1.8 %collective-permute-start = (f32[272,128]{1,0:T(8,128)S(1)}, f32[272,128]{1,0:T(8,128)S(1)}, u32[]{:S(2)}, u32[]{:S(2)}) collective-permute-start(f32[272,128]{1,0:T(8,128)S(1)} %get-tuple-element.12.refs_0_), channel_id=1, source_target_pairs={{0,1},{1,0},{2,3},{3,2},{4,5},{5,4},{6,7},{7,6},{8,9},{9,8},{10,11... | collective-permute-start | bytes 417800 | tf_op jit(solution)/shard_map/ppermute | solution.py:20
  2.0 3.9 %collective-permute-start.2 = (f32[64,128]{1,0:T(8,128)S(1)}, f32[64,128]{1,0:T(8,128)S(1)}, u32[]{:S(2)}, u32[]{:S(2)}) collective-permute-start(f32[64,128]{1,0:T(8,128)S(1)} %get-tuple-element.15.refs_0_), channel_id=1, source_target_pairs={{0,2},{1,3},{2,0},{3,1},{4,6},{5,7},{6,4},{7,5},{8,10},{9,11},{10,... | collective-permute-start | bytes 98312 | tf_op jit(solution)/shard_map/ppermute | solution.py:24
  4.0 4.2 %collective-permute-start.1 = (f32[112,128]{1,0:T(8,128)S(1)}, f32[112,128]{1,0:T(8,128)S(1)}, u32[]{:S(2)}, u32[]{:S(2)}) collective-permute-start(f32[112,128]{1,0:T(8,128)S(1)} %shard_map.77.refs_1_.refs_0_), channel_id=1, source_target_pairs={{0,2},{1,3},{2,0},{3,1},{4,6},{5,7},{6,4},{7,5},{8,10},{9,11},{10,... | collective-permute-start | bytes 172040 | tf_op jit(solution)/shard_map/ppermute | solution.py:24
  8.7 10.9 %collective-permute-start.3 = (f32[16,2048]{1,0:T(8,128)S(1)}, f32[16,2048]{1,0:T(8,128)S(1)}, u32[]{:S(2)}, u32[]{:S(2)}) collective-permute-start(f32[16,2048]{1,0:T(8,128)S(1)} %get-tuple-element.16), channel_id=1, source_target_pairs={{0,16},{4,20},{8,24},{12,28},{16,0},{20,4},{24,8},{28,12},{1,17},{... | collective-permute-start | bytes 393224 | tf_op jit(solution)/shard_map/ppermute | solution.py:16
  9.1 10.5 %collective-permute-start.4 = (f32[16,2048]{1,0:T(8,128)S(1)}, f32[16,2048]{1,0:T(8,128)S(1)}, u32[]{:S(2)}, u32[]{:S(2)}) collective-permute-start(f32[16,2048]{1,0:T(8,128)S(1)} %get-tuple-element.17), channel_id=1, source_target_pairs={{0,28},{4,0},{8,4},{12,8},{16,12},{20,16},{24,20},{28,24},{1,29},{... | collective-permute-start | bytes 393224 | tf_op jit(solution)/shard_map/ppermute | solution.py:16

commit v25 on v20

--- a/solution.py
+++ b/solution.py
@@ -111,15 +111,13 @@
     return sum(product[level * k : (level + 1) * k] for level in range(levels))
 
 
-def three_terms(value):
+def two_terms(value):
     high = value.astype(BF16)
-    rest = value - high.astype(F32)
-    middle = rest.astype(BF16)
-    return high, middle, (rest - middle.astype(F32)).astype(BF16)
+    return high, (value - high.astype(F32)).astype(BF16)
 
 
 def factor_terms(levels, compact):
-    return three_terms(block_diagonal(compact, levels))
+    return two_terms(block_diagonal(compact, levels))
 
 
 def build_terms(levels, compact_ref, *refs):
@@ -133,9 +131,9 @@
 
 def terms_dot(value, terms):
     count = value.shape[0]
-    stacked = jnp.concatenate(three_terms(value), axis=0)
+    stacked = jnp.concatenate(two_terms(value), axis=0)
     sums = sum(jnp.dot(stacked, term, preferred_element_type=F32) for term in reversed(terms))
-    return sums[:count] + (sums[count : 2 * count] + sums[2 * count :])
+    return sums[:count] + sums[count:]
 
 
 def exact_dot(value, factor):
@@ -203,9 +201,9 @@
     count = (here_ref.shape[0] - rank_size) // 3
     here = jnp.concatenate([here_ref[:count, :], here_ref[count : 2 * count, :]], axis=1)
     there = jnp.concatenate([there_ref[:count, :], there_ref[count : 2 * count, :]], axis=1)
-    mine = here_ref[2 * count : 3 * count, :] + terms_dot(there, [terms_ref[n] for n in range(3)])
+    mine = here_ref[2 * count : 3 * count, :] + terms_dot(there, [terms_ref[n] for n in range(2)])
     behind = factor_terms(levels, there_ref[3 * count :, :])
-    far_terms = [jnp.concatenate([far_ref[n], behind[n]], axis=0) for n in range(3)]
+    far_terms = [jnp.concatenate([far_ref[n], behind[n]], axis=0) for n in range(2)]
     far = there_ref[2 * count : 3 * count, :] + terms_dot(here, far_terms)
     finish(section_product(mine, far, mine_ref[3]), rank_size, half_shift, *refs)
 
@@ -280,7 +278,7 @@
 
     def terms(*compacts, scale=1):
         return call(
-            lambda *refs: build_terms(levels, *refs), array(3, len(compacts) * width, width, kind=BF16),
+            lambda *refs: build_terms(levels, *refs), array(2, len(compacts) * width, width, kind=BF16),
             [VMEM] * len(compacts), *[scale * cost for cost in weight_cost], *compacts,
         )
 

time: 20.3 us -> 20.2 us (level)
  transfers between devices with their start and end apart: 5 -> 5, of which waited for: 3 -> 3; matrix products, arithmetic and copies ran while one was open for 0% -> 0% of each run, Pallas kernels for 12% -> 11%
where the time goes in v25:
time: 20.2 us; the launch traced here: 20 us
  waiting for transfers between devices  10.2 us (50%)
  Pallas kernels  5.13 us (25%)
  starting transfers between devices  4.68 us (23%)
    ppermute x2, waiting for transfers between devices, shifted(): lax.ppermute(value, axis, [(source, (source + distance) % size) for sourc...  7.26 us
    pallas_call x9, Pallas kernels, call(): pl.pallas_call(body, out_shape=shapes, in_specs=specs, out_specs=jax.tree...  5.13 us
    ppermute x2, waiting for transfers between devices, across(): lax.ppermute(value, 'bf', [(n, n ^ 1 << bit) for n in range(lax.axis_size...  2.9 us
    ppermute x2, starting transfers between devices, across(): lax.ppermute(value, 'bf', [(n, n ^ 1 << bit) for n in range(lax.axis_size...  2.84 us
    ppermute x2, starting transfers between devices, shifted(): lax.ppermute(value, axis, [(source, (source + distance) % size) for sourc...  1.77 us
  transfers between devices with their start and end apart: 5, of which 3 were waited for; matrix products, arithmetic and copies ran while one was open for 0% of the time, Pallas kernels for 11%

profile of v25, /device:TPU:24, one launch (start us, length us, event | category | flops | bytes accessed | tf_op | source)
XLA Modules:
  0.0 20.0 jit_solution(10530916176695190941)
XLA Ops:
  0.0 0.0 copy-start
  0.0 0.0 copy-start.1
  0.0 1.7 %shard_map.73 = (bf16[16,2048]{1,0:T(8,128)(2,1)S(1)}, f32[272,128]{1,0:T(8,128)S(1)}, f32[256,128]{1,0:T(8,128)S(1)}, f32[64,128]{1,0:T(8,128)S(1)}) custom-call(f32[16,2048]{1,0:T(8,128)} %refs_0_.1, bf16[128,2048]{1,0:T(8,128)(2,1)} %bitcast.4, bf16[2,4,2,64,64]{4,3,2,1,0:T(8,128)(2,1)} %bitcast.5, s32[2,64]{1,0:T(2,128)} %refs_3_.1), custom_call_target="tpu_custom_call" | custom-call | flops 8388608 | bytes 786432 | tf_op jit(solution)/shard_map/pallas_call | solution.py:28
  1.7 0.1 collective-permute-start
  1.8 1.6 %collective-permute-start.2 = (f32[64,128]{1,0:T(8,128)S(1)}, f32[64,128]{1,0:T(8,128)S(1)}, u32[]{:S(2)}, u32[]{:S(2)}) collective-permute-start(f32[64,128]{1,0:T(8,128)S(1)} %get-tuple-element.13.refs_0_), channel_id=1, source_target_pairs={{0,2},{1,3},{2,0},{3,1},{4,6},{5,7},{6,4},{7,5},{8,10},{9,11},{10,... | collective-permute-start | bytes 98312 | tf_op jit(solution)/shard_map/ppermute | solution.py:24
  3.4 0.0 collective-permute-done.refs_0_.refs_1_
  3.4 0.4 %shard_map.76.refs_1_.refs_0_ = f32[112,128]{1,0:T(8,128)S(1)} custom-call(f32[272,128]{1,0:T(8,128)S(1)} %get-tuple-element.11.refs_0_, f32[272,128]{1,0:T(8,128)S(1)} %collective-permute-done.refs_0_.refs_1_, bf16[4,256,128]{2,1,0:T(8,128)(2,1)S(1)} %shard_map.74.refs_2_, bf16[2,256,128]{2,1,0:T(8,128)(2,1)S(1)} %shard_map.75.refs_3_), custom_call_target="tpu_custom_call" | custom-call | flops 6291456 | bytes 131072 | tf_op jit(solution)/shard_map/pallas_call | solution.py:28
  3.8 1.3 %collective-permute-start.1 = (f32[112,128]{1,0:T(8,128)S(1)}, f32[112,128]{1,0:T(8,128)S(1)}, u32[]{:S(2)}, u32[]{:S(2)}) collective-permute-start(f32[112,128]{1,0:T(8,128)S(1)} %shard_map.76.refs_1_.refs_0_), channel_id=1, source_target_pairs={{0,2},{1,3},{2,0},{3,1},{4,6},{5,7},{6,4},{7,5},{8,10},{9,11},{10,... | collective-permute-start | bytes 172040 | tf_op jit(solution)/shard_map/ppermute | solution.py:24
  5.0 0.7 %collective-permute-done.2.refs_0_ = f32[64,128]{1,0:T(8,128)S(1)} collective-permute-done((f32[64,128]{1,0:T(8,128)S(1)}, f32[64,128]{1,0:T(8,128)S(1)}, u32[]{:S(2)}, u32[]{:S(2)}) %collective-permute-start.2) | collective-permute-done | bytes 32800 | tf_op jit(solution)/shard_map/ppermute | solution.py:24
  5.8 2.2 %collective-permute-done.1.refs_1_ = f32[112,128]{1,0:T(8,128)S(1)} collective-permute-done((f32[112,128]{1,0:T(8,128)S(1)}, f32[112,128]{1,0:T(8,128)S(1)}, u32[]{:S(2)}, u32[]{:S(2)}) %collective-permute-start.1) | collective-permute-done | bytes 57376 | tf_op jit(solution)/shard_map/ppermute | solution.py:24
  8.0 0.0 copy-done
  8.0 0.0 copy-done.1
  8.0 0.5 %shard_map.79 = (f32[16,2048]{1,0:T(8,128)S(1)}, f32[16,2048]{1,0:T(8,128)S(1)}) custom-call(f32[112,128]{1,0:T(8,128)S(1)} %shard_map.76.refs_1_.refs_0_, f32[112,128]{1,0:T(8,128)S(1)} %collective-permute-done.1.refs_1_, bf16[4,256,128]{2,1,0:T(8,128)(2,1)S(1)} %shard_map.74.refs_2_, bf16[2,256,128]{2,1,0:T(8,128)(2,1)S(1)} %shard_map.77.refs_3_, ...), custom_call_target="tpu_custom_call" | custom-call | flops 8388608 | bytes 1048576 | tf_op jit(solution)/shard_map/pallas_call | solution.py:28
  8.5 0.4 %collective-permute-start.3 = (f32[16,2048]{1,0:T(8,128)S(1)}, f32[16,2048]{1,0:T(8,128)S(1)}, u32[]{:S(2)}, u32[]{:S(2)}) collective-permute-start(f32[16,2048]{1,0:T(8,128)S(1)} %get-tuple-element.14), channel_id=1, source_target_pairs={{0,16},{4,20},{8,24},{12,28},{16,0},{20,4},{24,8},{28,12},{1,17},{... | collective-permute-start | bytes 393224 | tf_op jit(solution)/shard_map/ppermute | solution.py:16
  8.9 1.4 %collective-permute-start.4 = (f32[16,2048]{1,0:T(8,128)S(1)}, f32[16,2048]{1,0:T(8,128)S(1)}, u32[]{:S(2)}, u32[]{:S(2)}) collective-permute-start(f32[16,2048]{1,0:T(8,128)S(1)} %get-tuple-element.15), channel_id=1, source_target_pairs={{0,28},{4,0},{8,4},{12,8},{16,12},{20,16},{24,20},{28,24},{1,29},{... | collective-permute-start | bytes 393224 | tf_op jit(solution)/shard_map/ppermute | solution.py:16
  10.2 1.8 %shard_map.80.diag_ref = f32[16,2048]{1,0:T(8,128)S(1)} custom-call(bf16[16,2048]{1,0:T(8,128)(2,1)S(1)} %get-tuple-element.16.xb_ref, bf16[4,512,512]{2,1,0:T(8,128)(2,1)} %leaf_hbm.1), custom_call_target="tpu_custom_call" | custom-call | flops 33554432 | bytes 2097152 | tf_op jit(solution)/shard_map/pallas_call | solution.py:28
  12.1 7.3 %collective-permute-done.3.half_ref = f32[16,2048]{1,0:T(8,128)S(1)} collective-permute-done((f32[16,2048]{1,0:T(8,128)S(1)}, f32[16,2048]{1,0:T(8,128)S(1)}, u32[]{:S(2)}, u32[]{:S(2)}) %collective-permute-start.3) | collective-permute-done | bytes 131104 | tf_op jit(solution)/shard_map/ppermute | solution.py:16
  19.3 0.0 collective-permute-done.4.below_ref
  19.4 0.7 %shard_map.81 = f32[16,2048]{1,0:T(8,128)} custom-call(f32[16,2048]{1,0:T(8,128)S(1)} %collective-permute-done.3.half_ref, f32[16,2048]{1,0:T(8,128)S(1)} %collective-permute-done.4.below_ref, f32[16,2048]{1,0:T(8,128)S(1)} %shard_map.80.diag_ref), custom_call_target="tpu_custom_call" | custom-call | flops 65536 | bytes 524288 | tf_op jit(solution)/shard_map/pallas_call | solution.py:28
  (4 shorter events, 0.1 us)
Async XLA Ops:
  0.0 8.0 %copy-start = (bf16[2,64,2048]{2,1,0:T(8,128)(2,1)S(1)}, bf16[2,64,2048]{2,1,0:T(8,128)(2,1)}, u32[]{:S(2)}) copy-start(bf16[2,64,2048]{2,1,0:T(8,128)(2,1)} %param.10) | copy-start | bytes 1572868
  0.0 8.0 %copy-start.1 = (s32[2,8]{1,0:T(2,128)S(1)}, s32[2,8]{1,0:T(2,128)}, u32[]{:S(2)}) copy-start(s32[2,8]{1,0:T(2,128)} %refs_6_.1) | copy-start | bytes 196
  1.7 1.7 %collective-permute-start = (f32[272,128]{1,0:T(8,128)S(1)}, f32[272,128]{1,0:T(8,128)S(1)}, u32[]{:S(2)}, u32[]{:S(2)}) collective-permute-start(f32[272,128]{1,0:T(8,128)S(1)} %get-tuple-element.11.refs_0_), channel_id=1, source_target_pairs={{0,1},{1,0},{2,3},{3,2},{4,5},{5,4},{6,7},{7,6},{8,9},{9,8},{10,11... | collective-permute-start | bytes 417800 | tf_op jit(solution)/shard_map/ppermute | solution.py:20
  1.8 4.0 %collective-permute-start.2 = (f32[64,128]{1,0:T(8,128)S(1)}, f32[64,128]{1,0:T(8,128)S(1)}, u32[]{:S(2)}, u32[]{:S(2)}) collective-permute-start(f32[64,128]{1,0:T(8,128)S(1)} %get-tuple-element.13.refs_0_), channel_id=1, source_target_pairs={{0,2},{1,3},{2,0},{3,1},{4,6},{5,7},{6,4},{7,5},{8,10},{9,11},{10,... | collective-permute-start | bytes 98312 | tf_op jit(solution)/shard_map/ppermute | solution.py:24
  3.8 4.2 %collective-permute-start.1 = (f32[112,128]{1,0:T(8,128)S(1)}, f32[112,128]{1,0:T(8,128)S(1)}, u32[]{:S(2)}, u32[]{:S(2)}) collective-permute-start(f32[112,128]{1,0:T(8,128)S(1)} %shard_map.76.refs_1_.refs_0_), channel_id=1, source_target_pairs={{0,2},{1,3},{2,0},{3,1},{4,6},{5,7},{6,4},{7,5},{8,10},{9,11},{10,... | collective-permute-start | bytes 172040 | tf_op jit(solution)/shard_map/ppermute | solution.py:24
  8.5 10.9 %collective-permute-start.3 = (f32[16,2048]{1,0:T(8,128)S(1)}, f32[16,2048]{1,0:T(8,128)S(1)}, u32[]{:S(2)}, u32[]{:S(2)}) collective-permute-start(f32[16,2048]{1,0:T(8,128)S(1)} %get-tuple-element.14), channel_id=1, source_target_pairs={{0,16},{4,20},{8,24},{12,28},{16,0},{20,4},{24,8},{28,12},{1,17},{... | collective-permute-start | bytes 393224 | tf_op jit(solution)/shard_map/ppermute | solution.py:16
  8.9 10.5 %collective-permute-start.4 = (f32[16,2048]{1,0:T(8,128)S(1)}, f32[16,2048]{1,0:T(8,128)S(1)}, u32[]{:S(2)}, u32[]{:S(2)}) collective-permute-start(f32[16,2048]{1,0:T(8,128)S(1)} %get-tuple-element.15), channel_id=1, source_target_pairs={{0,28},{4,0},{8,4},{12,8},{16,12},{20,16},{24,20},{28,24},{1,29},{... | collective-permute-start | bytes 393224 | tf_op jit(solution)/shard_map/ppermute | solution.py:16

commit v26 on v21

--- a/solution.py
+++ b/solution.py
@@ -78,7 +78,10 @@
         copy.wait()
     xb = field_ref[...].astype(BF16)
     xb_ref[...] = xb
-    sent_ref[:vectors, :] = lax.dot_general(col_ref[...], xb, NT, preferred_element_type=F32).T
+    parts = [
+        lax.dot_general(xb, col_ref[level * k : (level + 1) * k, :], NT, preferred_element_type=F32) for level in range(levels)
+    ]
+    sent_ref[:vectors, :] = jnp.concatenate(parts, axis=1)
     row = lax.broadcasted_iota(jnp.int32, (k, k), 0)
     picks = jnp.concatenate([(row == perm_ref[level : level + 1, :]).astype(F32) for level in range(levels)], axis=1)
     picks = block_diagonal(picks, levels).astype(BF16)
@@ -187,11 +190,15 @@
     return (jnp.where(chosen, state, 0.0) if half else jnp.where(chosen, 0.0, state)).astype(BF16)
 
 
-def finish(state, rank_size, half_shift, row_ref, owner_ref, half_ref, below_ref):
-    ranks = [level_rank(state, rank_size, half_shift, owner_ref, half) for half in (True, False)]
-    outs = jnp.dot(jnp.concatenate(ranks, axis=0), row_ref[...], preferred_element_type=F32)
-    half_ref[...] = outs[: state.shape[0]]
-    below_ref[...] = outs[state.shape[0] :]
+def finish(state, rank_size, half_shift, row_ref, owner_ref, state_ref, half_ref):
+    state_ref[...] = state
+    rank = level_rank(state, rank_size, half_shift, owner_ref, True)
+    half_ref[...] = jnp.dot(rank, row_ref[...], preferred_element_type=F32)
+
+
+def expand_below(rank_size, half_shift, state_ref, row_ref, owner_ref, below_ref):
+    rank = level_rank(state_ref[...], rank_size, half_shift, owner_ref, False)
+    below_ref[...] = jnp.dot(rank, row_ref[...], preferred_element_type=F32)
 
 
 def last_step(sections, final, rank_size, half_shift, first_ref, second_ref, mine_ref, theirs_ref, *refs):
@@ -224,7 +231,11 @@
         out_ref[:, part] = jnp.dot(xb_ref[:, part], leaf_ref[n], preferred_element_type=F32)
 
 
-def combine(half_ref, below_ref, diag_ref, out_hbm, sum_ref, sems):
+def arrived(half_ref, out_ref):
+    out_ref[...] = half_ref[: out_ref.shape[0], : out_ref.shape[1]]
+
+
+def combine(half_ref, below_ref, diag_ref, _, out_hbm, sum_ref, sems):
     parts = sems.shape[0]
     count = sum_ref.shape[1] // parts
     copies = []
@@ -318,9 +329,13 @@
         last_weights = (mine, theirs)
     expand_cost = (2 * vectors * width * rows, 4 * width * rows)
     expand = row_factor.reshape(width, rows)
-    out_half, out_below = call(
-        lambda *refs: last_body(rank_size, groups // 2, *refs), [array(vectors, rows)] * 2,
+    state, out_half = call(
+        lambda *refs: last_body(rank_size, groups // 2, *refs), [array(vectors, width), array(vectors, rows)],
         [VMEM] * (4 + len(last_weights)), *expand_cost, *first_states, *last_weights, expand, row_owner,
+    )
+    out_below = call(
+        lambda *refs: expand_below(rank_size, groups // 2, *refs), array(vectors, rows),
+        [VMEM] * 3, *expand_cost, state, expand, row_owner,
     )
     out_half = shifted(out_half, "grp", groups // 2)
     out_below = shifted(out_below, "grp", groups - 1)
@@ -329,8 +344,9 @@
         xb, pltpu.with_memory_space_constraint(leaf_inverse, pltpu.HBM),
         scratch=[pltpu.VMEM(leaf_inverse.shape, BF16), pltpu.SemaphoreType.DMA((2 * leaf_inverse.shape[0],))],
     )
+    token = call(arrived, array(8, 128), [VMEM], *[1000 * cost for cost in weight_cost], out_half)
     return call(
-        combine, array(vectors, rows), [VMEM] * 3, 2 * vectors * rows, 16 * vectors * rows, out_half, out_below, diag,
+        combine, array(vectors, rows), [VMEM] * 4, 2 * vectors * rows, 16 * vectors * rows, out_half, out_below, diag, token,
         scratch=[pltpu.VMEM((vectors, rows), F32), pltpu.SemaphoreType.DMA((4,))], out=HBM,
     )
 

time: 20.4 us -> 20.3 us (level)
    ppermute x2, waiting for transfers between devices: 7.27 us -> 7.04 us  [shifted(): lax.ppermute(value, axis, [(source, (source + distance) % size) for sourc...]
    pallas_call x9 -> x11, Pallas kernels: 5.27 us -> 5.41 us  [call(): pl.pallas_call(body, out_shape=shapes, in_specs=specs, out_specs=jax.tree...]
  transfers between devices with their start and end apart: 5 -> 5, of which waited for: 3 -> 3; matrix products, arithmetic and copies ran while one was open for 0% -> 0% of each run, Pallas kernels for 12% -> 13%
where the time goes in v26:
time: 20.3 us; the launch traced here: 20.1 us
  waiting for transfers between devices  9.93 us (49%)
  Pallas kernels  5.41 us (27%)
  starting transfers between devices  4.72 us (23%)
    ppermute x2, waiting for transfers between devices, shifted(): lax.ppermute(value, axis, [(source, (source + distance) % size) for sourc...  7.04 us
    pallas_call x11, Pallas kernels, call(): pl.pallas_call(body, out_shape=shapes, in_specs=specs, out_specs=jax.tree...  5.41 us
    ppermute x2, starting transfers between devices, across(): lax.ppermute(value, 'bf', [(n, n ^ 1 << bit) for n in range(lax.axis_size...  2.88 us
    ppermute x2, waiting for transfers between devices, across(): lax.ppermute(value, 'bf', [(n, n ^ 1 << bit) for n in range(lax.axis_size...  2.88 us
    ppermute x2, starting transfers between devices, shifted(): lax.ppermute(value, axis, [(source, (source + distance) % size) for sourc...  1.77 us
  transfers between devices with their start and end apart: 5, of which 3 were waited for; matrix products, arithmetic and copies ran while one was open for 0% of the time, Pallas kernels for 13%

profile of v26, /device:TPU:24, one launch (start us, length us, event | category | flops | bytes accessed | tf_op | source)
XLA Modules:
  0.0 20.1 jit_solution(6825006905151893383)
XLA Ops:
  0.0 0.0 copy-start
  0.0 0.0 copy-start.1
  0.0 1.7 %shard_map.73 = (bf16[16,2048]{1,0:T(8,128)(2,1)S(1)}, f32[272,128]{1,0:T(8,128)S(1)}, f32[256,128]{1,0:T(8,128)S(1)}, f32[64,128]{1,0:T(8,128)S(1)}) custom-call(f32[16,2048]{1,0:T(8,128)} %refs_0_.1, bf16[128,2048]{1,0:T(8,128)(2,1)} %bitcast.5, bf16[2,4,2,64,64]{4,3,2,1,0:T(8,128)(2,1)} %bitcast.6, s32[2,64]{1,0:T(2,128)} %refs_3_.1), custom_call_target="tpu_custom_call" | custom-call | flops 8388608 | bytes 786432 | tf_op jit(solution)/shard_map/pallas_call | solution.py:28
  1.7 0.1 collective-permute-start
  1.8 1.6 %collective-permute-start.2 = (f32[64,128]{1,0:T(8,128)S(1)}, f32[64,128]{1,0:T(8,128)S(1)}, u32[]{:S(2)}, u32[]{:S(2)}) collective-permute-start(f32[64,128]{1,0:T(8,128)S(1)} %get-tuple-element.13.refs_0_), channel_id=1, source_target_pairs={{0,2},{1,3},{2,0},{3,1},{4,6},{5,7},{6,4},{7,5},{8,10},{9,11},{10,... | collective-permute-start | bytes 98312 | tf_op jit(solution)/shard_map/ppermute | solution.py:24
  3.4 0.0 collective-permute-done.refs_0_.refs_1_
  3.4 0.4 %shard_map.76.refs_1_.refs_0_ = f32[112,128]{1,0:T(8,128)S(1)} custom-call(f32[272,128]{1,0:T(8,128)S(1)} %get-tuple-element.11.refs_0_, f32[272,128]{1,0:T(8,128)S(1)} %collective-permute-done.refs_0_.refs_1_, bf16[4,256,128]{2,1,0:T(8,128)(2,1)S(1)} %shard_map.74.refs_2_, bf16[2,256,128]{2,1,0:T(8,128)(2,1)S(1)} %shard_map.75.refs_3_), custom_call_target="tpu_custom_call" | custom-call | flops 6291456 | bytes 131072 | tf_op jit(solution)/shard_map/pallas_call | solution.py:28
  3.8 1.3 %collective-permute-start.1 = (f32[112,128]{1,0:T(8,128)S(1)}, f32[112,128]{1,0:T(8,128)S(1)}, u32[]{:S(2)}, u32[]{:S(2)}) collective-permute-start(f32[112,128]{1,0:T(8,128)S(1)} %shard_map.76.refs_1_.refs_0_), channel_id=1, source_target_pairs={{0,2},{1,3},{2,0},{3,1},{4,6},{5,7},{6,4},{7,5},{8,10},{9,11},{10,... | collective-permute-start | bytes 172040 | tf_op jit(solution)/shard_map/ppermute | solution.py:24
  5.1 0.6 %collective-permute-done.2.refs_0_ = f32[64,128]{1,0:T(8,128)S(1)} collective-permute-done((f32[64,128]{1,0:T(8,128)S(1)}, f32[64,128]{1,0:T(8,128)S(1)}, u32[]{:S(2)}, u32[]{:S(2)}) %collective-permute-start.2) | collective-permute-done | bytes 32800 | tf_op jit(solution)/shard_map/ppermute | solution.py:24
  5.8 2.3 %collective-permute-done.1.refs_1_ = f32[112,128]{1,0:T(8,128)S(1)} collective-permute-done((f32[112,128]{1,0:T(8,128)S(1)}, f32[112,128]{1,0:T(8,128)S(1)}, u32[]{:S(2)}, u32[]{:S(2)}) %collective-permute-start.1) | collective-permute-done | bytes 57376 | tf_op jit(solution)/shard_map/ppermute | solution.py:24
  8.1 0.0 copy-done
  8.1 0.0 copy-done.1
  8.1 0.5 %shard_map.79 = (f32[16,128]{1,0:T(8,128)S(1)}, f32[16,2048]{1,0:T(8,128)S(1)}) custom-call(f32[112,128]{1,0:T(8,128)S(1)} %shard_map.76.refs_1_.refs_0_, f32[112,128]{1,0:T(8,128)S(1)} %collective-permute-done.1.refs_1_, bf16[4,256,128]{2,1,0:T(8,128)(2,1)S(1)} %shard_map.74.refs_2_, bf16[3,256,128]{2,1,0:T(8,128)(2,1)S(1)} %shard_map.77.refs_3_, ...), custom_call_target="tpu_custom_call" | custom-call | flops 8388608 | bytes 1048576 | tf_op jit(solution)/shard_map/pallas_call | solution.py:28
  8.6 0.4 %collective-permute-start.3 = (f32[16,2048]{1,0:T(8,128)S(1)}, f32[16,2048]{1,0:T(8,128)S(1)}, u32[]{:S(2)}, u32[]{:S(2)}) collective-permute-start(f32[16,2048]{1,0:T(8,128)S(1)} %get-tuple-element.14), channel_id=1, source_target_pairs={{0,16},{4,20},{8,24},{12,28},{16,0},{20,4},{24,8},{28,12},{1,17},{... | collective-permute-start | bytes 393224 | tf_op jit(solution)/shard_map/ppermute | solution.py:16
  9.0 0.2 shard_map.80
  9.1 1.4 %collective-permute-start.4 = (f32[16,2048]{1,0:T(8,128)S(1)}, f32[16,2048]{1,0:T(8,128)S(1)}, u32[]{:S(2)}, u32[]{:S(2)}) collective-permute-start(f32[16,2048]{1,0:T(8,128)S(1)} %shard_map.80), channel_id=1, source_target_pairs={{0,28},{4,0},{8,4},{12,8},{16,12},{20,16},{24,20},{28,24},{1,29},{... | collective-permute-start | bytes 393224 | tf_op jit(solution)/shard_map/ppermute | solution.py:16
  10.5 1.8 %shard_map.81.diag_ref = f32[16,2048]{1,0:T(8,128)S(1)} custom-call(bf16[16,2048]{1,0:T(8,128)(2,1)S(1)} %get-tuple-element.16.xb_ref, bf16[4,512,512]{2,1,0:T(8,128)(2,1)} %leaf_hbm.1), custom_call_target="tpu_custom_call" | custom-call | flops 33554432 | bytes 2097152 | tf_op jit(solution)/shard_map/pallas_call | solution.py:28
  12.4 7.0 %collective-permute-done.3.half_ref = f32[16,2048]{1,0:T(8,128)S(1)} collective-permute-done((f32[16,2048]{1,0:T(8,128)S(1)}, f32[16,2048]{1,0:T(8,128)S(1)}, u32[]{:S(2)}, u32[]{:S(2)}) %collective-permute-start.3) | collective-permute-done | bytes 131104 | tf_op jit(solution)/shard_map/ppermute | solution.py:16
  19.4 0.0 collective-permute-done.4.below_ref
  19.4 0.7 %shard_map.83 = f32[16,2048]{1,0:T(8,128)} custom-call(f32[16,2048]{1,0:T(8,128)S(1)} %collective-permute-done.3.half_ref, f32[16,2048]{1,0:T(8,128)S(1)} %collective-permute-done.4.below_ref, f32[16,2048]{1,0:T(8,128)S(1)} %shard_map.81.diag_ref, f32[8,128]{1,0:T(8,128)S(1)} %shard_map.82._), custom_call_target="tpu_custom_call" | custom-call | flops 65536 | bytes 524288 | tf_op jit(solution)/shard_map/pallas_call | solution.py:28
  (5 shorter events, 0.1 us)
Async XLA Ops:
  0.0 8.1 %copy-start = (bf16[2,64,2048]{2,1,0:T(8,128)(2,1)S(1)}, bf16[2,64,2048]{2,1,0:T(8,128)(2,1)}, u32[]{:S(2)}) copy-start(bf16[2,64,2048]{2,1,0:T(8,128)(2,1)} %param.10) | copy-start | bytes 1572868
  0.0 8.1 %copy-start.1 = (s32[2,8]{1,0:T(2,128)S(1)}, s32[2,8]{1,0:T(2,128)}, u32[]{:S(2)}) copy-start(s32[2,8]{1,0:T(2,128)} %refs_2_.1) | copy-start | bytes 196
  1.7 1.7 %collective-permute-start = (f32[272,128]{1,0:T(8,128)S(1)}, f32[272,128]{1,0:T(8,128)S(1)}, u32[]{:S(2)}, u32[]{:S(2)}) collective-permute-start(f32[272,128]{1,0:T(8,128)S(1)} %get-tuple-element.11.refs_0_), channel_id=1, source_target_pairs={{0,1},{1,0},{2,3},{3,2},{4,5},{5,4},{6,7},{7,6},{8,9},{9,8},{10,11... | collective-permute-start | bytes 417800 | tf_op jit(solution)/shard_map/ppermute | solution.py:20
  1.8 4.0 %collective-permute-start.2 = (f32[64,128]{1,0:T(8,128)S(1)}, f32[64,128]{1,0:T(8,128)S(1)}, u32[]{:S(2)}, u32[]{:S(2)}) collective-permute-start(f32[64,128]{1,0:T(8,128)S(1)} %get-tuple-element.13.refs_0_), channel_id=1, source_target_pairs={{0,2},{1,3},{2,0},{3,1},{4,6},{5,7},{6,4},{7,5},{8,10},{9,11},{10,... | collective-permute-start | bytes 98312 | tf_op jit(solution)/shard_map/ppermute | solution.py:24
  3.8 4.2 %collective-permute-start.1 = (f32[112,128]{1,0:T(8,128)S(1)}, f32[112,128]{1,0:T(8,128)S(1)}, u32[]{:S(2)}, u32[]{:S(2)}) collective-permute-start(f32[112,128]{1,0:T(8,128)S(1)} %shard_map.76.refs_1_.refs_0_), channel_id=1, source_target_pairs={{0,2},{1,3},{2,0},{3,1},{4,6},{5,7},{6,4},{7,5},{8,10},{9,11},{10,... | collective-permute-start | bytes 172040 | tf_op jit(solution)/shard_map/ppermute | solution.py:24
  8.6 10.9 %collective-permute-start.3 = (f32[16,2048]{1,0:T(8,128)S(1)}, f32[16,2048]{1,0:T(8,128)S(1)}, u32[]{:S(2)}, u32[]{:S(2)}) collective-permute-start(f32[16,2048]{1,0:T(8,128)S(1)} %get-tuple-element.14), channel_id=1, source_target_pairs={{0,16},{4,20},{8,24},{12,28},{16,0},{20,4},{24,8},{28,12},{1,17},{... | collective-permute-start | bytes 393224 | tf_op jit(solution)/shard_map/ppermute | solution.py:16
  9.1 10.3 %collective-permute-start.4 = (f32[16,2048]{1,0:T(8,128)S(1)}, f32[16,2048]{1,0:T(8,128)S(1)}, u32[]{:S(2)}, u32[]{:S(2)}) collective-permute-start(f32[16,2048]{1,0:T(8,128)S(1)} %shard_map.80), channel_id=1, source_target_pairs={{0,28},{4,0},{8,4},{12,8},{16,12},{20,16},{24,20},{28,24},{1,29},{... | collective-permute-start | bytes 393224 | tf_op jit(solution)/shard_map/ppermute | solution.py:16

commit v27 on v26

--- a/solution.py
+++ b/solution.py
@@ -78,10 +78,7 @@
         copy.wait()
     xb = field_ref[...].astype(BF16)
     xb_ref[...] = xb
-    parts = [
-        lax.dot_general(xb, col_ref[level * k : (level + 1) * k, :], NT, preferred_element_type=F32) for level in range(levels)
-    ]
-    sent_ref[:vectors, :] = jnp.concatenate(parts, axis=1)
+    sent_ref[:vectors, :] = lax.dot_general(xb, col_ref[...], NT, preferred_element_type=F32)
     row = lax.broadcasted_iota(jnp.int32, (k, k), 0)
     picks = jnp.concatenate([(row == perm_ref[level : level + 1, :]).astype(F32) for level in range(levels)], axis=1)
     picks = block_diagonal(picks, levels).astype(BF16)
@@ -114,15 +111,13 @@
     return sum(product[level * k : (level + 1) * k] for level in range(levels))
 
 
-def three_terms(value):
+def two_terms(value):
     high = value.astype(BF16)
-    rest = value - high.astype(F32)
-    middle = rest.astype(BF16)
-    return high, middle, (rest - middle.astype(F32)).astype(BF16)
+    return high, (value - high.astype(F32)).astype(BF16)
 
 
 def factor_terms(levels, compact):
-    return three_terms(block_diagonal(compact, levels))
+    return two_terms(block_diagonal(compact, levels))
 
 
 def build_terms(levels, compact_ref, *refs):
@@ -136,9 +131,9 @@
 
 def terms_dot(value, terms):
     count = value.shape[0]
-    stacked = jnp.concatenate(three_terms(value), axis=0)
+    stacked = jnp.concatenate(two_terms(value), axis=0)
     sums = sum(jnp.dot(stacked, term, preferred_element_type=F32) for term in reversed(terms))
-    return sums[:count] + (sums[count : 2 * count] + sums[2 * count :])
+    return sums[:count] + sums[count:]
 
 
 def exact_dot(value, factor):
@@ -210,9 +205,9 @@
     count = (here_ref.shape[0] - rank_size) // 3
     here = jnp.concatenate([here_ref[:count, :], here_ref[count : 2 * count, :]], axis=1)
     there = jnp.concatenate([there_ref[:count, :], there_ref[count : 2 * count, :]], axis=1)
-    mine = here_ref[2 * count : 3 * count, :] + terms_dot(there, [terms_ref[n] for n in range(3)])
+    mine = here_ref[2 * count : 3 * count, :] + terms_dot(there, [terms_ref[n] for n in range(2)])
     behind = factor_terms(levels, there_ref[3 * count :, :])
-    far_terms = [jnp.concatenate([far_ref[n], behind[n]], axis=0) for n in range(3)]
+    far_terms = [jnp.concatenate([far_ref[n], behind[n]], axis=0) for n in range(2)]
     far = there_ref[2 * count : 3 * count, :] + terms_dot(here, far_terms)
     finish(section_product(mine, far, mine_ref[3]), rank_size, half_shift, *refs)
 
@@ -291,7 +286,7 @@
 
     def terms(*compacts, scale=1):
         return call(
-            lambda *refs: build_terms(levels, *refs), array(3, len(compacts) * width, width, kind=BF16),
+            lambda *refs: build_terms(levels, *refs), array(2, len(compacts) * width, width, kind=BF16),
             [VMEM] * len(compacts), *[scale * cost for cost in weight_cost], *compacts,
         )
 

time: 20.3 us -> 20.1 us (level)
  transfers between devices with their start and end apart: 5 -> 5, of which waited for: 3 -> 3; matrix products, arithmetic and copies ran while one was open for 0% -> 0% of each run, Pallas kernels for 13% -> 12%
where the time goes in v27:
time: 20.1 us; the launch traced here: 20 us
  waiting for transfers between devices  9.94 us (49%)
  Pallas kernels  5.3 us (26%)
  starting transfers between devices  4.68 us (23%)
    ppermute x2, waiting for transfers between devices, shifted(): lax.ppermute(value, axis, [(source, (source + distance) % size) for sourc...  7.04 us
    pallas_call x11, Pallas kernels, call(): pl.pallas_call(body, out_shape=shapes, in_specs=specs, out_specs=jax.tree...  5.3 us
    ppermute x2, waiting for transfers between devices, across(): lax.ppermute(value, 'bf', [(n, n ^ 1 << bit) for n in range(lax.axis_size...  2.9 us
    ppermute x2, starting transfers between devices, across(): lax.ppermute(value, 'bf', [(n, n ^ 1 << bit) for n in range(lax.axis_size...  2.84 us
    ppermute x2, starting transfers between devices, shifted(): lax.ppermute(value, axis, [(source, (source + distance) % size) for sourc...  1.77 us
  transfers between devices with their start and end apart: 5, of which 3 were waited for; matrix products, arithmetic and copies ran while one was open for 0% of the time, Pallas kernels for 12%

profile of v27, /device:TPU:24, one launch (start us, length us, event | category | flops | bytes accessed | tf_op | source)
XLA Modules:
  0.0 20.0 jit_solution(1000493223315268394)
XLA Ops:
  0.0 0.0 copy-start
  0.0 0.0 copy-start.1
  0.0 1.7 %shard_map.73 = (bf16[16,2048]{1,0:T(8,128)(2,1)S(1)}, f32[272,128]{1,0:T(8,128)S(1)}, f32[256,128]{1,0:T(8,128)S(1)}, f32[64,128]{1,0:T(8,128)S(1)}) custom-call(f32[16,2048]{1,0:T(8,128)} %refs_0_.1, bf16[128,2048]{1,0:T(8,128)(2,1)} %bitcast.5, bf16[2,4,2,64,64]{4,3,2,1,0:T(8,128)(2,1)} %bitcast.6, s32[2,64]{1,0:T(2,128)} %refs_3_.1), custom_call_target="tpu_custom_call" | custom-call | flops 8388608 | bytes 786432 | tf_op jit(solution)/shard_map/pallas_call | solution.py:28
  1.7 0.1 collective-permute-start
  1.8 1.6 %collective-permute-start.2 = (f32[64,128]{1,0:T(8,128)S(1)}, f32[64,128]{1,0:T(8,128)S(1)}, u32[]{:S(2)}, u32[]{:S(2)}) collective-permute-start(f32[64,128]{1,0:T(8,128)S(1)} %get-tuple-element.13.refs_0_), channel_id=1, source_target_pairs={{0,2},{1,3},{2,0},{3,1},{4,6},{5,7},{6,4},{7,5},{8,10},{9,11},{10,... | collective-permute-start | bytes 98312 | tf_op jit(solution)/shard_map/ppermute | solution.py:24
  3.4 0.0 collective-permute-done.refs_0_.refs_1_
  3.4 0.4 %shard_map.76.refs_1_.refs_0_ = f32[112,128]{1,0:T(8,128)S(1)} custom-call(f32[272,128]{1,0:T(8,128)S(1)} %get-tuple-element.11.refs_0_, f32[272,128]{1,0:T(8,128)S(1)} %collective-permute-done.refs_0_.refs_1_, bf16[4,256,128]{2,1,0:T(8,128)(2,1)S(1)} %shard_map.74.refs_2_, bf16[2,256,128]{2,1,0:T(8,128)(2,1)S(1)} %shard_map.75.refs_3_), custom_call_target="tpu_custom_call" | custom-call | flops 6291456 | bytes 131072 | tf_op jit(solution)/shard_map/pallas_call | solution.py:28
  3.8 1.3 %collective-permute-start.1 = (f32[112,128]{1,0:T(8,128)S(1)}, f32[112,128]{1,0:T(8,128)S(1)}, u32[]{:S(2)}, u32[]{:S(2)}) collective-permute-start(f32[112,128]{1,0:T(8,128)S(1)} %shard_map.76.refs_1_.refs_0_), channel_id=1, source_target_pairs={{0,2},{1,3},{2,0},{3,1},{4,6},{5,7},{6,4},{7,5},{8,10},{9,11},{10,... | collective-permute-start | bytes 172040 | tf_op jit(solution)/shard_map/ppermute | solution.py:24
  5.0 0.7 %collective-permute-done.2.refs_0_ = f32[64,128]{1,0:T(8,128)S(1)} collective-permute-done((f32[64,128]{1,0:T(8,128)S(1)}, f32[64,128]{1,0:T(8,128)S(1)}, u32[]{:S(2)}, u32[]{:S(2)}) %collective-permute-start.2) | collective-permute-done | bytes 32800 | tf_op jit(solution)/shard_map/ppermute | solution.py:24
  5.8 2.2 %collective-permute-done.1.refs_1_ = f32[112,128]{1,0:T(8,128)S(1)} collective-permute-done((f32[112,128]{1,0:T(8,128)S(1)}, f32[112,128]{1,0:T(8,128)S(1)}, u32[]{:S(2)}, u32[]{:S(2)}) %collective-permute-start.1) | collective-permute-done | bytes 57376 | tf_op jit(solution)/shard_map/ppermute | solution.py:24
  8.0 0.0 copy-done
  8.0 0.0 copy-done.1
  8.0 0.5 %shard_map.79 = (f32[16,128]{1,0:T(8,128)S(1)}, f32[16,2048]{1,0:T(8,128)S(1)}) custom-call(f32[112,128]{1,0:T(8,128)S(1)} %shard_map.76.refs_1_.refs_0_, f32[112,128]{1,0:T(8,128)S(1)} %collective-permute-done.1.refs_1_, bf16[4,256,128]{2,1,0:T(8,128)(2,1)S(1)} %shard_map.74.refs_2_, bf16[2,256,128]{2,1,0:T(8,128)(2,1)S(1)} %shard_map.77.refs_3_, ...), custom_call_target="tpu_custom_call" | custom-call | flops 8388608 | bytes 1048576 | tf_op jit(solution)/shard_map/pallas_call | solution.py:28
  8.4 0.4 %collective-permute-start.3 = (f32[16,2048]{1,0:T(8,128)S(1)}, f32[16,2048]{1,0:T(8,128)S(1)}, u32[]{:S(2)}, u32[]{:S(2)}) collective-permute-start(f32[16,2048]{1,0:T(8,128)S(1)} %get-tuple-element.14), channel_id=1, source_target_pairs={{0,16},{4,20},{8,24},{12,28},{16,0},{20,4},{24,8},{28,12},{1,17},{... | collective-permute-start | bytes 393224 | tf_op jit(solution)/shard_map/ppermute | solution.py:16
  8.8 0.2 shard_map.80
  9.0 1.4 %collective-permute-start.4 = (f32[16,2048]{1,0:T(8,128)S(1)}, f32[16,2048]{1,0:T(8,128)S(1)}, u32[]{:S(2)}, u32[]{:S(2)}) collective-permute-start(f32[16,2048]{1,0:T(8,128)S(1)} %shard_map.80), channel_id=1, source_target_pairs={{0,28},{4,0},{8,4},{12,8},{16,12},{20,16},{24,20},{28,24},{1,29},{... | collective-permute-start | bytes 393224 | tf_op jit(solution)/shard_map/ppermute | solution.py:16
  10.4 1.8 %shard_map.81.diag_ref = f32[16,2048]{1,0:T(8,128)S(1)} custom-call(bf16[16,2048]{1,0:T(8,128)(2,1)S(1)} %get-tuple-element.16.xb_ref, bf16[4,512,512]{2,1,0:T(8,128)(2,1)} %leaf_hbm.1), custom_call_target="tpu_custom_call" | custom-call | flops 33554432 | bytes 2097152 | tf_op jit(solution)/shard_map/pallas_call | solution.py:28
  12.3 7.0 %collective-permute-done.3.half_ref = f32[16,2048]{1,0:T(8,128)S(1)} collective-permute-done((f32[16,2048]{1,0:T(8,128)S(1)}, f32[16,2048]{1,0:T(8,128)S(1)}, u32[]{:S(2)}, u32[]{:S(2)}) %collective-permute-start.3) | collective-permute-done | bytes 131104 | tf_op jit(solution)/shard_map/ppermute | solution.py:16
  19.3 0.0 collective-permute-done.4.below_ref
  19.3 0.7 %shard_map.83 = f32[16,2048]{1,0:T(8,128)} custom-call(f32[16,2048]{1,0:T(8,128)S(1)} %collective-permute-done.3.half_ref, f32[16,2048]{1,0:T(8,128)S(1)} %collective-permute-done.4.below_ref, f32[16,2048]{1,0:T(8,128)S(1)} %shard_map.81.diag_ref, f32[8,128]{1,0:T(8,128)S(1)} %shard_map.82._), custom_call_target="tpu_custom_call" | custom-call | flops 65536 | bytes 524288 | tf_op jit(solution)/shard_map/pallas_call | solution.py:28
  (5 shorter events, 0.1 us)
Async XLA Ops:
  0.0 8.0 %copy-start = (bf16[2,64,2048]{2,1,0:T(8,128)(2,1)S(1)}, bf16[2,64,2048]{2,1,0:T(8,128)(2,1)}, u32[]{:S(2)}) copy-start(bf16[2,64,2048]{2,1,0:T(8,128)(2,1)} %param.10) | copy-start | bytes 1572868
  0.0 8.0 %copy-start.1 = (s32[2,8]{1,0:T(2,128)S(1)}, s32[2,8]{1,0:T(2,128)}, u32[]{:S(2)}) copy-start(s32[2,8]{1,0:T(2,128)} %refs_2_.1) | copy-start | bytes 196
  1.7 1.7 %collective-permute-start = (f32[272,128]{1,0:T(8,128)S(1)}, f32[272,128]{1,0:T(8,128)S(1)}, u32[]{:S(2)}, u32[]{:S(2)}) collective-permute-start(f32[272,128]{1,0:T(8,128)S(1)} %get-tuple-element.11.refs_0_), channel_id=1, source_target_pairs={{0,1},{1,0},{2,3},{3,2},{4,5},{5,4},{6,7},{7,6},{8,9},{9,8},{10,11... | collective-permute-start | bytes 417800 | tf_op jit(solution)/shard_map/ppermute | solution.py:20
  1.8 4.0 %collective-permute-start.2 = (f32[64,128]{1,0:T(8,128)S(1)}, f32[64,128]{1,0:T(8,128)S(1)}, u32[]{:S(2)}, u32[]{:S(2)}) collective-permute-start(f32[64,128]{1,0:T(8,128)S(1)} %get-tuple-element.13.refs_0_), channel_id=1, source_target_pairs={{0,2},{1,3},{2,0},{3,1},{4,6},{5,7},{6,4},{7,5},{8,10},{9,11},{10,... | collective-permute-start | bytes 98312 | tf_op jit(solution)/shard_map/ppermute | solution.py:24
  3.8 4.2 %collective-permute-start.1 = (f32[112,128]{1,0:T(8,128)S(1)}, f32[112,128]{1,0:T(8,128)S(1)}, u32[]{:S(2)}, u32[]{:S(2)}) collective-permute-start(f32[112,128]{1,0:T(8,128)S(1)} %shard_map.76.refs_1_.refs_0_), channel_id=1, source_target_pairs={{0,2},{1,3},{2,0},{3,1},{4,6},{5,7},{6,4},{7,5},{8,10},{9,11},{10,... | collective-permute-start | bytes 172040 | tf_op jit(solution)/shard_map/ppermute | solution.py:24
  8.4 10.9 %collective-permute-start.3 = (f32[16,2048]{1,0:T(8,128)S(1)}, f32[16,2048]{1,0:T(8,128)S(1)}, u32[]{:S(2)}, u32[]{:S(2)}) collective-permute-start(f32[16,2048]{1,0:T(8,128)S(1)} %get-tuple-element.14), channel_id=1, source_target_pairs={{0,16},{4,20},{8,24},{12,28},{16,0},{20,4},{24,8},{28,12},{1,17},{... | collective-permute-start | bytes 393224 | tf_op jit(solution)/shard_map/ppermute | solution.py:16
  9.0 10.3 %collective-permute-start.4 = (f32[16,2048]{1,0:T(8,128)S(1)}, f32[16,2048]{1,0:T(8,128)S(1)}, u32[]{:S(2)}, u32[]{:S(2)}) collective-permute-start(f32[16,2048]{1,0:T(8,128)S(1)} %shard_map.80), channel_id=1, source_target_pairs={{0,28},{4,0},{8,4},{12,8},{16,12},{20,16},{24,20},{28,24},{1,29},{... | collective-permute-start | bytes 393224 | tf_op jit(solution)/shard_map/ppermute | solution.py:16

commit v28 on v27

--- a/solution.py
+++ b/solution.py
@@ -68,17 +68,26 @@
     compact = {}
     levels, sections, _, k, _ = mixing_ref.shape
     vectors = field_ref.shape[0]
-    pairs = split(col_hbm, col_ref, 4, 0) + split(field_hbm, field_ref, 2, 0)
-    pairs += [(mixing_hbm.at[level], mixing_ref.at[level]) for level in range(levels)]
-    pairs.append((perm_hbm, perm_ref))
-    copies = [pltpu.make_async_copy(*pair, sems.at[n]) for n, pair in enumerate(pairs)]
-    for copy in copies:
-        copy.start()
-    for copy in copies:
+    vectors_in, factors_in = split(field_hbm, field_ref, 2, 0), split(col_hbm, col_ref, levels, 0)
+    mixing_in = [(mixing_hbm.at[level], mixing_ref.at[level]) for level in range(levels)] + [(perm_hbm, perm_ref)]
+    stages = [vectors_in + factors_in[:1], mixing_in, factors_in[1:]]
+    copies = []
+    for stage in stages:
+        copies.append([])
+        for pair in stage:
+            copies[-1].append(pltpu.make_async_copy(*pair, sems.at[sum(len(done) for done in copies)]))
+            copies[-1][-1].start()
+
+    def projected(xb, level):
+        return lax.dot_general(xb, col_ref[level * k : (level + 1) * k, :], NT, preferred_element_type=F32)
+
+    for copy in copies[0]:
         copy.wait()
     xb = field_ref[...].astype(BF16)
     xb_ref[...] = xb
-    sent_ref[:vectors, :] = lax.dot_general(xb, col_ref[...], NT, preferred_element_type=F32)
+    states = [projected(xb, 0)]
+    for copy in copies[1]:
+        copy.wait()
     row = lax.broadcasted_iota(jnp.int32, (k, k), 0)
     picks = jnp.concatenate([(row == perm_ref[level : level + 1, :]).astype(F32) for level in range(levels)], axis=1)
     picks = block_diagonal(picks, levels).astype(BF16)
@@ -96,6 +105,10 @@
     if len(out_refs) == len(groups):
         left, right = [block_diagonal(compact[which], levels).astype(BF16) for which in ((1, 1), (2, 0))]
         out_refs[-1][...] = compact_product(levels, left, right)
+    for copy in copies[2]:
+        copy.wait()
+    states += [projected(xb, level) for level in range(1, levels)]
+    sent_ref[:vectors, :] = jnp.concatenate(states, axis=1)
 
 
 def build_weights(levels, chosen, *refs):

time: 20.1 us -> 20.5 us (1.020)
  Pallas kernels: 5.3 us -> 5.6 us
    pallas_call x11, Pallas kernels: 5.3 us -> 5.6 us  [call(): pl.pallas_call(body, out_shape=shapes, in_specs=specs, out_specs=jax.tree...]
where the time goes in v28:
time: 20.5 us; the launch traced here: 20.3 us
  waiting for transfers between devices  9.94 us (48%)
  Pallas kernels  5.6 us (27%)
  starting transfers between devices  4.69 us (23%)
    ppermute x2, waiting for transfers between devices, shifted(): lax.ppermute(value, axis, [(source, (source + distance) % size) for sourc...  7.04 us
    pallas_call x11, Pallas kernels, call(): pl.pallas_call(body, out_shape=shapes, in_specs=specs, out_specs=jax.tree...  5.6 us
    ppermute x2, waiting for transfers between devices, across(): lax.ppermute(value, 'bf', [(n, n ^ 1 << bit) for n in range(lax.axis_size...  2.9 us
    ppermute x2, starting transfers between devices, across(): lax.ppermute(value, 'bf', [(n, n ^ 1 << bit) for n in range(lax.axis_size...  2.84 us
    ppermute x2, starting transfers between devices, shifted(): lax.ppermute(value, axis, [(source, (source + distance) % size) for sourc...  1.77 us
  transfers between devices with their start and end apart: 5, of which 3 were waited for; matrix products, arithmetic and copies ran while one was open for 0% of the time, Pallas kernels for 12%

profile of v28, /device:TPU:24, one launch (start us, length us, event | category | flops | bytes accessed | tf_op | source)
XLA Modules:
  0.0 20.3 jit_solution(2940628241598520482)
XLA Ops:
  0.0 0.0 copy-start
  0.0 0.0 copy-start.1
  0.0 2.0 %shard_map.73 = (bf16[16,2048]{1,0:T(8,128)(2,1)S(1)}, f32[272,128]{1,0:T(8,128)S(1)}, f32[256,128]{1,0:T(8,128)S(1)}, f32[64,128]{1,0:T(8,128)S(1)}) custom-call(f32[16,2048]{1,0:T(8,128)} %refs_0_.1, bf16[128,2048]{1,0:T(8,128)(2,1)} %bitcast.5, bf16[2,4,2,64,64]{4,3,2,1,0:T(8,128)(2,1)} %bitcast.6, s32[2,64]{1,0:T(2,128)} %refs_3_.1), custom_call_target="tpu_custom_call" | custom-call | flops 8388608 | bytes 786432 | tf_op jit(solution)/shard_map/pallas_call | solution.py:28
  2.0 0.1 collective-permute-start
  2.1 1.6 %collective-permute-start.2 = (f32[64,128]{1,0:T(8,128)S(1)}, f32[64,128]{1,0:T(8,128)S(1)}, u32[]{:S(2)}, u32[]{:S(2)}) collective-permute-start(f32[64,128]{1,0:T(8,128)S(1)} %get-tuple-element.13.refs_0_), channel_id=1, source_target_pairs={{0,2},{1,3},{2,0},{3,1},{4,6},{5,7},{6,4},{7,5},{8,10},{9,11},{10,... | collective-permute-start | bytes 98312 | tf_op jit(solution)/shard_map/ppermute | solution.py:24
  3.7 0.0 collective-permute-done.refs_0_.refs_1_
  3.7 0.4 %shard_map.76.refs_1_.refs_0_ = f32[112,128]{1,0:T(8,128)S(1)} custom-call(f32[272,128]{1,0:T(8,128)S(1)} %get-tuple-element.11.refs_0_, f32[272,128]{1,0:T(8,128)S(1)} %collective-permute-done.refs_0_.refs_1_, bf16[4,256,128]{2,1,0:T(8,128)(2,1)S(1)} %shard_map.74.refs_2_, bf16[2,256,128]{2,1,0:T(8,128)(2,1)S(1)} %shard_map.75.refs_3_), custom_call_target="tpu_custom_call" | custom-call | flops 6291456 | bytes 131072 | tf_op jit(solution)/shard_map/pallas_call | solution.py:28
  4.1 1.3 %collective-permute-start.1 = (f32[112,128]{1,0:T(8,128)S(1)}, f32[112,128]{1,0:T(8,128)S(1)}, u32[]{:S(2)}, u32[]{:S(2)}) collective-permute-start(f32[112,128]{1,0:T(8,128)S(1)} %shard_map.76.refs_1_.refs_0_), channel_id=1, source_target_pairs={{0,2},{1,3},{2,0},{3,1},{4,6},{5,7},{6,4},{7,5},{8,10},{9,11},{10,... | collective-permute-start | bytes 172040 | tf_op jit(solution)/shard_map/ppermute | solution.py:24
  5.3 0.7 %collective-permute-done.2.refs_0_ = f32[64,128]{1,0:T(8,128)S(1)} collective-permute-done((f32[64,128]{1,0:T(8,128)S(1)}, f32[64,128]{1,0:T(8,128)S(1)}, u32[]{:S(2)}, u32[]{:S(2)}) %collective-permute-start.2) | collective-permute-done | bytes 32800 | tf_op jit(solution)/shard_map/ppermute | solution.py:24
  6.1 2.2 %collective-permute-done.1.refs_1_ = f32[112,128]{1,0:T(8,128)S(1)} collective-permute-done((f32[112,128]{1,0:T(8,128)S(1)}, f32[112,128]{1,0:T(8,128)S(1)}, u32[]{:S(2)}, u32[]{:S(2)}) %collective-permute-start.1) | collective-permute-done | bytes 57376 | tf_op jit(solution)/shard_map/ppermute | solution.py:24
  8.3 0.0 copy-done
  8.3 0.0 copy-done.1
  8.3 0.5 %shard_map.79 = (f32[16,128]{1,0:T(8,128)S(1)}, f32[16,2048]{1,0:T(8,128)S(1)}) custom-call(f32[112,128]{1,0:T(8,128)S(1)} %shard_map.76.refs_1_.refs_0_, f32[112,128]{1,0:T(8,128)S(1)} %collective-permute-done.1.refs_1_, bf16[4,256,128]{2,1,0:T(8,128)(2,1)S(1)} %shard_map.74.refs_2_, bf16[2,256,128]{2,1,0:T(8,128)(2,1)S(1)} %shard_map.77.refs_3_, ...), custom_call_target="tpu_custom_call" | custom-call | flops 8388608 | bytes 1048576 | tf_op jit(solution)/shard_map/pallas_call | solution.py:28
  8.7 0.4 %collective-permute-start.3 = (f32[16,2048]{1,0:T(8,128)S(1)}, f32[16,2048]{1,0:T(8,128)S(1)}, u32[]{:S(2)}, u32[]{:S(2)}) collective-permute-start(f32[16,2048]{1,0:T(8,128)S(1)} %get-tuple-element.14), channel_id=1, source_target_pairs={{0,16},{4,20},{8,24},{12,28},{16,0},{20,4},{24,8},{28,12},{1,17},{... | collective-permute-start | bytes 393224 | tf_op jit(solution)/shard_map/ppermute | solution.py:16
  9.1 0.2 shard_map.80
  9.3 1.4 %collective-permute-start.4 = (f32[16,2048]{1,0:T(8,128)S(1)}, f32[16,2048]{1,0:T(8,128)S(1)}, u32[]{:S(2)}, u32[]{:S(2)}) collective-permute-start(f32[16,2048]{1,0:T(8,128)S(1)} %shard_map.80), channel_id=1, source_target_pairs={{0,28},{4,0},{8,4},{12,8},{16,12},{20,16},{24,20},{28,24},{1,29},{... | collective-permute-start | bytes 393224 | tf_op jit(solution)/shard_map/ppermute | solution.py:16
  10.7 1.8 %shard_map.81.diag_ref = f32[16,2048]{1,0:T(8,128)S(1)} custom-call(bf16[16,2048]{1,0:T(8,128)(2,1)S(1)} %get-tuple-element.16.xb_ref, bf16[4,512,512]{2,1,0:T(8,128)(2,1)} %leaf_hbm.1), custom_call_target="tpu_custom_call" | custom-call | flops 33554432 | bytes 2097152 | tf_op jit(solution)/shard_map/pallas_call | solution.py:28
  12.6 7.0 %collective-permute-done.3.half_ref = f32[16,2048]{1,0:T(8,128)S(1)} collective-permute-done((f32[16,2048]{1,0:T(8,128)S(1)}, f32[16,2048]{1,0:T(8,128)S(1)}, u32[]{:S(2)}, u32[]{:S(2)}) %collective-permute-start.3) | collective-permute-done | bytes 131104 | tf_op jit(solution)/shard_map/ppermute | solution.py:16
  19.6 0.0 collective-permute-done.4.below_ref
  19.6 0.7 %shard_map.83 = f32[16,2048]{1,0:T(8,128)} custom-call(f32[16,2048]{1,0:T(8,128)S(1)} %collective-permute-done.3.half_ref, f32[16,2048]{1,0:T(8,128)S(1)} %collective-permute-done.4.below_ref, f32[16,2048]{1,0:T(8,128)S(1)} %shard_map.81.diag_ref, f32[8,128]{1,0:T(8,128)S(1)} %shard_map.82._), custom_call_target="tpu_custom_call" | custom-call | flops 65536 | bytes 524288 | tf_op jit(solution)/shard_map/pallas_call | solution.py:28
  (5 shorter events, 0.1 us)
Async XLA Ops:
  0.0 8.3 %copy-start = (bf16[2,64,2048]{2,1,0:T(8,128)(2,1)S(1)}, bf16[2,64,2048]{2,1,0:T(8,128)(2,1)}, u32[]{:S(2)}) copy-start(bf16[2,64,2048]{2,1,0:T(8,128)(2,1)} %param.10) | copy-start | bytes 1572868
  0.0 8.3 %copy-start.1 = (s32[2,8]{1,0:T(2,128)S(1)}, s32[2,8]{1,0:T(2,128)}, u32[]{:S(2)}) copy-start(s32[2,8]{1,0:T(2,128)} %refs_2_.1) | copy-start | bytes 196
  2.0 1.7 %collective-permute-start = (f32[272,128]{1,0:T(8,128)S(1)}, f32[272,128]{1,0:T(8,128)S(1)}, u32[]{:S(2)}, u32[]{:S(2)}) collective-permute-start(f32[272,128]{1,0:T(8,128)S(1)} %get-tuple-element.11.refs_0_), channel_id=1, source_target_pairs={{0,1},{1,0},{2,3},{3,2},{4,5},{5,4},{6,7},{7,6},{8,9},{9,8},{10,11... | collective-permute-start | bytes 417800 | tf_op jit(solution)/shard_map/ppermute | solution.py:20
  2.1 4.0 %collective-permute-start.2 = (f32[64,128]{1,0:T(8,128)S(1)}, f32[64,128]{1,0:T(8,128)S(1)}, u32[]{:S(2)}, u32[]{:S(2)}) collective-permute-start(f32[64,128]{1,0:T(8,128)S(1)} %get-tuple-element.13.refs_0_), channel_id=1, source_target_pairs={{0,2},{1,3},{2,0},{3,1},{4,6},{5,7},{6,4},{7,5},{8,10},{9,11},{10,... | collective-permute-start | bytes 98312 | tf_op jit(solution)/shard_map/ppermute | solution.py:24
  4.1 4.2 %collective-permute-start.1 = (f32[112,128]{1,0:T(8,128)S(1)}, f32[112,128]{1,0:T(8,128)S(1)}, u32[]{:S(2)}, u32[]{:S(2)}) collective-permute-start(f32[112,128]{1,0:T(8,128)S(1)} %shard_map.76.refs_1_.refs_0_), channel_id=1, source_target_pairs={{0,2},{1,3},{2,0},{3,1},{4,6},{5,7},{6,4},{7,5},{8,10},{9,11},{10,... | collective-permute-start | bytes 172040 | tf_op jit(solution)/shard_map/ppermute | solution.py:24
  8.7 10.9 %collective-permute-start.3 = (f32[16,2048]{1,0:T(8,128)S(1)}, f32[16,2048]{1,0:T(8,128)S(1)}, u32[]{:S(2)}, u32[]{:S(2)}) collective-permute-start(f32[16,2048]{1,0:T(8,128)S(1)} %get-tuple-element.14), channel_id=1, source_target_pairs={{0,16},{4,20},{8,24},{12,28},{16,0},{20,4},{24,8},{28,12},{1,17},{... | collective-permute-start | bytes 393224 | tf_op jit(solution)/shard_map/ppermute | solution.py:16
  9.3 10.3 %collective-permute-start.4 = (f32[16,2048]{1,0:T(8,128)S(1)}, f32[16,2048]{1,0:T(8,128)S(1)}, u32[]{:S(2)}, u32[]{:S(2)}) collective-permute-start(f32[16,2048]{1,0:T(8,128)S(1)} %shard_map.80), channel_id=1, source_target_pairs={{0,28},{4,0},{8,4},{12,8},{16,12},{20,16},{24,20},{28,24},{1,29},{... | collective-permute-start | bytes 393224 | tf_op jit(solution)/shard_map/ppermute | solution.py:16

commit v29 on v27

--- a/solution.py
+++ b/solution.py
@@ -83,16 +83,21 @@
     picks = jnp.concatenate([(row == perm_ref[level : level + 1, :]).astype(F32) for level in range(levels)], axis=1)
     picks = block_diagonal(picks, levels).astype(BF16)
     for section in range(sections):
+        mats = [
+            jnp.concatenate([mixing_ref[level, section, side].astype(F32) for level in range(levels)], axis=1)
+            for side in range(2)
+        ]
+        if section == 0:
+            both = jnp.concatenate([block_diagonal(one, levels) for one in mats], axis=1).astype(BF16)
+            both = jnp.dot(picks, both, preferred_element_type=F32)
+            both = sum(both[level * k : (level + 1) * k] for level in range(levels))
+            mats = [both[:, : levels * k], both[:, levels * k :]]
         for side in range(2):
-            mats = jnp.concatenate([mixing_ref[level, section, side].astype(F32) for level in range(levels)], axis=1)
-            if section == 0:
-                mats = jnp.dot(picks, block_diagonal(mats, levels).astype(BF16), preferred_element_type=F32)
-                mats = sum(mats[level * k : (level + 1) * k] for level in range(levels))
-            compact[section, side] = mats
+            compact[section, side] = mats[side]
             for n, (group, out_ref) in enumerate(zip(groups, (sent_ref, *out_refs))):
                 if section in group:
                     start = (0 if n else vectors) + (2 * group.index(section) + side) * k
-                    out_ref[start : start + k, :] = mats
+                    out_ref[start : start + k, :] = mats[side]
     if len(out_refs) == len(groups):
         left, right = [block_diagonal(compact[which], levels).astype(BF16) for which in ((1, 1), (2, 0))]
         out_refs[-1][...] = compact_product(levels, left, right)

time: 20.1 us -> 20.1 us (level)
  no operation moved by 1% of the time
where the time goes in v29:
time: 20.1 us; the launch traced here: 20 us
  waiting for transfers between devices  9.94 us (49%)
  Pallas kernels  5.29 us (26%)
  starting transfers between devices  4.68 us (23%)
    ppermute x2, waiting for transfers between devices, shifted(): lax.ppermute(value, axis, [(source, (source + distance) % size) for sourc...  7.04 us
    pallas_call x11, Pallas kernels, call(): pl.pallas_call(body, out_shape=shapes, in_specs=specs, out_specs=jax.tree...  5.29 us
    ppermute x2, waiting for transfers between devices, across(): lax.ppermute(value, 'bf', [(n, n ^ 1 << bit) for n in range(lax.axis_size...  2.9 us
    ppermute x2, starting transfers between devices, across(): lax.ppermute(value, 'bf', [(n, n ^ 1 << bit) for n in range(lax.axis_size...  2.84 us
    ppermute x2, starting transfers between devices, shifted(): lax.ppermute(value, axis, [(source, (source + distance) % size) for sourc...  1.77 us
  transfers between devices with their start and end apart: 5, of which 3 were waited for; matrix products, arithmetic and copies ran while one was open for 0% of the time, Pallas kernels for 12%

profile of v29, /device:TPU:24, one launch (start us, length us, event | category | flops | bytes accessed | tf_op | source)
XLA Modules:
  0.0 20.0 jit_solution(10978281811739703197)
XLA Ops:
  0.0 0.0 copy-start
  0.0 0.0 copy-start.1
  0.0 1.7 %shard_map.73 = (bf16[16,2048]{1,0:T(8,128)(2,1)S(1)}, f32[272,128]{1,0:T(8,128)S(1)}, f32[256,128]{1,0:T(8,128)S(1)}, f32[64,128]{1,0:T(8,128)S(1)}) custom-call(f32[16,2048]{1,0:T(8,128)} %refs_0_.1, bf16[128,2048]{1,0:T(8,128)(2,1)} %bitcast.5, bf16[2,4,2,64,64]{4,3,2,1,0:T(8,128)(2,1)} %bitcast.6, s32[2,64]{1,0:T(2,128)} %refs_3_.1), custom_call_target="tpu_custom_call" | custom-call | flops 8388608 | bytes 786432 | tf_op jit(solution)/shard_map/pallas_call | solution.py:28
  1.7 0.1 collective-permute-start
  1.8 1.6 %collective-permute-start.2 = (f32[64,128]{1,0:T(8,128)S(1)}, f32[64,128]{1,0:T(8,128)S(1)}, u32[]{:S(2)}, u32[]{:S(2)}) collective-permute-start(f32[64,128]{1,0:T(8,128)S(1)} %get-tuple-element.13.refs_0_), channel_id=1, source_target_pairs={{0,2},{1,3},{2,0},{3,1},{4,6},{5,7},{6,4},{7,5},{8,10},{9,11},{10,... | collective-permute-start | bytes 98312 | tf_op jit(solution)/shard_map/ppermute | solution.py:24
  3.4 0.0 collective-permute-done.refs_0_.refs_1_
  3.4 0.4 %shard_map.76.refs_1_.refs_0_ = f32[112,128]{1,0:T(8,128)S(1)} custom-call(f32[272,128]{1,0:T(8,128)S(1)} %get-tuple-element.11.refs_0_, f32[272,128]{1,0:T(8,128)S(1)} %collective-permute-done.refs_0_.refs_1_, bf16[4,256,128]{2,1,0:T(8,128)(2,1)S(1)} %shard_map.74.refs_2_, bf16[2,256,128]{2,1,0:T(8,128)(2,1)S(1)} %shard_map.75.refs_3_), custom_call_target="tpu_custom_call" | custom-call | flops 6291456 | bytes 131072 | tf_op jit(solution)/shard_map/pallas_call | solution.py:28
  3.8 1.3 %collective-permute-start.1 = (f32[112,128]{1,0:T(8,128)S(1)}, f32[112,128]{1,0:T(8,128)S(1)}, u32[]{:S(2)}, u32[]{:S(2)}) collective-permute-start(f32[112,128]{1,0:T(8,128)S(1)} %shard_map.76.refs_1_.refs_0_), channel_id=1, source_target_pairs={{0,2},{1,3},{2,0},{3,1},{4,6},{5,7},{6,4},{7,5},{8,10},{9,11},{10,... | collective-permute-start | bytes 172040 | tf_op jit(solution)/shard_map/ppermute | solution.py:24
  5.0 0.7 %collective-permute-done.2.refs_0_ = f32[64,128]{1,0:T(8,128)S(1)} collective-permute-done((f32[64,128]{1,0:T(8,128)S(1)}, f32[64,128]{1,0:T(8,128)S(1)}, u32[]{:S(2)}, u32[]{:S(2)}) %collective-permute-start.2) | collective-permute-done | bytes 32800 | tf_op jit(solution)/shard_map/ppermute | solution.py:24
  5.8 2.2 %collective-permute-done.1.refs_1_ = f32[112,128]{1,0:T(8,128)S(1)} collective-permute-done((f32[112,128]{1,0:T(8,128)S(1)}, f32[112,128]{1,0:T(8,128)S(1)}, u32[]{:S(2)}, u32[]{:S(2)}) %collective-permute-start.1) | collective-permute-done | bytes 57376 | tf_op jit(solution)/shard_map/ppermute | solution.py:24
  8.0 0.0 copy-done
  8.0 0.0 copy-done.1
  8.0 0.5 %shard_map.79 = (f32[16,128]{1,0:T(8,128)S(1)}, f32[16,2048]{1,0:T(8,128)S(1)}) custom-call(f32[112,128]{1,0:T(8,128)S(1)} %shard_map.76.refs_1_.refs_0_, f32[112,128]{1,0:T(8,128)S(1)} %collective-permute-done.1.refs_1_, bf16[4,256,128]{2,1,0:T(8,128)(2,1)S(1)} %shard_map.74.refs_2_, bf16[2,256,128]{2,1,0:T(8,128)(2,1)S(1)} %shard_map.77.refs_3_, ...), custom_call_target="tpu_custom_call" | custom-call | flops 8388608 | bytes 1048576 | tf_op jit(solution)/shard_map/pallas_call | solution.py:28
  8.4 0.4 %collective-permute-start.3 = (f32[16,2048]{1,0:T(8,128)S(1)}, f32[16,2048]{1,0:T(8,128)S(1)}, u32[]{:S(2)}, u32[]{:S(2)}) collective-permute-start(f32[16,2048]{1,0:T(8,128)S(1)} %get-tuple-element.14), channel_id=1, source_target_pairs={{0,16},{4,20},{8,24},{12,28},{16,0},{20,4},{24,8},{28,12},{1,17},{... | collective-permute-start | bytes 393224 | tf_op jit(solution)/shard_map/ppermute | solution.py:16
  8.8 0.2 shard_map.80
  9.0 1.4 %collective-permute-start.4 = (f32[16,2048]{1,0:T(8,128)S(1)}, f32[16,2048]{1,0:T(8,128)S(1)}, u32[]{:S(2)}, u32[]{:S(2)}) collective-permute-start(f32[16,2048]{1,0:T(8,128)S(1)} %shard_map.80), channel_id=1, source_target_pairs={{0,28},{4,0},{8,4},{12,8},{16,12},{20,16},{24,20},{28,24},{1,29},{... | collective-permute-start | bytes 393224 | tf_op jit(solution)/shard_map/ppermute | solution.py:16
  10.4 1.8 %shard_map.81.diag_ref = f32[16,2048]{1,0:T(8,128)S(1)} custom-call(bf16[16,2048]{1,0:T(8,128)(2,1)S(1)} %get-tuple-element.16.xb_ref, bf16[4,512,512]{2,1,0:T(8,128)(2,1)} %leaf_hbm.1), custom_call_target="tpu_custom_call" | custom-call | flops 33554432 | bytes 2097152 | tf_op jit(solution)/shard_map/pallas_call | solution.py:28
  12.3 7.0 %collective-permute-done.3.half_ref = f32[16,2048]{1,0:T(8,128)S(1)} collective-permute-done((f32[16,2048]{1,0:T(8,128)S(1)}, f32[16,2048]{1,0:T(8,128)S(1)}, u32[]{:S(2)}, u32[]{:S(2)}) %collective-permute-start.3) | collective-permute-done | bytes 131104 | tf_op jit(solution)/shard_map/ppermute | solution.py:16
  19.3 0.0 collective-permute-done.4.below_ref
  19.3 0.7 %shard_map.83 = f32[16,2048]{1,0:T(8,128)} custom-call(f32[16,2048]{1,0:T(8,128)S(1)} %collective-permute-done.3.half_ref, f32[16,2048]{1,0:T(8,128)S(1)} %collective-permute-done.4.below_ref, f32[16,2048]{1,0:T(8,128)S(1)} %shard_map.81.diag_ref, f32[8,128]{1,0:T(8,128)S(1)} %shard_map.82._), custom_call_target="tpu_custom_call" | custom-call | flops 65536 | bytes 524288 | tf_op jit(solution)/shard_map/pallas_call | solution.py:28
  (5 shorter events, 0.1 us)
Async XLA Ops:
  0.0 8.0 %copy-start = (bf16[2,64,2048]{2,1,0:T(8,128)(2,1)S(1)}, bf16[2,64,2048]{2,1,0:T(8,128)(2,1)}, u32[]{:S(2)}) copy-start(bf16[2,64,2048]{2,1,0:T(8,128)(2,1)} %param.10) | copy-start | bytes 1572868
  0.0 8.0 %copy-start.1 = (s32[2,8]{1,0:T(2,128)S(1)}, s32[2,8]{1,0:T(2,128)}, u32[]{:S(2)}) copy-start(s32[2,8]{1,0:T(2,128)} %refs_2_.1) | copy-start | bytes 196
  1.7 1.7 %collective-permute-start = (f32[272,128]{1,0:T(8,128)S(1)}, f32[272,128]{1,0:T(8,128)S(1)}, u32[]{:S(2)}, u32[]{:S(2)}) collective-permute-start(f32[272,128]{1,0:T(8,128)S(1)} %get-tuple-element.11.refs_0_), channel_id=1, source_target_pairs={{0,1},{1,0},{2,3},{3,2},{4,5},{5,4},{6,7},{7,6},{8,9},{9,8},{10,11... | collective-permute-start | bytes 417800 | tf_op jit(solution)/shard_map/ppermute | solution.py:20
  1.8 4.0 %collective-permute-start.2 = (f32[64,128]{1,0:T(8,128)S(1)}, f32[64,128]{1,0:T(8,128)S(1)}, u32[]{:S(2)}, u32[]{:S(2)}) collective-permute-start(f32[64,128]{1,0:T(8,128)S(1)} %get-tuple-element.13.refs_0_), channel_id=1, source_target_pairs={{0,2},{1,3},{2,0},{3,1},{4,6},{5,7},{6,4},{7,5},{8,10},{9,11},{10,... | collective-permute-start | bytes 98312 | tf_op jit(solution)/shard_map/ppermute | solution.py:24
  3.8 4.2 %collective-permute-start.1 = (f32[112,128]{1,0:T(8,128)S(1)}, f32[112,128]{1,0:T(8,128)S(1)}, u32[]{:S(2)}, u32[]{:S(2)}) collective-permute-start(f32[112,128]{1,0:T(8,128)S(1)} %shard_map.76.refs_1_.refs_0_), channel_id=1, source_target_pairs={{0,2},{1,3},{2,0},{3,1},{4,6},{5,7},{6,4},{7,5},{8,10},{9,11},{10,... | collective-permute-start | bytes 172040 | tf_op jit(solution)/shard_map/ppermute | solution.py:24
  8.4 10.9 %collective-permute-start.3 = (f32[16,2048]{1,0:T(8,128)S(1)}, f32[16,2048]{1,0:T(8,128)S(1)}, u32[]{:S(2)}, u32[]{:S(2)}) collective-permute-start(f32[16,2048]{1,0:T(8,128)S(1)} %get-tuple-element.14), channel_id=1, source_target_pairs={{0,16},{4,20},{8,24},{12,28},{16,0},{20,4},{24,8},{28,12},{1,17},{... | collective-permute-start | bytes 393224 | tf_op jit(solution)/shard_map/ppermute | solution.py:16
  9.0 10.3 %collective-permute-start.4 = (f32[16,2048]{1,0:T(8,128)S(1)}, f32[16,2048]{1,0:T(8,128)S(1)}, u32[]{:S(2)}, u32[]{:S(2)}) collective-permute-start(f32[16,2048]{1,0:T(8,128)S(1)} %shard_map.80), channel_id=1, source_target_pairs={{0,28},{4,0},{8,4},{12,8},{16,12},{20,16},{24,20},{28,24},{1,29},{... | collective-permute-start | bytes 393224 | tf_op jit(solution)/shard_map/ppermute | solution.py:16

commit v30 on v27

--- a/solution.py
+++ b/solution.py
@@ -68,7 +68,7 @@
     compact = {}
     levels, sections, _, k, _ = mixing_ref.shape
     vectors = field_ref.shape[0]
-    pairs = split(col_hbm, col_ref, 4, 0) + split(field_hbm, field_ref, 2, 0)
+    pairs = [(col_hbm, col_ref), (field_hbm, field_ref)]
     pairs += [(mixing_hbm.at[level], mixing_ref.at[level]) for level in range(levels)]
     pairs.append((perm_hbm, perm_ref))
     copies = [pltpu.make_async_copy(*pair, sems.at[n]) for n, pair in enumerate(pairs)]
@@ -273,7 +273,7 @@
             pltpu.VMEM((width, rows), BF16),
             pltpu.VMEM(mixing.shape[1:], BF16),
             pltpu.VMEM(rank_perm.shape, jnp.int32),
-            pltpu.SemaphoreType.DMA((1 + levels + 2 + 4,)),
+            pltpu.SemaphoreType.DMA((1 + levels + 2,)),
         ],
     )
     weight_cost = (4 * width * width * sections, 8 * width * width * sections)
@@ -342,7 +342,7 @@
     token = call(arrived, array(8, 128), [VMEM], *[1000 * cost for cost in weight_cost], out_half)
     return call(
         combine, array(vectors, rows), [VMEM] * 4, 2 * vectors * rows, 16 * vectors * rows, out_half, out_below, diag, token,
-        scratch=[pltpu.VMEM((vectors, rows), F32), pltpu.SemaphoreType.DMA((4,))], out=HBM,
+        scratch=[pltpu.VMEM((vectors, rows), F32), pltpu.SemaphoreType.DMA((2,))], out=HBM,
     )
 
 

time: 20.1 us -> 20 us (level)
  no operation moved by 1% of the time
where the time goes in v30:
time: 20 us; the launch traced here: 19.9 us
  waiting for transfers between devices  9.94 us (50%)
  Pallas kernels  5.16 us (26%)
  starting transfers between devices  4.68 us (23%)
    ppermute x2, waiting for transfers between devices, shifted(): lax.ppermute(value, axis, [(source, (source + distance) % size) for sourc...  7.04 us
    pallas_call x11, Pallas kernels, call(): pl.pallas_call(body, out_shape=shapes, in_specs=specs, out_specs=jax.tree...  5.16 us
    ppermute x2, waiting for transfers between devices, across(): lax.ppermute(value, 'bf', [(n, n ^ 1 << bit) for n in range(lax.axis_size...  2.9 us
    ppermute x2, starting transfers between devices, across(): lax.ppermute(value, 'bf', [(n, n ^ 1 << bit) for n in range(lax.axis_size...  2.84 us
    ppermute x2, starting transfers between devices, shifted(): lax.ppermute(value, axis, [(source, (source + distance) % size) for sourc...  1.77 us
  transfers between devices with their start and end apart: 5, of which 3 were waited for; matrix products, arithmetic and copies ran while one was open for 0% of the time, Pallas kernels for 12%

profile of v30, /device:TPU:24, one launch (start us, length us, event | category | flops | bytes accessed | tf_op | source)
XLA Modules:
  0.0 19.9 jit_solution(9553936860050282510)
XLA Ops:
  0.0 0.0 copy-start
  0.0 0.0 copy-start.1
  0.0 1.5 %shard_map.73 = (bf16[16,2048]{1,0:T(8,128)(2,1)S(1)}, f32[272,128]{1,0:T(8,128)S(1)}, f32[256,128]{1,0:T(8,128)S(1)}, f32[64,128]{1,0:T(8,128)S(1)}) custom-call(f32[16,2048]{1,0:T(8,128)} %refs_0_.1, bf16[128,2048]{1,0:T(8,128)(2,1)} %bitcast.5, bf16[2,4,2,64,64]{4,3,2,1,0:T(8,128)(2,1)} %bitcast.6, s32[2,64]{1,0:T(2,128)} %refs_3_.1), custom_call_target="tpu_custom_call" | custom-call | flops 8388608 | bytes 786432 | tf_op jit(solution)/shard_map/pallas_call | solution.py:28
  1.5 0.1 collective-permute-start
  1.6 1.6 %collective-permute-start.2 = (f32[64,128]{1,0:T(8,128)S(1)}, f32[64,128]{1,0:T(8,128)S(1)}, u32[]{:S(2)}, u32[]{:S(2)}) collective-permute-start(f32[64,128]{1,0:T(8,128)S(1)} %get-tuple-element.13.refs_0_), channel_id=1, source_target_pairs={{0,2},{1,3},{2,0},{3,1},{4,6},{5,7},{6,4},{7,5},{8,10},{9,11},{10,... | collective-permute-start | bytes 98312 | tf_op jit(solution)/shard_map/ppermute | solution.py:24
  3.2 0.0 collective-permute-done.refs_0_.refs_1_
  3.3 0.4 %shard_map.76.refs_1_.refs_0_ = f32[112,128]{1,0:T(8,128)S(1)} custom-call(f32[272,128]{1,0:T(8,128)S(1)} %get-tuple-element.11.refs_0_, f32[272,128]{1,0:T(8,128)S(1)} %collective-permute-done.refs_0_.refs_1_, bf16[4,256,128]{2,1,0:T(8,128)(2,1)S(1)} %shard_map.74.refs_2_, bf16[2,256,128]{2,1,0:T(8,128)(2,1)S(1)} %shard_map.75.refs_3_), custom_call_target="tpu_custom_call" | custom-call | flops 6291456 | bytes 131072 | tf_op jit(solution)/shard_map/pallas_call | solution.py:28
  3.6 1.3 %collective-permute-start.1 = (f32[112,128]{1,0:T(8,128)S(1)}, f32[112,128]{1,0:T(8,128)S(1)}, u32[]{:S(2)}, u32[]{:S(2)}) collective-permute-start(f32[112,128]{1,0:T(8,128)S(1)} %shard_map.76.refs_1_.refs_0_), channel_id=1, source_target_pairs={{0,2},{1,3},{2,0},{3,1},{4,6},{5,7},{6,4},{7,5},{8,10},{9,11},{10,... | collective-permute-start | bytes 172040 | tf_op jit(solution)/shard_map/ppermute | solution.py:24
  4.9 0.7 %collective-permute-done.2.refs_0_ = f32[64,128]{1,0:T(8,128)S(1)} collective-permute-done((f32[64,128]{1,0:T(8,128)S(1)}, f32[64,128]{1,0:T(8,128)S(1)}, u32[]{:S(2)}, u32[]{:S(2)}) %collective-permute-start.2) | collective-permute-done | bytes 32800 | tf_op jit(solution)/shard_map/ppermute | solution.py:24
  5.7 2.2 %collective-permute-done.1.refs_1_ = f32[112,128]{1,0:T(8,128)S(1)} collective-permute-done((f32[112,128]{1,0:T(8,128)S(1)}, f32[112,128]{1,0:T(8,128)S(1)}, u32[]{:S(2)}, u32[]{:S(2)}) %collective-permute-start.1) | collective-permute-done | bytes 57376 | tf_op jit(solution)/shard_map/ppermute | solution.py:24
  7.8 0.0 copy-done
  7.8 0.0 copy-done.1
  7.9 0.5 %shard_map.79 = (f32[16,128]{1,0:T(8,128)S(1)}, f32[16,2048]{1,0:T(8,128)S(1)}) custom-call(f32[112,128]{1,0:T(8,128)S(1)} %shard_map.76.refs_1_.refs_0_, f32[112,128]{1,0:T(8,128)S(1)} %collective-permute-done.1.refs_1_, bf16[4,256,128]{2,1,0:T(8,128)(2,1)S(1)} %shard_map.74.refs_2_, bf16[2,256,128]{2,1,0:T(8,128)(2,1)S(1)} %shard_map.77.refs_3_, ...), custom_call_target="tpu_custom_call" | custom-call | flops 8388608 | bytes 1048576 | tf_op jit(solution)/shard_map/pallas_call | solution.py:28
  8.3 0.4 %collective-permute-start.3 = (f32[16,2048]{1,0:T(8,128)S(1)}, f32[16,2048]{1,0:T(8,128)S(1)}, u32[]{:S(2)}, u32[]{:S(2)}) collective-permute-start(f32[16,2048]{1,0:T(8,128)S(1)} %get-tuple-element.14), channel_id=1, source_target_pairs={{0,16},{4,20},{8,24},{12,28},{16,0},{20,4},{24,8},{28,12},{1,17},{... | collective-permute-start | bytes 393224 | tf_op jit(solution)/shard_map/ppermute | solution.py:16
  8.7 0.2 shard_map.80
  8.9 1.4 %collective-permute-start.4 = (f32[16,2048]{1,0:T(8,128)S(1)}, f32[16,2048]{1,0:T(8,128)S(1)}, u32[]{:S(2)}, u32[]{:S(2)}) collective-permute-start(f32[16,2048]{1,0:T(8,128)S(1)} %shard_map.80), channel_id=1, source_target_pairs={{0,28},{4,0},{8,4},{12,8},{16,12},{20,16},{24,20},{28,24},{1,29},{... | collective-permute-start | bytes 393224 | tf_op jit(solution)/shard_map/ppermute | solution.py:16
  10.3 1.8 %shard_map.81.diag_ref = f32[16,2048]{1,0:T(8,128)S(1)} custom-call(bf16[16,2048]{1,0:T(8,128)(2,1)S(1)} %get-tuple-element.16.xb_ref, bf16[4,512,512]{2,1,0:T(8,128)(2,1)} %leaf_hbm.1), custom_call_target="tpu_custom_call" | custom-call | flops 33554432 | bytes 2097152 | tf_op jit(solution)/shard_map/pallas_call | solution.py:28
  12.1 7.0 %collective-permute-done.3.half_ref = f32[16,2048]{1,0:T(8,128)S(1)} collective-permute-done((f32[16,2048]{1,0:T(8,128)S(1)}, f32[16,2048]{1,0:T(8,128)S(1)}, u32[]{:S(2)}, u32[]{:S(2)}) %collective-permute-start.3) | collective-permute-done | bytes 131104 | tf_op jit(solution)/shard_map/ppermute | solution.py:16
  19.2 0.0 collective-permute-done.4.below_ref
  19.2 0.7 %shard_map.83 = f32[16,2048]{1,0:T(8,128)} custom-call(f32[16,2048]{1,0:T(8,128)S(1)} %collective-permute-done.3.half_ref, f32[16,2048]{1,0:T(8,128)S(1)} %collective-permute-done.4.below_ref, f32[16,2048]{1,0:T(8,128)S(1)} %shard_map.81.diag_ref, f32[8,128]{1,0:T(8,128)S(1)} %shard_map.82._), custom_call_target="tpu_custom_call" | custom-call | flops 65536 | bytes 524288 | tf_op jit(solution)/shard_map/pallas_call | solution.py:28
  (5 shorter events, 0.1 us)
Async XLA Ops:
  0.0 7.8 %copy-start = (bf16[2,64,2048]{2,1,0:T(8,128)(2,1)S(1)}, bf16[2,64,2048]{2,1,0:T(8,128)(2,1)}, u32[]{:S(2)}) copy-start(bf16[2,64,2048]{2,1,0:T(8,128)(2,1)} %param.10) | copy-start | bytes 1572868
  0.0 7.8 %copy-start.1 = (s32[2,8]{1,0:T(2,128)S(1)}, s32[2,8]{1,0:T(2,128)}, u32[]{:S(2)}) copy-start(s32[2,8]{1,0:T(2,128)} %refs_2_.1) | copy-start | bytes 196
  1.5 1.7 %collective-permute-start = (f32[272,128]{1,0:T(8,128)S(1)}, f32[272,128]{1,0:T(8,128)S(1)}, u32[]{:S(2)}, u32[]{:S(2)}) collective-permute-start(f32[272,128]{1,0:T(8,128)S(1)} %get-tuple-element.11.refs_0_), channel_id=1, source_target_pairs={{0,1},{1,0},{2,3},{3,2},{4,5},{5,4},{6,7},{7,6},{8,9},{9,8},{10,11... | collective-permute-start | bytes 417800 | tf_op jit(solution)/shard_map/ppermute | solution.py:20
  1.6 4.0 %collective-permute-start.2 = (f32[64,128]{1,0:T(8,128)S(1)}, f32[64,128]{1,0:T(8,128)S(1)}, u32[]{:S(2)}, u32[]{:S(2)}) collective-permute-start(f32[64,128]{1,0:T(8,128)S(1)} %get-tuple-element.13.refs_0_), channel_id=1, source_target_pairs={{0,2},{1,3},{2,0},{3,1},{4,6},{5,7},{6,4},{7,5},{8,10},{9,11},{10,... | collective-permute-start | bytes 98312 | tf_op jit(solution)/shard_map/ppermute | solution.py:24
  3.6 4.2 %collective-permute-start.1 = (f32[112,128]{1,0:T(8,128)S(1)}, f32[112,128]{1,0:T(8,128)S(1)}, u32[]{:S(2)}, u32[]{:S(2)}) collective-permute-start(f32[112,128]{1,0:T(8,128)S(1)} %shard_map.76.refs_1_.refs_0_), channel_id=1, source_target_pairs={{0,2},{1,3},{2,0},{3,1},{4,6},{5,7},{6,4},{7,5},{8,10},{9,11},{10,... | collective-permute-start | bytes 172040 | tf_op jit(solution)/shard_map/ppermute | solution.py:24
  8.3 10.9 %collective-permute-start.3 = (f32[16,2048]{1,0:T(8,128)S(1)}, f32[16,2048]{1,0:T(8,128)S(1)}, u32[]{:S(2)}, u32[]{:S(2)}) collective-permute-start(f32[16,2048]{1,0:T(8,128)S(1)} %get-tuple-element.14), channel_id=1, source_target_pairs={{0,16},{4,20},{8,24},{12,28},{16,0},{20,4},{24,8},{28,12},{1,17},{... | collective-permute-start | bytes 393224 | tf_op jit(solution)/shard_map/ppermute | solution.py:16
  8.9 10.3 %collective-permute-start.4 = (f32[16,2048]{1,0:T(8,128)S(1)}, f32[16,2048]{1,0:T(8,128)S(1)}, u32[]{:S(2)}, u32[]{:S(2)}) collective-permute-start(f32[16,2048]{1,0:T(8,128)S(1)} %shard_map.80), channel_id=1, source_target_pairs={{0,28},{4,0},{8,4},{12,8},{16,12},{20,16},{24,20},{28,24},{1,29},{... | collective-permute-start | bytes 393224 | tf_op jit(solution)/shard_map/ppermute | solution.py:16

commit v31 on v30

--- a/solution.py
+++ b/solution.py
@@ -69,8 +69,7 @@
     levels, sections, _, k, _ = mixing_ref.shape
     vectors = field_ref.shape[0]
     pairs = [(col_hbm, col_ref), (field_hbm, field_ref)]
-    pairs += [(mixing_hbm.at[level], mixing_ref.at[level]) for level in range(levels)]
-    pairs.append((perm_hbm, perm_ref))
+    pairs += [(mixing_hbm, mixing_ref), (perm_hbm, perm_ref)]
     copies = [pltpu.make_async_copy(*pair, sems.at[n]) for n, pair in enumerate(pairs)]
     for copy in copies:
         copy.start()
@@ -273,7 +272,7 @@
             pltpu.VMEM((width, rows), BF16),
             pltpu.VMEM(mixing.shape[1:], BF16),
             pltpu.VMEM(rank_perm.shape, jnp.int32),
-            pltpu.SemaphoreType.DMA((1 + levels + 2,)),
+            pltpu.SemaphoreType.DMA((4,)),
         ],
     )
     weight_cost = (4 * width * width * sections, 8 * width * width * sections)

time: 20 us -> 20 us (level)
  no operation moved by 1% of the time
where the time goes in v31:
time: 20 us; the launch traced here: 19.9 us
  waiting for transfers between devices  9.94 us (50%)
  Pallas kernels  5.16 us (26%)
  starting transfers between devices  4.68 us (23%)
    ppermute x2, waiting for transfers between devices, shifted(): lax.ppermute(value, axis, [(source, (source + distance) % size) for sourc...  7.04 us
    pallas_call x11, Pallas kernels, call(): pl.pallas_call(body, out_shape=shapes, in_specs=specs, out_specs=jax.tree...  5.16 us
    ppermute x2, waiting for transfers between devices, across(): lax.ppermute(value, 'bf', [(n, n ^ 1 << bit) for n in range(lax.axis_size...  2.9 us
    ppermute x2, starting transfers between devices, across(): lax.ppermute(value, 'bf', [(n, n ^ 1 << bit) for n in range(lax.axis_size...  2.84 us
    ppermute x2, starting transfers between devices, shifted(): lax.ppermute(value, axis, [(source, (source + distance) % size) for sourc...  1.77 us
  transfers between devices with their start and end apart: 5, of which 3 were waited for; matrix products, arithmetic and copies ran while one was open for 0% of the time, Pallas kernels for 12%

profile of v31, /device:TPU:24, one launch (start us, length us, event | category | flops | bytes accessed | tf_op | source)
XLA Modules:
  0.0 19.9 jit_solution(5405008252904393540)
XLA Ops:
  0.0 0.0 copy-start
  0.0 0.0 copy-start.1
  0.0 1.5 %shard_map.73 = (bf16[16,2048]{1,0:T(8,128)(2,1)S(1)}, f32[272,128]{1,0:T(8,128)S(1)}, f32[256,128]{1,0:T(8,128)S(1)}, f32[64,128]{1,0:T(8,128)S(1)}) custom-call(f32[16,2048]{1,0:T(8,128)} %refs_0_.1, bf16[128,2048]{1,0:T(8,128)(2,1)} %bitcast.5, bf16[2,4,2,64,64]{4,3,2,1,0:T(8,128)(2,1)} %bitcast.6, s32[2,64]{1,0:T(2,128)} %refs_3_.1), custom_call_target="tpu_custom_call" | custom-call | flops 8388608 | bytes 786432 | tf_op jit(solution)/shard_map/pallas_call | solution.py:28
  1.5 0.1 collective-permute-start
  1.6 1.6 %collective-permute-start.2 = (f32[64,128]{1,0:T(8,128)S(1)}, f32[64,128]{1,0:T(8,128)S(1)}, u32[]{:S(2)}, u32[]{:S(2)}) collective-permute-start(f32[64,128]{1,0:T(8,128)S(1)} %get-tuple-element.13.refs_0_), channel_id=1, source_target_pairs={{0,2},{1,3},{2,0},{3,1},{4,6},{5,7},{6,4},{7,5},{8,10},{9,11},{10,... | collective-permute-start | bytes 98312 | tf_op jit(solution)/shard_map/ppermute | solution.py:24
  3.2 0.0 collective-permute-done.refs_0_.refs_1_
  3.3 0.4 %shard_map.76.refs_1_.refs_0_ = f32[112,128]{1,0:T(8,128)S(1)} custom-call(f32[272,128]{1,0:T(8,128)S(1)} %get-tuple-element.11.refs_0_, f32[272,128]{1,0:T(8,128)S(1)} %collective-permute-done.refs_0_.refs_1_, bf16[4,256,128]{2,1,0:T(8,128)(2,1)S(1)} %shard_map.74.refs_2_, bf16[2,256,128]{2,1,0:T(8,128)(2,1)S(1)} %shard_map.75.refs_3_), custom_call_target="tpu_custom_call" | custom-call | flops 6291456 | bytes 131072 | tf_op jit(solution)/shard_map/pallas_call | solution.py:28
  3.6 1.3 %collective-permute-start.1 = (f32[112,128]{1,0:T(8,128)S(1)}, f32[112,128]{1,0:T(8,128)S(1)}, u32[]{:S(2)}, u32[]{:S(2)}) collective-permute-start(f32[112,128]{1,0:T(8,128)S(1)} %shard_map.76.refs_1_.refs_0_), channel_id=1, source_target_pairs={{0,2},{1,3},{2,0},{3,1},{4,6},{5,7},{6,4},{7,5},{8,10},{9,11},{10,... | collective-permute-start | bytes 172040 | tf_op jit(solution)/shard_map/ppermute | solution.py:24
  4.9 0.7 %collective-permute-done.2.refs_0_ = f32[64,128]{1,0:T(8,128)S(1)} collective-permute-done((f32[64,128]{1,0:T(8,128)S(1)}, f32[64,128]{1,0:T(8,128)S(1)}, u32[]{:S(2)}, u32[]{:S(2)}) %collective-permute-start.2) | collective-permute-done | bytes 32800 | tf_op jit(solution)/shard_map/ppermute | solution.py:24
  5.7 2.2 %collective-permute-done.1.refs_1_ = f32[112,128]{1,0:T(8,128)S(1)} collective-permute-done((f32[112,128]{1,0:T(8,128)S(1)}, f32[112,128]{1,0:T(8,128)S(1)}, u32[]{:S(2)}, u32[]{:S(2)}) %collective-permute-start.1) | collective-permute-done | bytes 57376 | tf_op jit(solution)/shard_map/ppermute | solution.py:24
  7.8 0.0 copy-done
  7.8 0.0 copy-done.1
  7.8 0.5 %shard_map.79 = (f32[16,128]{1,0:T(8,128)S(1)}, f32[16,2048]{1,0:T(8,128)S(1)}) custom-call(f32[112,128]{1,0:T(8,128)S(1)} %shard_map.76.refs_1_.refs_0_, f32[112,128]{1,0:T(8,128)S(1)} %collective-permute-done.1.refs_1_, bf16[4,256,128]{2,1,0:T(8,128)(2,1)S(1)} %shard_map.74.refs_2_, bf16[2,256,128]{2,1,0:T(8,128)(2,1)S(1)} %shard_map.77.refs_3_, ...), custom_call_target="tpu_custom_call" | custom-call | flops 8388608 | bytes 1048576 | tf_op jit(solution)/shard_map/pallas_call | solution.py:28
  8.3 0.4 %collective-permute-start.3 = (f32[16,2048]{1,0:T(8,128)S(1)}, f32[16,2048]{1,0:T(8,128)S(1)}, u32[]{:S(2)}, u32[]{:S(2)}) collective-permute-start(f32[16,2048]{1,0:T(8,128)S(1)} %get-tuple-element.14), channel_id=1, source_target_pairs={{0,16},{4,20},{8,24},{12,28},{16,0},{20,4},{24,8},{28,12},{1,17},{... | collective-permute-start | bytes 393224 | tf_op jit(solution)/shard_map/ppermute | solution.py:16
  8.7 0.2 shard_map.80
  8.9 1.4 %collective-permute-start.4 = (f32[16,2048]{1,0:T(8,128)S(1)}, f32[16,2048]{1,0:T(8,128)S(1)}, u32[]{:S(2)}, u32[]{:S(2)}) collective-permute-start(f32[16,2048]{1,0:T(8,128)S(1)} %shard_map.80), channel_id=1, source_target_pairs={{0,28},{4,0},{8,4},{12,8},{16,12},{20,16},{24,20},{28,24},{1,29},{... | collective-permute-start | bytes 393224 | tf_op jit(solution)/shard_map/ppermute | solution.py:16
  10.3 1.8 %shard_map.81.diag_ref = f32[16,2048]{1,0:T(8,128)S(1)} custom-call(bf16[16,2048]{1,0:T(8,128)(2,1)S(1)} %get-tuple-element.16.xb_ref, bf16[4,512,512]{2,1,0:T(8,128)(2,1)} %leaf_hbm.1), custom_call_target="tpu_custom_call" | custom-call | flops 33554432 | bytes 2097152 | tf_op jit(solution)/shard_map/pallas_call | solution.py:28
  12.1 7.0 %collective-permute-done.3.half_ref = f32[16,2048]{1,0:T(8,128)S(1)} collective-permute-done((f32[16,2048]{1,0:T(8,128)S(1)}, f32[16,2048]{1,0:T(8,128)S(1)}, u32[]{:S(2)}, u32[]{:S(2)}) %collective-permute-start.3) | collective-permute-done | bytes 131104 | tf_op jit(solution)/shard_map/ppermute | solution.py:16
  19.2 0.0 collective-permute-done.4.below_ref
  19.2 0.7 %shard_map.83 = f32[16,2048]{1,0:T(8,128)} custom-call(f32[16,2048]{1,0:T(8,128)S(1)} %collective-permute-done.3.half_ref, f32[16,2048]{1,0:T(8,128)S(1)} %collective-permute-done.4.below_ref, f32[16,2048]{1,0:T(8,128)S(1)} %shard_map.81.diag_ref, f32[8,128]{1,0:T(8,128)S(1)} %shard_map.82._), custom_call_target="tpu_custom_call" | custom-call | flops 65536 | bytes 524288 | tf_op jit(solution)/shard_map/pallas_call | solution.py:28
  (5 shorter events, 0.1 us)
Async XLA Ops:
  0.0 7.8 %copy-start = (bf16[2,64,2048]{2,1,0:T(8,128)(2,1)S(1)}, bf16[2,64,2048]{2,1,0:T(8,128)(2,1)}, u32[]{:S(2)}) copy-start(bf16[2,64,2048]{2,1,0:T(8,128)(2,1)} %param.10) | copy-start | bytes 1572868
  0.0 7.8 %copy-start.1 = (s32[2,8]{1,0:T(2,128)S(1)}, s32[2,8]{1,0:T(2,128)}, u32[]{:S(2)}) copy-start(s32[2,8]{1,0:T(2,128)} %refs_2_.1) | copy-start | bytes 196
  1.5 1.7 %collective-permute-start = (f32[272,128]{1,0:T(8,128)S(1)}, f32[272,128]{1,0:T(8,128)S(1)}, u32[]{:S(2)}, u32[]{:S(2)}) collective-permute-start(f32[272,128]{1,0:T(8,128)S(1)} %get-tuple-element.11.refs_0_), channel_id=1, source_target_pairs={{0,1},{1,0},{2,3},{3,2},{4,5},{5,4},{6,7},{7,6},{8,9},{9,8},{10,11... | collective-permute-start | bytes 417800 | tf_op jit(solution)/shard_map/ppermute | solution.py:20
  1.6 4.0 %collective-permute-start.2 = (f32[64,128]{1,0:T(8,128)S(1)}, f32[64,128]{1,0:T(8,128)S(1)}, u32[]{:S(2)}, u32[]{:S(2)}) collective-permute-start(f32[64,128]{1,0:T(8,128)S(1)} %get-tuple-element.13.refs_0_), channel_id=1, source_target_pairs={{0,2},{1,3},{2,0},{3,1},{4,6},{5,7},{6,4},{7,5},{8,10},{9,11},{10,... | collective-permute-start | bytes 98312 | tf_op jit(solution)/shard_map/ppermute | solution.py:24
  3.6 4.2 %collective-permute-start.1 = (f32[112,128]{1,0:T(8,128)S(1)}, f32[112,128]{1,0:T(8,128)S(1)}, u32[]{:S(2)}, u32[]{:S(2)}) collective-permute-start(f32[112,128]{1,0:T(8,128)S(1)} %shard_map.76.refs_1_.refs_0_), channel_id=1, source_target_pairs={{0,2},{1,3},{2,0},{3,1},{4,6},{5,7},{6,4},{7,5},{8,10},{9,11},{10,... | collective-permute-start | bytes 172040 | tf_op jit(solution)/shard_map/ppermute | solution.py:24
  8.3 10.9 %collective-permute-start.3 = (f32[16,2048]{1,0:T(8,128)S(1)}, f32[16,2048]{1,0:T(8,128)S(1)}, u32[]{:S(2)}, u32[]{:S(2)}) collective-permute-start(f32[16,2048]{1,0:T(8,128)S(1)} %get-tuple-element.14), channel_id=1, source_target_pairs={{0,16},{4,20},{8,24},{12,28},{16,0},{20,4},{24,8},{28,12},{1,17},{... | collective-permute-start | bytes 393224 | tf_op jit(solution)/shard_map/ppermute | solution.py:16
  8.9 10.3 %collective-permute-start.4 = (f32[16,2048]{1,0:T(8,128)S(1)}, f32[16,2048]{1,0:T(8,128)S(1)}, u32[]{:S(2)}, u32[]{:S(2)}) collective-permute-start(f32[16,2048]{1,0:T(8,128)S(1)} %shard_map.80), channel_id=1, source_target_pairs={{0,28},{4,0},{8,4},{12,8},{16,12},{20,16},{24,20},{28,24},{1,29},{... | collective-permute-start | bytes 393224 | tf_op jit(solution)/shard_map/ppermute | solution.py:16
